TPU v7x, 256 devices: a whole 4x4x8 slice. The times are simulated.
256 devices in a mesh: section: 16 (over z_hi, x, core), dp: 16 (over z_lo, y).
Axes of the slice: x: 4, y: 4, z: 8 (z_hi: 2, z_lo: 4; z = z_hi * 4 + z_lo), core: 2. Of those that a mesh axis runs over, the one named last changes fastest.
Arguments:
- inputs: bfloat16 [3, 1024, 3072], P(None, 'dp'), may hold values from -6 to 6
- cotangent: bfloat16 [3, 1024, 3072], P(None, 'dp'), may hold values from -6 to 6
- weight: bfloat16 [16, 3072, 3072], P('section', 'dp'), may hold values from -0.109375 to 0.109375
- gain: float32 [16, 3072], replicated, may hold values from 0.25 to 1.75
Outputs:
- weight_grad: bfloat16 [16, 3072, 3072], P('section', 'dp')
- gain_grad: float32 [16, 3072], P('section')
- input_grad: bfloat16 [3, 1024, 3072], P(None, 'dp', 'section')
- final_hidden: bfloat16 [3, 1024, 3072], P(None, 'dp', 'section')
All inputs are finite; a program needn't handle non-finite values.
Results may differ from a plain program's by a relative error of at most 0.035.
Values may be sent and summed in bfloat16 or wider, within the bound.
No kernel may reach another device: no remote copies, remote signals or barrier semaphores. Data moves between devices by JAX's collectives and lax.ppermute only.
A program may use at most 128 MiB of HBM per device.

v0:
```python
import jax
import jax.numpy as jnp
from jax import lax
from jax.sharding import PartitionSpec as P

EPSILON = 1e-06
HALF_ROOT = 0.7071067811865476
DENSITY = 0.3989422804014327


def from_behind(block, axis, distance):
    devices = range(lax.axis_size(axis))
    route = [(i - distance, i) for i in devices if i - distance in devices]
    return lax.ppermute(block, axis, route)


def normalize(hidden):
    values = hidden.astype(jnp.float32)
    scale = lax.rsqrt(jnp.mean(values * values, axis=-1, keepdims=True) + EPSILON)
    return (values, scale, values * scale)


def gelu_value(pre):
    return 0.5 * pre * (1.0 + jax.scipy.special.erf(pre * HALF_ROOT))


def gelu_slope(pre):
    return (
        0.5 * (1.0 + jax.scipy.special.erf(pre * HALF_ROOT))
        + pre * jnp.exp(-0.5 * pre * pre) * DENSITY
    )


def layer_forward(hidden, gain_row, matrix):
    values, scale, unit = normalize(hidden)
    normed = (unit * gain_row).astype(jnp.bfloat16)
    pre = jnp.dot(normed, matrix, preferred_element_type=jnp.float32)
    return ((values + gelu_value(pre)).astype(jnp.bfloat16), pre)


def layer_backward(upstream, hidden, pre, gain_row, matrix):
    values, scale, unit = normalize(hidden)
    normed = (unit * gain_row).astype(jnp.bfloat16)
    arriving = upstream.astype(jnp.float32)
    slope = (arriving * gelu_slope(pre)).astype(jnp.bfloat16)
    normed_grad = lax.dot_general(
        slope, matrix, (((1,), (1,)), ((), ())), preferred_element_type=jnp.float32
    )
    gain_term = jnp.sum(normed_grad * unit, axis=0)
    unit_grad = normed_grad * gain_row
    centred = unit_grad - unit * jnp.mean(unit_grad * unit, axis=-1, keepdims=True)
    downstream = (arriving + scale * centred).astype(jnp.bfloat16)
    return (downstream, normed, slope, gain_term)


def place(stack, slot_index, value):
    return lax.dynamic_update_index_in_dim(stack, value, slot_index, 0)


def on_device(inputs, cotangent, weight, gain):
    segment_count = lax.axis_size("section")
    segment_index = lax.axis_index("section")
    micro_count, row_count, features = inputs.shape
    next_shard = from_behind(weight[0], "section", -1)
    own_matrix, next_matrix = (
        lax.all_gather(weight[0], "dp", axis=0, tiled=True),
        lax.all_gather(next_shard, "dp", axis=0, tiled=True),
    )
    gain_row = lax.dynamic_index_in_dim(gain, segment_index, 0, keepdims=False)
    next_index = jnp.minimum(segment_index + 1, segment_count - 1)
    next_gain = lax.dynamic_index_in_dim(gain, next_index, 0, keepdims=False)
    forward_total = micro_count + segment_count - 1

    def forward_step(step, carry):
        near_arrive, far_recent, far_older, hidden_stack, pre_stack, final_stack = carry
        slot = step - segment_index
        is_live = (slot >= 0) & (slot < micro_count)
        slot_index = jnp.clip(slot, 0, micro_count - 1)
        is_odd = slot_index % 2 == 1
        entering = lax.dynamic_index_in_dim(inputs, slot_index, 0, keepdims=False)
        use_far = (segment_index >= 2) & is_odd
        current = jnp.where(
            segment_index == 0, entering, jnp.where(use_far, far_older, near_arrive)
        )

        def forward_compute_step(operands):
            hiddens, pres, finals, present = operands
            result, pre = layer_forward(present, gain_row, own_matrix)
            ahead, _ = layer_forward(result, next_gain, next_matrix)
            keep_last = (segment_index == segment_count - 1) & jnp.logical_not(is_odd)
            keep_ahead = (segment_index == segment_count - 2) & is_odd
            existing = lax.dynamic_index_in_dim(finals, slot_index, 0, keepdims=False)
            chosen = jnp.where(keep_last, result, jnp.where(keep_ahead, ahead, existing))
            return (
                result,
                ahead,
                place(hiddens, slot_index, present),
                place(pres, slot_index, pre),
                place(finals, slot_index, chosen),
            )

        def forward_skip_step(operands):
            hiddens, pres, finals, present = operands
            return (jnp.zeros_like(present), jnp.zeros_like(present), hiddens, pres, finals)

        result, ahead, hidden_stack, pre_stack, final_stack = lax.cond(
            is_live,
            forward_compute_step,
            forward_skip_step,
            (hidden_stack, pre_stack, final_stack, current),
        )
        near_arrive = from_behind(result, "section", 1)
        far_arrive = from_behind(ahead, "section", 2)
        return (near_arrive, far_arrive, far_recent, hidden_stack, pre_stack, final_stack)

    hidden_stack = jnp.zeros((micro_count, row_count, features), jnp.bfloat16)
    pre_stack = jnp.zeros((micro_count, row_count, features), jnp.float32)
    final_stack = jnp.zeros((micro_count, row_count, features), jnp.bfloat16)
    start_arriving = jnp.zeros((row_count, features), jnp.bfloat16)
    carried_forward = (
        start_arriving,
        start_arriving,
        start_arriving,
        hidden_stack,
        pre_stack,
        final_stack,
    )
    _, _, _, hidden_stack, pre_stack, final_stack = lax.fori_loop(
        0, forward_total, forward_step, carried_forward
    )
    backward_total = micro_count + segment_count - 1

    def backward_step(step, carry):
        arriving, normed_stack, slope_stack, first_stack, gain_total = carry
        slot = step - (segment_count - 1 - segment_index)
        is_live = (slot >= 0) & (slot < micro_count)
        slot_index = jnp.clip(slot, 0, micro_count - 1)
        entering = lax.dynamic_index_in_dim(cotangent, slot_index, 0, keepdims=False)
        current = jnp.where(segment_index == segment_count - 1, entering, arriving)

        def backward_compute_step(operands):
            normeds, slopes, firsts, gains_sum, present = operands
            hidden = lax.dynamic_index_in_dim(hidden_stack, slot_index, 0, keepdims=False)
            pre = lax.dynamic_index_in_dim(pre_stack, slot_index, 0, keepdims=False)
            downstream, normed, slope, gain_term = layer_backward(
                present, hidden, pre, gain_row, own_matrix
            )
            return (
                downstream,
                place(normeds, slot_index, normed),
                place(slopes, slot_index, slope),
                place(firsts, slot_index, downstream),
                gains_sum + gain_term,
            )

        def backward_skip_step(operands):
            normeds, slopes, firsts, gains_sum, present = operands
            return (jnp.zeros_like(present), normeds, slopes, firsts, gains_sum)

        downstream, normed_stack, slope_stack, first_stack, gain_total = lax.cond(
            is_live,
            backward_compute_step,
            backward_skip_step,
            (normed_stack, slope_stack, first_stack, gain_total, current),
        )
        arriving = from_behind(downstream, "section", -1)
        return (arriving, normed_stack, slope_stack, first_stack, gain_total)

    empty_stack = jnp.zeros((micro_count, row_count, features), jnp.bfloat16)
    start_gain = jnp.zeros((features,), jnp.float32)
    carried = (start_arriving, empty_stack, empty_stack, empty_stack, start_gain)
    _, normed_stack, slope_stack, first_stack, gain_total = lax.fori_loop(
        0, backward_total, backward_step, carried
    )
    block_rows = micro_count * row_count
    normed_all = normed_stack.reshape(block_rows, features)
    slope_all = slope_stack.reshape(block_rows, features)
    summed = lax.psum_scatter(
        lax.dot_general(
            normed_all, slope_all, (((0,), (0,)), ((), ())), preferred_element_type=jnp.float32
        ).astype(jnp.bfloat16),
        "dp",
        scatter_dimension=0,
        tiled=True,
    )
    gain_grad = lax.psum(gain_total, "dp")
    first_terms = jnp.where(segment_index == 0, first_stack.astype(jnp.float32), 0.0)
    final_terms = final_stack.astype(jnp.float32)
    input_sum, final_sum = (
        lax.psum_scatter(
            first_terms.astype(jnp.bfloat16), "section", scatter_dimension=2, tiled=True
        ).astype(jnp.float32),
        lax.psum_scatter(
            final_terms.astype(jnp.bfloat16), "section", scatter_dimension=2, tiled=True
        ).astype(jnp.float32),
    )
    return (
        summed[None],
        gain_grad[None],
        input_sum.astype(jnp.bfloat16),
        final_sum.astype(jnp.bfloat16),
    )


def solution(mesh):
    in_specs = (P(None, "dp", None), P(None, "dp", None), P("section", "dp", None), P())
    out_specs = (
        P("section", "dp", None),
        P("section", None),
        P(None, "dp", "section"),
        P(None, "dp", "section"),
    )
    return jax.shard_map(
        on_device, mesh=mesh, in_specs=in_specs, out_specs=out_specs, check_vma=False
    )
```

profile of v0, /device:TPU:128, one launch (start us, length us, event | category | flops | bytes accessed | tf_op | source)
XLA Modules:
  0.0 1891.8 jit_solution(13895290676326311676)
XLA Ops:
  10.7 17.5 collective-permute-done.3
  30.9 191.7 %all-gather.6.cloned.1.call-done = bf16[1,3072,3072]{2,1,0:T(8,128)(2,1)} async-done(((bf16[1,192,3072]{2,1,0:T(8,128)(2,1)}), bf16[1,3072,3072]{2,1,0:T(8,128)(2,1)}) %all-gather.6.cloned.1.call-update) | async-done | bytes 18874384 | tf_op jit(solution)/shard_map/all_gather | solution.py:66
  222.6 213.4 %all-gather.4.cloned.1.call-done = bf16[3072,3072]{1,0:T(8,128)(2,1)} async-done(((bf16[192,3072]{1,0:T(8,128)(2,1)}), bf16[3072,3072]{1,0:T(8,128)(2,1)}) %all-gather.4.cloned.1.call-update) | async-done | bytes 18874384 | tf_op jit(solution)/shard_map/all_gather | solution.py:67
  438.7 638.7 %while.48 = (s32[]{:T(128)}, bf16[64,3072]{1,0:T(8,128)(2,1)S(1)}, bf16[64,3072]{1,0:T(8,128)(2,1)S(1)}, bf16[64,3072]{1,0:T(8,128)(2,1)}, bf16[3,64,3072]{2,1,0...) while((s32[]{:T(128)}, bf16[64,3072]{1,0:T(8,128)(2,1)S(1)}, ...), condition=%wide.region_5.6_spmd, body=%wide.region_0.5_spmd.sunk | while | flops 2422210816 | bytes 50801520 | solution.py:128
  446.3 14.2 collective-permute-done.1
  469.7 14.2 collective-permute-done.1
  491.4 14.2 collective-permute-done.1
  513.2 14.2 collective-permute-done.1
  534.9 29.7 %collective-permute-done.1 = bf16[64,3072]{1,0:T(8,128)(2,1)S(1)} collective-permute-done((bf16[64,3072]{1,0:T(8,128)(2,1)}, bf16[64,3072]{1,0:T(8,128)(2,1)S(1)}, u32[]{:S(2)}, u32[]{:S(2)}) %collective-permute-start.1) | collective-permute-done | bytes 393248 | tf_op jit(solution)/shard_map/while/body/eval_jaxpr/ppermute | solution.py:14
  570.8 55.5 %collective-permute-done.1 = bf16[64,3072]{1,0:T(8,128)(2,1)S(1)} collective-permute-done((bf16[64,3072]{1,0:T(8,128)(2,1)}, bf16[64,3072]{1,0:T(8,128)(2,1)S(1)}, u32[]{:S(2)}, u32[]{:S(2)}) %collective-permute-start.1) | collective-permute-done | bytes 393248 | tf_op jit(solution)/shard_map/while/body/eval_jaxpr/ppermute | solution.py:14
  632.5 56.3 %collective-permute-done.1 = bf16[64,3072]{1,0:T(8,128)(2,1)S(1)} collective-permute-done((bf16[64,3072]{1,0:T(8,128)(2,1)}, bf16[64,3072]{1,0:T(8,128)(2,1)S(1)}, u32[]{:S(2)}, u32[]{:S(2)}) %collective-permute-start.1) | collective-permute-done | bytes 393248 | tf_op jit(solution)/shard_map/while/body/eval_jaxpr/ppermute | solution.py:14
  695.0 33.6 %collective-permute-done.1 = bf16[64,3072]{1,0:T(8,128)(2,1)S(1)} collective-permute-done((bf16[64,3072]{1,0:T(8,128)(2,1)}, bf16[64,3072]{1,0:T(8,128)(2,1)S(1)}, u32[]{:S(2)}, u32[]{:S(2)}) %collective-permute-start.1) | collective-permute-done | bytes 393248 | tf_op jit(solution)/shard_map/while/body/eval_jaxpr/ppermute | solution.py:14
  728.8 24.2 %conditional.4 = (bf16[64,3072]{1,0:T(8,128)(2,1)}, bf16[64,3072]{1,0:T(8,128)(2,1)}, bf16[3,64,3072]{2,1,0:T(8,128)(2,1)S(1)}, f32[3,64,3072]{2,1,0:T(8,128)}, bf16[3,64,3072]{2,1,0:T(8,128)(2,1)S(1)}) conditional(s32[]{:T(128)} %convert_element_type.215, (bf16[3,64,3072]{2,1,0:T(8,128)(2,1)S(1)}, f32[3,64,3072]{2,1,0:T(8,128)}, ...), branch_computations={%region_1.1_spmd, %region_2.4_spmd} | conditional | flops 2422210816 | bytes 46082508 | solution.py:106
  730.2 10.8 fusion.4
  741.9 11.0 bitcast_dynamic-update-slice_fusion.1
  757.6 14.2 collective-permute-done.1
  773.2 24.3 %conditional.4 = (bf16[64,3072]{1,0:T(8,128)(2,1)}, bf16[64,3072]{1,0:T(8,128)(2,1)}, bf16[3,64,3072]{2,1,0:T(8,128)(2,1)S(1)}, f32[3,64,3072]{2,1,0:T(8,128)}, bf16[3,64,3072]{2,1,0:T(8,128)(2,1)S(1)}) conditional(s32[]{:T(128)} %convert_element_type.215, (bf16[3,64,3072]{2,1,0:T(8,128)(2,1)S(1)}, f32[3,64,3072]{2,1,0:T(8,128)}, ...), branch_computations={%region_1.1_spmd, %region_2.4_spmd} | conditional | flops 2422210816 | bytes 46082508 | solution.py:106
  774.6 10.8 fusion.4
  786.4 11.0 bitcast_dynamic-update-slice_fusion.1
  802.1 14.2 collective-permute-done.1
  817.7 24.2 %conditional.4 = (bf16[64,3072]{1,0:T(8,128)(2,1)}, bf16[64,3072]{1,0:T(8,128)(2,1)}, bf16[3,64,3072]{2,1,0:T(8,128)(2,1)S(1)}, f32[3,64,3072]{2,1,0:T(8,128)}, bf16[3,64,3072]{2,1,0:T(8,128)(2,1)S(1)}) conditional(s32[]{:T(128)} %convert_element_type.215, (bf16[3,64,3072]{2,1,0:T(8,128)(2,1)S(1)}, f32[3,64,3072]{2,1,0:T(8,128)}, ...), branch_computations={%region_1.1_spmd, %region_2.4_spmd} | conditional | flops 2422210816 | bytes 46082508 | solution.py:106
  819.0 10.8 fusion.4
  830.8 11.0 bitcast_dynamic-update-slice_fusion.1
  846.5 14.2 collective-permute-done.1
  863.6 14.4 collective-permute-start.1
  886.5 7.0 collective-permute-done
  895.0 21.3 %collective-permute-start.1 = (bf16[64,3072]{1,0:T(8,128)(2,1)}, bf16[64,3072]{1,0:T(8,128)(2,1)S(1)}, u32[]{:S(2)}, u32[]{:S(2)}) collective-permute-start(bf16[64,3072]{1,0:T(8,128)(2,1)} %get-tuple-element.1262), channel_id=1, source_target_pairs={{0,32},{16,48},{32,64},{48,80},{64,96},{80,112},{96,128},{112,144}... | collective-permute-start | bytes 1179656 | tf_op jit(solution)/shard_map/while/body/eval_jaxpr/ppermute | solution.py:14
  935.2 13.1 collective-permute-start
  955.1 9.8 collective-permute-start.1
  981.7 21.4 %collective-permute-start.1 = (bf16[64,3072]{1,0:T(8,128)(2,1)}, bf16[64,3072]{1,0:T(8,128)(2,1)S(1)}, u32[]{:S(2)}, u32[]{:S(2)}) collective-permute-start(bf16[64,3072]{1,0:T(8,128)(2,1)} %get-tuple-element.1262), channel_id=1, source_target_pairs={{0,32},{16,48},{32,64},{48,80},{64,96},{80,112},{96,128},{112,144}... | collective-permute-start | bytes 1179656 | tf_op jit(solution)/shard_map/while/body/eval_jaxpr/ppermute | solution.py:14
  1026.9 10.6 collective-permute-start
  1043.8 7.4 collective-permute-start.1
  1051.2 24.7 %collective-permute-start = (bf16[64,3072]{1,0:T(8,128)(2,1)}, bf16[64,3072]{1,0:T(8,128)(2,1)S(1)}, u32[]{:S(2)}, u32[]{:S(2)}) collective-permute-start(bf16[64,3072]{1,0:T(8,128)(2,1)} %get-tuple-element.1261), channel_id=1, source_target_pairs={{0,16},{16,32},{32,48},{48,64},{64,80},{80,96},{96,112},{112,128},... | collective-permute-start | bytes 1179656 | tf_op jit(solution)/shard_map/while/body/eval_jaxpr/ppermute | solution.py:14
  1081.1 377.5 %while.49 = (s32[]{:T(128)}, bf16[64,3072]{1,0:T(8,128)(2,1)S(1)}, bf16[3,64,3072]{2,1,0:T(8,128)(2,1)}, bf16[3,64,3072]{2,1,0:T(8,128)(2,1)}, bf16[3,64,3072]{2...) while((s32[]{:T(128)}, bf16[64,3072]{1,0:T(8,128)(2,1)S(1)}, ...), condition=%wide.region_12.13_spmd, body=%wide.region_6.12_spmd.sunk | while | flops 1214841088 | bytes 28009140 | solution.py:172
  1083.1 7.3 collective-permute-done.2
  1090.5 7.8 collective-permute-start.2
  1103.6 9.8 collective-permute-start.2
  1118.8 9.8 collective-permute-start.2
  1133.9 9.8 collective-permute-start.2
  1149.1 9.8 collective-permute-start.2
  1164.3 9.8 collective-permute-start.2
  1174.1 66.9 %collective-permute-done.2 = bf16[64,3072]{1,0:T(8,128)(2,1)S(1)} collective-permute-done((bf16[64,3072]{1,0:T(8,128)(2,1)S(1)}, bf16[64,3072]{1,0:T(8,128)(2,1)S(1)}, u32[]{:S(2)}, u32[]{:S(2)}) %collective-permute-start.2) | collective-permute-done | bytes 393248 | tf_op jit(solution)/shard_map/while/body/eval_jaxpr/ppermute | solution.py:14
  1241.0 14.7 conditional.5
  1243.6 9.8 fusion.29
  1257.6 7.2 collective-permute-done.2
  1264.9 14.7 conditional.5
  1267.4 9.8 fusion.29
  1279.6 7.9 collective-permute-start.2
  1292.7 14.7 conditional.5
  1295.3 9.8 fusion.29
  1307.4 9.8 collective-permute-start.2
  1322.6 24.5 %collective-permute-start.2 = (bf16[64,3072]{1,0:T(8,128)(2,1)S(1)}, bf16[64,3072]{1,0:T(8,128)(2,1)S(1)}, u32[]{:S(2)}, u32[]{:S(2)}) collective-permute-start(bf16[64,3072]{1,0:T(8,128)(2,1)S(1)} %get-tuple-element.1279), channel_id=1, source_target_pairs={{16,0},{32,16},{48,32},{64,48},{80,64},{96,80},{112,96},{128,112},... | collective-permute-start | bytes 1179656 | tf_op jit(solution)/shard_map/while/body/eval_jaxpr/ppermute | solution.py:14
  1352.4 9.8 collective-permute-start.2
  1367.6 9.8 collective-permute-start.2
  1382.8 9.8 collective-permute-start.2
  1397.9 9.8 collective-permute-start.2
  1413.1 9.8 collective-permute-start.2
  1428.3 9.8 collective-permute-start.2
  1443.4 9.8 collective-permute-start.2
  1482.1 9.3 bitcast_convert_fusion
  1491.4 88.0 %psum.7 = f32[1,3072]{1,0:T(1,128)} all-reduce(f32[1,3072]{1,0:T(1,128)S(1)} %bitcast.90), channel_id=1, replica_groups=mesh['section'=16,'dp'=16] {'dp'}, use_global_device_ids=true, to_apply=%region_14.15 | all-reduce | flops 3072 | bytes 24576 | tf_op jit(solution)/shard_map/psum | solution.py:186
  1579.4 13.1 reduce-scatter.10.cloned.1.call-done
  1594.3 82.2 %reduce-scatter.12.cloned.1.call-done = bf16[192,192]{1,0:T(8,128)(2,1)} async-done(((bf16[3072,192]{1,0:T(8,128)(2,1)}), bf16[192,192]{1,0:T(8,128)(2,1)}) %reduce-scatter.12.cloned.1.call-update) | async-done | bytes 73744
  1678.3 207.0 %reduce-scatter.8.cloned.1.call-done = bf16[192,3072]{1,0:T(8,128)(2,1)} async-done(((bf16[3072,3072]{1,0:T(8,128)(2,1)}), bf16[192,3072]{1,0:T(8,128)(2,1)}) %reduce-scatter.8.cloned.1.call-update) | async-done | bytes 1179664 | tf_op jit(solution)/shard_map/reduce_scatter | solution.py:178
  (263 shorter events, 329.4 us)
Async XLA Ops:
  7.2 1.3 copy-start.3
  7.2 215.4 %all-gather.6.cloned.1.call-start = ((), (), s32[]{:S(2)}) async-start(), calls=%async_computation.5 | async-start | bytes 20054016 | tf_op jit(solution)/shard_map/all_gather | solution.py:66
  7.9 428.1 %all-gather.4.cloned.1.call-start = ((), (), s32[]{:S(2)}) async-start(), calls=%async_computation.3 | async-start | bytes 20054016 | tf_op jit(solution)/shard_map/all_gather | solution.py:67
  8.4 19.8 %collective-permute-start.3 = (bf16[192,3072]{1,0:T(8,128)(2,1)S(1)}, bf16[192,3072]{1,0:T(8,128)(2,1)S(1)}, u32[]{:S(2)}, u32[]{:S(2)}) collective-permute-start(bf16[192,3072]{1,0:T(8,128)(2,1)S(1)} %bitcast.87), channel_id=1, source_target_pairs={{16,0},{32,16},{48,32},{64,48},{80,64},{96,80},{112,96},{128,112},... | collective-permute-start | bytes 3538952 | tf_op jit(solution)/shard_map/ppermute | solution.py:14
  29.3 1563.3 %reduce-scatter.10.cloned.1.call-start = ((), (), s32[]{:S(2)}) async-start(), calls=%async_computation.6 | async-start | bytes 1671168
  440.3 20.2 %collective-permute-start.1 = (bf16[64,3072]{1,0:T(8,128)(2,1)}, bf16[64,3072]{1,0:T(8,128)(2,1)S(1)}, u32[]{:S(2)}, u32[]{:S(2)}) collective-permute-start(bf16[64,3072]{1,0:T(8,128)(2,1)} %get-tuple-element.1262), channel_id=1, source_target_pairs={{0,32},{16,48},{32,64},{48,80},{64,96},{80,112},{96,128},{112,144}... | collective-permute-start | bytes 1179656 | tf_op jit(solution)/shard_map/while/body/eval_jaxpr/ppermute | solution.py:14
  443.7 19.9 %collective-permute-start = (bf16[64,3072]{1,0:T(8,128)(2,1)}, bf16[64,3072]{1,0:T(8,128)(2,1)S(1)}, u32[]{:S(2)}, u32[]{:S(2)}) collective-permute-start(bf16[64,3072]{1,0:T(8,128)(2,1)} %get-tuple-element.1261), channel_id=1, source_target_pairs={{0,16},{16,32},{32,48},{48,64},{64,80},{80,96},{96,112},{112,128},... | collective-permute-start | bytes 1179656 | tf_op jit(solution)/shard_map/while/body/eval_jaxpr/ppermute | solution.py:14
  465.1 18.8 collective-permute-start.1
  467.0 18.3 collective-permute-start
  486.8 18.8 collective-permute-start.1
  488.8 18.3 collective-permute-start
  508.6 18.8 collective-permute-start.1
  510.5 18.3 collective-permute-start
  530.3 34.3 %collective-permute-start.1 = (bf16[64,3072]{1,0:T(8,128)(2,1)}, bf16[64,3072]{1,0:T(8,128)(2,1)S(1)}, u32[]{:S(2)}, u32[]{:S(2)}) collective-permute-start(bf16[64,3072]{1,0:T(8,128)(2,1)} %get-tuple-element.1262), channel_id=1, source_target_pairs={{0,32},{16,48},{32,64},{48,80},{64,96},{80,112},{96,128},{112,144}... | collective-permute-start | bytes 1179656 | tf_op jit(solution)/shard_map/while/body/eval_jaxpr/ppermute | solution.py:14
  532.2 32.4 %collective-permute-start = (bf16[64,3072]{1,0:T(8,128)(2,1)}, bf16[64,3072]{1,0:T(8,128)(2,1)S(1)}, u32[]{:S(2)}, u32[]{:S(2)}) collective-permute-start(bf16[64,3072]{1,0:T(8,128)(2,1)} %get-tuple-element.1261), channel_id=1, source_target_pairs={{0,16},{16,32},{32,48},{48,64},{64,80},{80,96},{96,112},{112,128},... | collective-permute-start | bytes 1179656 | tf_op jit(solution)/shard_map/while/body/eval_jaxpr/ppermute | solution.py:14
  566.2 60.1 %collective-permute-start.1 = (bf16[64,3072]{1,0:T(8,128)(2,1)}, bf16[64,3072]{1,0:T(8,128)(2,1)S(1)}, u32[]{:S(2)}, u32[]{:S(2)}) collective-permute-start(bf16[64,3072]{1,0:T(8,128)(2,1)} %get-tuple-element.1262), channel_id=1, source_target_pairs={{0,32},{16,48},{32,64},{48,80},{64,96},{80,112},{96,128},{112,144}... | collective-permute-start | bytes 1179656 | tf_op jit(solution)/shard_map/while/body/eval_jaxpr/ppermute | solution.py:14
  568.2 58.2 %collective-permute-start = (bf16[64,3072]{1,0:T(8,128)(2,1)}, bf16[64,3072]{1,0:T(8,128)(2,1)S(1)}, u32[]{:S(2)}, u32[]{:S(2)}) collective-permute-start(bf16[64,3072]{1,0:T(8,128)(2,1)} %get-tuple-element.1261), channel_id=1, source_target_pairs={{0,16},{16,32},{32,48},{48,64},{64,80},{80,96},{96,112},{112,128},... | collective-permute-start | bytes 1179656 | tf_op jit(solution)/shard_map/while/body/eval_jaxpr/ppermute | solution.py:14
  627.9 60.9 %collective-permute-start.1 = (bf16[64,3072]{1,0:T(8,128)(2,1)}, bf16[64,3072]{1,0:T(8,128)(2,1)S(1)}, u32[]{:S(2)}, u32[]{:S(2)}) collective-permute-start(bf16[64,3072]{1,0:T(8,128)(2,1)} %get-tuple-element.1262), channel_id=1, source_target_pairs={{0,32},{16,48},{32,64},{48,80},{64,96},{80,112},{96,128},{112,144}... | collective-permute-start | bytes 1179656 | tf_op jit(solution)/shard_map/while/body/eval_jaxpr/ppermute | solution.py:14
  629.9 59.0 %collective-permute-start = (bf16[64,3072]{1,0:T(8,128)(2,1)}, bf16[64,3072]{1,0:T(8,128)(2,1)S(1)}, u32[]{:S(2)}, u32[]{:S(2)}) collective-permute-start(bf16[64,3072]{1,0:T(8,128)(2,1)} %get-tuple-element.1261), channel_id=1, source_target_pairs={{0,16},{16,32},{32,48},{48,64},{64,80},{80,96},{96,112},{112,128},... | collective-permute-start | bytes 1179656 | tf_op jit(solution)/shard_map/while/body/eval_jaxpr/ppermute | solution.py:14
  690.5 38.2 %collective-permute-start.1 = (bf16[64,3072]{1,0:T(8,128)(2,1)}, bf16[64,3072]{1,0:T(8,128)(2,1)S(1)}, u32[]{:S(2)}, u32[]{:S(2)}) collective-permute-start(bf16[64,3072]{1,0:T(8,128)(2,1)} %get-tuple-element.1262), channel_id=1, source_target_pairs={{0,32},{16,48},{32,64},{48,80},{64,96},{80,112},{96,128},{112,144}... | collective-permute-start | bytes 1179656 | tf_op jit(solution)/shard_map/while/body/eval_jaxpr/ppermute | solution.py:14
  692.4 36.3 %collective-permute-start = (bf16[64,3072]{1,0:T(8,128)(2,1)}, bf16[64,3072]{1,0:T(8,128)(2,1)S(1)}, u32[]{:S(2)}, u32[]{:S(2)}) collective-permute-start(bf16[64,3072]{1,0:T(8,128)(2,1)} %get-tuple-element.1261), channel_id=1, source_target_pairs={{0,16},{16,32},{32,48},{48,64},{64,80},{80,96},{96,112},{112,128},... | collective-permute-start | bytes 1179656 | tf_op jit(solution)/shard_map/while/body/eval_jaxpr/ppermute | solution.py:14
  753.0 18.8 collective-permute-start.1
  754.9 18.3 collective-permute-start
  797.5 18.8 collective-permute-start.1
  799.4 18.3 collective-permute-start
  841.9 18.8 collective-permute-start.1
  843.8 18.3 collective-permute-start
  863.6 22.9 %collective-permute-start.1 = (bf16[64,3072]{1,0:T(8,128)(2,1)}, bf16[64,3072]{1,0:T(8,128)(2,1)S(1)}, u32[]{:S(2)}, u32[]{:S(2)}) collective-permute-start(bf16[64,3072]{1,0:T(8,128)(2,1)} %get-tuple-element.1262), channel_id=1, source_target_pairs={{0,32},{16,48},{32,64},{48,80},{64,96},{80,112},{96,128},{112,144}... | collective-permute-start | bytes 1179656 | tf_op jit(solution)/shard_map/while/body/eval_jaxpr/ppermute | solution.py:14
  878.1 15.4 collective-permute-start
  895.0 29.7 %collective-permute-start.1 = (bf16[64,3072]{1,0:T(8,128)(2,1)}, bf16[64,3072]{1,0:T(8,128)(2,1)S(1)}, u32[]{:S(2)}, u32[]{:S(2)}) collective-permute-start(bf16[64,3072]{1,0:T(8,128)(2,1)} %get-tuple-element.1262), channel_id=1, source_target_pairs={{0,32},{16,48},{32,64},{48,80},{64,96},{80,112},{96,128},{112,144}... | collective-permute-start | bytes 1179656 | tf_op jit(solution)/shard_map/while/body/eval_jaxpr/ppermute | solution.py:14
  916.4 15.4 collective-permute-start
  933.3 18.8 collective-permute-start.1
  935.2 18.3 collective-permute-start
  955.1 19.2 %collective-permute-start.1 = (bf16[64,3072]{1,0:T(8,128)(2,1)}, bf16[64,3072]{1,0:T(8,128)(2,1)S(1)}, u32[]{:S(2)}, u32[]{:S(2)}) collective-permute-start(bf16[64,3072]{1,0:T(8,128)(2,1)} %get-tuple-element.1262), channel_id=1, source_target_pairs={{0,32},{16,48},{32,64},{48,80},{64,96},{80,112},{96,128},{112,144}... | collective-permute-start | bytes 1179656 | tf_op jit(solution)/shard_map/while/body/eval_jaxpr/ppermute | solution.py:14
  964.8 15.3 collective-permute-start
  981.7 31.1 %collective-permute-start.1 = (bf16[64,3072]{1,0:T(8,128)(2,1)}, bf16[64,3072]{1,0:T(8,128)(2,1)S(1)}, u32[]{:S(2)}, u32[]{:S(2)}) collective-permute-start(bf16[64,3072]{1,0:T(8,128)(2,1)} %get-tuple-element.1262), channel_id=1, source_target_pairs={{0,32},{16,48},{32,64},{48,80},{64,96},{80,112},{96,128},{112,144}... | collective-permute-start | bytes 1179656 | tf_op jit(solution)/shard_map/while/body/eval_jaxpr/ppermute | solution.py:14
  1003.1 15.3 collective-permute-start
  1020.0 18.4 collective-permute-start.1
  1026.9 15.3 collective-permute-start
  1043.8 32.8 %collective-permute-start.1 = (bf16[64,3072]{1,0:T(8,128)(2,1)}, bf16[64,3072]{1,0:T(8,128)(2,1)S(1)}, u32[]{:S(2)}, u32[]{:S(2)}) collective-permute-start(bf16[64,3072]{1,0:T(8,128)(2,1)} %get-tuple-element.1262), channel_id=1, source_target_pairs={{0,32},{16,48},{32,64},{48,80},{64,96},{80,112},{96,128},{112,144}... | collective-permute-start | bytes 1179656 | tf_op jit(solution)/shard_map/while/body/eval_jaxpr/ppermute | solution.py:14
  1051.2 26.2 %collective-permute-start = (bf16[64,3072]{1,0:T(8,128)(2,1)}, bf16[64,3072]{1,0:T(8,128)(2,1)S(1)}, u32[]{:S(2)}, u32[]{:S(2)}) collective-permute-start(bf16[64,3072]{1,0:T(8,128)(2,1)} %get-tuple-element.1261), channel_id=1, source_target_pairs={{0,16},{16,32},{32,48},{48,64},{64,80},{80,96},{96,112},{112,128},... | collective-permute-start | bytes 1179656 | tf_op jit(solution)/shard_map/while/body/eval_jaxpr/ppermute | solution.py:14
  1077.4 2.5 copy-start
  1081.2 9.3 collective-permute-start.2
  1090.5 13.1 collective-permute-start.2
  1103.6 15.1 collective-permute-start.2
  1118.8 15.1 collective-permute-start.2
  1133.9 15.1 collective-permute-start.2
  1149.1 15.1 collective-permute-start.2
  1164.3 76.7 %collective-permute-start.2 = (bf16[64,3072]{1,0:T(8,128)(2,1)S(1)}, bf16[64,3072]{1,0:T(8,128)(2,1)S(1)}, u32[]{:S(2)}, u32[]{:S(2)}) collective-permute-start(bf16[64,3072]{1,0:T(8,128)(2,1)S(1)} %get-tuple-element.1279), channel_id=1, source_target_pairs={{16,0},{32,16},{48,32},{64,48},{80,64},{96,80},{112,96},{128,112},... | collective-permute-start | bytes 1179656 | tf_op jit(solution)/shard_map/while/body/eval_jaxpr/ppermute | solution.py:14
  1255.7 9.1 collective-permute-start.2
  1279.6 13.1 collective-permute-start.2
  1307.4 15.1 collective-permute-start.2
  1322.6 29.8 %collective-permute-start.2 = (bf16[64,3072]{1,0:T(8,128)(2,1)S(1)}, bf16[64,3072]{1,0:T(8,128)(2,1)S(1)}, u32[]{:S(2)}, u32[]{:S(2)}) collective-permute-start(bf16[64,3072]{1,0:T(8,128)(2,1)S(1)} %get-tuple-element.1279), channel_id=1, source_target_pairs={{16,0},{32,16},{48,32},{64,48},{80,64},{96,80},{112,96},{128,112},... | collective-permute-start | bytes 1179656 | tf_op jit(solution)/shard_map/while/body/eval_jaxpr/ppermute | solution.py:14
  1352.4 15.1 collective-permute-start.2
  1367.6 15.1 collective-permute-start.2
  1382.8 15.1 collective-permute-start.2
  1397.9 15.1 collective-permute-start.2
  1413.1 15.1 collective-permute-start.2
  1428.3 15.1 collective-permute-start.2
  1443.4 15.1 collective-permute-start.2
  1469.1 1.3 copy-start.1
  1469.1 207.4 %reduce-scatter.12.cloned.1.call-start = ((), (), s32[]{:S(2)}) async-start(), calls=%async_computation.7 | async-start | bytes 1671168
  1474.0 6.9 copy-start.6
  1480.8 404.5 %reduce-scatter.8.cloned.1.call-start = ((), (), s32[]{:S(2)}) async-start(), calls=%async_computation.4 | async-start | bytes 20054016 | tf_op jit(solution)/shard_map/reduce_scatter | solution.py:178
  (5 other events, 5.2 us)
Sparse Core Ops, SparseCore 0:
  9.8 212.7 all-gather.5
  225.0 210.9 all-gather.3
  1469.2 123.2 reduce-scatter.9
  1596.5 79.9 reduce-scatter.11
  1679.5 205.7 reduce-scatter.7
where the time goes:
time: 1900 us; the launch traced here: 1890 us
  waiting for transfers between devices  1230 us (65%)
  starting transfers between devices  358 us (19%)
  matrix products  104 us (5%)
  blocking collectives  88 us (5%)
  local copies, waits for them, and re-layouts  74 us (4%)
  other arithmetic  21.3 us (1%)
    ppermute x55, waiting for transfers between devices, from_behind(): return lax.ppermute(block, axis, route)  523 us
    ppermute x55, starting transfers between devices, from_behind(): return lax.ppermute(block, axis, route)  358 us
    all_gather x1, waiting for transfers between devices, on_device(): lax.all_gather(next_shard, 'dp', axis=0, tiled=True)  213 us
    reduce_scatter x1, waiting for transfers between devices, on_device(): lax.psum_scatter(lax.dot_general(normed_all, slope_all, (((0,), (0,)), ((...  207 us
    all_gather x1, waiting for transfers between devices, on_device(): lax.all_gather(weight[0], 'dp', axis=0, tiled=True)  192 us
    unnamed x7, waiting for transfers between devices  96.1 us
    psum x1, blocking collectives, on_device(): gain_grad = lax.psum(gain_total, 'dp')  88 us
    dot_general x6, matrix products, layer_forward(): pre = jnp.dot(normed, matrix, preferred_element_type=jnp.float32)  65.6 us
  transfers between devices with their start and end apart: 60, of which 54 were waited for; matrix products, arithmetic and copies ran while one was open for 2% of the time, Pallas kernels for 0%

commit v1 on v0

v1 whole, which is shorter than its diff:
```python
import functools

import jax
import jax.numpy as jnp
from jax import lax
from jax.experimental import pallas as pl
from jax.experimental.pallas import tpu as pltpu
from jax.sharding import PartitionSpec as P

EPSILON = 1e-06
HALF_ROOT = 0.7071067811865476
DENSITY = 0.3989422804014327
BF = jnp.bfloat16
F32 = jnp.float32
ANY = pl.BlockSpec(memory_space=pl.ANY)
HBM = pl.BlockSpec(memory_space=pltpu.HBM)
VMEM = pl.BlockSpec(memory_space=pltpu.VMEM)
SMEM = pl.BlockSpec(memory_space=pltpu.SMEM)
TILE = 512
LIMIT = 8 * 1024 * 1024


def call(kernel, outs, in_specs, out_specs, aliases, scratch, operands):
    return pl.pallas_call(
        kernel,
        out_shape=outs,
        in_specs=in_specs,
        out_specs=out_specs,
        input_output_aliases=aliases,
        scratch_shapes=scratch,
        compiler_params=pltpu.CompilerParams(vmem_limit_bytes=LIMIT),
    )(*operands)


def hold_kernel(source, held, sem):
    copy = pltpu.make_async_copy(source, held, sem)
    copy.start()
    copy.wait()


def hold(matrix):
    shape = pltpu.VMEM(matrix.shape, matrix.dtype)
    return call(
        hold_kernel, shape, [ANY], VMEM, {}, [pltpu.SemaphoreType.DMA], [matrix]
    )


def turn_kernel(source, turned):
    for i in range(0, source.shape[0], TILE):
        for j in range(0, source.shape[1], TILE):
            turned[pl.ds(j, TILE), pl.ds(i, TILE)] = source[pl.ds(i, TILE), pl.ds(j, TILE)].T


def turn(matrix):
    shape = pltpu.VMEM(matrix.shape, matrix.dtype)
    return call(turn_kernel, shape, [VMEM], VMEM, {}, [], [matrix])


def unit_of(values):
    scale = lax.rsqrt(jnp.mean(values * values, axis=-1, keepdims=True) + EPSILON)
    return scale, values * scale


def forward_kernel(t, m, section, x_in, gain, matrix, *refs):
    y, saved_out, normed_out, factor_out, saved, normed, factor, sems = refs[-8:]

    @pl.when(section[0] == t)
    def _():
        x = x_in.at[m] if m is not None else x_in
        saved[...] = x[...]
        keep = [pltpu.make_async_copy(saved, saved_out, sems.at[0])]
        keep[-1].start()
        _, unit = unit_of(saved[...].astype(F32))
        normed[...] = (unit * gain[...]).astype(BF)
        keep.append(pltpu.make_async_copy(normed, normed_out, sems.at[1]))
        keep[-1].start()
        for n in range(saved.shape[1] // TILE):
            at = pl.ds(n * TILE, TILE)
            pre = jnp.dot(normed[...], matrix[:, at], preferred_element_type=F32)
            bell = 0.5 * (1.0 + lax.erf(pre * HALF_ROOT))
            y[:, at] = (saved[:, at].astype(F32) + pre * bell).astype(BF)
            factor[:, at] = bell + pre * jnp.exp(-0.5 * pre * pre) * DENSITY
            copy = pltpu.make_async_copy(factor.at[:, at], factor_out.at[:, at], sems.at[2 + n])
            copy.start()
            keep.append(copy)
        for copy in keep:
            copy.wait()


def forward(t, m, section, x, gain_row, matrix, kept):
    shape = x.shape[-2:]
    wide, deep = pltpu.HBM(shape, BF), pltpu.HBM(shape, F32)
    return call(
        functools.partial(forward_kernel, t, m if x.ndim == 3 else None),
        (pltpu.VMEM(shape, BF), wide, wide, deep),
        [SMEM] + [VMEM] * 3 + [HBM] * len(kept),
        (VMEM, HBM, HBM, HBM),
        {4 + i: 1 + i for i in range(len(kept))},
        [
            pltpu.VMEM(shape, BF),
            pltpu.VMEM(shape, BF),
            pltpu.VMEM(shape, F32),
            pltpu.SemaphoreType.DMA((2 + shape[1] // TILE,)),
        ],
        [section, x, gain_row, matrix, *kept],
    )


def backward_kernel(t, m, section, u_in, saved, factor, gain, turned, *refs):
    d, slope_out, term_out, slope, term, grad, sems = refs[-7:]

    @pl.when(section[0] == t)
    def _():
        u = u_in.at[m] if m is not None else u_in
        slope[...] = (u[...].astype(F32) * factor[...]).astype(BF)
        keep_slope = pltpu.make_async_copy(slope, slope_out, sems.at[0])
        keep_slope.start()
        for k in range(0, saved.shape[1], TILE):
            at = pl.ds(k, TILE)
            grad[:, at] = jnp.dot(slope[...], turned[:, at], preferred_element_type=F32)
        scale, unit = unit_of(saved[...].astype(F32))
        normed_grad = grad[...]
        term[...] = jnp.sum(normed_grad * unit, axis=0, keepdims=True)
        keep_term = pltpu.make_async_copy(term, term_out, sems.at[1])
        keep_term.start()
        unit_grad = normed_grad * gain[...]
        centred = unit_grad - unit * jnp.mean(unit_grad * unit, axis=-1, keepdims=True)
        d[...] = (u[...].astype(F32) + scale * centred).astype(BF)
        keep_slope.wait()
        keep_term.wait()


def backward(t, m, section, u, saved, factor, gain_row, turned, kept):
    shape = saved.shape
    return call(
        functools.partial(backward_kernel, t, m if u.ndim == 3 else None),
        (
            pltpu.VMEM(shape, BF),
            pltpu.HBM(shape, BF),
            pltpu.HBM((1, shape[1]), F32),
        ),
        [SMEM] + [VMEM] * 5 + [HBM] * len(kept),
        (VMEM, HBM, HBM),
        {6 + i: 1 + i for i in range(len(kept))},
        [
            pltpu.VMEM(shape, BF),
            pltpu.VMEM((1, shape[1]), F32),
            pltpu.VMEM(shape, F32),
            pltpu.SemaphoreType.DMA((2,)),
        ],
        [section, u, saved, factor, gain_row, turned, *kept],
    )


def mirrored(index, count):
    return count - 4 - index // 4 * 4 + index % 4


def hop(block, source, target, half, count):
    crosses = (source < half) != (target < half)
    route = [
        (source * count + i, target * count + (mirrored(i, count) if crosses else i))
        for i in range(count)
    ]
    return lax.ppermute(block, ("section", "dp"), route)


def spread(block, owner, sections, count, turn):
    share = block.shape[1] // sections
    total = None
    for s in range(sections):
        route = [
            (owner * count + (mirrored(i, count) if turn else i), s * count + i)
            for i in range(count)
        ]
        piece = block[:, s * share : (s + 1) * share]
        part = lax.ppermute(piece, ("section", "dp"), route)
        total = part if total is None else total + part
    return total


def on_device(inputs, cotangent, weight, gain):
    sections = lax.axis_size("section")
    count = lax.axis_size("dp")
    half = sections // 2
    section = lax.axis_index("section")
    micros, rows, features = inputs.shape
    here = section.astype(jnp.int32).reshape(1)
    gain_row = lax.dynamic_index_in_dim(gain, section, 0, keepdims=True)
    across = [(i, mirrored(i, count)) for i in range(count)]
    upstream = lax.ppermute(cotangent, "dp", across)
    gathered = lax.all_gather(weight[0], "dp", axis=0, tiled=True)
    gathered, upstream, inputs, gain_row, here = lax.optimization_barrier(
        (gathered, upstream, inputs, gain_row, here)
    )
    matrix = hold(gathered)

    kept = [()] * micros
    current = [inputs] * micros
    for t in range(sections):
        if t == half:
            turned = turn(matrix)
        for m in range(micros):
            result, *kept[m] = forward(t, m, here, current[m], gain_row, matrix, kept[m])
            current[m] = hop(result, t, t + 1, half, count) if t + 1 < sections else result
    last = current

    passed = [()] * micros
    arriving = [upstream] * micros
    for t in reversed(range(sections)):
        for m in range(micros):
            saved, _, factor = kept[m]
            result, *passed[m] = backward(
                t, m, here, arriving[m], saved, factor, gain_row, turned, passed[m]
            )
            arriving[m] = hop(result, t, t - 1, half, count) if t else result
    slope = [passed[m][0] for m in range(micros)]
    total = sum(passed[m][1] for m in range(micros))
    normed = [kept[m][1] for m in range(micros)]
    last, first = jnp.concatenate(last, axis=0), jnp.concatenate(arriving, axis=0)

    summed = lax.psum_scatter(
        lax.dot_general(
            jnp.concatenate(normed, axis=0), jnp.concatenate(slope, axis=0),
            (((0,), (0,)), ((), ())), preferred_element_type=F32,
        ).astype(BF),
        "dp",
        scatter_dimension=0,
        tiled=True,
    )
    gain_grad = lax.psum(total, "dp")
    final_share = spread(last, sections - 1, sections, count, True)
    first_share = spread(first, 0, sections, count, False)
    shape = (micros, rows, features // sections)
    return (
        summed[None],
        gain_grad,
        first_share.reshape(shape),
        final_share.reshape(shape),
    )


def solution(mesh):
    in_specs = (P(None, "dp", None), P(None, "dp", None), P("section", "dp", None), P())
    out_specs = (
        P("section", "dp", None),
        P("section", None),
        P(None, "dp", "section"),
        P(None, "dp", "section"),
    )
    return jax.shard_map(
        on_device, mesh=mesh, in_specs=in_specs, out_specs=out_specs, check_vma=False
    )
```

time: 1900 us -> 1950 us (1.026)
  starting transfers between devices: 358 us -> 1500 us
  waiting for transfers between devices: 1230 us -> 221 us
  matrix products: 104 us -> 10.1 us
  Pallas kernels: 0 us -> 62.7 us
  local copies, waits for them, and re-layouts: 74 us -> 40.9 us
  other arithmetic: 21.3 us -> 1.49 us
    ppermute x55 -> x123, starting transfers between devices: 358 us -> 1500 us  [the longest x90 1110 us: hop(): return lax.ppermute(block, ('section', 'dp'), route)]
    ppermute x55 -> x123, waiting for transfers between devices: 523 us -> 52.8 us  [the longest x1 52.5 us: on_device(): upstream = lax.ppermute(cotangent, 'dp', across)]
    all_gather x2 -> x1, waiting for transfers between devices: 405 us -> 167 us  [on_device(): gathered = lax.all_gather(weight[0], 'dp', axis=0, tiled=True)]
    reduce_scatter x1, waiting for transfers between devices: 207 us -> 0.01 us  [on_device(): lax.psum_scatter(lax.dot_general(jnp.concatenate(normed, axis=0), jnp.con...]
    unnamed x7 -> x2, waiting for transfers between devices: 96.1 us -> 0.7 us
    dot_general x10 -> x1, matrix products: 104 us -> 10.1 us  [on_device(): lax.dot_general(jnp.concatenate(normed, axis=0), jnp.concatenate(slope, a...]
    pallas_call x0 -> x98, Pallas kernels: none -> 62.7 us  [call(): pl.pallas_call(kernel, out_shape=outs, in_specs=in_specs, out_specs=out_s...]
    another operation x54 -> x0, local copies, waits for them, and re-layouts: 28.2 us -> none
  transfers between devices with their start and end apart: 60 -> 125, of which waited for: 54 -> 2; matrix products, arithmetic and copies ran while one was open for 2% -> 0% of each run, Pallas kernels for 0% -> 3%
where the time goes in v1:
time: 1950 us; the launch traced here: 1930 us
  starting transfers between devices  1500 us (77%)
  waiting for transfers between devices  221 us (11%)
  blocking collectives  78.6 us (4%)
  Pallas kernels  62.7 us (3%)
  local copies, waits for them, and re-layouts  40.9 us (2%)
    ppermute x90, starting transfers between devices, hop(): return lax.ppermute(block, ('section', 'dp'), route)  1110 us
    ppermute x32, starting transfers between devices, spread(): part = lax.ppermute(piece, ('section', 'dp'), route)  372 us
    all_gather x1, waiting for transfers between devices, on_device(): gathered = lax.all_gather(weight[0], 'dp', axis=0, tiled=True)  167 us
    psum x1, blocking collectives, on_device(): gain_grad = lax.psum(total, 'dp')  78.6 us
    pallas_call x98, Pallas kernels, call(): pl.pallas_call(kernel, out_shape=outs, in_specs=in_specs, out_specs=out_s...  62.7 us
    ppermute x1, waiting for transfers between devices, on_device(): upstream = lax.ppermute(cotangent, 'dp', across)  52.5 us
    unnamed x66, local copies, waits for them, and re-layouts  40.1 us
  transfers between devices with their start and end apart: 125, of which 2 were waited for; matrix products, arithmetic and copies ran while one was open for 0% of the time, Pallas kernels for 3%

profile of v1, /device:TPU:128, one launch (start us, length us, event | category | flops | bytes accessed | tf_op | source)
XLA Modules:
  0.0 1929.5 jit_solution(5851400199541724987)
XLA Ops:
  20.5 52.5 %collective-permute-done.u_in = bf16[3,64,3072]{2,1,0:T(8,128)(2,1)S(1)} collective-permute-done((bf16[3,64,3072]{2,1,0:T(8,128)(2,1)S(1)}, bf16[3,64,3072]{2,1,0:T(8,128)(2,1)S(1)}, u32[]{:S(2)}, u32[]{:S(2)}) %collective-permute-start) | collective-permute-done | bytes 1179680 | tf_op jit(solution)/shard_map/ppermute | solution.py:191
  74.0 167.1 %all-gather.3.cloned.1.call-done = bf16[1,3072,3072]{2,1,0:T(8,128)(2,1)} async-done(((bf16[1,192,3072]{2,1,0:T(8,128)(2,1)}), bf16[1,3072,3072]{2,1,0:T(8,128)(2,1)}) %all-gather.3.cloned.1.call-update) | async-done | bytes 18874384 | tf_op jit(solution)/shard_map/all_gather | solution.py:192
  266.8 54.2 %collective-permute-start.34 = (bf16[64,3072]{1,0:T(8,128)(2,1)S(1)}, bf16[64,3072]{1,0:T(8,128)(2,1)S(1)}, u32[]{:S(2)}, u32[]{:S(2)}) collective-permute-start(bf16[64,3072]{1,0:T(8,128)(2,1)S(1)} %get-tuple-element.483), channel_id=1, source_target_pairs={{48,64},{49,65},{50,66},{51,67},{52,68},{53,69},{54,70},{55,71},{5... | collective-permute-start | bytes 1179656 | tf_op jit(solution)/shard_map/ppermute | solution.py:165
  321.5 14.5 collective-permute-start.5
  336.1 15.1 collective-permute-start.20
  351.3 15.1 collective-permute-start.35
  366.7 14.2 collective-permute-start.6
  381.1 14.9 collective-permute-start.21
  396.1 14.9 collective-permute-start.36
  411.3 14.2 collective-permute-start.7
  425.6 14.9 collective-permute-start.22
  440.5 14.9 collective-permute-start.37
  455.9 13.9 collective-permute-start.8
  469.9 14.6 collective-permute-start.23
  484.7 14.6 collective-permute-start.38
  559.0 14.8 collective-permute-start.25
  574.0 14.8 collective-permute-start.40
  589.3 15.3 collective-permute-start.11
  604.8 16.0 collective-permute-start.26
  620.9 16.0 collective-permute-start.41
  637.1 15.1 collective-permute-start.12
  652.3 15.7 collective-permute-start.27
  668.2 15.8 collective-permute-start.42
  684.3 16.9 collective-permute-start.13
  701.2 17.5 collective-permute-start.28
  718.9 17.5 collective-permute-start.43
  736.9 16.6 collective-permute-start.14
  753.6 17.3 collective-permute-start.29
  771.0 17.3 collective-permute-start.44
  788.5 16.6 collective-permute-start.15
  805.2 17.2 collective-permute-start.30
  822.6 17.5 collective-permute-start.45
  860.6 16.4 collective-permute-start.46
  886.0 21.0 %collective-permute-start.61 = (bf16[64,3072]{1,0:T(8,128)(2,1)S(1)}, bf16[64,3072]{1,0:T(8,128)(2,1)S(1)}, u32[]{:S(2)}, u32[]{:S(2)}) collective-permute-start(bf16[64,3072]{1,0:T(8,128)(2,1)S(1)} %get-tuple-element.583), channel_id=1, source_target_pairs={{240,224},{241,225},{242,226},{243,227},{244,228},{245,229},{246,2... | collective-permute-start | bytes 1179656 | tf_op jit(solution)/shard_map/ppermute | solution.py:165
  915.7 21.0 %collective-permute-start.76 = (bf16[64,3072]{1,0:T(8,128)(2,1)S(1)}, bf16[64,3072]{1,0:T(8,128)(2,1)S(1)}, u32[]{:S(2)}, u32[]{:S(2)}) collective-permute-start(bf16[64,3072]{1,0:T(8,128)(2,1)S(1)} %get-tuple-element.631), channel_id=1, source_target_pairs={{240,224},{241,225},{242,226},{243,227},{244,228},{245,229},{246,2... | collective-permute-start | bytes 1179656 | tf_op jit(solution)/shard_map/ppermute | solution.py:165
  936.9 16.2 collective-permute-start.47
  953.2 16.9 collective-permute-start.62
  970.2 16.9 collective-permute-start.77
  987.1 16.2 collective-permute-start.48
  1003.6 16.9 collective-permute-start.63
  1020.6 16.9 collective-permute-start.78
  1037.6 16.5 collective-permute-start.49
  1054.1 17.2 collective-permute-start.64
  1071.7 17.2 collective-permute-start.79
  1088.9 14.7 collective-permute-start.50
  1103.7 15.4 collective-permute-start.65
  1119.1 15.4 collective-permute-start.80
  1134.7 14.9 collective-permute-start.51
  1149.7 15.6 collective-permute-start.66
  1165.4 15.7 collective-permute-start.81
  1195.1 14.5 collective-permute-start.67
  1209.6 14.5 collective-permute-start.82
  1281.9 14.3 collective-permute-start.69
  1296.2 14.3 collective-permute-start.84
  1324.5 14.5 collective-permute-start.70
  1339.1 14.5 collective-permute-start.85
  1367.8 14.5 collective-permute-start.71
  1382.3 14.6 collective-permute-start.86
  1397.0 14.1 collective-permute-start.57
  1411.1 14.8 collective-permute-start.72
  1426.3 14.8 collective-permute-start.87
  1469.4 31.1 %collective-permute-start.107 = (bf16[192,192]{1,0:T(8,128)(2,1)S(1)}, bf16[192,192]{1,0:T(8,128)(2,1)S(1)}, u32[]{:S(2)}, u32[]{:S(2)}) collective-permute-start(bf16[192,192]{1,0:T(8,128)(2,1)S(1)} %get-tuple-element.701), channel_id=1, source_target_pairs={{252,0},{253,1},{254,2},{255,3},{248,4},{249,5},{250,6},{251,7},{2... | collective-permute-start | bytes 221192 | tf_op jit(solution)/shard_map/ppermute | solution.py:177
  1551.0 152.9 %collective-permute-start.112 = (bf16[192,192]{1,0:T(8,128)(2,1)S(1)}, bf16[192,192]{1,0:T(8,128)(2,1)S(1)}, u32[]{:S(2)}, u32[]{:S(2)}) collective-permute-start(bf16[192,192]{1,0:T(8,128)(2,1)S(1)} %get-tuple-element.697), channel_id=1, source_target_pairs={{252,80},{253,81},{254,82},{255,83},{248,84},{249,85},{250,86},{25... | collective-permute-start | bytes 221192 | tf_op jit(solution)/shard_map/ppermute | solution.py:177
  1842.9 78.6 %psum.7 = f32[1,3072]{1,0:T(1,128)} all-reduce(f32[1,3072]{1,0:T(1,128)S(1)} %add_add_fusion.2), channel_id=1, replica_groups=mesh['section'=16,'dp'=16] {'dp'}, use_global_device_ids=true, to_apply=%region_1.2 | all-reduce | flops 3072 | bytes 24576 | tf_op jit(solution)/shard_map/psum | solution.py:231
  (362 shorter events, 461.9 us)
Async XLA Ops:
  7.2 233.9 %all-gather.3.cloned.1.call-start = ((), (), s32[]{:S(2)}) async-start(), calls=%async_computation.2 | async-start | bytes 20054016 | tf_op jit(solution)/shard_map/all_gather | solution.py:192
  7.9 1914.3 %reduce-scatter.2.cloned.1.call-start = ((), (), s32[]{:S(2)}) async-start(), calls=%async_computation.1 | async-start | bytes 20054016 | tf_op jit(solution)/shard_map/reduce_scatter | solution.py:222
  8.5 64.4 %collective-permute-start = (bf16[3,64,3072]{2,1,0:T(8,128)(2,1)S(1)}, bf16[3,64,3072]{2,1,0:T(8,128)(2,1)S(1)}, u32[]{:S(2)}, u32[]{:S(2)}) collective-permute-start(bf16[3,64,3072]{2,1,0:T(8,128)(2,1)S(1)} %copy-done.30), channel_id=1, source_target_pairs={{0,12},{1,13},{2,14},{3,15},{4,8},{5,9},{6,10},{7,11},{8,4},{9,5},... | collective-permute-start | bytes 3538952 | tf_op jit(solution)/shard_map/ppermute | solution.py:191
  265.2 55.8 %collective-permute-start.4 = (bf16[64,3072]{1,0:T(8,128)(2,1)S(1)}, bf16[64,3072]{1,0:T(8,128)(2,1)S(1)}, u32[]{:S(2)}, u32[]{:S(2)}) collective-permute-start(bf16[64,3072]{1,0:T(8,128)(2,1)S(1)} %get-tuple-element.361), channel_id=1, source_target_pairs={{48,64},{49,65},{50,66},{51,67},{52,68},{53,69},{54,70},{55,71},{5... | collective-permute-start | bytes 1179656 | tf_op jit(solution)/shard_map/ppermute | solution.py:165
  266.0 70.0 %collective-permute-start.19 = (bf16[64,3072]{1,0:T(8,128)(2,1)S(1)}, bf16[64,3072]{1,0:T(8,128)(2,1)S(1)}, u32[]{:S(2)}, u32[]{:S(2)}) collective-permute-start(bf16[64,3072]{1,0:T(8,128)(2,1)S(1)} %get-tuple-element.422), channel_id=1, source_target_pairs={{48,64},{49,65},{50,66},{51,67},{52,68},{53,69},{54,70},{55,71},{5... | collective-permute-start | bytes 1179656 | tf_op jit(solution)/shard_map/ppermute | solution.py:165
  266.8 84.4 %collective-permute-start.34 = (bf16[64,3072]{1,0:T(8,128)(2,1)S(1)}, bf16[64,3072]{1,0:T(8,128)(2,1)S(1)}, u32[]{:S(2)}, u32[]{:S(2)}) collective-permute-start(bf16[64,3072]{1,0:T(8,128)(2,1)S(1)} %get-tuple-element.483), channel_id=1, source_target_pairs={{48,64},{49,65},{50,66},{51,67},{52,68},{53,69},{54,70},{55,71},{5... | collective-permute-start | bytes 1179656 | tf_op jit(solution)/shard_map/ppermute | solution.py:165
  321.5 45.0 %collective-permute-start.5 = (bf16[64,3072]{1,0:T(8,128)(2,1)S(1)}, bf16[64,3072]{1,0:T(8,128)(2,1)S(1)}, u32[]{:S(2)}, u32[]{:S(2)}) collective-permute-start(bf16[64,3072]{1,0:T(8,128)(2,1)S(1)} %get-tuple-element.365), channel_id=1, source_target_pairs={{64,80},{65,81},{66,82},{67,83},{68,84},{69,85},{70,86},{71,87},{7... | collective-permute-start | bytes 1179656 | tf_op jit(solution)/shard_map/ppermute | solution.py:165
  336.1 44.9 %collective-permute-start.20 = (bf16[64,3072]{1,0:T(8,128)(2,1)S(1)}, bf16[64,3072]{1,0:T(8,128)(2,1)S(1)}, u32[]{:S(2)}, u32[]{:S(2)}) collective-permute-start(bf16[64,3072]{1,0:T(8,128)(2,1)S(1)} %get-tuple-element.426), channel_id=1, source_target_pairs={{64,80},{65,81},{66,82},{67,83},{68,84},{69,85},{70,86},{71,87},{7... | collective-permute-start | bytes 1179656 | tf_op jit(solution)/shard_map/ppermute | solution.py:165
  351.3 44.7 %collective-permute-start.35 = (bf16[64,3072]{1,0:T(8,128)(2,1)S(1)}, bf16[64,3072]{1,0:T(8,128)(2,1)S(1)}, u32[]{:S(2)}, u32[]{:S(2)}) collective-permute-start(bf16[64,3072]{1,0:T(8,128)(2,1)S(1)} %get-tuple-element.487), channel_id=1, source_target_pairs={{64,80},{65,81},{66,82},{67,83},{68,84},{69,85},{70,86},{71,87},{7... | collective-permute-start | bytes 1179656 | tf_op jit(solution)/shard_map/ppermute | solution.py:165
  381.1 44.4 %collective-permute-start.21 = (bf16[64,3072]{1,0:T(8,128)(2,1)S(1)}, bf16[64,3072]{1,0:T(8,128)(2,1)S(1)}, u32[]{:S(2)}, u32[]{:S(2)}) collective-permute-start(bf16[64,3072]{1,0:T(8,128)(2,1)S(1)} %get-tuple-element.430), channel_id=1, source_target_pairs={{80,96},{81,97},{82,98},{83,99},{84,100},{85,101},{86,102},{87,103... | collective-permute-start | bytes 1179656 | tf_op jit(solution)/shard_map/ppermute | solution.py:165
  469.9 44.7 %collective-permute-start.23 = (bf16[64,3072]{1,0:T(8,128)(2,1)S(1)}, bf16[64,3072]{1,0:T(8,128)(2,1)S(1)}, u32[]{:S(2)}, u32[]{:S(2)}) collective-permute-start(bf16[64,3072]{1,0:T(8,128)(2,1)S(1)} %get-tuple-element.438), channel_id=1, source_target_pairs={{112,140},{113,141},{114,142},{115,143},{116,136},{117,137},{118,1... | collective-permute-start | bytes 1179656 | tf_op jit(solution)/shard_map/ppermute | solution.py:165
  484.7 45.2 %collective-permute-start.38 = (bf16[64,3072]{1,0:T(8,128)(2,1)S(1)}, bf16[64,3072]{1,0:T(8,128)(2,1)S(1)}, u32[]{:S(2)}, u32[]{:S(2)}) collective-permute-start(bf16[64,3072]{1,0:T(8,128)(2,1)S(1)} %get-tuple-element.499), channel_id=1, source_target_pairs={{112,140},{113,141},{114,142},{115,143},{116,136},{117,137},{118,1... | collective-permute-start | bytes 1179656 | tf_op jit(solution)/shard_map/ppermute | solution.py:165
  559.0 45.6 %collective-permute-start.25 = (bf16[64,3072]{1,0:T(8,128)(2,1)S(1)}, bf16[64,3072]{1,0:T(8,128)(2,1)S(1)}, u32[]{:S(2)}, u32[]{:S(2)}) collective-permute-start(bf16[64,3072]{1,0:T(8,128)(2,1)S(1)} %get-tuple-element.446), channel_id=1, source_target_pairs={{144,160},{145,161},{146,162},{147,163},{148,164},{149,165},{150,1... | collective-permute-start | bytes 1179656 | tf_op jit(solution)/shard_map/ppermute | solution.py:165
  574.0 46.8 %collective-permute-start.40 = (bf16[64,3072]{1,0:T(8,128)(2,1)S(1)}, bf16[64,3072]{1,0:T(8,128)(2,1)S(1)}, u32[]{:S(2)}, u32[]{:S(2)}) collective-permute-start(bf16[64,3072]{1,0:T(8,128)(2,1)S(1)} %get-tuple-element.507), channel_id=1, source_target_pairs={{144,160},{145,161},{146,162},{147,163},{148,164},{149,165},{150,1... | collective-permute-start | bytes 1179656 | tf_op jit(solution)/shard_map/ppermute | solution.py:165
  589.3 47.6 %collective-permute-start.11 = (bf16[64,3072]{1,0:T(8,128)(2,1)S(1)}, bf16[64,3072]{1,0:T(8,128)(2,1)S(1)}, u32[]{:S(2)}, u32[]{:S(2)}) collective-permute-start(bf16[64,3072]{1,0:T(8,128)(2,1)S(1)} %get-tuple-element.389), channel_id=1, source_target_pairs={{160,176},{161,177},{162,178},{163,179},{164,180},{165,181},{166,1... | collective-permute-start | bytes 1179656 | tf_op jit(solution)/shard_map/ppermute | solution.py:165
  604.8 47.5 %collective-permute-start.26 = (bf16[64,3072]{1,0:T(8,128)(2,1)S(1)}, bf16[64,3072]{1,0:T(8,128)(2,1)S(1)}, u32[]{:S(2)}, u32[]{:S(2)}) collective-permute-start(bf16[64,3072]{1,0:T(8,128)(2,1)S(1)} %get-tuple-element.450), channel_id=1, source_target_pairs={{160,176},{161,177},{162,178},{163,179},{164,180},{165,181},{166,1... | collective-permute-start | bytes 1179656 | tf_op jit(solution)/shard_map/ppermute | solution.py:165
  620.9 47.2 %collective-permute-start.41 = (bf16[64,3072]{1,0:T(8,128)(2,1)S(1)}, bf16[64,3072]{1,0:T(8,128)(2,1)S(1)}, u32[]{:S(2)}, u32[]{:S(2)}) collective-permute-start(bf16[64,3072]{1,0:T(8,128)(2,1)S(1)} %get-tuple-element.511), channel_id=1, source_target_pairs={{160,176},{161,177},{162,178},{163,179},{164,180},{165,181},{166,1... | collective-permute-start | bytes 1179656 | tf_op jit(solution)/shard_map/ppermute | solution.py:165
  637.1 46.8 %collective-permute-start.12 = (bf16[64,3072]{1,0:T(8,128)(2,1)S(1)}, bf16[64,3072]{1,0:T(8,128)(2,1)S(1)}, u32[]{:S(2)}, u32[]{:S(2)}) collective-permute-start(bf16[64,3072]{1,0:T(8,128)(2,1)S(1)} %get-tuple-element.393), channel_id=1, source_target_pairs={{176,192},{177,193},{178,194},{179,195},{180,196},{181,197},{182,1... | collective-permute-start | bytes 1179656 | tf_op jit(solution)/shard_map/ppermute | solution.py:165
  652.3 48.8 %collective-permute-start.27 = (bf16[64,3072]{1,0:T(8,128)(2,1)S(1)}, bf16[64,3072]{1,0:T(8,128)(2,1)S(1)}, u32[]{:S(2)}, u32[]{:S(2)}) collective-permute-start(bf16[64,3072]{1,0:T(8,128)(2,1)S(1)} %get-tuple-element.454), channel_id=1, source_target_pairs={{176,192},{177,193},{178,194},{179,195},{180,196},{181,197},{182,1... | collective-permute-start | bytes 1179656 | tf_op jit(solution)/shard_map/ppermute | solution.py:165
  668.2 50.6 %collective-permute-start.42 = (bf16[64,3072]{1,0:T(8,128)(2,1)S(1)}, bf16[64,3072]{1,0:T(8,128)(2,1)S(1)}, u32[]{:S(2)}, u32[]{:S(2)}) collective-permute-start(bf16[64,3072]{1,0:T(8,128)(2,1)S(1)} %get-tuple-element.515), channel_id=1, source_target_pairs={{176,192},{177,193},{178,194},{179,195},{180,196},{181,197},{182,1... | collective-permute-start | bytes 1179656 | tf_op jit(solution)/shard_map/ppermute | solution.py:165
  684.3 52.1 %collective-permute-start.13 = (bf16[64,3072]{1,0:T(8,128)(2,1)S(1)}, bf16[64,3072]{1,0:T(8,128)(2,1)S(1)}, u32[]{:S(2)}, u32[]{:S(2)}) collective-permute-start(bf16[64,3072]{1,0:T(8,128)(2,1)S(1)} %get-tuple-element.397), channel_id=1, source_target_pairs={{192,208},{193,209},{194,210},{195,211},{196,212},{197,213},{198,2... | collective-permute-start | bytes 1179656 | tf_op jit(solution)/shard_map/ppermute | solution.py:165
  701.2 52.3 %collective-permute-start.28 = (bf16[64,3072]{1,0:T(8,128)(2,1)S(1)}, bf16[64,3072]{1,0:T(8,128)(2,1)S(1)}, u32[]{:S(2)}, u32[]{:S(2)}) collective-permute-start(bf16[64,3072]{1,0:T(8,128)(2,1)S(1)} %get-tuple-element.458), channel_id=1, source_target_pairs={{192,208},{193,209},{194,210},{195,211},{196,212},{197,213},{198,2... | collective-permute-start | bytes 1179656 | tf_op jit(solution)/shard_map/ppermute | solution.py:165
  718.9 52.0 %collective-permute-start.43 = (bf16[64,3072]{1,0:T(8,128)(2,1)S(1)}, bf16[64,3072]{1,0:T(8,128)(2,1)S(1)}, u32[]{:S(2)}, u32[]{:S(2)}) collective-permute-start(bf16[64,3072]{1,0:T(8,128)(2,1)S(1)} %get-tuple-element.519), channel_id=1, source_target_pairs={{192,208},{193,209},{194,210},{195,211},{196,212},{197,213},{198,2... | collective-permute-start | bytes 1179656 | tf_op jit(solution)/shard_map/ppermute | solution.py:165
  736.9 51.4 %collective-permute-start.14 = (bf16[64,3072]{1,0:T(8,128)(2,1)S(1)}, bf16[64,3072]{1,0:T(8,128)(2,1)S(1)}, u32[]{:S(2)}, u32[]{:S(2)}) collective-permute-start(bf16[64,3072]{1,0:T(8,128)(2,1)S(1)} %get-tuple-element.401), channel_id=1, source_target_pairs={{208,224},{209,225},{210,226},{211,227},{212,228},{213,229},{214,2... | collective-permute-start | bytes 1179656 | tf_op jit(solution)/shard_map/ppermute | solution.py:165
  753.6 51.5 %collective-permute-start.29 = (bf16[64,3072]{1,0:T(8,128)(2,1)S(1)}, bf16[64,3072]{1,0:T(8,128)(2,1)S(1)}, u32[]{:S(2)}, u32[]{:S(2)}) collective-permute-start(bf16[64,3072]{1,0:T(8,128)(2,1)S(1)} %get-tuple-element.462), channel_id=1, source_target_pairs={{208,224},{209,225},{210,226},{211,227},{212,228},{213,229},{214,2... | collective-permute-start | bytes 1179656 | tf_op jit(solution)/shard_map/ppermute | solution.py:165
  771.0 51.5 %collective-permute-start.44 = (bf16[64,3072]{1,0:T(8,128)(2,1)S(1)}, bf16[64,3072]{1,0:T(8,128)(2,1)S(1)}, u32[]{:S(2)}, u32[]{:S(2)}) collective-permute-start(bf16[64,3072]{1,0:T(8,128)(2,1)S(1)} %get-tuple-element.523), channel_id=1, source_target_pairs={{208,224},{209,225},{210,226},{211,227},{212,228},{213,229},{214,2... | collective-permute-start | bytes 1179656 | tf_op jit(solution)/shard_map/ppermute | solution.py:165
  788.5 56.9 %collective-permute-start.15 = (bf16[64,3072]{1,0:T(8,128)(2,1)S(1)}, bf16[64,3072]{1,0:T(8,128)(2,1)S(1)}, u32[]{:S(2)}, u32[]{:S(2)}) collective-permute-start(bf16[64,3072]{1,0:T(8,128)(2,1)S(1)} %get-tuple-element.405), channel_id=1, source_target_pairs={{224,240},{225,241},{226,242},{227,243},{228,244},{229,245},{230,2... | collective-permute-start | bytes 1179656 | tf_op jit(solution)/shard_map/ppermute | solution.py:165
  805.2 71.8 %collective-permute-start.30 = (bf16[64,3072]{1,0:T(8,128)(2,1)S(1)}, bf16[64,3072]{1,0:T(8,128)(2,1)S(1)}, u32[]{:S(2)}, u32[]{:S(2)}) collective-permute-start(bf16[64,3072]{1,0:T(8,128)(2,1)S(1)} %get-tuple-element.466), channel_id=1, source_target_pairs={{224,240},{225,241},{226,242},{227,243},{228,244},{229,245},{230,2... | collective-permute-start | bytes 1179656 | tf_op jit(solution)/shard_map/ppermute | solution.py:165
  822.6 84.5 %collective-permute-start.45 = (bf16[64,3072]{1,0:T(8,128)(2,1)S(1)}, bf16[64,3072]{1,0:T(8,128)(2,1)S(1)}, u32[]{:S(2)}, u32[]{:S(2)}) collective-permute-start(bf16[64,3072]{1,0:T(8,128)(2,1)S(1)} %get-tuple-element.527), channel_id=1, source_target_pairs={{224,240},{225,241},{226,242},{227,243},{228,244},{229,245},{230,2... | collective-permute-start | bytes 1179656 | tf_op jit(solution)/shard_map/ppermute | solution.py:165
  860.6 76.1 %collective-permute-start.46 = (bf16[64,3072]{1,0:T(8,128)(2,1)S(1)}, bf16[64,3072]{1,0:T(8,128)(2,1)S(1)}, u32[]{:S(2)}, u32[]{:S(2)}) collective-permute-start(bf16[64,3072]{1,0:T(8,128)(2,1)S(1)} %get-tuple-element.535), channel_id=1, source_target_pairs={{240,224},{241,225},{242,226},{243,227},{244,228},{245,229},{246,2... | collective-permute-start | bytes 1179656 | tf_op jit(solution)/shard_map/ppermute | solution.py:165
  886.0 67.1 %collective-permute-start.61 = (bf16[64,3072]{1,0:T(8,128)(2,1)S(1)}, bf16[64,3072]{1,0:T(8,128)(2,1)S(1)}, u32[]{:S(2)}, u32[]{:S(2)}) collective-permute-start(bf16[64,3072]{1,0:T(8,128)(2,1)S(1)} %get-tuple-element.583), channel_id=1, source_target_pairs={{240,224},{241,225},{242,226},{243,227},{244,228},{245,229},{246,2... | collective-permute-start | bytes 1179656 | tf_op jit(solution)/shard_map/ppermute | solution.py:165
  915.7 54.5 %collective-permute-start.76 = (bf16[64,3072]{1,0:T(8,128)(2,1)S(1)}, bf16[64,3072]{1,0:T(8,128)(2,1)S(1)}, u32[]{:S(2)}, u32[]{:S(2)}) collective-permute-start(bf16[64,3072]{1,0:T(8,128)(2,1)S(1)} %get-tuple-element.631), channel_id=1, source_target_pairs={{240,224},{241,225},{242,226},{243,227},{244,228},{245,229},{246,2... | collective-permute-start | bytes 1179656 | tf_op jit(solution)/shard_map/ppermute | solution.py:165
  936.9 50.1 %collective-permute-start.47 = (bf16[64,3072]{1,0:T(8,128)(2,1)S(1)}, bf16[64,3072]{1,0:T(8,128)(2,1)S(1)}, u32[]{:S(2)}, u32[]{:S(2)}) collective-permute-start(bf16[64,3072]{1,0:T(8,128)(2,1)S(1)} %get-tuple-element.538), channel_id=1, source_target_pairs={{224,208},{225,209},{226,210},{227,211},{228,212},{229,213},{230,2... | collective-permute-start | bytes 1179656 | tf_op jit(solution)/shard_map/ppermute | solution.py:165
  953.2 50.1 %collective-permute-start.62 = (bf16[64,3072]{1,0:T(8,128)(2,1)S(1)}, bf16[64,3072]{1,0:T(8,128)(2,1)S(1)}, u32[]{:S(2)}, u32[]{:S(2)}) collective-permute-start(bf16[64,3072]{1,0:T(8,128)(2,1)S(1)} %get-tuple-element.586), channel_id=1, source_target_pairs={{224,208},{225,209},{226,210},{227,211},{228,212},{229,213},{230,2... | collective-permute-start | bytes 1179656 | tf_op jit(solution)/shard_map/ppermute | solution.py:165
  970.2 50.4 %collective-permute-start.77 = (bf16[64,3072]{1,0:T(8,128)(2,1)S(1)}, bf16[64,3072]{1,0:T(8,128)(2,1)S(1)}, u32[]{:S(2)}, u32[]{:S(2)}) collective-permute-start(bf16[64,3072]{1,0:T(8,128)(2,1)S(1)} %get-tuple-element.634), channel_id=1, source_target_pairs={{224,208},{225,209},{226,210},{227,211},{228,212},{229,213},{230,2... | collective-permute-start | bytes 1179656 | tf_op jit(solution)/shard_map/ppermute | solution.py:165
  987.1 50.4 %collective-permute-start.48 = (bf16[64,3072]{1,0:T(8,128)(2,1)S(1)}, bf16[64,3072]{1,0:T(8,128)(2,1)S(1)}, u32[]{:S(2)}, u32[]{:S(2)}) collective-permute-start(bf16[64,3072]{1,0:T(8,128)(2,1)S(1)} %get-tuple-element.541), channel_id=1, source_target_pairs={{208,192},{209,193},{210,194},{211,195},{212,196},{213,197},{214,1... | collective-permute-start | bytes 1179656 | tf_op jit(solution)/shard_map/ppermute | solution.py:165
  1003.6 50.4 %collective-permute-start.63 = (bf16[64,3072]{1,0:T(8,128)(2,1)S(1)}, bf16[64,3072]{1,0:T(8,128)(2,1)S(1)}, u32[]{:S(2)}, u32[]{:S(2)}) collective-permute-start(bf16[64,3072]{1,0:T(8,128)(2,1)S(1)} %get-tuple-element.589), channel_id=1, source_target_pairs={{208,192},{209,193},{210,194},{211,195},{212,196},{213,197},{214,1... | collective-permute-start | bytes 1179656 | tf_op jit(solution)/shard_map/ppermute | solution.py:165
  1020.6 50.7 %collective-permute-start.78 = (bf16[64,3072]{1,0:T(8,128)(2,1)S(1)}, bf16[64,3072]{1,0:T(8,128)(2,1)S(1)}, u32[]{:S(2)}, u32[]{:S(2)}) collective-permute-start(bf16[64,3072]{1,0:T(8,128)(2,1)S(1)} %get-tuple-element.637), channel_id=1, source_target_pairs={{208,192},{209,193},{210,194},{211,195},{212,196},{213,197},{214,1... | collective-permute-start | bytes 1179656 | tf_op jit(solution)/shard_map/ppermute | solution.py:165
  1037.6 51.3 %collective-permute-start.49 = (bf16[64,3072]{1,0:T(8,128)(2,1)S(1)}, bf16[64,3072]{1,0:T(8,128)(2,1)S(1)}, u32[]{:S(2)}, u32[]{:S(2)}) collective-permute-start(bf16[64,3072]{1,0:T(8,128)(2,1)S(1)} %get-tuple-element.544), channel_id=1, source_target_pairs={{192,176},{193,177},{194,178},{195,179},{196,180},{197,181},{198,1... | collective-permute-start | bytes 1179656 | tf_op jit(solution)/shard_map/ppermute | solution.py:165
  1054.1 49.5 %collective-permute-start.64 = (bf16[64,3072]{1,0:T(8,128)(2,1)S(1)}, bf16[64,3072]{1,0:T(8,128)(2,1)S(1)}, u32[]{:S(2)}, u32[]{:S(2)}) collective-permute-start(bf16[64,3072]{1,0:T(8,128)(2,1)S(1)} %get-tuple-element.592), channel_id=1, source_target_pairs={{192,176},{193,177},{194,178},{195,179},{196,180},{197,181},{198,1... | collective-permute-start | bytes 1179656 | tf_op jit(solution)/shard_map/ppermute | solution.py:165
  1071.7 47.4 %collective-permute-start.79 = (bf16[64,3072]{1,0:T(8,128)(2,1)S(1)}, bf16[64,3072]{1,0:T(8,128)(2,1)S(1)}, u32[]{:S(2)}, u32[]{:S(2)}) collective-permute-start(bf16[64,3072]{1,0:T(8,128)(2,1)S(1)} %get-tuple-element.640), channel_id=1, source_target_pairs={{192,176},{193,177},{194,178},{195,179},{196,180},{197,181},{198,1... | collective-permute-start | bytes 1179656 | tf_op jit(solution)/shard_map/ppermute | solution.py:165
  1088.9 45.6 %collective-permute-start.50 = (bf16[64,3072]{1,0:T(8,128)(2,1)S(1)}, bf16[64,3072]{1,0:T(8,128)(2,1)S(1)}, u32[]{:S(2)}, u32[]{:S(2)}) collective-permute-start(bf16[64,3072]{1,0:T(8,128)(2,1)S(1)} %get-tuple-element.547), channel_id=1, source_target_pairs={{176,160},{177,161},{178,162},{179,163},{180,164},{181,165},{182,1... | collective-permute-start | bytes 1179656 | tf_op jit(solution)/shard_map/ppermute | solution.py:165
  1103.7 46.0 %collective-permute-start.65 = (bf16[64,3072]{1,0:T(8,128)(2,1)S(1)}, bf16[64,3072]{1,0:T(8,128)(2,1)S(1)}, u32[]{:S(2)}, u32[]{:S(2)}) collective-permute-start(bf16[64,3072]{1,0:T(8,128)(2,1)S(1)} %get-tuple-element.595), channel_id=1, source_target_pairs={{176,160},{177,161},{178,162},{179,163},{180,164},{181,165},{182,1... | collective-permute-start | bytes 1179656 | tf_op jit(solution)/shard_map/ppermute | solution.py:165
  1119.1 46.2 %collective-permute-start.80 = (bf16[64,3072]{1,0:T(8,128)(2,1)S(1)}, bf16[64,3072]{1,0:T(8,128)(2,1)S(1)}, u32[]{:S(2)}, u32[]{:S(2)}) collective-permute-start(bf16[64,3072]{1,0:T(8,128)(2,1)S(1)} %get-tuple-element.643), channel_id=1, source_target_pairs={{176,160},{177,161},{178,162},{179,163},{180,164},{181,165},{182,1... | collective-permute-start | bytes 1179656 | tf_op jit(solution)/shard_map/ppermute | solution.py:165
  1134.7 46.3 %collective-permute-start.51 = (bf16[64,3072]{1,0:T(8,128)(2,1)S(1)}, bf16[64,3072]{1,0:T(8,128)(2,1)S(1)}, u32[]{:S(2)}, u32[]{:S(2)}) collective-permute-start(bf16[64,3072]{1,0:T(8,128)(2,1)S(1)} %get-tuple-element.550), channel_id=1, source_target_pairs={{160,144},{161,145},{162,146},{163,147},{164,148},{165,149},{166,1... | collective-permute-start | bytes 1179656 | tf_op jit(solution)/shard_map/ppermute | solution.py:165
  1149.7 45.2 %collective-permute-start.66 = (bf16[64,3072]{1,0:T(8,128)(2,1)S(1)}, bf16[64,3072]{1,0:T(8,128)(2,1)S(1)}, u32[]{:S(2)}, u32[]{:S(2)}) collective-permute-start(bf16[64,3072]{1,0:T(8,128)(2,1)S(1)} %get-tuple-element.598), channel_id=1, source_target_pairs={{160,144},{161,145},{162,146},{163,147},{164,148},{165,149},{166,1... | collective-permute-start | bytes 1179656 | tf_op jit(solution)/shard_map/ppermute | solution.py:165
  1469.4 81.6 %collective-permute-start.107 = (bf16[192,192]{1,0:T(8,128)(2,1)S(1)}, bf16[192,192]{1,0:T(8,128)(2,1)S(1)}, u32[]{:S(2)}, u32[]{:S(2)}) collective-permute-start(bf16[192,192]{1,0:T(8,128)(2,1)S(1)} %get-tuple-element.701), channel_id=1, source_target_pairs={{252,0},{253,1},{254,2},{255,3},{248,4},{249,5},{250,6},{251,7},{2... | collective-permute-start | bytes 221192 | tf_op jit(solution)/shard_map/ppermute | solution.py:177
  1500.5 203.4 %collective-permute-start.108 = (bf16[192,192]{1,0:T(8,128)(2,1)S(1)}, bf16[192,192]{1,0:T(8,128)(2,1)S(1)}, u32[]{:S(2)}, u32[]{:S(2)}) collective-permute-start(bf16[192,192]{1,0:T(8,128)(2,1)S(1)} %get-tuple-element.686), channel_id=1, source_target_pairs={{252,16},{253,17},{254,18},{255,19},{248,20},{249,21},{250,22},{25... | collective-permute-start | bytes 221192 | tf_op jit(solution)/shard_map/ppermute | solution.py:177
  1513.1 203.5 %collective-permute-start.109 = (bf16[192,192]{1,0:T(8,128)(2,1)S(1)}, bf16[192,192]{1,0:T(8,128)(2,1)S(1)}, u32[]{:S(2)}, u32[]{:S(2)}) collective-permute-start(bf16[192,192]{1,0:T(8,128)(2,1)S(1)} %get-tuple-element.700), channel_id=1, source_target_pairs={{252,32},{253,33},{254,34},{255,35},{248,36},{249,37},{250,38},{25... | collective-permute-start | bytes 221192 | tf_op jit(solution)/shard_map/ppermute | solution.py:177
  1525.7 203.5 %collective-permute-start.110 = (bf16[192,192]{1,0:T(8,128)(2,1)S(1)}, bf16[192,192]{1,0:T(8,128)(2,1)S(1)}, u32[]{:S(2)}, u32[]{:S(2)}) collective-permute-start(bf16[192,192]{1,0:T(8,128)(2,1)S(1)} %get-tuple-element.699), channel_id=1, source_target_pairs={{252,48},{253,49},{254,50},{255,51},{248,52},{249,53},{250,54},{25... | collective-permute-start | bytes 221192 | tf_op jit(solution)/shard_map/ppermute | solution.py:177
  1538.3 203.5 %collective-permute-start.111 = (bf16[192,192]{1,0:T(8,128)(2,1)S(1)}, bf16[192,192]{1,0:T(8,128)(2,1)S(1)}, u32[]{:S(2)}, u32[]{:S(2)}) collective-permute-start(bf16[192,192]{1,0:T(8,128)(2,1)S(1)} %get-tuple-element.698), channel_id=1, source_target_pairs={{252,64},{253,65},{254,66},{255,67},{248,68},{249,69},{250,70},{25... | collective-permute-start | bytes 221192 | tf_op jit(solution)/shard_map/ppermute | solution.py:177
  1551.0 203.4 %collective-permute-start.112 = (bf16[192,192]{1,0:T(8,128)(2,1)S(1)}, bf16[192,192]{1,0:T(8,128)(2,1)S(1)}, u32[]{:S(2)}, u32[]{:S(2)}) collective-permute-start(bf16[192,192]{1,0:T(8,128)(2,1)S(1)} %get-tuple-element.697), channel_id=1, source_target_pairs={{252,80},{253,81},{254,82},{255,83},{248,84},{249,85},{250,86},{25... | collective-permute-start | bytes 221192 | tf_op jit(solution)/shard_map/ppermute | solution.py:177
  1703.9 63.1 %collective-permute-start.113 = (bf16[192,192]{1,0:T(8,128)(2,1)S(1)}, bf16[192,192]{1,0:T(8,128)(2,1)S(1)}, u32[]{:S(2)}, u32[]{:S(2)}) collective-permute-start(bf16[192,192]{1,0:T(8,128)(2,1)S(1)} %get-tuple-element.696), channel_id=1, source_target_pairs={{252,96},{253,97},{254,98},{255,99},{248,100},{249,101},{250,102},... | collective-permute-start | bytes 221192 | tf_op jit(solution)/shard_map/ppermute | solution.py:177
  1716.6 63.5 %collective-permute-start.114 = (bf16[192,192]{1,0:T(8,128)(2,1)S(1)}, bf16[192,192]{1,0:T(8,128)(2,1)S(1)}, u32[]{:S(2)}, u32[]{:S(2)}) collective-permute-start(bf16[192,192]{1,0:T(8,128)(2,1)S(1)} %get-tuple-element.695), channel_id=1, source_target_pairs={{252,112},{253,113},{254,114},{255,115},{248,116},{249,117},{250,1... | collective-permute-start | bytes 221192 | tf_op jit(solution)/shard_map/ppermute | solution.py:177
  1729.2 63.5 %collective-permute-start.115 = (bf16[192,192]{1,0:T(8,128)(2,1)S(1)}, bf16[192,192]{1,0:T(8,128)(2,1)S(1)}, u32[]{:S(2)}, u32[]{:S(2)}) collective-permute-start(bf16[192,192]{1,0:T(8,128)(2,1)S(1)} %get-tuple-element.694), channel_id=1, source_target_pairs={{252,128},{253,129},{254,130},{255,131},{248,132},{249,133},{250,1... | collective-permute-start | bytes 221192 | tf_op jit(solution)/shard_map/ppermute | solution.py:177
  1741.8 63.5 %collective-permute-start.116 = (bf16[192,192]{1,0:T(8,128)(2,1)S(1)}, bf16[192,192]{1,0:T(8,128)(2,1)S(1)}, u32[]{:S(2)}, u32[]{:S(2)}) collective-permute-start(bf16[192,192]{1,0:T(8,128)(2,1)S(1)} %get-tuple-element.693), channel_id=1, source_target_pairs={{252,144},{253,145},{254,146},{255,147},{248,148},{249,149},{250,1... | collective-permute-start | bytes 221192 | tf_op jit(solution)/shard_map/ppermute | solution.py:177
  1754.4 63.5 %collective-permute-start.117 = (bf16[192,192]{1,0:T(8,128)(2,1)S(1)}, bf16[192,192]{1,0:T(8,128)(2,1)S(1)}, u32[]{:S(2)}, u32[]{:S(2)}) collective-permute-start(bf16[192,192]{1,0:T(8,128)(2,1)S(1)} %get-tuple-element.692), channel_id=1, source_target_pairs={{252,160},{253,161},{254,162},{255,163},{248,164},{249,165},{250,1... | collective-permute-start | bytes 221192 | tf_op jit(solution)/shard_map/ppermute | solution.py:177
  1767.0 63.5 %collective-permute-start.118 = (bf16[192,192]{1,0:T(8,128)(2,1)S(1)}, bf16[192,192]{1,0:T(8,128)(2,1)S(1)}, u32[]{:S(2)}, u32[]{:S(2)}) collective-permute-start(bf16[192,192]{1,0:T(8,128)(2,1)S(1)} %get-tuple-element.691), channel_id=1, source_target_pairs={{252,176},{253,177},{254,178},{255,179},{248,180},{249,181},{250,1... | collective-permute-start | bytes 221192 | tf_op jit(solution)/shard_map/ppermute | solution.py:177
  1780.1 51.1 %collective-permute-start.119 = (bf16[192,192]{1,0:T(8,128)(2,1)S(1)}, bf16[192,192]{1,0:T(8,128)(2,1)S(1)}, u32[]{:S(2)}, u32[]{:S(2)}) collective-permute-start(bf16[192,192]{1,0:T(8,128)(2,1)S(1)} %get-tuple-element.690), channel_id=1, source_target_pairs={{252,192},{253,193},{254,194},{255,195},{248,196},{249,197},{250,1... | collective-permute-start | bytes 221192 | tf_op jit(solution)/shard_map/ppermute | solution.py:177
  1838.8 82.7 %collective-permute-start.95 = (bf16[192,192]{1,0:T(8,128)(2,1)S(1)}, bf16[192,192]{1,0:T(8,128)(2,1)S(1)}, u32[]{:S(2)}, u32[]{:S(2)}) collective-permute-start(bf16[192,192]{1,0:T(8,128)(2,1)S(1)} %get-tuple-element.714), channel_id=1, source_target_pairs={{0,64},{1,65},{2,66},{3,67},{4,68},{5,69},{6,70},{7,71},{8,72},{9,... | collective-permute-start | bytes 221192 | tf_op jit(solution)/shard_map/ppermute | solution.py:177
  1839.5 82.0 %collective-permute-start.96 = (bf16[192,192]{1,0:T(8,128)(2,1)S(1)}, bf16[192,192]{1,0:T(8,128)(2,1)S(1)}, u32[]{:S(2)}, u32[]{:S(2)}) collective-permute-start(bf16[192,192]{1,0:T(8,128)(2,1)S(1)} %get-tuple-element.713), channel_id=1, source_target_pairs={{0,80},{1,81},{2,82},{3,83},{4,84},{5,85},{6,86},{7,87},{8,88},{9,... | collective-permute-start | bytes 221192 | tf_op jit(solution)/shard_map/ppermute | solution.py:177
  1840.2 81.3 %collective-permute-start.97 = (bf16[192,192]{1,0:T(8,128)(2,1)S(1)}, bf16[192,192]{1,0:T(8,128)(2,1)S(1)}, u32[]{:S(2)}, u32[]{:S(2)}) collective-permute-start(bf16[192,192]{1,0:T(8,128)(2,1)S(1)} %get-tuple-element.712), channel_id=1, source_target_pairs={{0,96},{1,97},{2,98},{3,99},{4,100},{5,101},{6,102},{7,103},{8,104... | collective-permute-start | bytes 221192 | tf_op jit(solution)/shard_map/ppermute | solution.py:177
  1840.8 80.6 %collective-permute-start.98 = (bf16[192,192]{1,0:T(8,128)(2,1)S(1)}, bf16[192,192]{1,0:T(8,128)(2,1)S(1)}, u32[]{:S(2)}, u32[]{:S(2)}) collective-permute-start(bf16[192,192]{1,0:T(8,128)(2,1)S(1)} %get-tuple-element.711), channel_id=1, source_target_pairs={{0,112},{1,113},{2,114},{3,115},{4,116},{5,117},{6,118},{7,119},{8... | collective-permute-start | bytes 221192 | tf_op jit(solution)/shard_map/ppermute | solution.py:177
  1841.5 80.0 %collective-permute-start.99 = (bf16[192,192]{1,0:T(8,128)(2,1)S(1)}, bf16[192,192]{1,0:T(8,128)(2,1)S(1)}, u32[]{:S(2)}, u32[]{:S(2)}) collective-permute-start(bf16[192,192]{1,0:T(8,128)(2,1)S(1)} %get-tuple-element.710), channel_id=1, source_target_pairs={{0,128},{1,129},{2,130},{3,131},{4,132},{5,133},{6,134},{7,135},{8... | collective-permute-start | bytes 221192 | tf_op jit(solution)/shard_map/ppermute | solution.py:177
  (92 other events, 1859.2 us)
Sparse Core Ops, SparseCore 0:
  9.8 231.2 all-gather.2
  1469.0 225.6 reduce-scatter.1

commit v2 on v1

--- a/solution.py
+++ b/solution.py
@@ -156,27 +156,25 @@
     return count - 4 - index // 4 * 4 + index % 4
 
 
-def hop(block, source, target, half, count):
-    crosses = (source < half) != (target < half)
-    route = [
-        (source * count + i, target * count + (mirrored(i, count) if crosses else i))
-        for i in range(count)
-    ]
-    return lax.ppermute(block, ("section", "dp"), route)
-
-
-def spread(block, owner, sections, count, turn):
-    share = block.shape[1] // sections
-    total = None
-    for s in range(sections):
-        route = [
-            (owner * count + (mirrored(i, count) if turn else i), s * count + i)
-            for i in range(count)
-        ]
-        piece = block[:, s * share : (s + 1) * share]
-        part = lax.ppermute(piece, ("section", "dp"), route)
-        total = part if total is None else total + part
-    return total
+def hop(block, lower, half, count):
+    if lower == half - 1:
+        lowers = [lower]
+    elif lower % 2:
+        lowers = [s for s in range(1, 2 * half - 1, 2) if s != half - 1]
+    else:
+        lowers = list(range(0, 2 * half, 2))
+    pairs = []
+    for s in lowers:
+        for i in range(count):
+            j = mirrored(i, count) if s == half - 1 else i
+            near, far = s * count + i, (s + 1) * count + j
+            pairs += [(near, far), (far, near)]
+    return lax.ppermute(block, ("section", "dp"), sorted(pairs))
+
+
+def shares(blocks, sections):
+    cut = jnp.stack([block.reshape(block.shape[0], sections, -1) for block in blocks])
+    return lax.all_to_all(cut, "section", split_axis=2, concat_axis=2)
 
 
 def on_device(inputs, cotangent, weight, gain):
@@ -188,12 +186,12 @@
     here = section.astype(jnp.int32).reshape(1)
     gain_row = lax.dynamic_index_in_dim(gain, section, 0, keepdims=True)
     across = [(i, mirrored(i, count)) for i in range(count)]
+    gathered = lax.all_gather(weight[0], "dp", axis=0, tiled=True)
+    gathered, cotangent, inputs, gain_row, here = lax.optimization_barrier(
+        (gathered, cotangent, inputs, gain_row, here)
+    )
+    matrix = hold(gathered)
     upstream = lax.ppermute(cotangent, "dp", across)
-    gathered = lax.all_gather(weight[0], "dp", axis=0, tiled=True)
-    gathered, upstream, inputs, gain_row, here = lax.optimization_barrier(
-        (gathered, upstream, inputs, gain_row, here)
-    )
-    matrix = hold(gathered)
 
     kept = [()] * micros
     current = [inputs] * micros
@@ -202,7 +200,7 @@
             turned = turn(matrix)
         for m in range(micros):
             result, *kept[m] = forward(t, m, here, current[m], gain_row, matrix, kept[m])
-            current[m] = hop(result, t, t + 1, half, count) if t + 1 < sections else result
+            current[m] = hop(result, t, half, count) if t + 1 < sections else result
     last = current
 
     passed = [()] * micros
@@ -213,7 +211,7 @@
             result, *passed[m] = backward(
                 t, m, here, arriving[m], saved, factor, gain_row, turned, passed[m]
             )
-            arriving[m] = hop(result, t, t - 1, half, count) if t else result
+            arriving[m] = hop(result, t - 1, half, count) if t else result
     slope = [passed[m][0] for m in range(micros)]
     total = sum(passed[m][1] for m in range(micros))
     normed = [kept[m][1] for m in range(micros)]
@@ -229,8 +227,9 @@
         tiled=True,
     )
     gain_grad = lax.psum(total, "dp")
-    final_share = spread(last, sections - 1, sections, count, True)
-    first_share = spread(first, 0, sections, count, False)
+    shared = shares((first, last), sections)
+    first_share = shared[0, :, 0]
+    final_share = lax.ppermute(shared[1, :, sections - 1], "dp", across)
     shape = (micros, rows, features // sections)
     return (
         summed[None],

time: 1950 us -> 1160 us (0.59)
  starting transfers between devices: 1500 us -> 401 us
  blocking collectives: 78.6 us -> 348 us
  Pallas kernels: 62.7 us -> 88.2 us
    ppermute x122 -> x91, starting transfers between devices: 1490 us -> 399 us  [the longest x90 364 us: hop(): return lax.ppermute(block, ('section', 'dp'), sorted(pairs))]
    psum x1, blocking collectives: 78.6 us -> 216 us  [on_device(): gain_grad = lax.psum(total, 'dp')]
    all_to_all x0 -> x1, blocking collectives: none -> 132 us  [shares(): return lax.all_to_all(cut, 'section', split_axis=2, concat_axis=2)]
    ppermute x1, waiting for transfers between devices: 52.5 us -> 0.01 us  [on_device(): upstream = lax.ppermute(cotangent, 'dp', across)]
    all_gather x1, waiting for transfers between devices: 167 us -> 208 us  [on_device(): gathered = lax.all_gather(weight[0], 'dp', axis=0, tiled=True)]
    pallas_call x98, Pallas kernels: 62.7 us -> 88.2 us  [call(): pl.pallas_call(kernel, out_shape=outs, in_specs=in_specs, out_specs=out_s...]
    ppermute x122 -> x91, waiting for transfers between devices: 0.32 us -> 22.6 us  [the longest x90 22.6 us: hop(): return lax.ppermute(block, ('section', 'dp'), sorted(pairs))]
    unnamed x66 -> x59, local copies, waits for them, and re-layouts: 40.1 us -> 41.5 us
  transfers between devices with their start and end apart: 125 -> 94, of which waited for: 2 -> 9; matrix products, arithmetic and copies ran while one was open for 0% -> 1% of each run, Pallas kernels for 3% -> 8%
where the time goes in v2:
time: 1160 us; the launch traced here: 1150 us
  starting transfers between devices  401 us (35%)
  blocking collectives  348 us (30%)
  waiting for transfers between devices  232 us (20%)
  Pallas kernels  88.2 us (8%)
  local copies, waits for them, and re-layouts  54 us (5%)
  between operations  16.2 us (1%)
    ppermute x90, starting transfers between devices, hop(): return lax.ppermute(block, ('section', 'dp'), sorted(pairs))  364 us
    psum x1, blocking collectives, on_device(): gain_grad = lax.psum(total, 'dp')  216 us
    all_gather x1, waiting for transfers between devices, on_device(): gathered = lax.all_gather(weight[0], 'dp', axis=0, tiled=True)  208 us
    all_to_all x1, blocking collectives, shares(): return lax.all_to_all(cut, 'section', split_axis=2, concat_axis=2)  132 us
    pallas_call x98, Pallas kernels, call(): pl.pallas_call(kernel, out_shape=outs, in_specs=in_specs, out_specs=out_s...  88.2 us
    unnamed x59, local copies, waits for them, and re-layouts  41.5 us
    ppermute x1, starting transfers between devices, on_device(): final_share = lax.ppermute(shared[1, :, sections - 1], 'dp', across)  34.2 us
  transfers between devices with their start and end apart: 94, of which 9 were waited for; matrix products, arithmetic and copies ran while one was open for 1% of the time, Pallas kernels for 8%

profile of v2, /device:TPU:128, one launch (start us, length us, event | category | flops | bytes accessed | tf_op | source)
XLA Modules:
  0.0 1151.4 jit_solution(2571759043451274079)
XLA Ops:
  8.1 208.4 %all-gather.3.cloned.1.call-done = bf16[1,3072,3072]{2,1,0:T(8,128)(2,1)} async-done(((bf16[1,192,3072]{2,1,0:T(8,128)(2,1)}), bf16[1,3072,3072]{2,1,0:T(8,128)(2,1)}) %all-gather.3.cloned.1.call-update) | async-done | bytes 18874384 | tf_op jit(solution)/shard_map/all_gather | solution.py:189
  216.5 6.4 copy-done.18
  228.6 5.5 shard_map.78
  236.3 3.7 collective-permute-start.32
  240.0 4.1 collective-permute-start.17
  246.7 5.3 shard_map.80
  254.2 3.8 collective-permute-start.34
  258.0 4.1 collective-permute-start.19
  264.9 5.2 shard_map.82
  272.7 3.6 collective-permute-start.36
  276.3 4.1 collective-permute-start.21
  280.7 68.5 %collective-permute-start.7 = (bf16[64,3072]{1,0:T(8,128)(2,1)S(1)}, bf16[64,3072]{1,0:T(8,128)(2,1)S(1)}, u32[]{:S(2)}, u32[]{:S(2)}) collective-permute-start(bf16[64,3072]{1,0:T(8,128)(2,1)S(1)} %get-tuple-element.377), channel_id=1, source_target_pairs={{112,140},{113,141},{114,142},{115,143},{116,136},{117,137},{118,1... | collective-permute-start | bytes 1179656 | tf_op jit(solution)/shard_map/ppermute | solution.py:172
  349.4 6.3 collective-permute-start.37
  355.8 7.0 collective-permute-start.22
  363.0 4.8 shard_map.84
  367.9 3.5 collective-permute-done.37.x_in
  371.5 4.4 shard_map.116
  376.0 4.4 shard_map.100
  383.2 5.3 shard_map.86
  388.4 12.4 %collective-permute-start.10 = (bf16[64,3072]{1,0:T(8,128)(2,1)S(1)}, bf16[64,3072]{1,0:T(8,128)(2,1)S(1)}, u32[]{:S(2)}, u32[]{:S(2)}) collective-permute-start(bf16[64,3072]{1,0:T(8,128)(2,1)S(1)} %get-tuple-element.389), channel_id=1, source_target_pairs={{0,16},{1,17},{2,18},{3,19},{4,20},{5,21},{6,22},{7,23},{8,24},{9,... | collective-permute-start | bytes 1179656 | tf_op jit(solution)/shard_map/ppermute | solution.py:172
  401.4 6.3 collective-permute-start.25
  410.5 5.6 shard_map.88
  416.1 8.5 collective-permute-start.12
  424.7 3.6 collective-permute-start.42
  435.1 5.5 shard_map.90
  440.6 11.8 %collective-permute-start.14 = (bf16[64,3072]{1,0:T(8,128)(2,1)S(1)}, bf16[64,3072]{1,0:T(8,128)(2,1)S(1)}, u32[]{:S(2)}, u32[]{:S(2)}) collective-permute-start(bf16[64,3072]{1,0:T(8,128)(2,1)S(1)} %get-tuple-element.405), channel_id=1, source_target_pairs={{0,16},{1,17},{2,18},{3,19},{4,20},{5,21},{6,22},{7,23},{8,24},{9,... | collective-permute-start | bytes 1179656 | tf_op jit(solution)/shard_map/ppermute | solution.py:172
  452.4 3.7 collective-permute-start.44
  456.2 4.0 collective-permute-start.29
  460.2 5.3 shard_map.124.turned
  465.7 6.3 copy-done.2
  472.0 6.4 copy-done.3
  480.9 6.4 copy-done.4
  490.1 6.4 copy-done.5
  502.3 3.8 shard_map.142
  506.8 11.5 %collective-permute-start.48 = (bf16[64,3072]{1,0:T(8,128)(2,1)S(1)}, bf16[64,3072]{1,0:T(8,128)(2,1)S(1)}, u32[]{:S(2)}, u32[]{:S(2)}) collective-permute-start(bf16[64,3072]{1,0:T(8,128)(2,1)S(1)} %get-tuple-element.541), channel_id=1, source_target_pairs={{0,16},{1,17},{2,18},{3,19},{4,20},{5,21},{6,22},{7,23},{8,24},{9,... | collective-permute-start | bytes 1179656 | tf_op jit(solution)/shard_map/ppermute | solution.py:172
  518.3 3.5 collective-permute-start.78
  522.1 4.2 collective-permute-start.63
  530.1 15.7 %collective-permute-start.50 = (bf16[64,3072]{1,0:T(8,128)(2,1)S(1)}, bf16[64,3072]{1,0:T(8,128)(2,1)S(1)}, u32[]{:S(2)}, u32[]{:S(2)}) collective-permute-start(bf16[64,3072]{1,0:T(8,128)(2,1)S(1)} %get-tuple-element.547), channel_id=1, source_target_pairs={{0,16},{1,17},{2,18},{3,19},{4,20},{5,21},{6,22},{7,23},{8,24},{9,... | collective-permute-start | bytes 1179656 | tf_op jit(solution)/shard_map/ppermute | solution.py:172
  545.9 3.5 collective-permute-start.80
  549.6 4.2 collective-permute-start.65
  557.4 76.9 %collective-permute-start.52 = (bf16[64,3072]{1,0:T(8,128)(2,1)S(1)}, bf16[64,3072]{1,0:T(8,128)(2,1)S(1)}, u32[]{:S(2)}, u32[]{:S(2)}) collective-permute-start(bf16[64,3072]{1,0:T(8,128)(2,1)S(1)} %get-tuple-element.553), channel_id=1, source_target_pairs={{0,16},{1,17},{2,18},{3,19},{4,20},{5,21},{6,22},{7,23},{8,24},{9,... | collective-permute-start | bytes 1179656 | tf_op jit(solution)/shard_map/ppermute | solution.py:172
  634.3 4.1 collective-permute-start.82
  638.9 4.2 collective-permute-start.67
  643.0 4.0 shard_map.132
  649.0 4.0 shard_map.164
  656.0 4.2 shard_map.148
  662.2 3.9 collective-permute-done.53.u_in
  666.2 8.3 collective-permute-done.83.u_in
  674.6 4.1 collective-permute-done.68.u_in
  680.7 5.5 shard_map.150
  688.8 4.2 collective-permute-start.86
  693.2 4.2 collective-permute-start.71
  701.0 5.6 collective-permute-start.58
  706.6 4.2 collective-permute-start.88
  711.2 4.2 collective-permute-start.73
  719.0 5.7 collective-permute-start.60
  724.7 4.2 collective-permute-start.90
  729.1 4.2 collective-permute-start.75
  736.1 10.1 convolution_convert_fusion
  747.4 3.9 stack_reshape.7
  754.3 3.9 stack_reshape.6
  760.8 131.5 %all_to_all.5 = bf16[2,192,16,192]{3,1,0,2:T(8,128)(2,1)S(1)} all-to-all(bf16[2,192,16,192]{3,1,0,2:T(8,128)(2,1)S(1)} %pad_maximum_fusion), channel_id=1, replica_groups=mesh['section'=16,'dp'=16] {'section'}, dimensions={2} | all-to-all | bytes 4718592 | tf_op jit(solution)/shard_map/all_to_all | solution.py:177
  893.0 34.2 %collective-permute-start.91 = (bf16[192,192]{1,0:T(8,128)(2,1)S(1)}, bf16[192,192]{1,0:T(8,128)(2,1)S(1)}, u32[]{:S(2)}, u32[]{:S(2)}) collective-permute-start(bf16[192,192]{1,0:T(8,128)(2,1)S(1)} %get-tuple-element.686), channel_id=1, source_target_pairs={{0,12},{1,13},{2,14},{3,15},{4,8},{5,9},{6,10},{7,11},{8,4},{9,5},... | collective-permute-start | bytes 221192 | tf_op jit(solution)/shard_map/ppermute | solution.py:232
  927.2 216.3 %psum.7 = f32[1,3072]{1,0:T(1,128)} all-reduce(f32[1,3072]{1,0:T(1,128)S(1)} %add_add_fusion), channel_id=1, replica_groups=mesh['section'=16,'dp'=16] {'dp'}, use_global_device_ids=true, to_apply=%region_1.2 | all-reduce | flops 3072 | bytes 24576 | tf_op jit(solution)/shard_map/psum | solution.py:229
  (296 shorter events, 82.7 us)
Async XLA Ops:
  7.2 209.3 %all-gather.3.cloned.1.call-start = ((), (), s32[]{:S(2)}) async-start(), calls=%async_computation.3 | async-start | bytes 20054016 | tf_op jit(solution)/shard_map/all_gather | solution.py:189
  7.9 1135.6 %reduce-scatter.2.cloned.1.call-start = ((), (), s32[]{:S(2)}) async-start(), calls=%async_computation.2 | async-start | bytes 20054016 | tf_op jit(solution)/shard_map/reduce_scatter | solution.py:220
  227.1 9.1 collective-permute-start.31
  227.9 12.0 %collective-permute-start.16 = (bf16[64,3072]{1,0:T(8,128)(2,1)S(1)}, bf16[64,3072]{1,0:T(8,128)(2,1)S(1)}, u32[]{:S(2)}, u32[]{:S(2)}) collective-permute-start(bf16[64,3072]{1,0:T(8,128)(2,1)S(1)} %get-tuple-element.414), channel_id=1, source_target_pairs={{16,32},{17,33},{18,34},{19,35},{20,36},{21,37},{22,38},{23,39},{2... | collective-permute-start | bytes 1179656 | tf_op jit(solution)/shard_map/ppermute | solution.py:172
  234.1 10.1 collective-permute-start.2
  236.3 8.8 collective-permute-start.32
  245.2 8.9 collective-permute-start.33
  246.0 11.9 %collective-permute-start.18 = (bf16[64,3072]{1,0:T(8,128)(2,1)S(1)}, bf16[64,3072]{1,0:T(8,128)(2,1)S(1)}, u32[]{:S(2)}, u32[]{:S(2)}) collective-permute-start(bf16[64,3072]{1,0:T(8,128)(2,1)S(1)} %get-tuple-element.422), channel_id=1, source_target_pairs={{16,32},{17,33},{18,34},{19,35},{20,36},{21,37},{22,38},{23,39},{2... | collective-permute-start | bytes 1179656 | tf_op jit(solution)/shard_map/ppermute | solution.py:172
  252.0 10.2 collective-permute-start.4
  254.2 9.1 collective-permute-start.34
  263.4 9.2 collective-permute-start.35
  264.2 12.1 %collective-permute-start.20 = (bf16[64,3072]{1,0:T(8,128)(2,1)S(1)}, bf16[64,3072]{1,0:T(8,128)(2,1)S(1)}, u32[]{:S(2)}, u32[]{:S(2)}) collective-permute-start(bf16[64,3072]{1,0:T(8,128)(2,1)S(1)} %get-tuple-element.430), channel_id=1, source_target_pairs={{16,32},{17,33},{18,34},{19,35},{20,36},{21,37},{22,38},{23,39},{2... | collective-permute-start | bytes 1179656 | tf_op jit(solution)/shard_map/ppermute | solution.py:172
  270.2 10.3 collective-permute-start.6
  272.7 76.6 %collective-permute-start.36 = (bf16[64,3072]{1,0:T(8,128)(2,1)S(1)}, bf16[64,3072]{1,0:T(8,128)(2,1)S(1)}, u32[]{:S(2)}, u32[]{:S(2)}) collective-permute-start(bf16[64,3072]{1,0:T(8,128)(2,1)S(1)} %get-tuple-element.495), channel_id=1, source_target_pairs={{0,16},{1,17},{2,18},{3,19},{4,20},{5,21},{6,22},{7,23},{8,24},{9,... | collective-permute-start | bytes 1179656 | tf_op jit(solution)/shard_map/ppermute | solution.py:172
  276.3 79.3 %collective-permute-start.21 = (bf16[64,3072]{1,0:T(8,128)(2,1)S(1)}, bf16[64,3072]{1,0:T(8,128)(2,1)S(1)}, u32[]{:S(2)}, u32[]{:S(2)}) collective-permute-start(bf16[64,3072]{1,0:T(8,128)(2,1)S(1)} %get-tuple-element.434), channel_id=1, source_target_pairs={{0,16},{1,17},{2,18},{3,19},{4,20},{5,21},{6,22},{7,23},{8,24},{9,... | collective-permute-start | bytes 1179656 | tf_op jit(solution)/shard_map/ppermute | solution.py:172
  280.7 82.2 %collective-permute-start.7 = (bf16[64,3072]{1,0:T(8,128)(2,1)S(1)}, bf16[64,3072]{1,0:T(8,128)(2,1)S(1)}, u32[]{:S(2)}, u32[]{:S(2)}) collective-permute-start(bf16[64,3072]{1,0:T(8,128)(2,1)S(1)} %get-tuple-element.377), channel_id=1, source_target_pairs={{112,140},{113,141},{114,142},{115,143},{116,136},{117,137},{118,1... | collective-permute-start | bytes 1179656 | tf_op jit(solution)/shard_map/ppermute | solution.py:172
  349.4 22.1 %collective-permute-start.37 = (bf16[64,3072]{1,0:T(8,128)(2,1)S(1)}, bf16[64,3072]{1,0:T(8,128)(2,1)S(1)}, u32[]{:S(2)}, u32[]{:S(2)}) collective-permute-start(bf16[64,3072]{1,0:T(8,128)(2,1)S(1)} %get-tuple-element.499), channel_id=1, source_target_pairs={{112,140},{113,141},{114,142},{115,143},{116,136},{117,137},{118,1... | collective-permute-start | bytes 1179656 | tf_op jit(solution)/shard_map/ppermute | solution.py:172
  355.8 20.3 %collective-permute-start.22 = (bf16[64,3072]{1,0:T(8,128)(2,1)S(1)}, bf16[64,3072]{1,0:T(8,128)(2,1)S(1)}, u32[]{:S(2)}, u32[]{:S(2)}) collective-permute-start(bf16[64,3072]{1,0:T(8,128)(2,1)S(1)} %get-tuple-element.438), channel_id=1, source_target_pairs={{112,140},{113,141},{114,142},{115,143},{116,136},{117,137},{118,1... | collective-permute-start | bytes 1179656 | tf_op jit(solution)/shard_map/ppermute | solution.py:172
  367.8 12.8 %collective-permute-start.8 = (bf16[64,3072]{1,0:T(8,128)(2,1)S(1)}, bf16[64,3072]{1,0:T(8,128)(2,1)S(1)}, u32[]{:S(2)}, u32[]{:S(2)}) collective-permute-start(bf16[64,3072]{1,0:T(8,128)(2,1)S(1)} %get-tuple-element.381), channel_id=1, source_target_pairs={{0,16},{1,17},{2,18},{3,19},{4,20},{5,21},{6,22},{7,23},{8,24},{9,... | collective-permute-start | bytes 1179656 | tf_op jit(solution)/shard_map/ppermute | solution.py:172
  381.7 19.2 %collective-permute-start.39 = (bf16[64,3072]{1,0:T(8,128)(2,1)S(1)}, bf16[64,3072]{1,0:T(8,128)(2,1)S(1)}, u32[]{:S(2)}, u32[]{:S(2)}) collective-permute-start(bf16[64,3072]{1,0:T(8,128)(2,1)S(1)} %get-tuple-element.507), channel_id=1, source_target_pairs={{16,32},{17,33},{18,34},{19,35},{20,36},{21,37},{22,38},{23,39},{2... | collective-permute-start | bytes 1179656 | tf_op jit(solution)/shard_map/ppermute | solution.py:172
  382.4 18.9 %collective-permute-start.24 = (bf16[64,3072]{1,0:T(8,128)(2,1)S(1)}, bf16[64,3072]{1,0:T(8,128)(2,1)S(1)}, u32[]{:S(2)}, u32[]{:S(2)}) collective-permute-start(bf16[64,3072]{1,0:T(8,128)(2,1)S(1)} %get-tuple-element.446), channel_id=1, source_target_pairs={{16,32},{17,33},{18,34},{19,35},{20,36},{21,37},{22,38},{23,39},{2... | collective-permute-start | bytes 1179656 | tf_op jit(solution)/shard_map/ppermute | solution.py:172
  388.4 19.3 %collective-permute-start.10 = (bf16[64,3072]{1,0:T(8,128)(2,1)S(1)}, bf16[64,3072]{1,0:T(8,128)(2,1)S(1)}, u32[]{:S(2)}, u32[]{:S(2)}) collective-permute-start(bf16[64,3072]{1,0:T(8,128)(2,1)S(1)} %get-tuple-element.389), channel_id=1, source_target_pairs={{0,16},{1,17},{2,18},{3,19},{4,20},{5,21},{6,22},{7,23},{8,24},{9,... | collective-permute-start | bytes 1179656 | tf_op jit(solution)/shard_map/ppermute | solution.py:172
  401.4 8.3 collective-permute-start.25
  409.0 15.6 %collective-permute-start.41 = (bf16[64,3072]{1,0:T(8,128)(2,1)S(1)}, bf16[64,3072]{1,0:T(8,128)(2,1)S(1)}, u32[]{:S(2)}, u32[]{:S(2)}) collective-permute-start(bf16[64,3072]{1,0:T(8,128)(2,1)S(1)} %get-tuple-element.515), channel_id=1, source_target_pairs={{16,32},{17,33},{18,34},{19,35},{20,36},{21,37},{22,38},{23,39},{2... | collective-permute-start | bytes 1179656 | tf_op jit(solution)/shard_map/ppermute | solution.py:172
  409.8 20.6 %collective-permute-start.26 = (bf16[64,3072]{1,0:T(8,128)(2,1)S(1)}, bf16[64,3072]{1,0:T(8,128)(2,1)S(1)}, u32[]{:S(2)}, u32[]{:S(2)}) collective-permute-start(bf16[64,3072]{1,0:T(8,128)(2,1)S(1)} %get-tuple-element.454), channel_id=1, source_target_pairs={{16,32},{17,33},{18,34},{19,35},{20,36},{21,37},{22,38},{23,39},{2... | collective-permute-start | bytes 1179656 | tf_op jit(solution)/shard_map/ppermute | solution.py:172
  416.1 16.4 %collective-permute-start.12 = (bf16[64,3072]{1,0:T(8,128)(2,1)S(1)}, bf16[64,3072]{1,0:T(8,128)(2,1)S(1)}, u32[]{:S(2)}, u32[]{:S(2)}) collective-permute-start(bf16[64,3072]{1,0:T(8,128)(2,1)S(1)} %get-tuple-element.397), channel_id=1, source_target_pairs={{0,16},{1,17},{2,18},{3,19},{4,20},{5,21},{6,22},{7,23},{8,24},{9,... | collective-permute-start | bytes 1179656 | tf_op jit(solution)/shard_map/ppermute | solution.py:172
  424.7 8.8 collective-permute-start.42
  428.3 43.6 %collective-permute-start.45 = (bf16[3,64,3072]{2,1,0:T(8,128)(2,1)S(1)}, bf16[3,64,3072]{2,1,0:T(8,128)(2,1)S(1)}, u32[]{:S(2)}, u32[]{:S(2)}) collective-permute-start(bf16[3,64,3072]{2,1,0:T(8,128)(2,1)S(1)} %copy-done.28), channel_id=1, source_target_pairs={{0,12},{1,13},{2,14},{3,15},{4,8},{5,9},{6,10},{7,11},{8,4},{9,5},... | collective-permute-start | bytes 3538952 | tf_op jit(solution)/shard_map/ppermute | solution.py:194
  433.6 18.7 %collective-permute-start.43 = (bf16[64,3072]{1,0:T(8,128)(2,1)S(1)}, bf16[64,3072]{1,0:T(8,128)(2,1)S(1)}, u32[]{:S(2)}, u32[]{:S(2)}) collective-permute-start(bf16[64,3072]{1,0:T(8,128)(2,1)S(1)} %get-tuple-element.523), channel_id=1, source_target_pairs={{16,32},{17,33},{18,34},{19,35},{20,36},{21,37},{22,38},{23,39},{2... | collective-permute-start | bytes 1179656 | tf_op jit(solution)/shard_map/ppermute | solution.py:172
  434.4 21.7 %collective-permute-start.28 = (bf16[64,3072]{1,0:T(8,128)(2,1)S(1)}, bf16[64,3072]{1,0:T(8,128)(2,1)S(1)}, u32[]{:S(2)}, u32[]{:S(2)}) collective-permute-start(bf16[64,3072]{1,0:T(8,128)(2,1)S(1)} %get-tuple-element.462), channel_id=1, source_target_pairs={{16,32},{17,33},{18,34},{19,35},{20,36},{21,37},{22,38},{23,39},{2... | collective-permute-start | bytes 1179656 | tf_op jit(solution)/shard_map/ppermute | solution.py:172
  440.6 25.0 %collective-permute-start.14 = (bf16[64,3072]{1,0:T(8,128)(2,1)S(1)}, bf16[64,3072]{1,0:T(8,128)(2,1)S(1)}, u32[]{:S(2)}, u32[]{:S(2)}) collective-permute-start(bf16[64,3072]{1,0:T(8,128)(2,1)S(1)} %get-tuple-element.405), channel_id=1, source_target_pairs={{0,16},{1,17},{2,18},{3,19},{4,20},{5,21},{6,22},{7,23},{8,24},{9,... | collective-permute-start | bytes 1179656 | tf_op jit(solution)/shard_map/ppermute | solution.py:172
  452.4 28.1 %collective-permute-start.44 = (bf16[64,3072]{1,0:T(8,128)(2,1)S(1)}, bf16[64,3072]{1,0:T(8,128)(2,1)S(1)}, u32[]{:S(2)}, u32[]{:S(2)}) collective-permute-start(bf16[64,3072]{1,0:T(8,128)(2,1)S(1)} %get-tuple-element.527), channel_id=1, source_target_pairs={{0,16},{1,17},{2,18},{3,19},{4,20},{5,21},{6,22},{7,23},{8,24},{9,... | collective-permute-start | bytes 1179656 | tf_op jit(solution)/shard_map/ppermute | solution.py:172
  456.2 33.8 %collective-permute-start.29 = (bf16[64,3072]{1,0:T(8,128)(2,1)S(1)}, bf16[64,3072]{1,0:T(8,128)(2,1)S(1)}, u32[]{:S(2)}, u32[]{:S(2)}) collective-permute-start(bf16[64,3072]{1,0:T(8,128)(2,1)S(1)} %get-tuple-element.466), channel_id=1, source_target_pairs={{0,16},{1,17},{2,18},{3,19},{4,20},{5,21},{6,22},{7,23},{8,24},{9,... | collective-permute-start | bytes 1179656 | tf_op jit(solution)/shard_map/ppermute | solution.py:172
  480.5 18.6 %collective-permute-start.46 = (bf16[64,3072]{1,0:T(8,128)(2,1)S(1)}, bf16[64,3072]{1,0:T(8,128)(2,1)S(1)}, u32[]{:S(2)}, u32[]{:S(2)}) collective-permute-start(bf16[64,3072]{1,0:T(8,128)(2,1)S(1)} %get-tuple-element.535), channel_id=1, source_target_pairs={{0,16},{1,17},{2,18},{3,19},{4,20},{5,21},{6,22},{7,23},{8,24},{9,... | collective-permute-start | bytes 1179656 | tf_op jit(solution)/shard_map/ppermute | solution.py:172
  489.4 11.2 collective-permute-start.76
  501.1 17.3 %collective-permute-start.77 = (bf16[64,3072]{1,0:T(8,128)(2,1)S(1)}, bf16[64,3072]{1,0:T(8,128)(2,1)S(1)}, u32[]{:S(2)}, u32[]{:S(2)}) collective-permute-start(bf16[64,3072]{1,0:T(8,128)(2,1)S(1)} %get-tuple-element.634), channel_id=1, source_target_pairs={{16,32},{17,33},{18,34},{19,35},{20,36},{21,37},{22,38},{23,39},{2... | collective-permute-start | bytes 1179656 | tf_op jit(solution)/shard_map/ppermute | solution.py:172
  506.0 15.8 %collective-permute-start.62 = (bf16[64,3072]{1,0:T(8,128)(2,1)S(1)}, bf16[64,3072]{1,0:T(8,128)(2,1)S(1)}, u32[]{:S(2)}, u32[]{:S(2)}) collective-permute-start(bf16[64,3072]{1,0:T(8,128)(2,1)S(1)} %get-tuple-element.586), channel_id=1, source_target_pairs={{16,32},{17,33},{18,34},{19,35},{20,36},{21,37},{22,38},{23,39},{2... | collective-permute-start | bytes 1179656 | tf_op jit(solution)/shard_map/ppermute | solution.py:172
  506.8 19.5 %collective-permute-start.48 = (bf16[64,3072]{1,0:T(8,128)(2,1)S(1)}, bf16[64,3072]{1,0:T(8,128)(2,1)S(1)}, u32[]{:S(2)}, u32[]{:S(2)}) collective-permute-start(bf16[64,3072]{1,0:T(8,128)(2,1)S(1)} %get-tuple-element.541), channel_id=1, source_target_pairs={{0,16},{1,17},{2,18},{3,19},{4,20},{5,21},{6,22},{7,23},{8,24},{9,... | collective-permute-start | bytes 1179656 | tf_op jit(solution)/shard_map/ppermute | solution.py:172
  518.3 8.7 collective-permute-start.78
  527.0 18.8 %collective-permute-start.79 = (bf16[64,3072]{1,0:T(8,128)(2,1)S(1)}, bf16[64,3072]{1,0:T(8,128)(2,1)S(1)}, u32[]{:S(2)}, u32[]{:S(2)}) collective-permute-start(bf16[64,3072]{1,0:T(8,128)(2,1)S(1)} %get-tuple-element.640), channel_id=1, source_target_pairs={{16,32},{17,33},{18,34},{19,35},{20,36},{21,37},{22,38},{23,39},{2... | collective-permute-start | bytes 1179656 | tf_op jit(solution)/shard_map/ppermute | solution.py:172
  529.4 20.0 %collective-permute-start.64 = (bf16[64,3072]{1,0:T(8,128)(2,1)S(1)}, bf16[64,3072]{1,0:T(8,128)(2,1)S(1)}, u32[]{:S(2)}, u32[]{:S(2)}) collective-permute-start(bf16[64,3072]{1,0:T(8,128)(2,1)S(1)} %get-tuple-element.592), channel_id=1, source_target_pairs={{16,32},{17,33},{18,34},{19,35},{20,36},{21,37},{22,38},{23,39},{2... | collective-permute-start | bytes 1179656 | tf_op jit(solution)/shard_map/ppermute | solution.py:172
  530.1 23.6 %collective-permute-start.50 = (bf16[64,3072]{1,0:T(8,128)(2,1)S(1)}, bf16[64,3072]{1,0:T(8,128)(2,1)S(1)}, u32[]{:S(2)}, u32[]{:S(2)}) collective-permute-start(bf16[64,3072]{1,0:T(8,128)(2,1)S(1)} %get-tuple-element.547), channel_id=1, source_target_pairs={{0,16},{1,17},{2,18},{3,19},{4,20},{5,21},{6,22},{7,23},{8,24},{9,... | collective-permute-start | bytes 1179656 | tf_op jit(solution)/shard_map/ppermute | solution.py:172
  545.9 8.6 collective-permute-start.80
  554.5 79.8 %collective-permute-start.81 = (bf16[64,3072]{1,0:T(8,128)(2,1)S(1)}, bf16[64,3072]{1,0:T(8,128)(2,1)S(1)}, u32[]{:S(2)}, u32[]{:S(2)}) collective-permute-start(bf16[64,3072]{1,0:T(8,128)(2,1)S(1)} %get-tuple-element.646), channel_id=1, source_target_pairs={{16,32},{17,33},{18,34},{19,35},{20,36},{21,37},{22,38},{23,39},{2... | collective-permute-start | bytes 1179656 | tf_op jit(solution)/shard_map/ppermute | solution.py:172
  556.7 81.8 %collective-permute-start.66 = (bf16[64,3072]{1,0:T(8,128)(2,1)S(1)}, bf16[64,3072]{1,0:T(8,128)(2,1)S(1)}, u32[]{:S(2)}, u32[]{:S(2)}) collective-permute-start(bf16[64,3072]{1,0:T(8,128)(2,1)S(1)} %get-tuple-element.598), channel_id=1, source_target_pairs={{16,32},{17,33},{18,34},{19,35},{20,36},{21,37},{22,38},{23,39},{2... | collective-permute-start | bytes 1179656 | tf_op jit(solution)/shard_map/ppermute | solution.py:172
  557.4 85.6 %collective-permute-start.52 = (bf16[64,3072]{1,0:T(8,128)(2,1)S(1)}, bf16[64,3072]{1,0:T(8,128)(2,1)S(1)}, u32[]{:S(2)}, u32[]{:S(2)}) collective-permute-start(bf16[64,3072]{1,0:T(8,128)(2,1)S(1)} %get-tuple-element.553), channel_id=1, source_target_pairs={{0,16},{1,17},{2,18},{3,19},{4,20},{5,21},{6,22},{7,23},{8,24},{9,... | collective-permute-start | bytes 1179656 | tf_op jit(solution)/shard_map/ppermute | solution.py:172
  634.3 14.7 %collective-permute-start.82 = (bf16[64,3072]{1,0:T(8,128)(2,1)S(1)}, bf16[64,3072]{1,0:T(8,128)(2,1)S(1)}, u32[]{:S(2)}, u32[]{:S(2)}) collective-permute-start(bf16[64,3072]{1,0:T(8,128)(2,1)S(1)} %get-tuple-element.649), channel_id=1, source_target_pairs={{0,16},{1,17},{2,18},{3,19},{4,20},{5,21},{6,22},{7,23},{8,24},{9,... | collective-permute-start | bytes 1179656 | tf_op jit(solution)/shard_map/ppermute | solution.py:172
  638.9 17.2 %collective-permute-start.67 = (bf16[64,3072]{1,0:T(8,128)(2,1)S(1)}, bf16[64,3072]{1,0:T(8,128)(2,1)S(1)}, u32[]{:S(2)}, u32[]{:S(2)}) collective-permute-start(bf16[64,3072]{1,0:T(8,128)(2,1)S(1)} %get-tuple-element.601), channel_id=1, source_target_pairs={{0,16},{1,17},{2,18},{3,19},{4,20},{5,21},{6,22},{7,23},{8,24},{9,... | collective-permute-start | bytes 1179656 | tf_op jit(solution)/shard_map/ppermute | solution.py:172
  647.1 19.0 %collective-permute-start.53 = (bf16[64,3072]{1,0:T(8,128)(2,1)S(1)}, bf16[64,3072]{1,0:T(8,128)(2,1)S(1)}, u32[]{:S(2)}, u32[]{:S(2)}) collective-permute-start(bf16[64,3072]{1,0:T(8,128)(2,1)S(1)} %get-tuple-element.556), channel_id=1, source_target_pairs={{112,140},{113,141},{114,142},{115,143},{116,136},{117,137},{118,1... | collective-permute-start | bytes 1179656 | tf_op jit(solution)/shard_map/ppermute | solution.py:172
  653.1 21.4 %collective-permute-start.83 = (bf16[64,3072]{1,0:T(8,128)(2,1)S(1)}, bf16[64,3072]{1,0:T(8,128)(2,1)S(1)}, u32[]{:S(2)}, u32[]{:S(2)}) collective-permute-start(bf16[64,3072]{1,0:T(8,128)(2,1)S(1)} %get-tuple-element.652), channel_id=1, source_target_pairs={{112,140},{113,141},{114,142},{115,143},{116,136},{117,137},{118,1... | collective-permute-start | bytes 1179656 | tf_op jit(solution)/shard_map/ppermute | solution.py:172
  660.3 18.4 %collective-permute-start.68 = (bf16[64,3072]{1,0:T(8,128)(2,1)S(1)}, bf16[64,3072]{1,0:T(8,128)(2,1)S(1)}, u32[]{:S(2)}, u32[]{:S(2)}) collective-permute-start(bf16[64,3072]{1,0:T(8,128)(2,1)S(1)} %get-tuple-element.604), channel_id=1, source_target_pairs={{112,140},{113,141},{114,142},{115,143},{116,136},{117,137},{118,1... | collective-permute-start | bytes 1179656 | tf_op jit(solution)/shard_map/ppermute | solution.py:172
  666.1 12.9 %collective-permute-start.54 = (bf16[64,3072]{1,0:T(8,128)(2,1)S(1)}, bf16[64,3072]{1,0:T(8,128)(2,1)S(1)}, u32[]{:S(2)}, u32[]{:S(2)}) collective-permute-start(bf16[64,3072]{1,0:T(8,128)(2,1)S(1)} %get-tuple-element.559), channel_id=1, source_target_pairs={{0,16},{1,17},{2,18},{3,19},{4,20},{5,21},{6,22},{7,23},{8,24},{9,... | collective-permute-start | bytes 1179656 | tf_op jit(solution)/shard_map/ppermute | solution.py:172
  679.8 9.0 collective-permute-start.85
  687.0 10.4 collective-permute-start.56
  688.8 9.3 collective-permute-start.86
  698.1 8.5 collective-permute-start.87
  700.3 10.6 collective-permute-start.72
  701.0 14.4 %collective-permute-start.58 = (bf16[64,3072]{1,0:T(8,128)(2,1)S(1)}, bf16[64,3072]{1,0:T(8,128)(2,1)S(1)}, u32[]{:S(2)}, u32[]{:S(2)}) collective-permute-start(bf16[64,3072]{1,0:T(8,128)(2,1)S(1)} %get-tuple-element.571), channel_id=1, source_target_pairs={{0,16},{1,17},{2,18},{3,19},{4,20},{5,21},{6,22},{7,23},{8,24},{9,... | collective-permute-start | bytes 1179656 | tf_op jit(solution)/shard_map/ppermute | solution.py:172
  706.6 9.5 collective-permute-start.88
  716.2 8.5 collective-permute-start.89
  718.3 10.6 collective-permute-start.74
  719.0 14.3 %collective-permute-start.60 = (bf16[64,3072]{1,0:T(8,128)(2,1)S(1)}, bf16[64,3072]{1,0:T(8,128)(2,1)S(1)}, u32[]{:S(2)}, u32[]{:S(2)}) collective-permute-start(bf16[64,3072]{1,0:T(8,128)(2,1)S(1)} %get-tuple-element.577), channel_id=1, source_target_pairs={{0,16},{1,17},{2,18},{3,19},{4,20},{5,21},{6,22},{7,23},{8,24},{9,... | collective-permute-start | bytes 1179656 | tf_op jit(solution)/shard_map/ppermute | solution.py:172
  724.7 8.6 collective-permute-start.90
  893.0 250.6 %collective-permute-start.91 = (bf16[192,192]{1,0:T(8,128)(2,1)S(1)}, bf16[192,192]{1,0:T(8,128)(2,1)S(1)}, u32[]{:S(2)}, u32[]{:S(2)}) collective-permute-start(bf16[192,192]{1,0:T(8,128)(2,1)S(1)} %get-tuple-element.686), channel_id=1, source_target_pairs={{0,12},{1,13},{2,14},{3,15},{4,8},{5,9},{6,10},{7,11},{8,4},{9,5},... | collective-permute-start | bytes 221192 | tf_op jit(solution)/shard_map/ppermute | solution.py:232
  (59 other events, 1066.8 us)
Sparse Core Ops, SparseCore 0:
  9.8 206.6 all-gather.2
  746.4 325.8 reduce-scatter.1

commit v3 on v2

--- a/solution.py
+++ b/solution.py
@@ -2,6 +2,7 @@
 
 import jax
 import jax.numpy as jnp
+import numpy as np
 from jax import lax
 from jax.experimental import pallas as pl
 from jax.experimental.pallas import tpu as pltpu
@@ -54,6 +55,10 @@
 def turn(matrix):
     shape = pltpu.VMEM(matrix.shape, matrix.dtype)
     return call(turn_kernel, shape, [VMEM], VMEM, {}, [], [matrix])
+
+
+def in_hbm(array):
+    return pltpu.with_memory_space_constraint(array, pltpu.HBM)
 
 
 def unit_of(values):
@@ -87,13 +92,13 @@
             copy.wait()
 
 
-def forward(t, m, section, x, gain_row, matrix, kept):
+def forward(t, m, section, x, gain_row, matrix, kept, after):
     shape = x.shape[-2:]
     wide, deep = pltpu.HBM(shape, BF), pltpu.HBM(shape, F32)
     return call(
         functools.partial(forward_kernel, t, m if x.ndim == 3 else None),
         (pltpu.VMEM(shape, BF), wide, wide, deep),
-        [SMEM] + [VMEM] * 3 + [HBM] * len(kept),
+        [SMEM] + [VMEM] * 3 + [HBM] * (len(kept) + len(after)),
         (VMEM, HBM, HBM, HBM),
         {4 + i: 1 + i for i in range(len(kept))},
         [
@@ -102,12 +107,13 @@
             pltpu.VMEM(shape, F32),
             pltpu.SemaphoreType.DMA((2 + shape[1] // TILE,)),
         ],
-        [section, x, gain_row, matrix, *kept],
-    )
-
-
-def backward_kernel(t, m, section, u_in, saved, factor, gain, turned, *refs):
-    d, slope_out, term_out, slope, term, grad, sems = refs[-7:]
+        [section, x, gain_row, matrix, *kept, *after],
+    )
+
+
+def backward_kernel(t, m, pins, section, u_in, saved, factor, gain, turned, *refs):
+    slope, term, grad, sems = refs[-4:]
+    d, slope_out, term_out = refs[-7 - pins : len(refs) - 4 - pins]
 
     @pl.when(section[0] == t)
     def _():
@@ -130,25 +136,29 @@
         keep_term.wait()
 
 
-def backward(t, m, section, u, saved, factor, gain_row, turned, kept):
+def backward(t, m, section, u, saved, factor, gain_row, turned, kept, after, pinned):
     shape = saved.shape
+    first = 6 + len(kept) + len(after)
+    aliases = {6 + i: 1 + i for i in range(len(kept))}
+    aliases.update({first + i: 3 + i for i in range(len(pinned))})
     return call(
-        functools.partial(backward_kernel, t, m if u.ndim == 3 else None),
+        functools.partial(backward_kernel, t, m if u.ndim == 3 else None, len(pinned)),
         (
             pltpu.VMEM(shape, BF),
             pltpu.HBM(shape, BF),
             pltpu.HBM((1, shape[1]), F32),
+            *(pltpu.HBM(p.shape, p.dtype) for p in pinned),
         ),
-        [SMEM] + [VMEM] * 5 + [HBM] * len(kept),
-        (VMEM, HBM, HBM),
-        {6 + i: 1 + i for i in range(len(kept))},
+        [SMEM] + [VMEM] * 5 + [HBM] * (first - 6 + len(pinned)),
+        (VMEM,) + (HBM,) * (2 + len(pinned)),
+        aliases,
         [
             pltpu.VMEM(shape, BF),
             pltpu.VMEM((1, shape[1]), F32),
             pltpu.VMEM(shape, F32),
             pltpu.SemaphoreType.DMA((2,)),
         ],
-        [section, u, saved, factor, gain_row, turned, *kept],
+        [section, u, saved, factor, gain_row, turned, *kept, *after, *pinned],
     )
 
 
@@ -157,24 +167,68 @@
 
 
 def hop(block, lower, half, count):
-    if lower == half - 1:
-        lowers = [lower]
-    elif lower % 2:
-        lowers = [s for s in range(1, 2 * half - 1, 2) if s != half - 1]
-    else:
-        lowers = list(range(0, 2 * half, 2))
     pairs = []
-    for s in lowers:
+    for t in [lower] if lower == half - 1 else [lower % half, lower % half + half]:
         for i in range(count):
-            j = mirrored(i, count) if s == half - 1 else i
-            near, far = s * count + i, (s + 1) * count + j
+            j = mirrored(i, count) if t == half - 1 else i
+            near, far = t * count + i, (t + 1) * count + j
             pairs += [(near, far), (far, near)]
     return lax.ppermute(block, ("section", "dp"), sorted(pairs))
 
 
-def shares(blocks, sections):
-    cut = jnp.stack([block.reshape(block.shape[0], sections, -1) for block in blocks])
-    return lax.all_to_all(cut, "section", split_axis=2, concat_axis=2)
+def order(sections, micros):
+    steps = [(t, m) for t in range(sections) for m in range(micros)]
+    return sorted(steps, key=lambda p: micros * p[0] + (micros - 1) * p[1])
+
+
+def spread(block, owner, sections, section):
+    bit = sections // 2
+    while bit:
+        width = block.shape[1] // 2
+        low, high = block[:, :width], block[:, width:]
+        upper = (section & bit) != 0
+        pairs = [(s, s ^ bit) for s in range(sections)]
+        arrived = lax.ppermute(jnp.where(upper, low, high), "section", pairs)
+        block = jnp.where(upper == bool(owner & bit), jnp.where(upper, high, low), arrived)
+        bit //= 2
+    return block
+
+
+RING = (0, 2, 3, 1)
+
+
+def z_after(z, k):
+    return RING[(RING.index(z) + k) % len(RING)]
+
+
+def shift_z(block, k, count):
+    pairs = [(i, 4 * z_after(i // 4, k) + i % 4) for i in range(count)]
+    return lax.ppermute(block, "dp", pairs)
+
+
+def shift_y(block, k, count):
+    pairs = [(i, i // 4 * 4 + (i + k) % 4) for i in range(count)]
+    return lax.ppermute(block, "dp", pairs)
+
+
+def pick(blocks, at):
+    return lax.dynamic_index_in_dim(blocks, at, 0, keepdims=False)
+
+
+def from_all_y(block, count):
+    left, right = shift_y(block, 1, count), shift_y(block, 3, count)
+    rows = block.shape[0] // 2
+    far = jnp.concatenate(
+        [shift_y(left[:rows], 1, count), shift_y(right[rows:], 3, count)], axis=0
+    )
+    return [block, left, far, right]
+
+
+def from_all_z(block, count):
+    blocks = [block]
+    for _ in range(3):
+        blocks.append(shift_z(blocks[-1], 1, count))
+    return blocks
 
 
 def on_device(inputs, cotangent, weight, gain):
@@ -182,6 +236,12 @@
     count = lax.axis_size("dp")
     half = sections // 2
     section = lax.axis_index("section")
+    place = lax.axis_index("dp")
+    z, y = place // 4, place % 4
+    ahead = jnp.asarray([[z_after(i, k) for i in range(4)] for k in range(4)], jnp.int32)
+    behind = jnp.asarray([[z_after(i, -k) for i in range(4)] for k in range(4)], jnp.int32)
+    to_z = [ahead[k, z] for k in range(4)]
+    from_z = [behind[k, z] for k in range(4)]
     micros, rows, features = inputs.shape
     here = section.astype(jnp.int32).reshape(1)
     gain_row = lax.dynamic_index_in_dim(gain, section, 0, keepdims=True)
@@ -195,45 +255,64 @@
 
     kept = [()] * micros
     current = [inputs] * micros
-    for t in range(sections):
-        if t == half:
+    after = ()
+    turned = None
+    for t, m in order(sections, micros):
+        if t == half and turned is None:
             turned = turn(matrix)
-        for m in range(micros):
-            result, *kept[m] = forward(t, m, here, current[m], gain_row, matrix, kept[m])
-            current[m] = hop(result, t, half, count) if t + 1 < sections else result
-    last = current
+        result, *kept[m] = forward(t, m, here, current[m], gain_row, matrix, kept[m], after)
+        after = (in_hbm(kept[m][0]),)
+        current[m] = hop(result, t, half, count) if t + 1 < sections else result
 
     passed = [()] * micros
     arriving = [upstream] * micros
-    for t in reversed(range(sections)):
-        for m in range(micros):
-            saved, _, factor = kept[m]
-            result, *passed[m] = backward(
-                t, m, here, arriving[m], saved, factor, gain_row, turned, passed[m]
-            )
-            arriving[m] = hop(result, t - 1, half, count) if t else result
-    slope = [passed[m][0] for m in range(micros)]
+    parked = [kept[m][1] for m in range(micros)] + current
+    for step, m in order(sections, micros):
+        t = sections - 1 - step
+        pinned = parked if (t, m) == (sections - 6, micros - 1) else []
+        result, *rest = backward(
+            t, m, here, arriving[m], kept[m][0], kept[m][2], gain_row, turned,
+            passed[m], after, pinned,
+        )
+        passed[m] = rest[:2]
+        after = (in_hbm(passed[m][0]),)
+        if pinned:
+            parked = rest[2:]
+            last = jnp.concatenate(parked[micros:], axis=0)
+            final_share = spread(lax.ppermute(last, "dp", across), sections - 1, sections, section)
+            normed = jnp.concatenate(parked[:micros], axis=0)
+            cut = normed.reshape(micros * rows, 4, 4, -1).transpose(2, 0, 1, 3)
+            cut = cut.reshape(4, micros * rows, features // 4)
+            normed = [pick(cut, y)]
+            normed += [shift_y(pick(cut, (y + k) % 4), k, count) for k in (1, 2, 3)]
+            normed = from_all_z(jnp.stack(normed), count)
+        arriving[m] = hop(result, t - 1, half, count) if t else result
+
+    slope = jnp.concatenate([passed[m][0] for m in range(micros)], axis=0)
+    cut = slope.reshape(micros * rows, 4, features // 4).transpose(1, 0, 2)
+    slope = [pick(cut, z)]
+    slope += [shift_z(pick(cut, to_z[k]), k, count) for k in (1, 2, 3)]
+    slope = from_all_y(jnp.concatenate(slope, axis=0), count)
+    slope = jnp.stack(slope).reshape(4, 4, micros * rows, features // 4)
+    product = jnp.einsum(
+        "jkra,kjrb->ab", jnp.stack(normed), slope, preferred_element_type=F32
+    ).astype(BF)
+    product = product.reshape(4, features // 16, features // 4)
+    weight_grad = jnp.zeros((features // 16, features), BF)
+    for k in range(4):
+        piece = pick(product, to_z[k])
+        piece = shift_z(piece, k, count) if k else piece
+        at = from_z[k] * (features // 4)
+        weight_grad = lax.dynamic_update_slice_in_dim(weight_grad, piece, at, 1)
+
     total = sum(passed[m][1] for m in range(micros))
-    normed = [kept[m][1] for m in range(micros)]
-    last, first = jnp.concatenate(last, axis=0), jnp.concatenate(arriving, axis=0)
-
-    summed = lax.psum_scatter(
-        lax.dot_general(
-            jnp.concatenate(normed, axis=0), jnp.concatenate(slope, axis=0),
-            (((0,), (0,)), ((), ())), preferred_element_type=F32,
-        ).astype(BF),
-        "dp",
-        scatter_dimension=0,
-        tiled=True,
-    )
-    gain_grad = lax.psum(total, "dp")
-    shared = shares((first, last), sections)
-    first_share = shared[0, :, 0]
-    final_share = lax.ppermute(shared[1, :, sections - 1], "dp", across)
+    total = total + (shift_y(total, 1, count) + shift_y(total, 2, count) + shift_y(total, 3, count))
+    total = total + (shift_z(total, 1, count) + shift_z(total, 2, count) + shift_z(total, 3, count))
+    first_share = spread(jnp.concatenate(arriving, axis=0), 0, sections, section)
     shape = (micros, rows, features // sections)
     return (
-        summed[None],
-        gain_grad,
+        weight_grad[None],
+        total,
         first_share.reshape(shape),
         final_share.reshape(shape),
     )

time: 1160 us -> 1030 us (0.89)
  blocking collectives: 348 us -> 0 us
  waiting for transfers between devices: 232 us -> 350 us
  Pallas kernels: 88.2 us -> 118 us
  starting transfers between devices: 401 us -> 423 us
  local copies, waits for them, and re-layouts: 54 us -> 71 us
  other arithmetic: 2.74 us -> 16.4 us
    psum x1 -> x0, blocking collectives: 216 us -> none  [on_device(): gain_grad = lax.psum(total, 'dp')]
    all_to_all x1 -> x0, blocking collectives: 132 us -> none  [shares(): return lax.all_to_all(cut, 'section', split_axis=2, concat_axis=2)]
    ppermute x1 -> x31, waiting for transfers between devices: 0.01 us -> 125 us  [the longest x12 86.7 us: shift_z(): return lax.ppermute(block, 'dp', pairs)]
    ppermute x1 -> x31, starting transfers between devices: 34.2 us -> 112 us  [the longest x8 68.7 us: spread(): arrived = lax.ppermute(jnp.where(upper, low, high), 'section', pairs)]
    ppermute x90, starting transfers between devices: 364 us -> 308 us  [hop(): return lax.ppermute(block, ('section', 'dp'), sorted(pairs))]
    pallas_call x98, Pallas kernels: 88.2 us -> 118 us  [call(): pl.pallas_call(kernel, out_shape=outs, in_specs=in_specs, out_specs=out_s...]
    unnamed x59 -> x154, local copies, waits for them, and re-layouts: 41.5 us -> 52.6 us
  transfers between devices with their start and end apart: 94 -> 123, of which waited for: 9 -> 18; matrix products, arithmetic and copies ran while one was open for 1% -> 4% of each run, Pallas kernels for 8% -> 12%
where the time goes in v3:
time: 1030 us; the launch traced here: 1010 us
  starting transfers between devices  423 us (41%)
  waiting for transfers between devices  350 us (34%)
  Pallas kernels  118 us (11%)
  local copies, waits for them, and re-layouts  71 us (7%)
  between operations  27.6 us (3%)
  other arithmetic  16.4 us (2%)
    ppermute x90, starting transfers between devices, hop(): return lax.ppermute(block, ('section', 'dp'), sorted(pairs))  308 us
    all_gather x1, waiting for transfers between devices, on_device(): gathered = lax.all_gather(weight[0], 'dp', axis=0, tiled=True)  208 us
    pallas_call x98, Pallas kernels, call(): pl.pallas_call(kernel, out_shape=outs, in_specs=in_specs, out_specs=out_s...  118 us
    ppermute x12, waiting for transfers between devices, shift_z(): return lax.ppermute(block, 'dp', pairs)  86.7 us
    ppermute x8, starting transfers between devices, spread(): arrived = lax.ppermute(jnp.where(upper, low, high), 'section', pairs)  68.7 us
    unnamed x154, local copies, waits for them, and re-layouts  52.6 us
    ppermute x12, starting transfers between devices, shift_z(): return lax.ppermute(block, 'dp', pairs)  28.6 us
    ppermute x10, waiting for transfers between devices, shift_y(): return lax.ppermute(block, 'dp', pairs)  21.6 us
  transfers between devices with their start and end apart: 123, of which 18 were waited for; matrix products, arithmetic and copies ran while one was open for 4% of the time, Pallas kernels for 12%

profile of v3, /device:TPU:128, one launch (start us, length us, event | category | flops | bytes accessed | tf_op | source)
XLA Modules:
  0.0 1011.5 jit_solution(7760613565613534749)
XLA Ops:
  8.1 208.4 %all-gather.3.cloned.1.call-done = bf16[1,3072,3072]{2,1,0:T(8,128)(2,1)} async-done(((bf16[1,192,3072]{2,1,0:T(8,128)(2,1)}), bf16[1,3072,3072]{2,1,0:T(8,128)(2,1)}) %all-gather.3.cloned.1.call-update) | async-done | bytes 18874384 | tf_op jit(solution)/shard_map/all_gather | solution.py:249
  216.5 6.4 copy-done.21
  230.0 3.2 collective-permute-start.2
  239.1 4.5 shard_map.103
  245.8 4.7 shard_map.106
  252.8 4.4 shard_map.109
  259.6 4.5 shard_map.112
  265.6 72.9 %collective-permute-start.21 = (bf16[64,3072]{1,0:T(8,128)(2,1)S(1)}, bf16[64,3072]{1,0:T(8,128)(2,1)S(1)}, u32[]{:S(2)}, u32[]{:S(2)}) collective-permute-start(bf16[64,3072]{1,0:T(8,128)(2,1)S(1)} %get-tuple-element.438), channel_id=1, source_target_pairs={{112,140},{113,141},{114,142},{115,143},{116,136},{117,137},{118,1... | collective-permute-start | bytes 1179656 | tf_op jit(solution)/shard_map/ppermute | solution.py:176
  339.9 7.5 collective-permute-start.25
  348.1 4.5 shard_map.117
  354.8 5.8 collective-permute-start.23
  360.7 4.5 shard_map.119
  367.9 3.6 collective-permute-done.23.x_in
  371.4 4.7 shard_map.121
  382.5 4.4 shard_map.127
  389.2 4.5 shard_map.130
  396.0 5.0 shard_map.133
  401.7 2.5 collective-permute-start
  409.3 5.7 shard_map.139
  415.8 5.3 shard_map.142.turned
  421.2 6.3 copy-done.2
  429.5 6.4 copy-done.3
  442.2 5.5 shard_map.150
  450.7 5.7 shard_map.154
  459.3 5.5 shard_map.158
  466.3 123.5 %collective-permute-start.68 = (bf16[64,3072]{1,0:T(8,128)(2,1)S(1)}, bf16[64,3072]{1,0:T(8,128)(2,1)S(1)}, u32[]{:S(2)}, u32[]{:S(2)}) collective-permute-start(bf16[64,3072]{1,0:T(8,128)(2,1)S(1)} %get-tuple-element.601), channel_id=1, source_target_pairs={{0,16},{1,17},{2,18},{3,19},{4,20},{5,21},{6,22},{7,23},{8,24},{9,... | collective-permute-start | bytes 1179656 | tf_op jit(solution)/shard_map/ppermute | solution.py:176
  591.0 7.4 collective-permute-start.71
  601.1 4.1 shard_map.163
  609.1 4.5 shard_map.165
  615.5 3.2 collective-permute-done.70.u_in
  620.1 4.8 shard_map.167
  625.0 5.0 collective-permute-start.78
  632.2 6.4 copy-done.4
  640.6 7.0 collective-permute-done.78.u_in
  652.3 2.9 broadcast_select_fusion
  661.4 6.4 copy-done.5
  674.7 7.1 collective-permute-done.118
  683.1 17.0 %collective-permute-start.119 = (bf16[192,768]{1,0:T(8,128)(2,1)S(1)}, bf16[192,768]{1,0:T(8,128)(2,1)}, u32[]{:S(2)}, u32[]{:S(2)}) collective-permute-start(bf16[192,768]{1,0:T(8,128)(2,1)S(1)} %broadcast_select_fusion.2), channel_id=1, source_target_pairs={{0,64},{16,80},{32,96},{48,112},{64,0},{80,16},{96,32},{112,48},{1... | collective-permute-start | bytes 884744 | tf_op jit(solution)/shard_map/ppermute | solution.py:191
  707.4 4.5 reshape.64
  711.9 3.2 copy.242
  715.1 4.0 reshape.65
  723.9 6.4 copy-done.6
  743.4 8.8 collective-permute-start.120
  758.9 2.9 fusion.20
  761.8 14.2 %collective-permute-start.65 = (bf16[4,192,768]{2,1,0:T(8,128)(2,1)}, bf16[4,192,768]{2,1,0:T(8,128)(2,1)}, u32[]{:S(2)}, u32[]{:S(2)}) collective-permute-start(bf16[4,192,768]{2,1,0:T(8,128)(2,1)} %get-tuple-element.703), channel_id=1, source_target_pairs={{0,8},{1,9},{2,10},{3,11},{4,0},{5,1},{6,2},{7,3},{8,12},{9,13},{1... | collective-permute-start | bytes 3538952 | tf_op jit(solution)/shard_map/ppermute | solution.py:206
  776.0 6.4 copy-done.7
  789.4 3.6 collective-permute-start.94
  794.0 5.5 collective-permute-start.96
  801.1 42.6 %collective-permute-start.113 = (bf16[192,1536]{1,0:T(8,128)(2,1)S(1)}, bf16[192,1536]{1,0:T(8,128)(2,1)S(1)}, u32[]{:S(2)}, u32[]{:S(2)}) collective-permute-start(bf16[192,1536]{1,0:T(8,128)(2,1)S(1)} %broadcast_select_fusion.1), channel_id=1, source_target_pairs={{0,128},{16,144},{32,160},{48,176},{64,192},{80,208},{96,224},{112... | collective-permute-start | bytes 1769480 | tf_op jit(solution)/shard_map/ppermute | solution.py:191
  844.7 2.4 constant_dynamic-slice_fusion.5
  847.6 2.5 collective-permute-start.98
  859.7 20.0 %collective-permute-done.97 = bf16[192,768]{1,0:T(8,128)(2,1)S(1)} collective-permute-done((bf16[192,768]{1,0:T(8,128)(2,1)S(1)}, bf16[192,768]{1,0:T(8,128)(2,1)S(1)}, u32[]{:S(2)}, u32[]{:S(2)}) %collective-permute-start.97) | collective-permute-done | bytes 294944 | tf_op jit(solution)/shard_map/ppermute | solution.py:206
  881.3 33.1 %collective-permute-done.99 = bf16[192,768]{1,0:T(8,128)(2,1)S(1)} collective-permute-done((bf16[192,768]{1,0:T(8,128)(2,1)}, bf16[192,768]{1,0:T(8,128)(2,1)S(1)}, u32[]{:S(2)}, u32[]{:S(2)}) %collective-permute-start.99) | collective-permute-done | bytes 294944 | tf_op jit(solution)/shard_map/ppermute | solution.py:206
  915.0 2.9 collective-permute-start.102
  918.3 9.7 collective-permute-done.114
  930.0 14.1 %collective-permute-done.100 = bf16[768,768]{1,0:T(8,128)(2,1)S(1)} collective-permute-done((bf16[768,768]{1,0:T(8,128)(2,1)S(1)}, bf16[768,768]{1,0:T(8,128)(2,1)S(1)}, u32[]{:S(2)}, u32[]{:S(2)}) %collective-permute-start.100) | collective-permute-done | bytes 1179680 | tf_op jit(solution)/shard_map/ppermute | solution.py:211
  944.9 3.0 collective-permute-start.103
  949.9 2.5 collective-permute-start.111
  952.6 7.4 collective-permute-done.101
  961.8 9.7 collective-permute-done.67
  971.5 5.4 bitcast_convert_fusion
  980.9 6.0 collective-permute-done.104
  986.9 6.8 collective-permute-done.105
  993.7 9.4 collective-permute-done.106
  (482 shorter events, 151.4 us)
Async XLA Ops:
  7.2 209.3 %all-gather.3.cloned.1.call-start = ((), (), s32[]{:S(2)}) async-start(), calls=%async_computation | async-start | bytes 20054016 | tf_op jit(solution)/shard_map/all_gather | solution.py:249
  264.0 74.5 %collective-permute-start.17 = (bf16[64,3072]{1,0:T(8,128)(2,1)S(1)}, bf16[64,3072]{1,0:T(8,128)(2,1)S(1)}, u32[]{:S(2)}, u32[]{:S(2)}) collective-permute-start(bf16[64,3072]{1,0:T(8,128)(2,1)S(1)} %get-tuple-element.422), channel_id=1, source_target_pairs={{80,96},{81,97},{82,98},{83,99},{84,100},{85,101},{86,102},{87,103... | collective-permute-start | bytes 1179656 | tf_op jit(solution)/shard_map/ppermute | solution.py:176
  264.8 74.9 %collective-permute-start.22 = (bf16[64,3072]{1,0:T(8,128)(2,1)S(1)}, bf16[64,3072]{1,0:T(8,128)(2,1)S(1)}, u32[]{:S(2)}, u32[]{:S(2)}) collective-permute-start(bf16[64,3072]{1,0:T(8,128)(2,1)S(1)} %get-tuple-element.441), channel_id=1, source_target_pairs={{96,112},{97,113},{98,114},{99,115},{100,116},{101,117},{102,118},... | collective-permute-start | bytes 1179656 | tf_op jit(solution)/shard_map/ppermute | solution.py:176
  265.6 82.5 %collective-permute-start.21 = (bf16[64,3072]{1,0:T(8,128)(2,1)S(1)}, bf16[64,3072]{1,0:T(8,128)(2,1)S(1)}, u32[]{:S(2)}, u32[]{:S(2)}) collective-permute-start(bf16[64,3072]{1,0:T(8,128)(2,1)S(1)} %get-tuple-element.438), channel_id=1, source_target_pairs={{112,140},{113,141},{114,142},{115,143},{116,136},{117,137},{118,1... | collective-permute-start | bytes 1179656 | tf_op jit(solution)/shard_map/ppermute | solution.py:176
  339.1 15.5 %collective-permute-start.20 = (bf16[64,3072]{1,0:T(8,128)(2,1)S(1)}, bf16[64,3072]{1,0:T(8,128)(2,1)S(1)}, u32[]{:S(2)}, u32[]{:S(2)}) collective-permute-start(bf16[64,3072]{1,0:T(8,128)(2,1)S(1)} %get-tuple-element.434), channel_id=1, source_target_pairs={{96,112},{97,113},{98,114},{99,115},{100,116},{101,117},{102,118},... | collective-permute-start | bytes 1179656 | tf_op jit(solution)/shard_map/ppermute | solution.py:176
  339.9 20.8 %collective-permute-start.25 = (bf16[64,3072]{1,0:T(8,128)(2,1)S(1)}, bf16[64,3072]{1,0:T(8,128)(2,1)S(1)}, u32[]{:S(2)}, u32[]{:S(2)}) collective-permute-start(bf16[64,3072]{1,0:T(8,128)(2,1)S(1)} %get-tuple-element.453), channel_id=1, source_target_pairs={{112,140},{113,141},{114,142},{115,143},{116,136},{117,137},{118,1... | collective-permute-start | bytes 1179656 | tf_op jit(solution)/shard_map/ppermute | solution.py:176
  352.6 14.5 %collective-permute-start.24 = (bf16[64,3072]{1,0:T(8,128)(2,1)S(1)}, bf16[64,3072]{1,0:T(8,128)(2,1)S(1)}, u32[]{:S(2)}, u32[]{:S(2)}) collective-permute-start(bf16[64,3072]{1,0:T(8,128)(2,1)S(1)} %get-tuple-element.450), channel_id=1, source_target_pairs={{0,16},{1,17},{2,18},{3,19},{4,20},{5,21},{6,22},{7,23},{8,24},{9,... | collective-permute-start | bytes 1179656 | tf_op jit(solution)/shard_map/ppermute | solution.py:176
  354.8 16.6 %collective-permute-start.23 = (bf16[64,3072]{1,0:T(8,128)(2,1)S(1)}, bf16[64,3072]{1,0:T(8,128)(2,1)S(1)}, u32[]{:S(2)}, u32[]{:S(2)}) collective-permute-start(bf16[64,3072]{1,0:T(8,128)(2,1)S(1)} %get-tuple-element.446), channel_id=1, source_target_pairs={{112,140},{113,141},{114,142},{115,143},{116,136},{117,137},{118,1... | collective-permute-start | bytes 1179656 | tf_op jit(solution)/shard_map/ppermute | solution.py:176
  365.1 12.9 %collective-permute-start.28 = (bf16[64,3072]{1,0:T(8,128)(2,1)S(1)}, bf16[64,3072]{1,0:T(8,128)(2,1)S(1)}, u32[]{:S(2)}, u32[]{:S(2)}) collective-permute-start(bf16[64,3072]{1,0:T(8,128)(2,1)S(1)} %get-tuple-element.465), channel_id=1, source_target_pairs={{0,16},{1,17},{2,18},{3,19},{4,20},{5,21},{6,22},{7,23},{8,24},{9,... | collective-permute-start | bytes 1179656 | tf_op jit(solution)/shard_map/ppermute | solution.py:176
  367.2 11.7 %collective-permute-start.27 = (bf16[64,3072]{1,0:T(8,128)(2,1)S(1)}, bf16[64,3072]{1,0:T(8,128)(2,1)S(1)}, u32[]{:S(2)}, u32[]{:S(2)}) collective-permute-start(bf16[64,3072]{1,0:T(8,128)(2,1)S(1)} %get-tuple-element.462), channel_id=1, source_target_pairs={{16,32},{17,33},{18,34},{19,35},{20,36},{21,37},{22,38},{23,39},{2... | collective-permute-start | bytes 1179656 | tf_op jit(solution)/shard_map/ppermute | solution.py:176
  401.7 27.0 %collective-permute-start = (bf16[3,64,3072]{2,1,0:T(8,128)(2,1)S(1)}, bf16[3,64,3072]{2,1,0:T(8,128)(2,1)S(1)}, u32[]{:S(2)}, u32[]{:S(2)}) collective-permute-start(bf16[3,64,3072]{2,1,0:T(8,128)(2,1)S(1)} %copy-done.48), channel_id=1, source_target_pairs={{0,12},{1,13},{2,14},{3,15},{4,8},{5,9},{6,10},{7,11},{8,4},{9,5},... | collective-permute-start | bytes 3538952 | tf_op jit(solution)/shard_map/ppermute | solution.py:254
  408.5 12.6 %collective-permute-start.45 = (bf16[64,3072]{1,0:T(8,128)(2,1)S(1)}, bf16[64,3072]{1,0:T(8,128)(2,1)S(1)}, u32[]{:S(2)}, u32[]{:S(2)}) collective-permute-start(bf16[64,3072]{1,0:T(8,128)(2,1)S(1)} %get-tuple-element.534), channel_id=1, source_target_pairs={{96,112},{97,113},{98,114},{99,115},{100,116},{101,117},{102,118},... | collective-permute-start | bytes 1179656 | tf_op jit(solution)/shard_map/ppermute | solution.py:176
  415.1 13.2 %collective-permute-start.44 = (bf16[64,3072]{1,0:T(8,128)(2,1)S(1)}, bf16[64,3072]{1,0:T(8,128)(2,1)S(1)}, u32[]{:S(2)}, u32[]{:S(2)}) collective-permute-start(bf16[64,3072]{1,0:T(8,128)(2,1)S(1)} %get-tuple-element.530), channel_id=1, source_target_pairs={{96,112},{97,113},{98,114},{99,115},{100,116},{101,117},{102,118},... | collective-permute-start | bytes 1179656 | tf_op jit(solution)/shard_map/ppermute | solution.py:176
  464.8 125.0 %collective-permute-start.59 = (bf16[64,3072]{1,0:T(8,128)(2,1)S(1)}, bf16[64,3072]{1,0:T(8,128)(2,1)S(1)}, u32[]{:S(2)}, u32[]{:S(2)}) collective-permute-start(bf16[64,3072]{1,0:T(8,128)(2,1)S(1)} %get-tuple-element.583), channel_id=1, source_target_pairs={{32,48},{33,49},{34,50},{35,51},{36,52},{37,53},{38,54},{39,55},{4... | collective-permute-start | bytes 1179656 | tf_op jit(solution)/shard_map/ppermute | solution.py:176
  465.5 125.1 %collective-permute-start.69 = (bf16[64,3072]{1,0:T(8,128)(2,1)S(1)}, bf16[64,3072]{1,0:T(8,128)(2,1)S(1)}, u32[]{:S(2)}, u32[]{:S(2)}) collective-permute-start(bf16[64,3072]{1,0:T(8,128)(2,1)S(1)} %get-tuple-element.603), channel_id=1, source_target_pairs={{16,32},{17,33},{18,34},{19,35},{20,36},{21,37},{22,38},{23,39},{2... | collective-permute-start | bytes 1179656 | tf_op jit(solution)/shard_map/ppermute | solution.py:176
  466.3 134.8 %collective-permute-start.68 = (bf16[64,3072]{1,0:T(8,128)(2,1)S(1)}, bf16[64,3072]{1,0:T(8,128)(2,1)S(1)}, u32[]{:S(2)}, u32[]{:S(2)}) collective-permute-start(bf16[64,3072]{1,0:T(8,128)(2,1)S(1)} %get-tuple-element.601), channel_id=1, source_target_pairs={{0,16},{1,17},{2,18},{3,19},{4,20},{5,21},{6,22},{7,23},{8,24},{9,... | collective-permute-start | bytes 1179656 | tf_op jit(solution)/shard_map/ppermute | solution.py:176
  589.8 17.2 %collective-permute-start.72 = (bf16[64,3072]{1,0:T(8,128)(2,1)S(1)}, bf16[64,3072]{1,0:T(8,128)(2,1)S(1)}, u32[]{:S(2)}, u32[]{:S(2)}) collective-permute-start(bf16[64,3072]{1,0:T(8,128)(2,1)S(1)} %get-tuple-element.612), channel_id=1, source_target_pairs={{16,32},{17,33},{18,34},{19,35},{20,36},{21,37},{22,38},{23,39},{2... | collective-permute-start | bytes 1179656 | tf_op jit(solution)/shard_map/ppermute | solution.py:176
  591.0 18.1 %collective-permute-start.71 = (bf16[64,3072]{1,0:T(8,128)(2,1)S(1)}, bf16[64,3072]{1,0:T(8,128)(2,1)S(1)}, u32[]{:S(2)}, u32[]{:S(2)}) collective-permute-start(bf16[64,3072]{1,0:T(8,128)(2,1)S(1)} %get-tuple-element.610), channel_id=1, source_target_pairs={{0,16},{1,17},{2,18},{3,19},{4,20},{5,21},{6,22},{7,23},{8,24},{9,... | collective-permute-start | bytes 1179656 | tf_op jit(solution)/shard_map/ppermute | solution.py:176
  599.6 52.7 %collective-permute-start.117 = (bf16[192,3072]{1,0:T(8,128)(2,1)}, bf16[192,3072]{1,0:T(8,128)(2,1)}, u32[]{:S(2)}, u32[]{:S(2)}) collective-permute-start(bf16[192,3072]{1,0:T(8,128)(2,1)} %pad_maximum_fusion.5), channel_id=1, source_target_pairs={{0,12},{1,13},{2,14},{3,15},{4,8},{5,9},{6,10},{7,11},{8,4},{9,5},... | collective-permute-start | bytes 3538952 | tf_op jit(solution)/shard_map/ppermute | solution.py:282
  605.1 13.5 %collective-permute-start.70 = (bf16[64,3072]{1,0:T(8,128)(2,1)S(1)}, bf16[64,3072]{1,0:T(8,128)(2,1)S(1)}, u32[]{:S(2)}, u32[]{:S(2)}) collective-permute-start(bf16[64,3072]{1,0:T(8,128)(2,1)S(1)} %get-tuple-element.607), channel_id=1, source_target_pairs={{112,140},{113,141},{114,142},{115,143},{116,136},{117,137},{118,1... | collective-permute-start | bytes 1179656 | tf_op jit(solution)/shard_map/ppermute | solution.py:176
  607.1 13.0 %collective-permute-start.75 = (bf16[64,3072]{1,0:T(8,128)(2,1)S(1)}, bf16[64,3072]{1,0:T(8,128)(2,1)S(1)}, u32[]{:S(2)}, u32[]{:S(2)}) collective-permute-start(bf16[64,3072]{1,0:T(8,128)(2,1)S(1)} %get-tuple-element.621), channel_id=1, source_target_pairs={{0,16},{1,17},{2,18},{3,19},{4,20},{5,21},{6,22},{7,23},{8,24},{9,... | collective-permute-start | bytes 1179656 | tf_op jit(solution)/shard_map/ppermute | solution.py:176
  613.5 16.5 %collective-permute-start.74 = (bf16[64,3072]{1,0:T(8,128)(2,1)S(1)}, bf16[64,3072]{1,0:T(8,128)(2,1)S(1)}, u32[]{:S(2)}, u32[]{:S(2)}) collective-permute-start(bf16[64,3072]{1,0:T(8,128)(2,1)S(1)} %get-tuple-element.619), channel_id=1, source_target_pairs={{112,140},{113,141},{114,142},{115,143},{116,136},{117,137},{118,1... | collective-permute-start | bytes 1179656 | tf_op jit(solution)/shard_map/ppermute | solution.py:176
  619.4 12.8 %collective-permute-start.73 = (bf16[64,3072]{1,0:T(8,128)(2,1)}, bf16[64,3072]{1,0:T(8,128)(2,1)S(1)}, u32[]{:S(2)}, u32[]{:S(2)}) collective-permute-start(bf16[64,3072]{1,0:T(8,128)(2,1)} %get-tuple-element.616), channel_id=1, source_target_pairs={{96,112},{97,113},{98,114},{99,115},{100,116},{101,117},{102,118},... | collective-permute-start | bytes 1179656 | tf_op jit(solution)/shard_map/ppermute | solution.py:176
  625.0 22.6 %collective-permute-start.78 = (bf16[64,3072]{1,0:T(8,128)(2,1)}, bf16[64,3072]{1,0:T(8,128)(2,1)}, u32[]{:S(2)}, u32[]{:S(2)}) collective-permute-start(bf16[64,3072]{1,0:T(8,128)(2,1)} %get-tuple-element.630), channel_id=1, source_target_pairs={{112,140},{113,141},{114,142},{115,143},{116,136},{117,137},{118,1... | collective-permute-start | bytes 1179656 | tf_op jit(solution)/shard_map/ppermute | solution.py:176
  630.8 18.8 %collective-permute-start.77 = (bf16[64,3072]{1,0:T(8,128)(2,1)}, bf16[64,3072]{1,0:T(8,128)(2,1)}, u32[]{:S(2)}, u32[]{:S(2)}) collective-permute-start(bf16[64,3072]{1,0:T(8,128)(2,1)} %get-tuple-element.628), channel_id=1, source_target_pairs={{96,112},{97,113},{98,114},{99,115},{100,116},{101,117},{102,118},... | collective-permute-start | bytes 1179656 | tf_op jit(solution)/shard_map/ppermute | solution.py:176
  639.9 15.3 %collective-permute-start.76 = (bf16[64,3072]{1,0:T(8,128)(2,1)S(1)}, bf16[64,3072]{1,0:T(8,128)(2,1)S(1)}, u32[]{:S(2)}, u32[]{:S(2)}) collective-permute-start(bf16[64,3072]{1,0:T(8,128)(2,1)S(1)} %get-tuple-element.625), channel_id=1, source_target_pairs={{80,96},{81,97},{82,98},{83,99},{84,100},{85,101},{86,102},{87,103... | collective-permute-start | bytes 1179656 | tf_op jit(solution)/shard_map/ppermute | solution.py:176
  655.2 26.6 %collective-permute-start.118 = (bf16[192,1536]{1,0:T(8,128)(2,1)}, bf16[192,1536]{1,0:T(8,128)(2,1)}, u32[]{:S(2)}, u32[]{:S(2)}) collective-permute-start(bf16[192,1536]{1,0:T(8,128)(2,1)} %broadcast_select_fusion), channel_id=1, source_target_pairs={{0,128},{16,144},{32,160},{48,176},{64,192},{80,208},{96,224},{112... | collective-permute-start | bytes 1769480 | tf_op jit(solution)/shard_map/ppermute | solution.py:191
  657.8 11.8 %collective-permute-start.84 = (bf16[64,3072]{1,0:T(8,128)(2,1)}, bf16[64,3072]{1,0:T(8,128)(2,1)}, u32[]{:S(2)}, u32[]{:S(2)}) collective-permute-start(bf16[64,3072]{1,0:T(8,128)(2,1)} %get-tuple-element.648), channel_id=1, source_target_pairs={{80,96},{81,97},{82,98},{83,99},{84,100},{85,101},{86,102},{87,103... | collective-permute-start | bytes 1179656 | tf_op jit(solution)/shard_map/ppermute | solution.py:176
  660.0 12.1 %collective-permute-start.83 = (bf16[64,3072]{1,0:T(8,128)(2,1)}, bf16[64,3072]{1,0:T(8,128)(2,1)}, u32[]{:S(2)}, u32[]{:S(2)}) collective-permute-start(bf16[64,3072]{1,0:T(8,128)(2,1)} %get-tuple-element.646), channel_id=1, source_target_pairs={{64,80},{65,81},{66,82},{67,83},{68,84},{69,85},{70,86},{71,87},{7... | collective-permute-start | bytes 1179656 | tf_op jit(solution)/shard_map/ppermute | solution.py:176
  668.9 31.2 %collective-permute-start.82 = (bf16[64,3072]{1,0:T(8,128)(2,1)S(1)}, bf16[64,3072]{1,0:T(8,128)(2,1)S(1)}, u32[]{:S(2)}, u32[]{:S(2)}) collective-permute-start(bf16[64,3072]{1,0:T(8,128)(2,1)S(1)} %get-tuple-element.643), channel_id=1, source_target_pairs={{48,64},{49,65},{50,66},{51,67},{52,68},{53,69},{54,70},{55,71},{5... | collective-permute-start | bytes 1179656 | tf_op jit(solution)/shard_map/ppermute | solution.py:176
  671.2 31.2 %collective-permute-start.87 = (bf16[64,3072]{1,0:T(8,128)(2,1)S(1)}, bf16[64,3072]{1,0:T(8,128)(2,1)S(1)}, u32[]{:S(2)}, u32[]{:S(2)}) collective-permute-start(bf16[64,3072]{1,0:T(8,128)(2,1)S(1)} %get-tuple-element.657), channel_id=1, source_target_pairs={{64,80},{65,81},{66,82},{67,83},{68,84},{69,85},{70,86},{71,87},{7... | collective-permute-start | bytes 1179656 | tf_op jit(solution)/shard_map/ppermute | solution.py:176
  673.9 30.9 %collective-permute-start.86 = (bf16[64,3072]{1,0:T(8,128)(2,1)S(1)}, bf16[64,3072]{1,0:T(8,128)(2,1)S(1)}, u32[]{:S(2)}, u32[]{:S(2)}) collective-permute-start(bf16[64,3072]{1,0:T(8,128)(2,1)S(1)} %get-tuple-element.655), channel_id=1, source_target_pairs={{48,64},{49,65},{50,66},{51,67},{52,68},{53,69},{54,70},{55,71},{5... | collective-permute-start | bytes 1179656 | tf_op jit(solution)/shard_map/ppermute | solution.py:176
  683.1 54.1 %collective-permute-start.119 = (bf16[192,768]{1,0:T(8,128)(2,1)S(1)}, bf16[192,768]{1,0:T(8,128)(2,1)}, u32[]{:S(2)}, u32[]{:S(2)}) collective-permute-start(bf16[192,768]{1,0:T(8,128)(2,1)S(1)} %broadcast_select_fusion.2), channel_id=1, source_target_pairs={{0,64},{16,80},{32,96},{48,112},{64,0},{80,16},{96,32},{112,48},{1... | collective-permute-start | bytes 884744 | tf_op jit(solution)/shard_map/ppermute | solution.py:191
  701.0 20.7 %collective-permute-start.85 = (bf16[64,3072]{1,0:T(8,128)(2,1)}, bf16[64,3072]{1,0:T(8,128)(2,1)}, u32[]{:S(2)}, u32[]{:S(2)}) collective-permute-start(bf16[64,3072]{1,0:T(8,128)(2,1)} %get-tuple-element.652), channel_id=1, source_target_pairs={{32,48},{33,49},{34,50},{35,51},{36,52},{37,53},{38,54},{39,55},{4... | collective-permute-start | bytes 1179656 | tf_op jit(solution)/shard_map/ppermute | solution.py:176
  703.4 30.1 %collective-permute-start.90 = (bf16[64,3072]{1,0:T(8,128)(2,1)}, bf16[64,3072]{1,0:T(8,128)(2,1)}, u32[]{:S(2)}, u32[]{:S(2)}) collective-permute-start(bf16[64,3072]{1,0:T(8,128)(2,1)} %get-tuple-element.666), channel_id=1, source_target_pairs={{48,64},{49,65},{50,66},{51,67},{52,68},{53,69},{54,70},{55,71},{5... | collective-permute-start | bytes 1179656 | tf_op jit(solution)/shard_map/ppermute | solution.py:176
  705.6 33.1 %collective-permute-start.89 = (bf16[64,3072]{1,0:T(8,128)(2,1)}, bf16[64,3072]{1,0:T(8,128)(2,1)S(1)}, u32[]{:S(2)}, u32[]{:S(2)}) collective-permute-start(bf16[64,3072]{1,0:T(8,128)(2,1)} %get-tuple-element.664), channel_id=1, source_target_pairs={{32,48},{33,49},{34,50},{35,51},{36,52},{37,53},{38,54},{39,55},{4... | collective-permute-start | bytes 1179656 | tf_op jit(solution)/shard_map/ppermute | solution.py:176
  721.4 20.7 %collective-permute-start.62 = (bf16[192,768]{1,0:T(8,128)(2,1)}, bf16[192,768]{1,0:T(8,128)(2,1)}, u32[]{:S(2)}, u32[]{:S(2)}) collective-permute-start(bf16[192,768]{1,0:T(8,128)(2,1)} %get-tuple-element.707), channel_id=1, source_target_pairs={{0,1},{1,2},{2,3},{3,0},{4,5},{5,6},{6,7},{7,4},{8,9},{9,10},{10,1... | collective-permute-start | bytes 884744 | tf_op jit(solution)/shard_map/ppermute | solution.py:211
  721.7 21.7 %collective-permute-start.63 = (bf16[192,768]{1,0:T(8,128)(2,1)}, bf16[192,768]{1,0:T(8,128)(2,1)}, u32[]{:S(2)}, u32[]{:S(2)}) collective-permute-start(bf16[192,768]{1,0:T(8,128)(2,1)} %get-tuple-element.706), channel_id=1, source_target_pairs={{0,2},{1,3},{2,0},{3,1},{4,6},{5,7},{6,4},{7,5},{8,10},{9,11},{10,... | collective-permute-start | bytes 884744 | tf_op jit(solution)/shard_map/ppermute | solution.py:211
  733.5 25.4 %collective-permute-start.64 = (bf16[192,768]{1,0:T(8,128)(2,1)}, bf16[192,768]{1,0:T(8,128)(2,1)}, u32[]{:S(2)}, u32[]{:S(2)}) collective-permute-start(bf16[192,768]{1,0:T(8,128)(2,1)} %get-tuple-element.705), channel_id=1, source_target_pairs={{0,3},{1,0},{2,1},{3,2},{4,7},{5,4},{6,5},{7,6},{8,11},{9,8},{10,9... | collective-permute-start | bytes 884744 | tf_op jit(solution)/shard_map/ppermute | solution.py:211
  737.2 38.8 %collective-permute-start.88 = (bf16[64,3072]{1,0:T(8,128)(2,1)}, bf16[64,3072]{1,0:T(8,128)(2,1)}, u32[]{:S(2)}, u32[]{:S(2)}) collective-permute-start(bf16[64,3072]{1,0:T(8,128)(2,1)} %get-tuple-element.661), channel_id=1, source_target_pairs={{16,32},{17,33},{18,34},{19,35},{20,36},{21,37},{22,38},{23,39},{2... | collective-permute-start | bytes 1179656 | tf_op jit(solution)/shard_map/ppermute | solution.py:176
  738.8 47.5 %collective-permute-start.93 = (bf16[64,3072]{1,0:T(8,128)(2,1)}, bf16[64,3072]{1,0:T(8,128)(2,1)}, u32[]{:S(2)}, u32[]{:S(2)}) collective-permute-start(bf16[64,3072]{1,0:T(8,128)(2,1)} %get-tuple-element.675), channel_id=1, source_target_pairs={{32,48},{33,49},{34,50},{35,51},{36,52},{37,53},{38,54},{39,55},{4... | collective-permute-start | bytes 1179656 | tf_op jit(solution)/shard_map/ppermute | solution.py:176
  742.1 47.2 %collective-permute-start.92 = (bf16[64,3072]{1,0:T(8,128)(2,1)}, bf16[64,3072]{1,0:T(8,128)(2,1)S(1)}, u32[]{:S(2)}, u32[]{:S(2)}) collective-permute-start(bf16[64,3072]{1,0:T(8,128)(2,1)} %get-tuple-element.673), channel_id=1, source_target_pairs={{16,32},{17,33},{18,34},{19,35},{20,36},{21,37},{22,38},{23,39},{2... | collective-permute-start | bytes 1179656 | tf_op jit(solution)/shard_map/ppermute | solution.py:176
  743.4 44.9 %collective-permute-start.120 = (bf16[192,384]{1,0:T(8,128)(2,1)}, bf16[192,384]{1,0:T(8,128)(2,1)}, u32[]{:S(2)}, u32[]{:S(2)}) collective-permute-start(bf16[192,384]{1,0:T(8,128)(2,1)} %broadcast_select_fusion.4), channel_id=1, source_target_pairs={{0,32},{16,48},{32,0},{48,16},{64,96},{80,112},{96,64},{112,80},{1... | collective-permute-start | bytes 442376 | tf_op jit(solution)/shard_map/ppermute | solution.py:191
  761.8 89.0 %collective-permute-start.65 = (bf16[4,192,768]{2,1,0:T(8,128)(2,1)}, bf16[4,192,768]{2,1,0:T(8,128)(2,1)}, u32[]{:S(2)}, u32[]{:S(2)}) collective-permute-start(bf16[4,192,768]{2,1,0:T(8,128)(2,1)} %get-tuple-element.703), channel_id=1, source_target_pairs={{0,8},{1,9},{2,10},{3,11},{4,0},{5,1},{6,2},{7,3},{8,12},{9,13},{1... | collective-permute-start | bytes 3538952 | tf_op jit(solution)/shard_map/ppermute | solution.py:206
  793.8 62.1 %collective-permute-start.121 = (bf16[192,192]{1,0:T(8,128)(2,1)}, bf16[192,192]{1,0:T(8,128)(2,1)}, u32[]{:S(2)}, u32[]{:S(2)}) collective-permute-start(bf16[192,192]{1,0:T(8,128)(2,1)} %broadcast_select_fusion.6), channel_id=1, source_target_pairs={{0,16},{16,0},{32,48},{48,32},{64,80},{80,64},{96,112},{112,96},{1... | collective-permute-start | bytes 221192 | tf_op jit(solution)/shard_map/ppermute | solution.py:191
  801.1 116.8 %collective-permute-start.113 = (bf16[192,1536]{1,0:T(8,128)(2,1)S(1)}, bf16[192,1536]{1,0:T(8,128)(2,1)S(1)}, u32[]{:S(2)}, u32[]{:S(2)}) collective-permute-start(bf16[192,1536]{1,0:T(8,128)(2,1)S(1)} %broadcast_select_fusion.1), channel_id=1, source_target_pairs={{0,128},{16,144},{32,160},{48,176},{64,192},{80,208},{96,224},{112... | collective-permute-start | bytes 1769480 | tf_op jit(solution)/shard_map/ppermute | solution.py:191
  847.2 32.4 %collective-permute-start.97 = (bf16[192,768]{1,0:T(8,128)(2,1)S(1)}, bf16[192,768]{1,0:T(8,128)(2,1)S(1)}, u32[]{:S(2)}, u32[]{:S(2)}) collective-permute-start(bf16[192,768]{1,0:T(8,128)(2,1)S(1)} %bitcast.76), channel_id=1, source_target_pairs={{0,8},{1,9},{2,10},{3,11},{4,0},{5,1},{6,2},{7,3},{8,12},{9,13},{1... | collective-permute-start | bytes 884744 | tf_op jit(solution)/shard_map/ppermute | solution.py:206
  847.6 33.7 %collective-permute-start.98 = (bf16[192,768]{1,0:T(8,128)(2,1)S(1)}, bf16[192,768]{1,0:T(8,128)(2,1)S(1)}, u32[]{:S(2)}, u32[]{:S(2)}) collective-permute-start(bf16[192,768]{1,0:T(8,128)(2,1)S(1)} %bitcast.77), channel_id=1, source_target_pairs={{0,12},{1,13},{2,14},{3,15},{4,8},{5,9},{6,10},{7,11},{8,4},{9,5},... | collective-permute-start | bytes 884744 | tf_op jit(solution)/shard_map/ppermute | solution.py:206
  850.8 63.6 %collective-permute-start.99 = (bf16[192,768]{1,0:T(8,128)(2,1)}, bf16[192,768]{1,0:T(8,128)(2,1)S(1)}, u32[]{:S(2)}, u32[]{:S(2)}) collective-permute-start(bf16[192,768]{1,0:T(8,128)(2,1)} %bitcast.56), channel_id=1, source_target_pairs={{0,4},{1,5},{2,6},{3,7},{4,12},{5,13},{6,14},{7,15},{8,0},{9,1},{1... | collective-permute-start | bytes 884744 | tf_op jit(solution)/shard_map/ppermute | solution.py:206
  855.9 73.0 %collective-permute-start.66 = (bf16[4,192,768]{2,1,0:T(8,128)(2,1)}, bf16[4,192,768]{2,1,0:T(8,128)(2,1)S(1)}, u32[]{:S(2)}, u32[]{:S(2)}) collective-permute-start(bf16[4,192,768]{2,1,0:T(8,128)(2,1)} %collective-permute-done.65), channel_id=1, source_target_pairs={{0,8},{1,9},{2,10},{3,11},{4,0},{5,1},{6,2},{7,3},{8,12},{9,13},{1... | collective-permute-start | bytes 3538952 | tf_op jit(solution)/shard_map/ppermute | solution.py:206
  914.6 29.5 %collective-permute-start.100 = (bf16[768,768]{1,0:T(8,128)(2,1)S(1)}, bf16[768,768]{1,0:T(8,128)(2,1)S(1)}, u32[]{:S(2)}, u32[]{:S(2)}) collective-permute-start(bf16[768,768]{1,0:T(8,128)(2,1)S(1)} %pad_maximum_fusion.3), channel_id=1, source_target_pairs={{0,1},{1,2},{2,3},{3,0},{4,5},{5,6},{6,7},{7,4},{8,9},{9,10},{10,1... | collective-permute-start | bytes 3538952 | tf_op jit(solution)/shard_map/ppermute | solution.py:211
  915.0 29.1 %collective-permute-start.102 = (bf16[768,768]{1,0:T(8,128)(2,1)S(1)}, bf16[768,768]{1,0:T(8,128)(2,1)S(1)}, u32[]{:S(2)}, u32[]{:S(2)}) collective-permute-start(bf16[768,768]{1,0:T(8,128)(2,1)S(1)} %pad_maximum_fusion.3), channel_id=1, source_target_pairs={{0,3},{1,0},{2,1},{3,2},{4,7},{5,4},{6,5},{7,6},{8,11},{9,8},{10,9... | collective-permute-start | bytes 3538952 | tf_op jit(solution)/shard_map/ppermute | solution.py:211
  918.2 26.1 %collective-permute-start.107 = (f32[1,3072]{1,0:T(1,128)S(1)}, f32[1,3072]{1,0:T(1,128)S(1)}, u32[]{:S(2)}, u32[]{:S(2)}) collective-permute-start(f32[1,3072]{1,0:T(1,128)S(1)} %add_add_fusion.2), channel_id=1, source_target_pairs={{0,1},{1,2},{2,3},{3,0},{4,5},{5,6},{6,7},{7,4},{8,9},{9,10},{10,1... | collective-permute-start | bytes 36872 | tf_op jit(solution)/shard_map/ppermute | solution.py:211
  928.0 16.9 %collective-permute-start.108 = (f32[1,3072]{1,0:T(1,128)S(1)}, f32[1,3072]{1,0:T(1,128)S(1)}, u32[]{:S(2)}, u32[]{:S(2)}) collective-permute-start(f32[1,3072]{1,0:T(1,128)S(1)} %add_add_fusion.2), channel_id=1, source_target_pairs={{0,2},{1,3},{2,0},{3,1},{4,6},{5,7},{6,4},{7,5},{8,10},{9,11},{10,... | collective-permute-start | bytes 36872 | tf_op jit(solution)/shard_map/ppermute | solution.py:211
  928.9 19.0 %collective-permute-start.109 = (f32[1,3072]{1,0:T(1,128)S(1)}, f32[1,3072]{1,0:T(1,128)S(1)}, u32[]{:S(2)}, u32[]{:S(2)}) collective-permute-start(f32[1,3072]{1,0:T(1,128)S(1)} %add_add_fusion.2), channel_id=1, source_target_pairs={{0,3},{1,0},{2,1},{3,2},{4,7},{5,4},{6,5},{7,6},{8,11},{9,8},{10,9... | collective-permute-start | bytes 36872 | tf_op jit(solution)/shard_map/ppermute | solution.py:211
  944.1 27.4 %collective-permute-start.67 = (bf16[4,192,768]{2,1,0:T(8,128)(2,1)S(1)}, bf16[4,192,768]{2,1,0:T(8,128)(2,1)S(1)}, u32[]{:S(2)}, u32[]{:S(2)}) collective-permute-start(bf16[4,192,768]{2,1,0:T(8,128)(2,1)S(1)} %collective-permute-done.66), channel_id=1, source_target_pairs={{0,8},{1,9},{2,10},{3,11},{4,0},{5,1},{6,2},{7,3},{8,12},{9,13},{1... | collective-permute-start | bytes 3538952 | tf_op jit(solution)/shard_map/ppermute | solution.py:206
  944.3 15.6 %collective-permute-start.101 = (bf16[384,768]{1,0:T(8,128)(2,1)S(1)}, bf16[384,768]{1,0:T(8,128)(2,1)S(1)}, u32[]{:S(2)}, u32[]{:S(2)}) collective-permute-start(bf16[384,768]{1,0:T(8,128)(2,1)S(1)} %slice.72), channel_id=1, source_target_pairs={{0,1},{1,2},{2,3},{3,0},{4,5},{5,6},{6,7},{7,4},{8,9},{9,10},{10,1... | collective-permute-start | bytes 1769480 | tf_op jit(solution)/shard_map/ppermute | solution.py:211
  944.9 16.8 %collective-permute-start.103 = (bf16[384,768]{1,0:T(8,128)(2,1)S(1)}, bf16[384,768]{1,0:T(8,128)(2,1)S(1)}, u32[]{:S(2)}, u32[]{:S(2)}) collective-permute-start(bf16[384,768]{1,0:T(8,128)(2,1)S(1)} %slice.73), channel_id=1, source_target_pairs={{0,3},{1,0},{2,1},{3,2},{4,7},{5,4},{6,5},{7,6},{8,11},{9,8},{10,9... | collective-permute-start | bytes 1769480 | tf_op jit(solution)/shard_map/ppermute | solution.py:211
  947.9 30.3 %collective-permute-start.110 = (f32[1,3072]{1,0:T(1,128)S(1)}, f32[1,3072]{1,0:T(1,128)S(1)}, u32[]{:S(2)}, u32[]{:S(2)}) collective-permute-start(f32[1,3072]{1,0:T(1,128)S(1)} %add_add_fusion.1), channel_id=1, source_target_pairs={{0,8},{1,9},{2,10},{3,11},{4,0},{5,1},{6,2},{7,3},{8,12},{9,13},{1... | collective-permute-start | bytes 36872 | tf_op jit(solution)/shard_map/ppermute | solution.py:206
  949.9 28.3 %collective-permute-start.111 = (f32[1,3072]{1,0:T(1,128)S(1)}, f32[1,3072]{1,0:T(1,128)S(1)}, u32[]{:S(2)}, u32[]{:S(2)}) collective-permute-start(f32[1,3072]{1,0:T(1,128)S(1)} %add_add_fusion.1), channel_id=1, source_target_pairs={{0,12},{1,13},{2,14},{3,15},{4,8},{5,9},{6,10},{7,11},{8,4},{9,5},... | collective-permute-start | bytes 36872 | tf_op jit(solution)/shard_map/ppermute | solution.py:206
  960.0 18.2 %collective-permute-start.112 = (f32[1,3072]{1,0:T(1,128)S(1)}, f32[1,3072]{1,0:T(1,128)S(1)}, u32[]{:S(2)}, u32[]{:S(2)}) collective-permute-start(f32[1,3072]{1,0:T(1,128)S(1)} %add_add_fusion.1), channel_id=1, source_target_pairs={{0,4},{1,5},{2,6},{3,7},{4,12},{5,13},{6,14},{7,15},{8,0},{9,1},{1... | collective-permute-start | bytes 36872 | tf_op jit(solution)/shard_map/ppermute | solution.py:206
  961.7 18.4 %collective-permute-start.116 = (bf16[192,192]{1,0:T(8,128)(2,1)S(1)}, bf16[192,192]{1,0:T(8,128)(2,1)S(1)}, u32[]{:S(2)}, u32[]{:S(2)}) collective-permute-start(bf16[192,192]{1,0:T(8,128)(2,1)S(1)} %broadcast_select_fusion.7), channel_id=1, source_target_pairs={{0,16},{16,0},{32,48},{48,32},{64,80},{80,64},{96,112},{112,96},{1... | collective-permute-start | bytes 221192 | tf_op jit(solution)/shard_map/ppermute | solution.py:191
  978.9 14.8 %collective-permute-start.105 = (bf16[192,768]{1,0:T(8,128)(2,1)S(1)}, bf16[192,768]{1,0:T(8,128)(2,1)S(1)}, u32[]{:S(2)}, u32[]{:S(2)}) collective-permute-start(bf16[192,768]{1,0:T(8,128)(2,1)S(1)} %get-tuple-element.699), channel_id=1, source_target_pairs={{0,12},{1,13},{2,14},{3,15},{4,8},{5,9},{6,10},{7,11},{8,4},{9,5},... | collective-permute-start | bytes 884744 | tf_op jit(solution)/shard_map/ppermute | solution.py:206
  980.9 22.3 %collective-permute-start.106 = (bf16[192,768]{1,0:T(8,128)(2,1)S(1)}, bf16[192,768]{1,0:T(8,128)(2,1)S(1)}, u32[]{:S(2)}, u32[]{:S(2)}) collective-permute-start(bf16[192,768]{1,0:T(8,128)(2,1)S(1)} %get-tuple-element.698), channel_id=1, source_target_pairs={{0,4},{1,5},{2,6},{3,7},{4,12},{5,13},{6,14},{7,15},{8,0},{9,1},{1... | collective-permute-start | bytes 884744 | tf_op jit(solution)/shard_map/ppermute | solution.py:206
  (133 other events, 1066.1 us)
Sparse Core Ops, SparseCore 0:
  9.8 206.6 all-gather.2

commit v4 on v3

--- a/solution.py
+++ b/solution.py
@@ -19,6 +19,7 @@
 SMEM = pl.BlockSpec(memory_space=pltpu.SMEM)
 TILE = 512
 LIMIT = 8 * 1024 * 1024
+EARLY = 10
 
 
 def call(kernel, outs, in_specs, out_specs, aliases, scratch, operands):
@@ -30,19 +31,39 @@
         input_output_aliases=aliases,
         scratch_shapes=scratch,
         compiler_params=pltpu.CompilerParams(vmem_limit_bytes=LIMIT),
+        cost_estimate=pl.CostEstimate(flops=1, bytes_accessed=1, transcendentals=0),
     )(*operands)
 
 
-def hold_kernel(source, held, sem):
-    copy = pltpu.make_async_copy(source, held, sem)
-    copy.start()
-    copy.wait()
-
-
-def hold(matrix):
-    shape = pltpu.VMEM(matrix.shape, matrix.dtype)
+def hold_kernel(places, row_of, *refs):
+    *pieces, held, sems = refs
+    copies = []
+    for i, (piece, (slot, start, rows, offset, column)) in enumerate(
+        (piece, part) for piece, parts in zip(pieces, places) for part in parts
+    ):
+        row = pl.multiple_of(row_of[slot], 64) + offset
+        copies.append(
+            pltpu.make_async_copy(
+                piece.at[pl.ds(start, rows), :],
+                held.at[pl.ds(row, rows), pl.ds(column, piece.shape[1])],
+                sems.at[i],
+            )
+        )
+        copies[-1].start()
+    for copy in copies:
+        copy.wait()
+
+
+def hold(pieces, row_of, shape):
+    arrays, places = zip(*pieces)
     return call(
-        hold_kernel, shape, [ANY], VMEM, {}, [pltpu.SemaphoreType.DMA], [matrix]
+        functools.partial(hold_kernel, places),
+        pltpu.VMEM(shape, BF),
+        [SMEM] + [HBM] * len(arrays),
+        VMEM,
+        {},
+        [pltpu.SemaphoreType.DMA((sum(len(p) for p in places),))],
+        [row_of] + [in_hbm(array) for array in arrays],
     )
 
 
@@ -98,7 +119,7 @@
     return call(
         functools.partial(forward_kernel, t, m if x.ndim == 3 else None),
         (pltpu.VMEM(shape, BF), wide, wide, deep),
-        [SMEM] + [VMEM] * 3 + [HBM] * (len(kept) + len(after)),
+        [SMEM] + [VMEM] * 3 + [HBM] * (len(kept) + len(after[:1])) + [VMEM] * len(after[1:]),
         (VMEM, HBM, HBM, HBM),
         {4 + i: 1 + i for i in range(len(kept))},
         [
@@ -111,9 +132,8 @@
     )
 
 
-def backward_kernel(t, m, pins, section, u_in, saved, factor, gain, turned, *refs):
-    slope, term, grad, sems = refs[-4:]
-    d, slope_out, term_out = refs[-7 - pins : len(refs) - 4 - pins]
+def backward_kernel(t, m, section, u_in, saved, factor, gain, turned, *refs):
+    d, slope_out, term_out, slope, term, grad, sems = refs[-7:]
 
     @pl.when(section[0] == t)
     def _():
@@ -136,29 +156,21 @@
         keep_term.wait()
 
 
-def backward(t, m, section, u, saved, factor, gain_row, turned, kept, after, pinned):
+def backward(t, m, section, u, saved, factor, gain_row, turned, kept, after):
     shape = saved.shape
-    first = 6 + len(kept) + len(after)
-    aliases = {6 + i: 1 + i for i in range(len(kept))}
-    aliases.update({first + i: 3 + i for i in range(len(pinned))})
     return call(
-        functools.partial(backward_kernel, t, m if u.ndim == 3 else None, len(pinned)),
-        (
-            pltpu.VMEM(shape, BF),
-            pltpu.HBM(shape, BF),
-            pltpu.HBM((1, shape[1]), F32),
-            *(pltpu.HBM(p.shape, p.dtype) for p in pinned),
-        ),
-        [SMEM] + [VMEM] * 5 + [HBM] * (first - 6 + len(pinned)),
-        (VMEM,) + (HBM,) * (2 + len(pinned)),
-        aliases,
+        functools.partial(backward_kernel, t, m if u.ndim == 3 else None),
+        (pltpu.VMEM(shape, BF), pltpu.HBM(shape, BF), pltpu.HBM((1, shape[1]), F32)),
+        [SMEM] + [VMEM] * 5 + [HBM] * (len(kept) + len(after)),
+        (VMEM, HBM, HBM),
+        {6 + i: 1 + i for i in range(len(kept))},
         [
             pltpu.VMEM(shape, BF),
             pltpu.VMEM((1, shape[1]), F32),
             pltpu.VMEM(shape, F32),
             pltpu.SemaphoreType.DMA((2,)),
         ],
-        [section, u, saved, factor, gain_row, turned, *kept, *after, *pinned],
+        [section, u, saved, factor, gain_row, turned, *kept, *after],
     )
 
 
@@ -178,10 +190,12 @@
 
 def order(sections, micros):
     steps = [(t, m) for t in range(sections) for m in range(micros)]
-    return sorted(steps, key=lambda p: micros * p[0] + (micros - 1) * p[1])
-
-
-def spread(block, owner, sections, section):
+    return sorted(steps, key=lambda p: (37 * (p[0] // 2) + 14 * (p[0] % 2) + 16 * p[1]))
+
+
+def spread(first, last, sections, section):
+    block, rows = jnp.concatenate([first, last], axis=0), first.shape[0]
+    owned = lax.broadcasted_iota(jnp.int32, (2 * rows, 1), 0) >= rows
     bit = sections // 2
     while bit:
         width = block.shape[1] // 2
@@ -189,9 +203,97 @@
         upper = (section & bit) != 0
         pairs = [(s, s ^ bit) for s in range(sections)]
         arrived = lax.ppermute(jnp.where(upper, low, high), "section", pairs)
-        block = jnp.where(upper == bool(owner & bit), jnp.where(upper, high, low), arrived)
+        block = jnp.where(owned == upper, jnp.where(upper, high, low), arrived)
         bit //= 2
-    return block
+    return block[:rows], block[rows:]
+
+
+def cut_kernel(low, high, here, *refs):
+    first, second, third, *out, whole, cut, sems = refs
+
+    @pl.when((here[0] >= low) & (here[0] < high))
+    def _():
+        rows = first.shape[0]
+        loads = [
+            pltpu.make_async_copy(part, whole.at[pl.ds(i * rows, rows), :], sems.at[i])
+            for i, part in enumerate((first, second, third))
+        ]
+        for load in loads:
+            load.start()
+        for load in loads:
+            load.wait()
+        width = whole.shape[1] // 16
+        for y in range(4):
+
+            @pl.when(here[1] == y)
+            def _():
+                for k in range(4):
+                    for z in range(4):
+                        column = (4 * z + (y + k) % 4) * width
+                        cut[k, :, pl.ds(z * width, width)] = whole[:, pl.ds(column, width)]
+
+        stores = [pltpu.make_async_copy(cut.at[k], out[k], sems.at[k]) for k in range(4)]
+        for store in stores:
+            store.start()
+        for store in stores:
+            store.wait()
+
+
+def cut_columns(parts, here, low, high):
+    rows, features = 3 * parts[0].shape[0], parts[0].shape[1]
+    return call(
+        functools.partial(cut_kernel, low, high),
+        tuple(pltpu.HBM((rows, features // 4), BF) for _ in range(4)),
+        [SMEM] + [HBM] * 3,
+        (HBM,) * 4,
+        {},
+        [
+            pltpu.VMEM((rows, features), BF),
+            pltpu.VMEM((4, rows, features // 4), BF),
+            pltpu.SemaphoreType.DMA((4,)),
+        ],
+        [here, *(in_hbm(part) for part in parts)],
+    )
+
+
+def pile_kernel(low, high, here, *refs):
+    *parts, out, sems = refs
+
+    @pl.when((here[0] >= low) & (here[0] < high))
+    def _():
+        copies = [
+            pltpu.make_async_copy(part, out.at[k], sems.at[k]) for k, part in enumerate(parts)
+        ]
+        for copy in copies:
+            copy.start()
+        for copy in copies:
+            copy.wait()
+
+
+def pile(parts, here, low, high):
+    return call(
+        functools.partial(pile_kernel, low, high),
+        pltpu.HBM((len(parts), *parts[0].shape), BF),
+        [SMEM] + [HBM] * len(parts),
+        HBM,
+        {},
+        [pltpu.SemaphoreType.DMA((len(parts),))],
+        [here, *(in_hbm(part) for part in parts)],
+    )
+
+
+def exchange(parts, here, low, high, count):
+    sections = range(low, high)
+    cut = cut_columns(parts, here, low, high)
+    pieces = [cut[0]]
+    for k in (1, 2, 3):
+        pairs = [(s * count + i, s * count + i // 4 * 4 + (i + k) % 4) for s in sections for i in range(count)]
+        pieces.append(lax.ppermute(cut[k], ("section", "dp"), pairs))
+    blocks = [pile(pieces, here, low, high)]
+    pairs = [(s * count + i, s * count + 4 * z_after(i // 4, 1) + i % 4) for s in sections for i in range(count)]
+    for _ in range(3):
+        blocks.append(lax.ppermute(blocks[-1], ("section", "dp"), pairs))
+    return blocks
 
 
 RING = (0, 2, 3, 1)
@@ -229,6 +331,31 @@
     for _ in range(3):
         blocks.append(shift_z(blocks[-1], 1, count))
     return blocks
+
+
+def gather(shard, count):
+    rows, features = shard.shape
+    part, border = rows // 2, features * 3 // 4
+    pieces = []
+    first, second = shard[:, :border], shard[:, border:]
+    left, right = shift_y(second, 1, count), shift_y(second, 3, count)
+    far = shift_y(left[:part], 1, count), shift_y(right[part:], 3, count)
+    second = jnp.concatenate([second, left, *far, right], axis=0)
+    for k in range(4):
+        if k:
+            first = shift_z(first, 1, count)
+            second = shift_z(second, 1, count)
+        left, right = shift_y(first, 1, count), shift_y(first, 3, count)
+        far = shift_y(left[:part], 1, count), shift_y(right[part:], 3, count)
+        pieces += [
+            (first, [(4 * k, 0, rows, 0, 0)]),
+            (left, [(4 * k + 1, 0, rows, 0, 0)]),
+            (right, [(4 * k + 3, 0, rows, 0, 0)]),
+            (far[0], [(4 * k + 2, 0, part, 0, 0)]),
+            (far[1], [(4 * k + 2, 0, part, part, 0)]),
+            (second, [(4 * k + j, rows * j, rows, 0, border) for j in range(4)]),
+        ]
+    return pieces
 
 
 def on_device(inputs, cotangent, weight, gain):
@@ -243,14 +370,13 @@
     to_z = [ahead[k, z] for k in range(4)]
     from_z = [behind[k, z] for k in range(4)]
     micros, rows, features = inputs.shape
-    here = section.astype(jnp.int32).reshape(1)
+    here = jnp.stack([section, y]).astype(jnp.int32)
     gain_row = lax.dynamic_index_in_dim(gain, section, 0, keepdims=True)
     across = [(i, mirrored(i, count)) for i in range(count)]
-    gathered = lax.all_gather(weight[0], "dp", axis=0, tiled=True)
-    gathered, cotangent, inputs, gain_row, here = lax.optimization_barrier(
-        (gathered, cotangent, inputs, gain_row, here)
-    )
-    matrix = hold(gathered)
+    row_of = jnp.stack([from_z[k] * 4 + (y - j) % 4 for k in range(4) for j in range(4)])
+    row_of = (row_of * weight.shape[1]).astype(jnp.int32)
+    matrix = hold(gather(weight[0], count), row_of, (features, features))
+    cotangent, matrix = lax.optimization_barrier((cotangent, matrix))
     upstream = lax.ppermute(cotangent, "dp", across)
 
     kept = [()] * micros
@@ -260,38 +386,33 @@
     for t, m in order(sections, micros):
         if t == half and turned is None:
             turned = turn(matrix)
+            after += (turned,)
         result, *kept[m] = forward(t, m, here, current[m], gain_row, matrix, kept[m], after)
         after = (in_hbm(kept[m][0]),)
         current[m] = hop(result, t, half, count) if t + 1 < sections else result
 
     passed = [()] * micros
     arriving = [upstream] * micros
-    parked = [kept[m][1] for m in range(micros)] + current
+    normed = [kept[m][1] for m in range(micros)]
+    early = exchange(normed, here, 0, EARLY, count)
+    after += (in_hbm(early[-1]),)
     for step, m in order(sections, micros):
         t = sections - 1 - step
-        pinned = parked if (t, m) == (sections - 6, micros - 1) else []
-        result, *rest = backward(
-            t, m, here, arriving[m], kept[m][0], kept[m][2], gain_row, turned,
-            passed[m], after, pinned,
+        result, *passed[m] = backward(
+            t, m, here, arriving[m], kept[m][0], kept[m][2], gain_row, turned, passed[m], after
         )
-        passed[m] = rest[:2]
         after = (in_hbm(passed[m][0]),)
-        if pinned:
-            parked = rest[2:]
-            last = jnp.concatenate(parked[micros:], axis=0)
-            final_share = spread(lax.ppermute(last, "dp", across), sections - 1, sections, section)
-            normed = jnp.concatenate(parked[:micros], axis=0)
-            cut = normed.reshape(micros * rows, 4, 4, -1).transpose(2, 0, 1, 3)
-            cut = cut.reshape(4, micros * rows, features // 4)
-            normed = [pick(cut, y)]
-            normed += [shift_y(pick(cut, (y + k) % 4), k, count) for k in (1, 2, 3)]
-            normed = from_all_z(jnp.stack(normed), count)
         arriving[m] = hop(result, t - 1, half, count) if t else result
+    held = lax.optimization_barrier((*normed, after[0]))
+    late = exchange(held[:micros], here, EARLY, sections, count)
+    normed = [jnp.where(section < EARLY, a, b) for a, b in zip(early, late)]
 
     slope = jnp.concatenate([passed[m][0] for m in range(micros)], axis=0)
-    cut = slope.reshape(micros * rows, 4, features // 4).transpose(1, 0, 2)
-    slope = [pick(cut, z)]
-    slope += [shift_z(pick(cut, to_z[k]), k, count) for k in (1, 2, 3)]
+    wide = features // 4
+    slope = [
+        lax.dynamic_slice_in_dim(slope, to_z[k] * wide, wide, axis=1) for k in range(4)
+    ]
+    slope = slope[:1] + [shift_z(slope[k], k, count) for k in (1, 2, 3)]
     slope = from_all_y(jnp.concatenate(slope, axis=0), count)
     slope = jnp.stack(slope).reshape(4, 4, micros * rows, features // 4)
     product = jnp.einsum(
@@ -308,7 +429,8 @@
     total = sum(passed[m][1] for m in range(micros))
     total = total + (shift_y(total, 1, count) + shift_y(total, 2, count) + shift_y(total, 3, count))
     total = total + (shift_z(total, 1, count) + shift_z(total, 2, count) + shift_z(total, 3, count))
-    first_share = spread(jnp.concatenate(arriving, axis=0), 0, sections, section)
+    last = lax.ppermute(jnp.concatenate(current, axis=0), "dp", across)
+    first_share, final_share = spread(jnp.concatenate(arriving, axis=0), last, sections, section)
     shape = (micros, rows, features // sections)
     return (
         weight_grad[None],

time: 1030 us -> 1080 us (1.049)
  the two profiles are of different devices: /device:TPU:128 before, /device:TPU:134 now
where the time goes in v4:
time: 1080 us; the launch traced here: 1070 us
  starting transfers between devices  525 us (49%)
  waiting for transfers between devices  244 us (23%)
  Pallas kernels  171 us (16%)
  local copies, waits for them, and re-layouts  98.8 us (9%)
  between operations  19 us (2%)
    ppermute x90, starting transfers between devices, hop(): return lax.ppermute(block, ('section', 'dp'), sorted(pairs))  270 us
    pallas_call x102, Pallas kernels, call(): pl.pallas_call(kernel, out_shape=outs, in_specs=in_specs, out_specs=out_s...  171 us
    ppermute x15, waiting for transfers between devices, shift_z(): return lax.ppermute(block, 'dp', pairs)  123 us
    ppermute x4, starting transfers between devices, spread(): arrived = lax.ppermute(jnp.where(upper, low, high), 'section', pairs)  116 us
    unnamed x218, local copies, waits for them, and re-layouts  88.8 us
    ppermute x15, starting transfers between devices, shift_z(): return lax.ppermute(block, 'dp', pairs)  61 us
    ppermute x27, starting transfers between devices, shift_y(): return lax.ppermute(block, 'dp', pairs)  45.2 us
    ppermute x6, waiting for transfers between devices, exchange(): blocks.append(lax.ppermute(blocks[-1], ('section', 'dp'), pairs))  37.9 us
  transfers between devices with their start and end apart: 150, of which 37 were waited for; matrix products, arithmetic and copies ran while one was open for 5% of the time, Pallas kernels for 12%

profile of v4, /device:TPU:134, one launch (start us, length us, event | category | flops | bytes accessed | tf_op | source)
XLA Modules:
  0.0 1065.1 jit_solution(16794552307307501400)
XLA Ops:
  7.8 6.5 collective-permute-done.4
  18.1 4.3 collective-permute-done.5
  29.0 17.0 %collective-permute-done.14.refs_12_ = bf16[192,2304]{1,0:T(8,128)(2,1)S(1)} collective-permute-done((bf16[192,2304]{1,0:T(8,128)(2,1)S(1)}, bf16[192,2304]{1,0:T(8,128)(2,1)S(1)}, u32[]{:S(2)}, u32[]{:S(2)}) %collective-permute-start.14) | collective-permute-done | bytes 884768 | tf_op jit(solution)/shard_map/ppermute | solution.py:308
  46.0 3.3 collective-permute-start.20
  52.3 19.0 %collective-permute-done.13.refs_11_ = bf16[768,768]{1,0:T(8,128)(2,1)S(1)} collective-permute-done((bf16[768,768]{1,0:T(8,128)(2,1)S(1)}, bf16[768,768]{1,0:T(8,128)(2,1)S(1)}, u32[]{:S(2)}, u32[]{:S(2)}) %collective-permute-start.13) | collective-permute-done | bytes 1179680 | tf_op jit(solution)/shard_map/ppermute | solution.py:308
  71.3 3.3 collective-permute-start.19
  77.8 12.4 %collective-permute-done.20.refs_18_ = bf16[192,2304]{1,0:T(8,128)(2,1)S(1)} collective-permute-done((bf16[192,2304]{1,0:T(8,128)(2,1)S(1)}, bf16[192,2304]{1,0:T(8,128)(2,1)S(1)}, u32[]{:S(2)}, u32[]{:S(2)}) %collective-permute-start.20) | collective-permute-done | bytes 884768 | tf_op jit(solution)/shard_map/ppermute | solution.py:308
  93.7 20.0 %collective-permute-done.19.refs_17_ = bf16[768,768]{1,0:T(8,128)(2,1)} collective-permute-done((bf16[768,768]{1,0:T(8,128)(2,1)S(1)}, bf16[768,768]{1,0:T(8,128)(2,1)}, u32[]{:S(2)}, u32[]{:S(2)}) %collective-permute-start.19) | collective-permute-done | bytes 1179680 | tf_op jit(solution)/shard_map/ppermute | solution.py:308
  137.2 5.9 collective-permute-done.11.refs_9_
  146.8 5.8 collective-permute-done.17.refs_15_
  153.3 5.6 collective-permute-done.23.refs_21_
  160.0 7.2 shard_map.93.matrix.source
  182.5 3.4 shard_map.101
  196.3 3.4 shard_map.107
  201.7 24.2 %collective-permute-start.37 = (bf16[64,3072]{1,0:T(8,128)(2,1)S(1)}, bf16[64,3072]{1,0:T(8,128)(2,1)S(1)}, u32[]{:S(2)}, u32[]{:S(2)}) collective-permute-start(bf16[64,3072]{1,0:T(8,128)(2,1)S(1)} %get-tuple-element.400), channel_id=1, source_target_pairs={{80,96},{81,97},{82,98},{83,99},{84,100},{85,101},{86,102},{87,103... | collective-permute-start | bytes 1179656 | tf_op jit(solution)/shard_map/ppermute | solution.py:188
  233.9 4.5 collective-permute-start.45
  249.6 6.4 copy-done.8
  255.9 5.3 shard_map.117.refs_4_.turned
  268.1 3.6 slice-done.11
  289.2 3.4 shard_map.125
  302.8 3.6 shard_map.131
  309.1 106.4 %collective-permute-start.61 = (bf16[64,3072]{1,0:T(8,128)(2,1)S(1)}, bf16[64,3072]{1,0:T(8,128)(2,1)S(1)}, u32[]{:S(2)}, u32[]{:S(2)}) collective-permute-start(bf16[64,3072]{1,0:T(8,128)(2,1)S(1)} %get-tuple-element.496), channel_id=1, source_target_pairs={{80,96},{81,97},{82,98},{83,99},{84,100},{85,101},{86,102},{87,103... | collective-permute-start | bytes 1179656 | tf_op jit(solution)/shard_map/ppermute | solution.py:188
  420.9 5.0 shard_map.136
  427.9 4.3 collective-permute-start.67
  434.4 3.2 collective-permute-done.67.x_in
  437.6 5.0 shard_map.139
  450.0 3.6 collective-permute-done.69.x_in
  453.6 5.0 shard_map.141
  472.0 23.8 %collective-permute-done.74.u_in = bf16[3,64,3072]{2,1,0:T(8,128)(2,1)S(1)} collective-permute-done((bf16[3,64,3072]{2,1,0:T(8,128)(2,1)S(1)}, bf16[3,64,3072]{2,1,0:T(8,128)(2,1)S(1)}, u32[]{:S(2)}, u32[]{:S(2)}) %collective-permute-start.74) | collective-permute-done | bytes 1179680 | tf_op jit(solution)/shard_map/ppermute | solution.py:380
  497.7 9.7 collective-permute-start.78
  509.2 4.6 shard_map.146
  520.7 4.6 shard_map.148
  529.3 5.2 collective-permute-start.83
  534.5 4.6 shard_map.151
  541.6 8.9 collective-permute-start.82
  571.7 4.9 shard_map.165
  590.6 6.8 collective-permute-start.105
  604.1 16.8 %collective-permute-start.107 = (bf16[64,3072]{1,0:T(8,128)(2,1)S(1)}, bf16[64,3072]{1,0:T(8,128)(2,1)S(1)}, u32[]{:S(2)}, u32[]{:S(2)}) collective-permute-start(bf16[64,3072]{1,0:T(8,128)(2,1)S(1)} %get-tuple-element.637), channel_id=1, source_target_pairs={{80,96},{81,97},{82,98},{83,99},{84,100},{85,101},{86,102},{87,103... | collective-permute-start | bytes 1179656 | tf_op jit(solution)/shard_map/ppermute | solution.py:188
  622.0 4.3 collective-permute-done.107.u_in
  628.0 4.9 collective-permute-start.106
  650.5 6.4 copy-done.3
  686.0 6.4 copy-done.4
  693.6 6.9 copy-done.5
  702.2 7.1 copy-done.6
  717.7 78.3 %collective-permute-start.146 = (bf16[384,1536]{1,0:T(8,128)(2,1)S(1)}, bf16[384,1536]{1,0:T(8,128)(2,1)S(1)}, u32[]{:S(2)}, u32[]{:S(2)}) collective-permute-start(bf16[384,1536]{1,0:T(8,128)(2,1)S(1)} %broadcast_select_fusion), channel_id=1, source_target_pairs={{0,128},{16,144},{32,160},{48,176},{64,192},{80,208},{96,224},{112... | collective-permute-start | bytes 3538952 | tf_op jit(solution)/shard_map/ppermute | solution.py:205
  798.2 3.1 shard_map.193
  803.2 4.5 collective-permute-start.124
  807.7 3.8 collective-permute-start.125
  817.3 38.3 %collective-permute-start.129 = (bf16[192,768]{1,0:T(8,128)(2,1)S(1)}, bf16[192,768]{1,0:T(8,128)(2,1)S(1)}, u32[]{:S(2)}, u32[]{:S(2)}) collective-permute-start(bf16[192,768]{1,0:T(8,128)(2,1)S(1)} %get-tuple-element.709), channel_id=1, source_target_pairs={{0,8},{1,9},{2,10},{3,11},{4,0},{5,1},{6,2},{7,3},{8,12},{9,13},{1... | collective-permute-start | bytes 884744 | tf_op jit(solution)/shard_map/ppermute | solution.py:308
  855.6 37.4 %shard_map.194 = bf16[4,192,768]{2,1,0:T(8,128)(2,1)} custom-call(s32[2]{0:T(128)S(1)} %pad_add_fusion.section.here, bf16[192,768]{1,0:T(8,128)(2,1)} %get-tuple-element.689.refs_0_, bf16[192,768]{1,0:T(8,128)(2,1)} %copy-done.66, bf16[192,768]{1,0:T(8,128)(2,1)} %copy-done.67, bf16[192,768]{1,0:T(8,128)(2,1)} %copy-done.68), custom_call_target="tpu_custom_call" | custom-call | flops 1 | bytes 1 | tf_op jit(solution)/shard_map/pallas_call | solution.py:26
  894.9 4.8 collective-permute-start.126
  899.9 5.1 collective-permute-done.130
  906.8 28.5 %collective-permute-done.131 = bf16[192,768]{1,0:T(8,128)(2,1)S(1)} collective-permute-done((bf16[192,768]{1,0:T(8,128)(2,1)S(1)}, bf16[192,768]{1,0:T(8,128)(2,1)S(1)}, u32[]{:S(2)}, u32[]{:S(2)}) %collective-permute-start.131) | collective-permute-done | bytes 294944 | tf_op jit(solution)/shard_map/ppermute | solution.py:308
  935.3 4.3 collective-permute-start.132
  940.2 37.2 %collective-permute-start.147 = (bf16[384,768]{1,0:T(8,128)(2,1)S(1)}, bf16[384,768]{1,0:T(8,128)(2,1)S(1)}, u32[]{:S(2)}, u32[]{:S(2)}) collective-permute-start(bf16[384,768]{1,0:T(8,128)(2,1)S(1)} %broadcast_select_fusion.1), channel_id=1, source_target_pairs={{0,64},{16,80},{32,96},{48,112},{64,0},{80,16},{96,32},{112,48},{1... | collective-permute-start | bytes 1769480 | tf_op jit(solution)/shard_map/ppermute | solution.py:205
  977.4 4.8 collective-permute-start.127
  989.6 16.3 %collective-permute-done.127 = bf16[4,192,768]{2,1,0:T(8,128)(2,1)S(1)} collective-permute-done((bf16[4,192,768]{2,1,0:T(8,128)(2,1)S(1)}, bf16[4,192,768]{2,1,0:T(8,128)(2,1)S(1)}, u32[]{:S(2)}, u32[]{:S(2)}) %collective-permute-start.127) | collective-permute-done | bytes 1179680 | tf_op jit(solution)/shard_map/ppermute | solution.py:295
  1005.8 3.8 collective-permute-start.128
  1011.5 21.7 %collective-permute-done.128 = bf16[4,192,768]{2,1,0:T(8,128)(2,1)S(1)} collective-permute-done((bf16[4,192,768]{2,1,0:T(8,128)(2,1)S(1)}, bf16[4,192,768]{2,1,0:T(8,128)(2,1)S(1)}, u32[]{:S(2)}, u32[]{:S(2)}) %collective-permute-start.128) | collective-permute-done | bytes 1179680 | tf_op jit(solution)/shard_map/ppermute | solution.py:295
  1033.3 4.1 bitcast_convert_fusion
  1039.0 4.0 collective-permute-start.137
  1043.7 4.5 collective-permute-done.136
  1048.2 6.7 collective-permute-done.137
  1055.0 8.7 collective-permute-done.138
  (612 shorter events, 299.7 us)
Async XLA Ops:
  1.9 21.5 %collective-permute-start.8 = (bf16[192,2304]{1,0:T(8,128)(2,1)S(1)}, bf16[192,2304]{1,0:T(8,128)(2,1)S(1)}, u32[]{:S(2)}, u32[]{:S(2)}) collective-permute-start(bf16[192,2304]{1,0:T(8,128)(2,1)S(1)} %slice.96.refs_0_), channel_id=1, source_target_pairs={{0,8},{1,9},{2,10},{3,11},{4,0},{5,1},{6,2},{7,3},{8,12},{9,13},{1... | collective-permute-start | bytes 2654216 | tf_op jit(solution)/shard_map/ppermute | solution.py:308
  14.7 34.6 %collective-permute-start = (bf16[192,2304]{1,0:T(8,128)(2,1)S(1)}, bf16[192,2304]{1,0:T(8,128)(2,1)S(1)}, u32[]{:S(2)}, u32[]{:S(2)}) collective-permute-start(bf16[192,2304]{1,0:T(8,128)(2,1)S(1)} %slice.96.refs_0_), channel_id=1, source_target_pairs={{0,1},{1,2},{2,3},{3,0},{4,5},{5,6},{6,7},{7,4},{8,9},{9,10},{10,1... | collective-permute-start | bytes 2654216 | tf_op jit(solution)/shard_map/ppermute | solution.py:313
  23.4 22.6 %collective-permute-start.14 = (bf16[192,2304]{1,0:T(8,128)(2,1)S(1)}, bf16[192,2304]{1,0:T(8,128)(2,1)S(1)}, u32[]{:S(2)}, u32[]{:S(2)}) collective-permute-start(bf16[192,2304]{1,0:T(8,128)(2,1)S(1)} %collective-permute-done.8.refs_6_), channel_id=1, source_target_pairs={{0,8},{1,9},{2,10},{3,11},{4,0},{5,1},{6,2},{7,3},{8,12},{9,13},{1... | collective-permute-start | bytes 2654216 | tf_op jit(solution)/shard_map/ppermute | solution.py:308
  25.8 45.5 %collective-permute-start.13 = (bf16[768,768]{1,0:T(8,128)(2,1)S(1)}, bf16[768,768]{1,0:T(8,128)(2,1)S(1)}, u32[]{:S(2)}, u32[]{:S(2)}) collective-permute-start(bf16[768,768]{1,0:T(8,128)(2,1)S(1)} %constant_dynamic-update-slice_fusion.refs_5_), channel_id=1, source_target_pairs={{0,8},{1,9},{2,10},{3,11},{4,0},{5,1},{6,2},{7,3},{8,12},{9,13},{1... | collective-permute-start | bytes 3538952 | tf_op jit(solution)/shard_map/ppermute | solution.py:308
  26.0 48.5 %collective-permute-start.1 = (bf16[192,2304]{1,0:T(8,128)(2,1)S(1)}, bf16[192,2304]{1,0:T(8,128)(2,1)S(1)}, u32[]{:S(2)}, u32[]{:S(2)}) collective-permute-start(bf16[192,2304]{1,0:T(8,128)(2,1)S(1)} %slice.96.refs_0_), channel_id=1, source_target_pairs={{0,3},{1,0},{2,1},{3,2},{4,7},{5,4},{6,5},{7,6},{8,11},{9,8},{10,9... | collective-permute-start | bytes 2654216 | tf_op jit(solution)/shard_map/ppermute | solution.py:313
  29.0 47.1 %collective-permute-start.9 = (bf16[192,2304]{1,0:T(8,128)(2,1)S(1)}, bf16[192,2304]{1,0:T(8,128)(2,1)S(1)}, u32[]{:S(2)}, u32[]{:S(2)}) collective-permute-start(bf16[192,2304]{1,0:T(8,128)(2,1)S(1)} %collective-permute-done.8.refs_6_), channel_id=1, source_target_pairs={{0,1},{1,2},{2,3},{3,0},{4,5},{5,6},{6,7},{7,4},{8,9},{9,10},{10,1... | collective-permute-start | bytes 2654216 | tf_op jit(solution)/shard_map/ppermute | solution.py:313
  46.0 44.2 %collective-permute-start.20 = (bf16[192,2304]{1,0:T(8,128)(2,1)S(1)}, bf16[192,2304]{1,0:T(8,128)(2,1)S(1)}, u32[]{:S(2)}, u32[]{:S(2)}) collective-permute-start(bf16[192,2304]{1,0:T(8,128)(2,1)S(1)} %collective-permute-done.14.refs_12_), channel_id=1, source_target_pairs={{0,8},{1,9},{2,10},{3,11},{4,0},{5,1},{6,2},{7,3},{8,12},{9,13},{1... | collective-permute-start | bytes 2654216 | tf_op jit(solution)/shard_map/ppermute | solution.py:308
  49.3 42.7 %collective-permute-start.10 = (bf16[192,2304]{1,0:T(8,128)(2,1)S(1)}, bf16[192,2304]{1,0:T(8,128)(2,1)S(1)}, u32[]{:S(2)}, u32[]{:S(2)}) collective-permute-start(bf16[192,2304]{1,0:T(8,128)(2,1)S(1)} %collective-permute-done.8.refs_6_), channel_id=1, source_target_pairs={{0,3},{1,0},{2,1},{3,2},{4,7},{5,4},{6,5},{7,6},{8,11},{9,8},{10,9... | collective-permute-start | bytes 2654216 | tf_op jit(solution)/shard_map/ppermute | solution.py:313
  71.3 42.4 %collective-permute-start.19 = (bf16[768,768]{1,0:T(8,128)(2,1)S(1)}, bf16[768,768]{1,0:T(8,128)(2,1)}, u32[]{:S(2)}, u32[]{:S(2)}) collective-permute-start(bf16[768,768]{1,0:T(8,128)(2,1)S(1)} %collective-permute-done.13.refs_11_), channel_id=1, source_target_pairs={{0,8},{1,9},{2,10},{3,11},{4,0},{5,1},{6,2},{7,3},{8,12},{9,13},{1... | collective-permute-start | bytes 3538952 | tf_op jit(solution)/shard_map/ppermute | solution.py:308
  74.5 44.7 %collective-permute-start.15 = (bf16[192,2304]{1,0:T(8,128)(2,1)S(1)}, bf16[192,2304]{1,0:T(8,128)(2,1)S(1)}, u32[]{:S(2)}, u32[]{:S(2)}) collective-permute-start(bf16[192,2304]{1,0:T(8,128)(2,1)S(1)} %collective-permute-done.14.refs_12_), channel_id=1, source_target_pairs={{0,1},{1,2},{2,3},{3,0},{4,5},{5,6},{6,7},{7,4},{8,9},{9,10},{10,1... | collective-permute-start | bytes 2654216 | tf_op jit(solution)/shard_map/ppermute | solution.py:313
  76.1 44.8 %collective-permute-start.16 = (bf16[192,2304]{1,0:T(8,128)(2,1)S(1)}, bf16[192,2304]{1,0:T(8,128)(2,1)}, u32[]{:S(2)}, u32[]{:S(2)}) collective-permute-start(bf16[192,2304]{1,0:T(8,128)(2,1)S(1)} %collective-permute-done.14.refs_12_), channel_id=1, source_target_pairs={{0,3},{1,0},{2,1},{3,2},{4,7},{5,4},{6,5},{7,6},{8,11},{9,8},{10,9... | collective-permute-start | bytes 2654216 | tf_op jit(solution)/shard_map/ppermute | solution.py:313
  90.2 32.5 %collective-permute-start.21 = (bf16[192,2304]{1,0:T(8,128)(2,1)S(1)}, bf16[192,2304]{1,0:T(8,128)(2,1)}, u32[]{:S(2)}, u32[]{:S(2)}) collective-permute-start(bf16[192,2304]{1,0:T(8,128)(2,1)S(1)} %collective-permute-done.20.refs_18_), channel_id=1, source_target_pairs={{0,1},{1,2},{2,3},{3,0},{4,5},{5,6},{6,7},{7,4},{8,9},{9,10},{10,1... | collective-permute-start | bytes 2654216 | tf_op jit(solution)/shard_map/ppermute | solution.py:313
  92.0 31.1 %collective-permute-start.22 = (bf16[192,2304]{1,0:T(8,128)(2,1)S(1)}, bf16[192,2304]{1,0:T(8,128)(2,1)}, u32[]{:S(2)}, u32[]{:S(2)}) collective-permute-start(bf16[192,2304]{1,0:T(8,128)(2,1)S(1)} %collective-permute-done.20.refs_18_), channel_id=1, source_target_pairs={{0,3},{1,0},{2,1},{3,2},{4,7},{5,4},{6,5},{7,6},{8,11},{9,8},{10,9... | collective-permute-start | bytes 2654216 | tf_op jit(solution)/shard_map/ppermute | solution.py:313
  113.7 45.5 %collective-permute-start.25 = (bf16[768,768]{1,0:T(8,128)(2,1)}, bf16[768,768]{1,0:T(8,128)(2,1)}, u32[]{:S(2)}, u32[]{:S(2)}) collective-permute-start(bf16[768,768]{1,0:T(8,128)(2,1)} %collective-permute-done.19.refs_17_), channel_id=1, source_target_pairs={{0,8},{1,9},{2,10},{3,11},{4,0},{5,1},{6,2},{7,3},{8,12},{9,13},{1... | collective-permute-start | bytes 3538952 | tf_op jit(solution)/shard_map/ppermute | solution.py:308
  119.3 14.4 %collective-permute-start.2 = (bf16[96,2304]{1,0:T(8,128)(2,1)S(1)}, bf16[96,2304]{1,0:T(8,128)(2,1)S(1)}, u32[]{:S(2)}, u32[]{:S(2)}) collective-permute-start(bf16[96,2304]{1,0:T(8,128)(2,1)S(1)} %slice.97), channel_id=1, source_target_pairs={{0,1},{1,2},{2,3},{3,0},{4,5},{5,6},{6,7},{7,4},{8,9},{9,10},{10,1... | collective-permute-start | bytes 1327112 | tf_op jit(solution)/shard_map/ppermute | solution.py:313
  121.0 13.4 %collective-permute-start.3 = (bf16[96,2304]{1,0:T(8,128)(2,1)}, bf16[96,2304]{1,0:T(8,128)(2,1)S(1)}, u32[]{:S(2)}, u32[]{:S(2)}) collective-permute-start(bf16[96,2304]{1,0:T(8,128)(2,1)} %slice.98), channel_id=1, source_target_pairs={{0,3},{1,0},{2,1},{3,2},{4,7},{5,4},{6,5},{7,6},{8,11},{9,8},{10,9... | collective-permute-start | bytes 1327112 | tf_op jit(solution)/shard_map/ppermute | solution.py:313
  122.7 20.5 %collective-permute-start.11 = (bf16[96,2304]{1,0:T(8,128)(2,1)}, bf16[96,2304]{1,0:T(8,128)(2,1)S(1)}, u32[]{:S(2)}, u32[]{:S(2)}) collective-permute-start(bf16[96,2304]{1,0:T(8,128)(2,1)} %slice.102), channel_id=1, source_target_pairs={{0,1},{1,2},{2,3},{3,0},{4,5},{5,6},{6,7},{7,4},{8,9},{9,10},{10,1... | collective-permute-start | bytes 1327112 | tf_op jit(solution)/shard_map/ppermute | solution.py:313
  123.1 20.8 %collective-permute-start.12 = (bf16[96,2304]{1,0:T(8,128)(2,1)}, bf16[96,2304]{1,0:T(8,128)(2,1)S(1)}, u32[]{:S(2)}, u32[]{:S(2)}) collective-permute-start(bf16[96,2304]{1,0:T(8,128)(2,1)} %slice.103), channel_id=1, source_target_pairs={{0,3},{1,0},{2,1},{3,2},{4,7},{5,4},{6,5},{7,6},{8,11},{9,8},{10,9... | collective-permute-start | bytes 1327112 | tf_op jit(solution)/shard_map/ppermute | solution.py:313
  133.7 19.0 %collective-permute-start.17 = (bf16[96,2304]{1,0:T(8,128)(2,1)S(1)}, bf16[96,2304]{1,0:T(8,128)(2,1)S(1)}, u32[]{:S(2)}, u32[]{:S(2)}) collective-permute-start(bf16[96,2304]{1,0:T(8,128)(2,1)S(1)} %slice.104), channel_id=1, source_target_pairs={{0,1},{1,2},{2,3},{3,0},{4,5},{5,6},{6,7},{7,4},{8,9},{9,10},{10,1... | collective-permute-start | bytes 1327112 | tf_op jit(solution)/shard_map/ppermute | solution.py:313
  134.4 19.0 %collective-permute-start.18 = (bf16[96,2304]{1,0:T(8,128)(2,1)S(1)}, bf16[96,2304]{1,0:T(8,128)(2,1)S(1)}, u32[]{:S(2)}, u32[]{:S(2)}) collective-permute-start(bf16[96,2304]{1,0:T(8,128)(2,1)S(1)} %slice.105), channel_id=1, source_target_pairs={{0,3},{1,0},{2,1},{3,2},{4,7},{5,4},{6,5},{7,6},{8,11},{9,8},{10,9... | collective-permute-start | bytes 1327112 | tf_op jit(solution)/shard_map/ppermute | solution.py:313
  143.2 15.7 %collective-permute-start.23 = (bf16[96,2304]{1,0:T(8,128)(2,1)S(1)}, bf16[96,2304]{1,0:T(8,128)(2,1)S(1)}, u32[]{:S(2)}, u32[]{:S(2)}) collective-permute-start(bf16[96,2304]{1,0:T(8,128)(2,1)S(1)} %slice.106), channel_id=1, source_target_pairs={{0,1},{1,2},{2,3},{3,0},{4,5},{5,6},{6,7},{7,4},{8,9},{9,10},{10,1... | collective-permute-start | bytes 1327112 | tf_op jit(solution)/shard_map/ppermute | solution.py:313
  143.8 15.4 %collective-permute-start.24 = (bf16[96,2304]{1,0:T(8,128)(2,1)S(1)}, bf16[96,2304]{1,0:T(8,128)(2,1)S(1)}, u32[]{:S(2)}, u32[]{:S(2)}) collective-permute-start(bf16[96,2304]{1,0:T(8,128)(2,1)S(1)} %slice.107), channel_id=1, source_target_pairs={{0,3},{1,0},{2,1},{3,2},{4,7},{5,4},{6,5},{7,6},{8,11},{9,8},{10,9... | collective-permute-start | bytes 1327112 | tf_op jit(solution)/shard_map/ppermute | solution.py:313
  200.3 27.4 %collective-permute-start.40 = (bf16[64,3072]{1,0:T(8,128)(2,1)S(1)}, bf16[64,3072]{1,0:T(8,128)(2,1)S(1)}, u32[]{:S(2)}, u32[]{:S(2)}) collective-permute-start(bf16[64,3072]{1,0:T(8,128)(2,1)S(1)} %get-tuple-element.410), channel_id=1, source_target_pairs={{64,80},{65,81},{66,82},{67,83},{68,84},{69,85},{70,86},{71,87},{7... | collective-permute-start | bytes 1179656 | tf_op jit(solution)/shard_map/ppermute | solution.py:188
  201.0 27.3 %collective-permute-start.38 = (bf16[64,3072]{1,0:T(8,128)(2,1)S(1)}, bf16[64,3072]{1,0:T(8,128)(2,1)S(1)}, u32[]{:S(2)}, u32[]{:S(2)}) collective-permute-start(bf16[64,3072]{1,0:T(8,128)(2,1)S(1)} %get-tuple-element.404), channel_id=1, source_target_pairs={{48,64},{49,65},{50,66},{51,67},{52,68},{53,69},{54,70},{55,71},{5... | collective-permute-start | bytes 1179656 | tf_op jit(solution)/shard_map/ppermute | solution.py:188
  201.7 29.7 %collective-permute-start.37 = (bf16[64,3072]{1,0:T(8,128)(2,1)S(1)}, bf16[64,3072]{1,0:T(8,128)(2,1)S(1)}, u32[]{:S(2)}, u32[]{:S(2)}) collective-permute-start(bf16[64,3072]{1,0:T(8,128)(2,1)S(1)} %get-tuple-element.400), channel_id=1, source_target_pairs={{80,96},{81,97},{82,98},{83,99},{84,100},{85,101},{86,102},{87,103... | collective-permute-start | bytes 1179656 | tf_op jit(solution)/shard_map/ppermute | solution.py:188
  244.5 17.5 %collective-permute-start.46 = (bf16[64,3072]{1,0:T(8,128)(2,1)S(1)}, bf16[64,3072]{1,0:T(8,128)(2,1)S(1)}, u32[]{:S(2)}, u32[]{:S(2)}) collective-permute-start(bf16[64,3072]{1,0:T(8,128)(2,1)S(1)} %get-tuple-element.434), channel_id=1, source_target_pairs={{96,112},{97,113},{98,114},{99,115},{100,116},{101,117},{102,118},... | collective-permute-start | bytes 1179656 | tf_op jit(solution)/shard_map/ppermute | solution.py:188
  246.4 17.1 %collective-permute-start.44 = (bf16[64,3072]{1,0:T(8,128)(2,1)}, bf16[64,3072]{1,0:T(8,128)(2,1)S(1)}, u32[]{:S(2)}, u32[]{:S(2)}) collective-permute-start(bf16[64,3072]{1,0:T(8,128)(2,1)} %get-tuple-element.428), channel_id=1, source_target_pairs={{80,96},{81,97},{82,98},{83,99},{84,100},{85,101},{86,102},{87,103... | collective-permute-start | bytes 1179656 | tf_op jit(solution)/shard_map/ppermute | solution.py:188
  248.9 17.6 %collective-permute-start.43 = (bf16[64,3072]{1,0:T(8,128)(2,1)}, bf16[64,3072]{1,0:T(8,128)(2,1)S(1)}, u32[]{:S(2)}, u32[]{:S(2)}) collective-permute-start(bf16[64,3072]{1,0:T(8,128)(2,1)} %get-tuple-element.424), channel_id=1, source_target_pairs={{112,140},{113,141},{114,142},{115,143},{116,136},{117,137},{118,1... | collective-permute-start | bytes 1179656 | tf_op jit(solution)/shard_map/ppermute | solution.py:188
  307.7 109.6 %collective-permute-start.64 = (bf16[64,3072]{1,0:T(8,128)(2,1)S(1)}, bf16[64,3072]{1,0:T(8,128)(2,1)S(1)}, u32[]{:S(2)}, u32[]{:S(2)}) collective-permute-start(bf16[64,3072]{1,0:T(8,128)(2,1)S(1)} %get-tuple-element.506), channel_id=1, source_target_pairs={{64,80},{65,81},{66,82},{67,83},{68,84},{69,85},{70,86},{71,87},{7... | collective-permute-start | bytes 1179656 | tf_op jit(solution)/shard_map/ppermute | solution.py:188
  308.4 109.7 %collective-permute-start.62 = (bf16[64,3072]{1,0:T(8,128)(2,1)S(1)}, bf16[64,3072]{1,0:T(8,128)(2,1)S(1)}, u32[]{:S(2)}, u32[]{:S(2)}) collective-permute-start(bf16[64,3072]{1,0:T(8,128)(2,1)S(1)} %get-tuple-element.500), channel_id=1, source_target_pairs={{48,64},{49,65},{50,66},{51,67},{52,68},{53,69},{54,70},{55,71},{5... | collective-permute-start | bytes 1179656 | tf_op jit(solution)/shard_map/ppermute | solution.py:188
  309.1 111.9 %collective-permute-start.61 = (bf16[64,3072]{1,0:T(8,128)(2,1)S(1)}, bf16[64,3072]{1,0:T(8,128)(2,1)S(1)}, u32[]{:S(2)}, u32[]{:S(2)}) collective-permute-start(bf16[64,3072]{1,0:T(8,128)(2,1)S(1)} %get-tuple-element.496), channel_id=1, source_target_pairs={{80,96},{81,97},{82,98},{83,99},{84,100},{85,101},{86,102},{87,103... | collective-permute-start | bytes 1179656 | tf_op jit(solution)/shard_map/ppermute | solution.py:188
  418.7 13.5 %collective-permute-start.66 = (bf16[64,3072]{1,0:T(8,128)(2,1)S(1)}, bf16[64,3072]{1,0:T(8,128)(2,1)S(1)}, u32[]{:S(2)}, u32[]{:S(2)}) collective-permute-start(bf16[64,3072]{1,0:T(8,128)(2,1)S(1)} %get-tuple-element.516), channel_id=1, source_target_pairs={{64,80},{65,81},{66,82},{67,83},{68,84},{69,85},{70,86},{71,87},{7... | collective-permute-start | bytes 1179656 | tf_op jit(solution)/shard_map/ppermute | solution.py:188
  468.9 26.9 %collective-permute-start.74 = (bf16[3,64,3072]{2,1,0:T(8,128)(2,1)S(1)}, bf16[3,64,3072]{2,1,0:T(8,128)(2,1)S(1)}, u32[]{:S(2)}, u32[]{:S(2)}) collective-permute-start(bf16[3,64,3072]{2,1,0:T(8,128)(2,1)S(1)} %copy-done.74), channel_id=1, source_target_pairs={{0,12},{1,13},{2,14},{3,15},{4,8},{5,9},{6,10},{7,11},{8,4},{9,5},... | collective-permute-start | bytes 3538952 | tf_op jit(solution)/shard_map/ppermute | solution.py:380
  471.3 24.5 %collective-permute-start.77 = (bf16[4,192,768]{2,1,0:T(8,128)(2,1)S(1)}, bf16[4,192,768]{2,1,0:T(8,128)(2,1)S(1)}, u32[]{:S(2)}, u32[]{:S(2)}) collective-permute-start(bf16[4,192,768]{2,1,0:T(8,128)(2,1)S(1)} %collective-permute-done.76), channel_id=1, source_target_pairs={{0,8},{1,9},{2,10},{3,11},{4,0},{5,1},{6,2},{7,3},{8,12},{9,13},{1... | collective-permute-start | bytes 3538952 | tf_op jit(solution)/shard_map/ppermute | solution.py:295
  541.6 14.4 %collective-permute-start.82 = (bf16[64,3072]{1,0:T(8,128)(2,1)S(1)}, bf16[64,3072]{1,0:T(8,128)(2,1)S(1)}, u32[]{:S(2)}, u32[]{:S(2)}) collective-permute-start(bf16[64,3072]{1,0:T(8,128)(2,1)S(1)} %get-tuple-element.562), channel_id=1, source_target_pairs={{80,96},{81,97},{82,98},{83,99},{84,100},{85,101},{86,102},{87,103... | collective-permute-start | bytes 1179656 | tf_op jit(solution)/shard_map/ppermute | solution.py:188
  600.5 20.3 %collective-permute-start.104 = (bf16[64,3072]{1,0:T(8,128)(2,1)S(1)}, bf16[64,3072]{1,0:T(8,128)(2,1)S(1)}, u32[]{:S(2)}, u32[]{:S(2)}) collective-permute-start(bf16[64,3072]{1,0:T(8,128)(2,1)S(1)} %get-tuple-element.628), channel_id=1, source_target_pairs={{96,112},{97,113},{98,114},{99,115},{100,116},{101,117},{102,118},... | collective-permute-start | bytes 1179656 | tf_op jit(solution)/shard_map/ppermute | solution.py:188
  603.4 18.1 %collective-permute-start.108 = (bf16[64,3072]{1,0:T(8,128)(2,1)S(1)}, bf16[64,3072]{1,0:T(8,128)(2,1)S(1)}, u32[]{:S(2)}, u32[]{:S(2)}) collective-permute-start(bf16[64,3072]{1,0:T(8,128)(2,1)S(1)} %get-tuple-element.639), channel_id=1, source_target_pairs={{64,80},{65,81},{66,82},{67,83},{68,84},{69,85},{70,86},{71,87},{7... | collective-permute-start | bytes 1179656 | tf_op jit(solution)/shard_map/ppermute | solution.py:188
  604.1 22.2 %collective-permute-start.107 = (bf16[64,3072]{1,0:T(8,128)(2,1)S(1)}, bf16[64,3072]{1,0:T(8,128)(2,1)S(1)}, u32[]{:S(2)}, u32[]{:S(2)}) collective-permute-start(bf16[64,3072]{1,0:T(8,128)(2,1)S(1)} %get-tuple-element.637), channel_id=1, source_target_pairs={{80,96},{81,97},{82,98},{83,99},{84,100},{85,101},{86,102},{87,103... | collective-permute-start | bytes 1179656 | tf_op jit(solution)/shard_map/ppermute | solution.py:188
  647.3 17.6 %collective-permute-start.117 = (bf16[64,3072]{1,0:T(8,128)(2,1)}, bf16[64,3072]{1,0:T(8,128)(2,1)}, u32[]{:S(2)}, u32[]{:S(2)}) collective-permute-start(bf16[64,3072]{1,0:T(8,128)(2,1)} %get-tuple-element.667), channel_id=1, source_target_pairs={{16,32},{17,33},{18,34},{19,35},{20,36},{21,37},{22,38},{23,39},{2... | collective-permute-start | bytes 1179656 | tf_op jit(solution)/shard_map/ppermute | solution.py:188
  663.3 22.7 %collective-permute-start.116 = (bf16[64,3072]{1,0:T(8,128)(2,1)}, bf16[64,3072]{1,0:T(8,128)(2,1)}, u32[]{:S(2)}, u32[]{:S(2)}) collective-permute-start(bf16[64,3072]{1,0:T(8,128)(2,1)} %get-tuple-element.664), channel_id=1, source_target_pairs={{32,48},{33,49},{34,50},{35,51},{36,52},{37,53},{38,54},{39,55},{4... | collective-permute-start | bytes 1179656 | tf_op jit(solution)/shard_map/ppermute | solution.py:188
  667.2 26.4 %collective-permute-start.120 = (bf16[64,3072]{1,0:T(8,128)(2,1)}, bf16[64,3072]{1,0:T(8,128)(2,1)}, u32[]{:S(2)}, u32[]{:S(2)}) collective-permute-start(bf16[64,3072]{1,0:T(8,128)(2,1)} %get-tuple-element.675), channel_id=1, source_target_pairs={{0,16},{1,17},{2,18},{3,19},{4,20},{5,21},{6,22},{7,23},{8,24},{9,... | collective-permute-start | bytes 1179656 | tf_op jit(solution)/shard_map/ppermute | solution.py:188
  668.7 33.5 %collective-permute-start.119 = (bf16[64,3072]{1,0:T(8,128)(2,1)}, bf16[64,3072]{1,0:T(8,128)(2,1)}, u32[]{:S(2)}, u32[]{:S(2)}) collective-permute-start(bf16[64,3072]{1,0:T(8,128)(2,1)} %get-tuple-element.673), channel_id=1, source_target_pairs={{16,32},{17,33},{18,34},{19,35},{20,36},{21,37},{22,38},{23,39},{2... | collective-permute-start | bytes 1179656 | tf_op jit(solution)/shard_map/ppermute | solution.py:188
  683.7 33.8 %collective-permute-start.145 = (bf16[192,3072]{1,0:T(8,128)(2,1)S(1)}, bf16[192,3072]{1,0:T(8,128)(2,1)S(1)}, u32[]{:S(2)}, u32[]{:S(2)}) collective-permute-start(bf16[192,3072]{1,0:T(8,128)(2,1)S(1)} %pad_maximum_fusion.2), channel_id=1, source_target_pairs={{0,12},{1,13},{2,14},{3,15},{4,8},{5,9},{6,10},{7,11},{8,4},{9,5},... | collective-permute-start | bytes 3538952 | tf_op jit(solution)/shard_map/ppermute | solution.py:432
  717.7 217.6 %collective-permute-start.146 = (bf16[384,1536]{1,0:T(8,128)(2,1)S(1)}, bf16[384,1536]{1,0:T(8,128)(2,1)S(1)}, u32[]{:S(2)}, u32[]{:S(2)}) collective-permute-start(bf16[384,1536]{1,0:T(8,128)(2,1)S(1)} %broadcast_select_fusion), channel_id=1, source_target_pairs={{0,128},{16,144},{32,160},{48,176},{64,192},{80,208},{96,224},{112... | collective-permute-start | bytes 3538952 | tf_op jit(solution)/shard_map/ppermute | solution.py:205
  796.0 97.0 %collective-permute-start.139 = (f32[1,3072]{1,0:T(1,128)S(1)}, f32[1,3072]{1,0:T(1,128)S(1)}, u32[]{:S(2)}, u32[]{:S(2)}) collective-permute-start(f32[1,3072]{1,0:T(1,128)S(1)} %add_add_fusion.2), channel_id=1, source_target_pairs={{0,1},{1,2},{2,3},{3,0},{4,5},{5,6},{6,7},{7,4},{8,9},{9,10},{10,1... | collective-permute-start | bytes 36872 | tf_op jit(solution)/shard_map/ppermute | solution.py:313
  814.5 80.4 %collective-permute-start.140 = (f32[1,3072]{1,0:T(1,128)S(1)}, f32[1,3072]{1,0:T(1,128)S(1)}, u32[]{:S(2)}, u32[]{:S(2)}) collective-permute-start(f32[1,3072]{1,0:T(1,128)S(1)} %add_add_fusion.2), channel_id=1, source_target_pairs={{0,2},{1,3},{2,0},{3,1},{4,6},{5,7},{6,4},{7,5},{8,10},{9,11},{10,... | collective-permute-start | bytes 36872 | tf_op jit(solution)/shard_map/ppermute | solution.py:313
  814.5 80.4 %collective-permute-start.141 = (f32[1,3072]{1,0:T(1,128)S(1)}, f32[1,3072]{1,0:T(1,128)S(1)}, u32[]{:S(2)}, u32[]{:S(2)}) collective-permute-start(f32[1,3072]{1,0:T(1,128)S(1)} %add_add_fusion.2), channel_id=1, source_target_pairs={{0,3},{1,0},{2,1},{3,2},{4,7},{5,4},{6,5},{7,6},{8,11},{9,8},{10,9... | collective-permute-start | bytes 36872 | tf_op jit(solution)/shard_map/ppermute | solution.py:313
  817.3 82.5 %collective-permute-start.129 = (bf16[192,768]{1,0:T(8,128)(2,1)S(1)}, bf16[192,768]{1,0:T(8,128)(2,1)S(1)}, u32[]{:S(2)}, u32[]{:S(2)}) collective-permute-start(bf16[192,768]{1,0:T(8,128)(2,1)S(1)} %get-tuple-element.709), channel_id=1, source_target_pairs={{0,8},{1,9},{2,10},{3,11},{4,0},{5,1},{6,2},{7,3},{8,12},{9,13},{1... | collective-permute-start | bytes 884744 | tf_op jit(solution)/shard_map/ppermute | solution.py:308
  894.9 40.3 %collective-permute-start.131 = (bf16[192,768]{1,0:T(8,128)(2,1)S(1)}, bf16[192,768]{1,0:T(8,128)(2,1)S(1)}, u32[]{:S(2)}, u32[]{:S(2)}) collective-permute-start(bf16[192,768]{1,0:T(8,128)(2,1)S(1)} %get-tuple-element.707), channel_id=1, source_target_pairs={{0,4},{1,5},{2,6},{3,7},{4,12},{5,13},{6,14},{7,15},{8,0},{9,1},{1... | collective-permute-start | bytes 884744 | tf_op jit(solution)/shard_map/ppermute | solution.py:308
  894.9 82.5 %collective-permute-start.126 = (bf16[4,192,768]{2,1,0:T(8,128)(2,1)}, bf16[4,192,768]{2,1,0:T(8,128)(2,1)S(1)}, u32[]{:S(2)}, u32[]{:S(2)}) collective-permute-start(bf16[4,192,768]{2,1,0:T(8,128)(2,1)} %shard_map.194), channel_id=1, source_target_pairs={{160,168},{161,169},{162,170},{163,171},{164,160},{165,161},{166,1... | collective-permute-start | bytes 3538952 | tf_op jit(solution)/shard_map/ppermute | solution.py:295
  899.8 40.1 %collective-permute-start.142 = (f32[1,3072]{1,0:T(1,128)S(1)}, f32[1,3072]{1,0:T(1,128)S(1)}, u32[]{:S(2)}, u32[]{:S(2)}) collective-permute-start(f32[1,3072]{1,0:T(1,128)S(1)} %add_add_fusion.1), channel_id=1, source_target_pairs={{0,8},{1,9},{2,10},{3,11},{4,0},{5,1},{6,2},{7,3},{8,12},{9,13},{1... | collective-permute-start | bytes 36872 | tf_op jit(solution)/shard_map/ppermute | solution.py:308
  905.0 35.2 %collective-permute-start.143 = (f32[1,3072]{1,0:T(1,128)S(1)}, f32[1,3072]{1,0:T(1,128)S(1)}, u32[]{:S(2)}, u32[]{:S(2)}) collective-permute-start(f32[1,3072]{1,0:T(1,128)S(1)} %add_add_fusion.1), channel_id=1, source_target_pairs={{0,12},{1,13},{2,14},{3,15},{4,8},{5,9},{6,10},{7,11},{8,4},{9,5},... | collective-permute-start | bytes 36872 | tf_op jit(solution)/shard_map/ppermute | solution.py:308
  935.2 47.0 %collective-permute-start.144 = (f32[1,3072]{1,0:T(1,128)S(1)}, f32[1,3072]{1,0:T(1,128)S(1)}, u32[]{:S(2)}, u32[]{:S(2)}) collective-permute-start(f32[1,3072]{1,0:T(1,128)S(1)} %add_add_fusion.1), channel_id=1, source_target_pairs={{0,4},{1,5},{2,6},{3,7},{4,12},{5,13},{6,14},{7,15},{8,0},{9,1},{1... | collective-permute-start | bytes 36872 | tf_op jit(solution)/shard_map/ppermute | solution.py:308
  935.3 47.7 %collective-permute-start.132 = (bf16[768,768]{1,0:T(8,128)(2,1)S(1)}, bf16[768,768]{1,0:T(8,128)(2,1)S(1)}, u32[]{:S(2)}, u32[]{:S(2)}) collective-permute-start(bf16[768,768]{1,0:T(8,128)(2,1)S(1)} %pad_maximum_fusion), channel_id=1, source_target_pairs={{0,1},{1,2},{2,3},{3,0},{4,5},{5,6},{6,7},{7,4},{8,9},{9,10},{10,1... | collective-permute-start | bytes 3538952 | tf_op jit(solution)/shard_map/ppermute | solution.py:313
  939.9 45.3 %collective-permute-start.134 = (bf16[768,768]{1,0:T(8,128)(2,1)S(1)}, bf16[768,768]{1,0:T(8,128)(2,1)S(1)}, u32[]{:S(2)}, u32[]{:S(2)}) collective-permute-start(bf16[768,768]{1,0:T(8,128)(2,1)S(1)} %pad_maximum_fusion), channel_id=1, source_target_pairs={{0,3},{1,0},{2,1},{3,2},{4,7},{5,4},{6,5},{7,6},{8,11},{9,8},{10,9... | collective-permute-start | bytes 3538952 | tf_op jit(solution)/shard_map/ppermute | solution.py:313
  940.2 49.1 %collective-permute-start.147 = (bf16[384,768]{1,0:T(8,128)(2,1)S(1)}, bf16[384,768]{1,0:T(8,128)(2,1)S(1)}, u32[]{:S(2)}, u32[]{:S(2)}) collective-permute-start(bf16[384,768]{1,0:T(8,128)(2,1)S(1)} %broadcast_select_fusion.1), channel_id=1, source_target_pairs={{0,64},{16,80},{32,96},{48,112},{64,0},{80,16},{96,32},{112,48},{1... | collective-permute-start | bytes 1769480 | tf_op jit(solution)/shard_map/ppermute | solution.py:205
  977.4 28.5 %collective-permute-start.127 = (bf16[4,192,768]{2,1,0:T(8,128)(2,1)S(1)}, bf16[4,192,768]{2,1,0:T(8,128)(2,1)S(1)}, u32[]{:S(2)}, u32[]{:S(2)}) collective-permute-start(bf16[4,192,768]{2,1,0:T(8,128)(2,1)S(1)} %collective-permute-done.126), channel_id=1, source_target_pairs={{160,168},{161,169},{162,170},{163,171},{164,160},{165,161},{166,1... | collective-permute-start | bytes 3538952 | tf_op jit(solution)/shard_map/ppermute | solution.py:295
  983.0 27.1 %collective-permute-start.133 = (bf16[384,768]{1,0:T(8,128)(2,1)S(1)}, bf16[384,768]{1,0:T(8,128)(2,1)S(1)}, u32[]{:S(2)}, u32[]{:S(2)}) collective-permute-start(bf16[384,768]{1,0:T(8,128)(2,1)S(1)} %slice.108), channel_id=1, source_target_pairs={{0,1},{1,2},{2,3},{3,0},{4,5},{5,6},{6,7},{7,4},{8,9},{9,10},{10,1... | collective-permute-start | bytes 1769480 | tf_op jit(solution)/shard_map/ppermute | solution.py:313
  985.2 25.0 %collective-permute-start.135 = (bf16[384,768]{1,0:T(8,128)(2,1)S(1)}, bf16[384,768]{1,0:T(8,128)(2,1)S(1)}, u32[]{:S(2)}, u32[]{:S(2)}) collective-permute-start(bf16[384,768]{1,0:T(8,128)(2,1)S(1)} %slice.109), channel_id=1, source_target_pairs={{0,3},{1,0},{2,1},{3,2},{4,7},{5,4},{6,5},{7,6},{8,11},{9,8},{10,9... | collective-permute-start | bytes 1769480 | tf_op jit(solution)/shard_map/ppermute | solution.py:313
  989.5 20.3 %collective-permute-start.148 = (bf16[384,384]{1,0:T(8,128)(2,1)S(1)}, bf16[384,384]{1,0:T(8,128)(2,1)S(1)}, u32[]{:S(2)}, u32[]{:S(2)}) collective-permute-start(bf16[384,384]{1,0:T(8,128)(2,1)S(1)} %broadcast_select_fusion.2), channel_id=1, source_target_pairs={{0,32},{16,48},{32,0},{48,16},{64,96},{80,112},{96,64},{112,80},{1... | collective-permute-start | bytes 884744 | tf_op jit(solution)/shard_map/ppermute | solution.py:205
  1005.8 27.3 %collective-permute-start.128 = (bf16[4,192,768]{2,1,0:T(8,128)(2,1)S(1)}, bf16[4,192,768]{2,1,0:T(8,128)(2,1)S(1)}, u32[]{:S(2)}, u32[]{:S(2)}) collective-permute-start(bf16[4,192,768]{2,1,0:T(8,128)(2,1)S(1)} %collective-permute-done.127), channel_id=1, source_target_pairs={{160,168},{161,169},{162,170},{163,171},{164,160},{165,161},{166,1... | collective-permute-start | bytes 3538952 | tf_op jit(solution)/shard_map/ppermute | solution.py:295
  1010.1 28.7 %collective-permute-start.149 = (bf16[384,192]{1,0:T(8,128)(2,1)S(1)}, bf16[384,192]{1,0:T(8,128)(2,1)S(1)}, u32[]{:S(2)}, u32[]{:S(2)}) collective-permute-start(bf16[384,192]{1,0:T(8,128)(2,1)S(1)} %broadcast_select_fusion.3), channel_id=1, source_target_pairs={{0,16},{16,0},{32,48},{48,32},{64,80},{80,64},{96,112},{112,96},{1... | collective-permute-start | bytes 442376 | tf_op jit(solution)/shard_map/ppermute | solution.py:205
  1039.0 15.9 %collective-permute-start.137 = (bf16[192,768]{1,0:T(8,128)(2,1)S(1)}, bf16[192,768]{1,0:T(8,128)(2,1)S(1)}, u32[]{:S(2)}, u32[]{:S(2)}) collective-permute-start(bf16[192,768]{1,0:T(8,128)(2,1)S(1)} %get-tuple-element.703), channel_id=1, source_target_pairs={{0,12},{1,13},{2,14},{3,15},{4,8},{5,9},{6,10},{7,11},{8,4},{9,5},... | collective-permute-start | bytes 884744 | tf_op jit(solution)/shard_map/ppermute | solution.py:308
  1043.7 20.0 %collective-permute-start.138 = (bf16[192,768]{1,0:T(8,128)(2,1)S(1)}, bf16[192,768]{1,0:T(8,128)(2,1)S(1)}, u32[]{:S(2)}, u32[]{:S(2)}) collective-permute-start(bf16[192,768]{1,0:T(8,128)(2,1)S(1)} %get-tuple-element.702), channel_id=1, source_target_pairs={{0,4},{1,5},{2,6},{3,7},{4,12},{5,13},{6,14},{7,15},{8,0},{9,1},{1... | collective-permute-start | bytes 884744 | tf_op jit(solution)/shard_map/ppermute | solution.py:308
  (181 other events, 2732.1 us)

commit v5 on v4

--- a/solution.py
+++ b/solution.py
@@ -19,7 +19,8 @@
 SMEM = pl.BlockSpec(memory_space=pltpu.SMEM)
 TILE = 512
 LIMIT = 8 * 1024 * 1024
-EARLY = 10
+EARLY = 8
+MICROS = 2
 
 
 def call(kernel, outs, in_specs, out_specs, aliases, scratch, operands):
@@ -119,7 +120,7 @@
     return call(
         functools.partial(forward_kernel, t, m if x.ndim == 3 else None),
         (pltpu.VMEM(shape, BF), wide, wide, deep),
-        [SMEM] + [VMEM] * 3 + [HBM] * (len(kept) + len(after[:1])) + [VMEM] * len(after[1:]),
+        [SMEM] + [VMEM] * 3 + [HBM] * len(kept) + [VMEM] * len(after),
         (VMEM, HBM, HBM, HBM),
         {4 + i: 1 + i for i in range(len(kept))},
         [
@@ -174,27 +175,21 @@
     )
 
 
-def mirrored(index, count):
-    return count - 4 - index // 4 * 4 + index % 4
-
-
 def hop(block, lower, half, count):
+    if lower % half == half - 1:
+        lowers = [lower]
+    else:
+        lowers = [t for t in range(2 * half) if t % 4 == lower % 4 and t % half != half - 1]
     pairs = []
-    for t in [lower] if lower == half - 1 else [lower % half, lower % half + half]:
+    for t in lowers:
         for i in range(count):
-            j = mirrored(i, count) if t == half - 1 else i
-            near, far = t * count + i, (t + 1) * count + j
+            near, far = t * count + i, (t + 1) * count + i
             pairs += [(near, far), (far, near)]
     return lax.ppermute(block, ("section", "dp"), sorted(pairs))
 
 
-def order(sections, micros):
-    steps = [(t, m) for t in range(sections) for m in range(micros)]
-    return sorted(steps, key=lambda p: (37 * (p[0] // 2) + 14 * (p[0] % 2) + 16 * p[1]))
-
-
-def spread(first, last, sections, section):
-    block, rows = jnp.concatenate([first, last], axis=0), first.shape[0]
+def spread(block, sections, section):
+    rows = block.shape[0] // 2
     owned = lax.broadcasted_iota(jnp.int32, (2 * rows, 1), 0) >= rows
     bit = sections // 2
     while bit:
@@ -209,14 +204,14 @@
 
 
 def cut_kernel(low, high, here, *refs):
-    first, second, third, *out, whole, cut, sems = refs
+    parts, (*out, whole, cut, sems) = refs[:MICROS], refs[-7:]
 
     @pl.when((here[0] >= low) & (here[0] < high))
     def _():
-        rows = first.shape[0]
+        rows = parts[0].shape[0]
         loads = [
             pltpu.make_async_copy(part, whole.at[pl.ds(i * rows, rows), :], sems.at[i])
-            for i, part in enumerate((first, second, third))
+            for i, part in enumerate(parts)
         ]
         for load in loads:
             load.start()
@@ -239,12 +234,12 @@
             store.wait()
 
 
-def cut_columns(parts, here, low, high):
-    rows, features = 3 * parts[0].shape[0], parts[0].shape[1]
+def cut_columns(parts, here, low, high, after):
+    rows, features = MICROS * parts[0].shape[0], parts[0].shape[1]
     return call(
         functools.partial(cut_kernel, low, high),
         tuple(pltpu.HBM((rows, features // 4), BF) for _ in range(4)),
-        [SMEM] + [HBM] * 3,
+        [SMEM] + [HBM] * (MICROS + len(after)),
         (HBM,) * 4,
         {},
         [
@@ -252,8 +247,18 @@
             pltpu.VMEM((4, rows, features // 4), BF),
             pltpu.SemaphoreType.DMA((4,)),
         ],
-        [here, *(in_hbm(part) for part in parts)],
-    )
+        [here, *(in_hbm(part) for part in (*parts, *after))],
+    )
+
+
+def echo_kernel(here, _after, out):
+    out[0] = here[0]
+    out[1] = here[1]
+
+
+def echo(here, after):
+    shape = jax.ShapeDtypeStruct(here.shape, here.dtype)
+    return call(echo_kernel, shape, [SMEM, HBM], SMEM, {}, [], [here, in_hbm(after)])
 
 
 def pile_kernel(low, high, here, *refs):
@@ -282,9 +287,9 @@
     )
 
 
-def exchange(parts, here, low, high, count):
+def exchange(parts, here, low, high, count, after=()):
     sections = range(low, high)
-    cut = cut_columns(parts, here, low, high)
+    cut = cut_columns(parts, here, low, high, after)
     pieces = [cut[0]]
     for k in (1, 2, 3):
         pairs = [(s * count + i, s * count + i // 4 * 4 + (i + k) % 4) for s in sections for i in range(count)]
@@ -369,42 +374,41 @@
     behind = jnp.asarray([[z_after(i, -k) for i in range(4)] for k in range(4)], jnp.int32)
     to_z = [ahead[k, z] for k in range(4)]
     from_z = [behind[k, z] for k in range(4)]
-    micros, rows, features = inputs.shape
+    *batches, features = inputs.shape
+    micros, rows = MICROS, batches[0] * batches[1] // MICROS
+    inputs = inputs.reshape(micros, rows, features)
+    cotangent = cotangent.reshape(micros, rows, features)
     here = jnp.stack([section, y]).astype(jnp.int32)
     gain_row = lax.dynamic_index_in_dim(gain, section, 0, keepdims=True)
-    across = [(i, mirrored(i, count)) for i in range(count)]
     row_of = jnp.stack([from_z[k] * 4 + (y - j) % 4 for k in range(4) for j in range(4)])
     row_of = (row_of * weight.shape[1]).astype(jnp.int32)
     matrix = hold(gather(weight[0], count), row_of, (features, features))
-    cotangent, matrix = lax.optimization_barrier((cotangent, matrix))
-    upstream = lax.ppermute(cotangent, "dp", across)
+    upstream = cotangent
 
     kept = [()] * micros
     current = [inputs] * micros
-    after = ()
-    turned = None
-    for t, m in order(sections, micros):
-        if t == half and turned is None:
+    for t in range(sections):
+        after = ()
+        if t == half:
             turned = turn(matrix)
-            after += (turned,)
-        result, *kept[m] = forward(t, m, here, current[m], gain_row, matrix, kept[m], after)
-        after = (in_hbm(kept[m][0]),)
-        current[m] = hop(result, t, half, count) if t + 1 < sections else result
-
+            after = (turned,)
+        for m in range(micros):
+            result, *kept[m] = forward(t, m, here, current[m], gain_row, matrix, kept[m], after)
+            current[m] = hop(result, t, half, count) if t + 1 < sections else result
+
+    normed = [kept[m][1] for m in range(micros)]
+    early = exchange(normed, here, 0, EARLY, count)
     passed = [()] * micros
     arriving = [upstream] * micros
-    normed = [kept[m][1] for m in range(micros)]
-    early = exchange(normed, here, 0, EARLY, count)
-    after += (in_hbm(early[-1]),)
-    for step, m in order(sections, micros):
-        t = sections - 1 - step
-        result, *passed[m] = backward(
-            t, m, here, arriving[m], kept[m][0], kept[m][2], gain_row, turned, passed[m], after
-        )
-        after = (in_hbm(passed[m][0]),)
-        arriving[m] = hop(result, t - 1, half, count) if t else result
-    held = lax.optimization_barrier((*normed, after[0]))
-    late = exchange(held[:micros], here, EARLY, sections, count)
+    for t in reversed(range(sections)):
+        after = (in_hbm(early[-1]),) if t == sections - 1 else ()
+        for m in range(micros):
+            result, *passed[m] = backward(
+                t, m, here, arriving[m], kept[m][0], kept[m][2], gain_row, turned, passed[m], after
+            )
+            arriving[m] = hop(result, t - 1, half, count) if t else result
+    ended = [passed[m][0] for m in range(micros)]
+    late = exchange(normed, here, EARLY, sections, count, ended)
     normed = [jnp.where(section < EARLY, a, b) for a, b in zip(early, late)]
 
     slope = jnp.concatenate([passed[m][0] for m in range(micros)], axis=0)
@@ -429,9 +433,9 @@
     total = sum(passed[m][1] for m in range(micros))
     total = total + (shift_y(total, 1, count) + shift_y(total, 2, count) + shift_y(total, 3, count))
     total = total + (shift_z(total, 1, count) + shift_z(total, 2, count) + shift_z(total, 3, count))
-    last = lax.ppermute(jnp.concatenate(current, axis=0), "dp", across)
-    first_share, final_share = spread(jnp.concatenate(arriving, axis=0), last, sections, section)
-    shape = (micros, rows, features // sections)
+    ends = pile((*arriving, *current), here, 0, sections).reshape(-1, features)
+    first_share, final_share = spread(ends, sections, echo(here, ended[-1])[0])
+    shape = (*batches, features // sections)
     return (
         weight_grad[None],
         total,

time: 1080 us -> 998 us (0.924)
  the two profiles are of different devices: /device:TPU:134 before, /device:TPU:128 now
where the time goes in v5:
time: 998 us; the launch traced here: 987 us
  starting transfers between devices  512 us (51%)
  Pallas kernels  221 us (22%)
  waiting for transfers between devices  193 us (19%)
  local copies, waits for them, and re-layouts  33.8 us (3%)
  between operations  18.4 us (2%)
    ppermute x60, starting transfers between devices, hop(): return lax.ppermute(block, ('section', 'dp'), sorted(pairs))  317 us
    pallas_call x72, Pallas kernels, call(): pl.pallas_call(kernel, out_shape=outs, in_specs=in_specs, out_specs=out_s...  221 us
    ppermute x15, waiting for transfers between devices, shift_z(): return lax.ppermute(block, 'dp', pairs)  98.4 us
    ppermute x15, starting transfers between devices, shift_z(): return lax.ppermute(block, 'dp', pairs)  65.8 us
    ppermute x4, starting transfers between devices, spread(): arrived = lax.ppermute(jnp.where(upper, low, high), 'section', pairs)  57.2 us
    ppermute x27, waiting for transfers between devices, shift_y(): return lax.ppermute(block, 'dp', pairs)  55.4 us
    ppermute x27, starting transfers between devices, shift_y(): return lax.ppermute(block, 'dp', pairs)  48.5 us
    unnamed x132, local copies, waits for them, and re-layouts  23.9 us
  transfers between devices with their start and end apart: 118, of which 36 were waited for; matrix products, arithmetic and copies ran while one was open for 2% of the time, Pallas kernels for 14%

profile of v5, /device:TPU:128, one launch (start us, length us, event | category | flops | bytes accessed | tf_op | source)
XLA Modules:
  0.0 987.0 jit_solution(11121877540649232643)
XLA Ops:
  7.8 6.5 collective-permute-done.4
  18.1 4.3 collective-permute-done.5
  26.0 3.0 collective-permute-start.1
  29.0 17.0 %collective-permute-done.14.refs_12_ = bf16[192,2304]{1,0:T(8,128)(2,1)S(1)} collective-permute-done((bf16[192,2304]{1,0:T(8,128)(2,1)S(1)}, bf16[192,2304]{1,0:T(8,128)(2,1)S(1)}, u32[]{:S(2)}, u32[]{:S(2)}) %collective-permute-start.14) | collective-permute-done | bytes 884768 | tf_op jit(solution)/shard_map/ppermute | solution.py:313
  46.0 3.3 collective-permute-start.20
  49.3 3.0 collective-permute-start.10
  52.3 19.0 %collective-permute-done.13.refs_11_ = bf16[768,768]{1,0:T(8,128)(2,1)S(1)} collective-permute-done((bf16[768,768]{1,0:T(8,128)(2,1)S(1)}, bf16[768,768]{1,0:T(8,128)(2,1)S(1)}, u32[]{:S(2)}, u32[]{:S(2)}) %collective-permute-start.13) | collective-permute-done | bytes 1179680 | tf_op jit(solution)/shard_map/ppermute | solution.py:313
  71.3 3.3 collective-permute-start.19
  77.8 12.4 %collective-permute-done.20.refs_18_ = bf16[192,2304]{1,0:T(8,128)(2,1)S(1)} collective-permute-done((bf16[192,2304]{1,0:T(8,128)(2,1)S(1)}, bf16[192,2304]{1,0:T(8,128)(2,1)S(1)}, u32[]{:S(2)}, u32[]{:S(2)}) %collective-permute-start.20) | collective-permute-done | bytes 884768 | tf_op jit(solution)/shard_map/ppermute | solution.py:313
  93.7 20.0 %collective-permute-done.19.refs_17_ = bf16[768,768]{1,0:T(8,128)(2,1)} collective-permute-done((bf16[768,768]{1,0:T(8,128)(2,1)S(1)}, bf16[768,768]{1,0:T(8,128)(2,1)}, u32[]{:S(2)}, u32[]{:S(2)}) %collective-permute-start.19) | collective-permute-done | bytes 1179680 | tf_op jit(solution)/shard_map/ppermute | solution.py:313
  113.7 3.1 collective-permute-start.25
  137.2 6.2 collective-permute-done.11.refs_9_
  146.8 6.0 collective-permute-done.17.refs_15_
  153.3 5.8 collective-permute-done.23.refs_21_
  160.0 7.2 shard_map.93.matrix.source
  181.5 3.9 shard_map.97
  186.8 11.5 %collective-permute-start.45 = (bf16[96,3072]{1,0:T(8,128)(2,1)S(1)}, bf16[96,3072]{1,0:T(8,128)(2,1)S(1)}, u32[]{:S(2)}, u32[]{:S(2)}) collective-permute-start(bf16[96,3072]{1,0:T(8,128)(2,1)S(1)} %get-tuple-element.313), channel_id=1, source_target_pairs={{0,16},{1,17},{2,18},{3,19},{4,20},{5,21},{6,22},{7,23},{8,24},{9,... | collective-permute-start | bytes 1769480 | tf_op jit(solution)/shard_map/ppermute | solution.py:188
  205.5 3.6 shard_map.100
  211.3 71.3 %collective-permute-start.48 = (bf16[96,3072]{1,0:T(8,128)(2,1)}, bf16[96,3072]{1,0:T(8,128)(2,1)S(1)}, u32[]{:S(2)}, u32[]{:S(2)}) collective-permute-start(bf16[96,3072]{1,0:T(8,128)(2,1)} %get-tuple-element.325), channel_id=1, source_target_pairs={{112,128},{113,129},{114,130},{115,131},{116,132},{117,133},{118,1... | collective-permute-start | bytes 1769480 | tf_op jit(solution)/shard_map/ppermute | solution.py:188
  283.3 6.6 collective-permute-start.33
  289.9 6.4 copy-done.6
  296.2 5.3 shard_map.102.refs_3_.turned
  301.6 6.0 shard_map.119
  309.6 5.1 shard_map.103
  321.2 3.6 shard_map.105
  328.3 3.9 shard_map.123
  332.2 18.7 %collective-permute-start.53 = (bf16[96,3072]{1,0:T(8,128)(2,1)S(1)}, bf16[96,3072]{1,0:T(8,128)(2,1)S(1)}, u32[]{:S(2)}, u32[]{:S(2)}) collective-permute-start(bf16[96,3072]{1,0:T(8,128)(2,1)S(1)} %get-tuple-element.345), channel_id=1, source_target_pairs={{0,16},{1,17},{2,18},{3,19},{4,20},{5,21},{6,22},{7,23},{8,24},{9,... | collective-permute-start | bytes 1769480 | tf_op jit(solution)/shard_map/ppermute | solution.py:188
  359.9 4.8 shard_map.126
  378.6 3.7 shard_map.147
  382.2 28.6 %collective-permute-start.79 = (bf16[96,3072]{1,0:T(8,128)(2,1)S(1)}, bf16[96,3072]{1,0:T(8,128)(2,1)S(1)}, u32[]{:S(2)}, u32[]{:S(2)}) collective-permute-start(bf16[96,3072]{1,0:T(8,128)(2,1)S(1)} %get-tuple-element.418), channel_id=1, source_target_pairs={{0,16},{1,17},{2,18},{3,19},{4,20},{5,21},{6,22},{7,23},{8,24},{9,... | collective-permute-start | bytes 1769480 | tf_op jit(solution)/shard_map/ppermute | solution.py:188
  411.4 5.3 collective-permute-start.64
  422.4 3.5 shard_map.150
  428.5 90.0 %collective-permute-start.83 = (bf16[96,3072]{1,0:T(8,128)(2,1)S(1)}, bf16[96,3072]{1,0:T(8,128)(2,1)S(1)}, u32[]{:S(2)}, u32[]{:S(2)}) collective-permute-start(bf16[96,3072]{1,0:T(8,128)(2,1)S(1)} %get-tuple-element.430), channel_id=1, source_target_pairs={{0,16},{1,17},{2,18},{3,19},{4,20},{5,21},{6,22},{7,23},{8,24},{9,... | collective-permute-start | bytes 1769480 | tf_op jit(solution)/shard_map/ppermute | solution.py:188
  519.4 6.0 collective-permute-start.68
  525.4 4.6 shard_map.152
  530.1 20.0 %collective-permute-start.84 = (bf16[96,3072]{1,0:T(8,128)(2,1)S(1)}, bf16[96,3072]{1,0:T(8,128)(2,1)S(1)}, u32[]{:S(2)}, u32[]{:S(2)}) collective-permute-start(bf16[96,3072]{1,0:T(8,128)(2,1)S(1)} %get-tuple-element.433), channel_id=1, source_target_pairs={{112,128},{113,129},{114,130},{115,131},{116,132},{117,133},{118,1... | collective-permute-start | bytes 1769480 | tf_op jit(solution)/shard_map/ppermute | solution.py:188
  550.1 4.6 shard_map.136
  559.2 12.9 %collective-permute-done.69.u_in = bf16[96,3072]{1,0:T(8,128)(2,1)S(1)} collective-permute-done((bf16[96,3072]{1,0:T(8,128)(2,1)S(1)}, bf16[96,3072]{1,0:T(8,128)(2,1)S(1)}, u32[]{:S(2)}, u32[]{:S(2)}) %collective-permute-start.69) | collective-permute-done | bytes 589856 | tf_op jit(solution)/shard_map/ppermute | solution.py:188
  586.0 3.4 shard_map.141
  592.7 4.3 shard_map.159
  597.0 8.4 collective-permute-start.91
  606.9 4.7 collective-permute-start.76
  623.9 6.4 copy-done.3
  635.1 4.3 copy-done.4
  640.6 3.1 shard_map.161
  643.9 73.2 %shard_map.164 = bf16[4,96,3072]{2,1,0:T(8,128)(2,1)} custom-call(s32[2]{0:T(128)S(1)} %pad_add_fusion.section.here, bf16[96,3072]{1,0:T(8,128)(2,1)} %copy-done.19, bf16[96,3072]{1,0:T(8,128)(2,1)} %copy-done.18, bf16[96,3072]{1,0:T(8,128)(2,1)} %copy-done.17, bf16[96,3072]{1,0:T(8,128)(2,1)} %copy-done.16), custom_call_target="tpu_custom_call" | custom-call | flops 1 | bytes 1 | tf_op jit(solution)/shard_map/pallas_call | solution.py:27
  719.0 56.9 %collective-permute-start.114 = (bf16[384,1536]{1,0:T(8,128)(2,1)S(1)}, bf16[384,1536]{1,0:T(8,128)(2,1)S(1)}, u32[]{:S(2)}, u32[]{:S(2)}) collective-permute-start(bf16[384,1536]{1,0:T(8,128)(2,1)S(1)} %broadcast_select_fusion), channel_id=1, source_target_pairs={{0,128},{16,144},{32,160},{48,176},{64,192},{80,208},{96,224},{112... | collective-permute-start | bytes 3538952 | tf_op jit(solution)/shard_map/ppermute | solution.py:200
  776.1 5.3 collective-permute-start.108
  783.3 3.8 collective-permute-start.93
  787.1 4.5 collective-permute-start.94
  791.8 3.3 collective-permute-done.92.refs_1_
  797.6 14.1 %collective-permute-start.100 = (bf16[192,768]{1,0:T(8,128)(2,1)S(1)}, bf16[192,768]{1,0:T(8,128)(2,1)S(1)}, u32[]{:S(2)}, u32[]{:S(2)}) collective-permute-start(bf16[192,768]{1,0:T(8,128)(2,1)S(1)} %get-tuple-element.473), channel_id=1, source_target_pairs={{0,4},{1,5},{2,6},{3,7},{4,12},{5,13},{6,14},{7,15},{8,0},{9,1},{1... | collective-permute-start | bytes 884744 | tf_op jit(solution)/shard_map/ppermute | solution.py:313
  811.8 37.4 %shard_map.162 = bf16[4,192,768]{2,1,0:T(8,128)(2,1)} custom-call(s32[2]{0:T(128)S(1)} %pad_add_fusion.section.here, bf16[192,768]{1,0:T(8,128)(2,1)} %get-tuple-element.458.refs_0_, bf16[192,768]{1,0:T(8,128)(2,1)} %copy-done.53, bf16[192,768]{1,0:T(8,128)(2,1)} %copy-done.54, bf16[192,768]{1,0:T(8,128)(2,1)} %copy-done.55), custom_call_target="tpu_custom_call" | custom-call | flops 1 | bytes 1 | tf_op jit(solution)/shard_map/pallas_call | solution.py:27
  861.6 5.0 collective-permute-done.99
  866.6 25.3 %collective-permute-start.113 = (f32[1,3072]{1,0:T(1,128)S(1)}, f32[1,3072]{1,0:T(1,128)S(1)}, u32[]{:S(2)}, u32[]{:S(2)}) collective-permute-start(f32[1,3072]{1,0:T(1,128)S(1)} %add_add_fusion.1), channel_id=1, source_target_pairs={{0,4},{1,5},{2,6},{3,7},{4,12},{5,13},{6,14},{7,15},{8,0},{9,1},{1... | collective-permute-start | bytes 36872 | tf_op jit(solution)/shard_map/ppermute | solution.py:313
  900.2 20.6 %collective-permute-done.101 = bf16[768,768]{1,0:T(8,128)(2,1)S(1)} collective-permute-done((bf16[768,768]{1,0:T(8,128)(2,1)S(1)}, bf16[768,768]{1,0:T(8,128)(2,1)S(1)}, u32[]{:S(2)}, u32[]{:S(2)}) %collective-permute-start.101) | collective-permute-done | bytes 1179680 | tf_op jit(solution)/shard_map/ppermute | solution.py:318
  921.5 3.8 collective-permute-start.104
  925.7 3.8 collective-permute-start.97
  936.7 16.9 %collective-permute-done.97 = bf16[4,192,768]{2,1,0:T(8,128)(2,1)S(1)} collective-permute-done((bf16[4,192,768]{2,1,0:T(8,128)(2,1)S(1)}, bf16[4,192,768]{2,1,0:T(8,128)(2,1)S(1)}, u32[]{:S(2)}, u32[]{:S(2)}) %collective-permute-start.97) | collective-permute-done | bytes 1179680 | tf_op jit(solution)/shard_map/ppermute | solution.py:300
  953.8 4.1 bitcast_convert_fusion
  958.1 3.2 collective-permute-start.105
  963.9 4.9 collective-permute-done.105
  968.8 8.1 collective-permute-done.106
  977.0 8.8 collective-permute-done.107
  (426 shorter events, 181.2 us)
Async XLA Ops:
  1.9 21.5 %collective-permute-start.8 = (bf16[192,2304]{1,0:T(8,128)(2,1)S(1)}, bf16[192,2304]{1,0:T(8,128)(2,1)S(1)}, u32[]{:S(2)}, u32[]{:S(2)}) collective-permute-start(bf16[192,2304]{1,0:T(8,128)(2,1)S(1)} %slice.100.refs_0_), channel_id=1, source_target_pairs={{0,8},{1,9},{2,10},{3,11},{4,0},{5,1},{6,2},{7,3},{8,12},{9,13},{1... | collective-permute-start | bytes 2654216 | tf_op jit(solution)/shard_map/ppermute | solution.py:313
  14.7 34.6 %collective-permute-start = (bf16[192,2304]{1,0:T(8,128)(2,1)S(1)}, bf16[192,2304]{1,0:T(8,128)(2,1)S(1)}, u32[]{:S(2)}, u32[]{:S(2)}) collective-permute-start(bf16[192,2304]{1,0:T(8,128)(2,1)S(1)} %slice.100.refs_0_), channel_id=1, source_target_pairs={{0,1},{1,2},{2,3},{3,0},{4,5},{5,6},{6,7},{7,4},{8,9},{9,10},{10,1... | collective-permute-start | bytes 2654216 | tf_op jit(solution)/shard_map/ppermute | solution.py:318
  23.4 22.6 %collective-permute-start.14 = (bf16[192,2304]{1,0:T(8,128)(2,1)S(1)}, bf16[192,2304]{1,0:T(8,128)(2,1)S(1)}, u32[]{:S(2)}, u32[]{:S(2)}) collective-permute-start(bf16[192,2304]{1,0:T(8,128)(2,1)S(1)} %collective-permute-done.8.refs_6_), channel_id=1, source_target_pairs={{0,8},{1,9},{2,10},{3,11},{4,0},{5,1},{6,2},{7,3},{8,12},{9,13},{1... | collective-permute-start | bytes 2654216 | tf_op jit(solution)/shard_map/ppermute | solution.py:313
  25.8 45.5 %collective-permute-start.13 = (bf16[768,768]{1,0:T(8,128)(2,1)S(1)}, bf16[768,768]{1,0:T(8,128)(2,1)S(1)}, u32[]{:S(2)}, u32[]{:S(2)}) collective-permute-start(bf16[768,768]{1,0:T(8,128)(2,1)S(1)} %constant_dynamic-update-slice_fusion.refs_5_), channel_id=1, source_target_pairs={{0,8},{1,9},{2,10},{3,11},{4,0},{5,1},{6,2},{7,3},{8,12},{9,13},{1... | collective-permute-start | bytes 3538952 | tf_op jit(solution)/shard_map/ppermute | solution.py:313
  26.0 48.5 %collective-permute-start.1 = (bf16[192,2304]{1,0:T(8,128)(2,1)S(1)}, bf16[192,2304]{1,0:T(8,128)(2,1)S(1)}, u32[]{:S(2)}, u32[]{:S(2)}) collective-permute-start(bf16[192,2304]{1,0:T(8,128)(2,1)S(1)} %slice.100.refs_0_), channel_id=1, source_target_pairs={{0,3},{1,0},{2,1},{3,2},{4,7},{5,4},{6,5},{7,6},{8,11},{9,8},{10,9... | collective-permute-start | bytes 2654216 | tf_op jit(solution)/shard_map/ppermute | solution.py:318
  29.0 47.1 %collective-permute-start.9 = (bf16[192,2304]{1,0:T(8,128)(2,1)S(1)}, bf16[192,2304]{1,0:T(8,128)(2,1)S(1)}, u32[]{:S(2)}, u32[]{:S(2)}) collective-permute-start(bf16[192,2304]{1,0:T(8,128)(2,1)S(1)} %collective-permute-done.8.refs_6_), channel_id=1, source_target_pairs={{0,1},{1,2},{2,3},{3,0},{4,5},{5,6},{6,7},{7,4},{8,9},{9,10},{10,1... | collective-permute-start | bytes 2654216 | tf_op jit(solution)/shard_map/ppermute | solution.py:318
  46.0 44.2 %collective-permute-start.20 = (bf16[192,2304]{1,0:T(8,128)(2,1)S(1)}, bf16[192,2304]{1,0:T(8,128)(2,1)S(1)}, u32[]{:S(2)}, u32[]{:S(2)}) collective-permute-start(bf16[192,2304]{1,0:T(8,128)(2,1)S(1)} %collective-permute-done.14.refs_12_), channel_id=1, source_target_pairs={{0,8},{1,9},{2,10},{3,11},{4,0},{5,1},{6,2},{7,3},{8,12},{9,13},{1... | collective-permute-start | bytes 2654216 | tf_op jit(solution)/shard_map/ppermute | solution.py:313
  49.3 42.7 %collective-permute-start.10 = (bf16[192,2304]{1,0:T(8,128)(2,1)S(1)}, bf16[192,2304]{1,0:T(8,128)(2,1)S(1)}, u32[]{:S(2)}, u32[]{:S(2)}) collective-permute-start(bf16[192,2304]{1,0:T(8,128)(2,1)S(1)} %collective-permute-done.8.refs_6_), channel_id=1, source_target_pairs={{0,3},{1,0},{2,1},{3,2},{4,7},{5,4},{6,5},{7,6},{8,11},{9,8},{10,9... | collective-permute-start | bytes 2654216 | tf_op jit(solution)/shard_map/ppermute | solution.py:318
  71.3 42.4 %collective-permute-start.19 = (bf16[768,768]{1,0:T(8,128)(2,1)S(1)}, bf16[768,768]{1,0:T(8,128)(2,1)}, u32[]{:S(2)}, u32[]{:S(2)}) collective-permute-start(bf16[768,768]{1,0:T(8,128)(2,1)S(1)} %collective-permute-done.13.refs_11_), channel_id=1, source_target_pairs={{0,8},{1,9},{2,10},{3,11},{4,0},{5,1},{6,2},{7,3},{8,12},{9,13},{1... | collective-permute-start | bytes 3538952 | tf_op jit(solution)/shard_map/ppermute | solution.py:313
  74.5 44.7 %collective-permute-start.15 = (bf16[192,2304]{1,0:T(8,128)(2,1)S(1)}, bf16[192,2304]{1,0:T(8,128)(2,1)S(1)}, u32[]{:S(2)}, u32[]{:S(2)}) collective-permute-start(bf16[192,2304]{1,0:T(8,128)(2,1)S(1)} %collective-permute-done.14.refs_12_), channel_id=1, source_target_pairs={{0,1},{1,2},{2,3},{3,0},{4,5},{5,6},{6,7},{7,4},{8,9},{9,10},{10,1... | collective-permute-start | bytes 2654216 | tf_op jit(solution)/shard_map/ppermute | solution.py:318
  76.1 44.8 %collective-permute-start.16 = (bf16[192,2304]{1,0:T(8,128)(2,1)S(1)}, bf16[192,2304]{1,0:T(8,128)(2,1)}, u32[]{:S(2)}, u32[]{:S(2)}) collective-permute-start(bf16[192,2304]{1,0:T(8,128)(2,1)S(1)} %collective-permute-done.14.refs_12_), channel_id=1, source_target_pairs={{0,3},{1,0},{2,1},{3,2},{4,7},{5,4},{6,5},{7,6},{8,11},{9,8},{10,9... | collective-permute-start | bytes 2654216 | tf_op jit(solution)/shard_map/ppermute | solution.py:318
  90.2 32.5 %collective-permute-start.21 = (bf16[192,2304]{1,0:T(8,128)(2,1)S(1)}, bf16[192,2304]{1,0:T(8,128)(2,1)}, u32[]{:S(2)}, u32[]{:S(2)}) collective-permute-start(bf16[192,2304]{1,0:T(8,128)(2,1)S(1)} %collective-permute-done.20.refs_18_), channel_id=1, source_target_pairs={{0,1},{1,2},{2,3},{3,0},{4,5},{5,6},{6,7},{7,4},{8,9},{9,10},{10,1... | collective-permute-start | bytes 2654216 | tf_op jit(solution)/shard_map/ppermute | solution.py:318
  92.0 31.1 %collective-permute-start.22 = (bf16[192,2304]{1,0:T(8,128)(2,1)S(1)}, bf16[192,2304]{1,0:T(8,128)(2,1)}, u32[]{:S(2)}, u32[]{:S(2)}) collective-permute-start(bf16[192,2304]{1,0:T(8,128)(2,1)S(1)} %collective-permute-done.20.refs_18_), channel_id=1, source_target_pairs={{0,3},{1,0},{2,1},{3,2},{4,7},{5,4},{6,5},{7,6},{8,11},{9,8},{10,9... | collective-permute-start | bytes 2654216 | tf_op jit(solution)/shard_map/ppermute | solution.py:318
  113.7 45.5 %collective-permute-start.25 = (bf16[768,768]{1,0:T(8,128)(2,1)}, bf16[768,768]{1,0:T(8,128)(2,1)}, u32[]{:S(2)}, u32[]{:S(2)}) collective-permute-start(bf16[768,768]{1,0:T(8,128)(2,1)} %collective-permute-done.19.refs_17_), channel_id=1, source_target_pairs={{0,8},{1,9},{2,10},{3,11},{4,0},{5,1},{6,2},{7,3},{8,12},{9,13},{1... | collective-permute-start | bytes 3538952 | tf_op jit(solution)/shard_map/ppermute | solution.py:313
  119.3 14.6 %collective-permute-start.2 = (bf16[96,2304]{1,0:T(8,128)(2,1)}, bf16[96,2304]{1,0:T(8,128)(2,1)S(1)}, u32[]{:S(2)}, u32[]{:S(2)}) collective-permute-start(bf16[96,2304]{1,0:T(8,128)(2,1)} %slice.101), channel_id=1, source_target_pairs={{0,1},{1,2},{2,3},{3,0},{4,5},{5,6},{6,7},{7,4},{8,9},{9,10},{10,1... | collective-permute-start | bytes 1327112 | tf_op jit(solution)/shard_map/ppermute | solution.py:318
  121.0 13.4 %collective-permute-start.3 = (bf16[96,2304]{1,0:T(8,128)(2,1)}, bf16[96,2304]{1,0:T(8,128)(2,1)S(1)}, u32[]{:S(2)}, u32[]{:S(2)}) collective-permute-start(bf16[96,2304]{1,0:T(8,128)(2,1)} %slice.102), channel_id=1, source_target_pairs={{0,3},{1,0},{2,1},{3,2},{4,7},{5,4},{6,5},{7,6},{8,11},{9,8},{10,9... | collective-permute-start | bytes 1327112 | tf_op jit(solution)/shard_map/ppermute | solution.py:318
  122.7 20.7 %collective-permute-start.11 = (bf16[96,2304]{1,0:T(8,128)(2,1)}, bf16[96,2304]{1,0:T(8,128)(2,1)S(1)}, u32[]{:S(2)}, u32[]{:S(2)}) collective-permute-start(bf16[96,2304]{1,0:T(8,128)(2,1)} %slice.106), channel_id=1, source_target_pairs={{0,1},{1,2},{2,3},{3,0},{4,5},{5,6},{6,7},{7,4},{8,9},{9,10},{10,1... | collective-permute-start | bytes 1327112 | tf_op jit(solution)/shard_map/ppermute | solution.py:318
  123.1 20.8 %collective-permute-start.12 = (bf16[96,2304]{1,0:T(8,128)(2,1)S(1)}, bf16[96,2304]{1,0:T(8,128)(2,1)S(1)}, u32[]{:S(2)}, u32[]{:S(2)}) collective-permute-start(bf16[96,2304]{1,0:T(8,128)(2,1)S(1)} %slice.107), channel_id=1, source_target_pairs={{0,3},{1,0},{2,1},{3,2},{4,7},{5,4},{6,5},{7,6},{8,11},{9,8},{10,9... | collective-permute-start | bytes 1327112 | tf_op jit(solution)/shard_map/ppermute | solution.py:318
  133.9 19.0 %collective-permute-start.17 = (bf16[96,2304]{1,0:T(8,128)(2,1)S(1)}, bf16[96,2304]{1,0:T(8,128)(2,1)S(1)}, u32[]{:S(2)}, u32[]{:S(2)}) collective-permute-start(bf16[96,2304]{1,0:T(8,128)(2,1)S(1)} %slice.108), channel_id=1, source_target_pairs={{0,1},{1,2},{2,3},{3,0},{4,5},{5,6},{6,7},{7,4},{8,9},{9,10},{10,1... | collective-permute-start | bytes 1327112 | tf_op jit(solution)/shard_map/ppermute | solution.py:318
  134.4 19.0 %collective-permute-start.18 = (bf16[96,2304]{1,0:T(8,128)(2,1)S(1)}, bf16[96,2304]{1,0:T(8,128)(2,1)S(1)}, u32[]{:S(2)}, u32[]{:S(2)}) collective-permute-start(bf16[96,2304]{1,0:T(8,128)(2,1)S(1)} %slice.109), channel_id=1, source_target_pairs={{0,3},{1,0},{2,1},{3,2},{4,7},{5,4},{6,5},{7,6},{8,11},{9,8},{10,9... | collective-permute-start | bytes 1327112 | tf_op jit(solution)/shard_map/ppermute | solution.py:318
  143.4 15.7 %collective-permute-start.23 = (bf16[96,2304]{1,0:T(8,128)(2,1)S(1)}, bf16[96,2304]{1,0:T(8,128)(2,1)S(1)}, u32[]{:S(2)}, u32[]{:S(2)}) collective-permute-start(bf16[96,2304]{1,0:T(8,128)(2,1)S(1)} %slice.110), channel_id=1, source_target_pairs={{0,1},{1,2},{2,3},{3,0},{4,5},{5,6},{6,7},{7,4},{8,9},{9,10},{10,1... | collective-permute-start | bytes 1327112 | tf_op jit(solution)/shard_map/ppermute | solution.py:318
  143.8 15.4 %collective-permute-start.24 = (bf16[96,2304]{1,0:T(8,128)(2,1)S(1)}, bf16[96,2304]{1,0:T(8,128)(2,1)S(1)}, u32[]{:S(2)}, u32[]{:S(2)}) collective-permute-start(bf16[96,2304]{1,0:T(8,128)(2,1)S(1)} %slice.111), channel_id=1, source_target_pairs={{0,3},{1,0},{2,1},{3,2},{4,7},{5,4},{6,5},{7,6},{8,11},{9,8},{10,9... | collective-permute-start | bytes 1327112 | tf_op jit(solution)/shard_map/ppermute | solution.py:318
  185.4 12.8 %collective-permute-start.29 = (bf16[96,3072]{1,0:T(8,128)(2,1)S(1)}, bf16[96,3072]{1,0:T(8,128)(2,1)S(1)}, u32[]{:S(2)}, u32[]{:S(2)}) collective-permute-start(bf16[96,3072]{1,0:T(8,128)(2,1)S(1)} %get-tuple-element.248), channel_id=1, source_target_pairs={{48,64},{49,65},{50,66},{51,67},{52,68},{53,69},{54,70},{55,71},{5... | collective-permute-start | bytes 1769480 | tf_op jit(solution)/shard_map/ppermute | solution.py:188
  186.8 14.1 %collective-permute-start.45 = (bf16[96,3072]{1,0:T(8,128)(2,1)S(1)}, bf16[96,3072]{1,0:T(8,128)(2,1)S(1)}, u32[]{:S(2)}, u32[]{:S(2)}) collective-permute-start(bf16[96,3072]{1,0:T(8,128)(2,1)S(1)} %get-tuple-element.313), channel_id=1, source_target_pairs={{0,16},{1,17},{2,18},{3,19},{4,20},{5,21},{6,22},{7,23},{8,24},{9,... | collective-permute-start | bytes 1769480 | tf_op jit(solution)/shard_map/ppermute | solution.py:188
  209.1 73.5 %collective-permute-start.32 = (bf16[96,3072]{1,0:T(8,128)(2,1)S(1)}, bf16[96,3072]{1,0:T(8,128)(2,1)S(1)}, u32[]{:S(2)}, u32[]{:S(2)}) collective-permute-start(bf16[96,3072]{1,0:T(8,128)(2,1)S(1)} %get-tuple-element.260), channel_id=1, source_target_pairs={{32,48},{33,49},{34,50},{35,51},{36,52},{37,53},{38,54},{39,55},{4... | collective-permute-start | bytes 1769480 | tf_op jit(solution)/shard_map/ppermute | solution.py:188
  211.3 90.3 %collective-permute-start.48 = (bf16[96,3072]{1,0:T(8,128)(2,1)}, bf16[96,3072]{1,0:T(8,128)(2,1)S(1)}, u32[]{:S(2)}, u32[]{:S(2)}) collective-permute-start(bf16[96,3072]{1,0:T(8,128)(2,1)} %get-tuple-element.325), channel_id=1, source_target_pairs={{112,128},{113,129},{114,130},{115,131},{116,132},{117,133},{118,1... | collective-permute-start | bytes 1769480 | tf_op jit(solution)/shard_map/ppermute | solution.py:188
  283.3 26.3 %collective-permute-start.33 = (bf16[96,3072]{1,0:T(8,128)(2,1)S(1)}, bf16[96,3072]{1,0:T(8,128)(2,1)S(1)}, u32[]{:S(2)}, u32[]{:S(2)}) collective-permute-start(bf16[96,3072]{1,0:T(8,128)(2,1)S(1)} %get-tuple-element.264), channel_id=1, source_target_pairs={{112,128},{113,129},{114,130},{115,131},{116,132},{117,133},{118,1... | collective-permute-start | bytes 1769480 | tf_op jit(solution)/shard_map/ppermute | solution.py:188
  327.6 23.3 %collective-permute-start.37 = (bf16[96,3072]{1,0:T(8,128)(2,1)S(1)}, bf16[96,3072]{1,0:T(8,128)(2,1)S(1)}, u32[]{:S(2)}, u32[]{:S(2)}) collective-permute-start(bf16[96,3072]{1,0:T(8,128)(2,1)S(1)} %get-tuple-element.280), channel_id=1, source_target_pairs={{48,64},{49,65},{50,66},{51,67},{52,68},{53,69},{54,70},{55,71},{5... | collective-permute-start | bytes 1769480 | tf_op jit(solution)/shard_map/ppermute | solution.py:188
  332.2 21.3 %collective-permute-start.53 = (bf16[96,3072]{1,0:T(8,128)(2,1)S(1)}, bf16[96,3072]{1,0:T(8,128)(2,1)S(1)}, u32[]{:S(2)}, u32[]{:S(2)}) collective-permute-start(bf16[96,3072]{1,0:T(8,128)(2,1)S(1)} %get-tuple-element.345), channel_id=1, source_target_pairs={{0,16},{1,17},{2,18},{3,19},{4,20},{5,21},{6,22},{7,23},{8,24},{9,... | collective-permute-start | bytes 1769480 | tf_op jit(solution)/shard_map/ppermute | solution.py:188
  377.9 33.0 %collective-permute-start.63 = (bf16[96,3072]{1,0:T(8,128)(2,1)S(1)}, bf16[96,3072]{1,0:T(8,128)(2,1)S(1)}, u32[]{:S(2)}, u32[]{:S(2)}) collective-permute-start(bf16[96,3072]{1,0:T(8,128)(2,1)S(1)} %get-tuple-element.367), channel_id=1, source_target_pairs={{16,32},{17,33},{18,34},{19,35},{20,36},{21,37},{22,38},{23,39},{2... | collective-permute-start | bytes 1769480 | tf_op jit(solution)/shard_map/ppermute | solution.py:188
  382.2 34.5 %collective-permute-start.79 = (bf16[96,3072]{1,0:T(8,128)(2,1)S(1)}, bf16[96,3072]{1,0:T(8,128)(2,1)S(1)}, u32[]{:S(2)}, u32[]{:S(2)}) collective-permute-start(bf16[96,3072]{1,0:T(8,128)(2,1)S(1)} %get-tuple-element.418), channel_id=1, source_target_pairs={{0,16},{1,17},{2,18},{3,19},{4,20},{5,21},{6,22},{7,23},{8,24},{9,... | collective-permute-start | bytes 1769480 | tf_op jit(solution)/shard_map/ppermute | solution.py:188
  427.2 91.3 %collective-permute-start.67 = (bf16[96,3072]{1,0:T(8,128)(2,1)S(1)}, bf16[96,3072]{1,0:T(8,128)(2,1)S(1)}, u32[]{:S(2)}, u32[]{:S(2)}) collective-permute-start(bf16[96,3072]{1,0:T(8,128)(2,1)S(1)} %get-tuple-element.379), channel_id=1, source_target_pairs={{16,32},{17,33},{18,34},{19,35},{20,36},{21,37},{22,38},{23,39},{2... | collective-permute-start | bytes 1769480 | tf_op jit(solution)/shard_map/ppermute | solution.py:188
  428.5 97.0 %collective-permute-start.83 = (bf16[96,3072]{1,0:T(8,128)(2,1)S(1)}, bf16[96,3072]{1,0:T(8,128)(2,1)S(1)}, u32[]{:S(2)}, u32[]{:S(2)}) collective-permute-start(bf16[96,3072]{1,0:T(8,128)(2,1)S(1)} %get-tuple-element.430), channel_id=1, source_target_pairs={{0,16},{1,17},{2,18},{3,19},{4,20},{5,21},{6,22},{7,23},{8,24},{9,... | collective-permute-start | bytes 1769480 | tf_op jit(solution)/shard_map/ppermute | solution.py:188
  519.4 30.6 %collective-permute-start.68 = (bf16[96,3072]{1,0:T(8,128)(2,1)S(1)}, bf16[96,3072]{1,0:T(8,128)(2,1)S(1)}, u32[]{:S(2)}, u32[]{:S(2)}) collective-permute-start(bf16[96,3072]{1,0:T(8,128)(2,1)S(1)} %get-tuple-element.382), channel_id=1, source_target_pairs={{0,16},{1,17},{2,18},{3,19},{4,20},{5,21},{6,22},{7,23},{8,24},{9,... | collective-permute-start | bytes 1769480 | tf_op jit(solution)/shard_map/ppermute | solution.py:188
  530.1 27.6 %collective-permute-start.84 = (bf16[96,3072]{1,0:T(8,128)(2,1)S(1)}, bf16[96,3072]{1,0:T(8,128)(2,1)S(1)}, u32[]{:S(2)}, u32[]{:S(2)}) collective-permute-start(bf16[96,3072]{1,0:T(8,128)(2,1)S(1)} %get-tuple-element.433), channel_id=1, source_target_pairs={{112,128},{113,129},{114,130},{115,131},{116,132},{117,133},{118,1... | collective-permute-start | bytes 1769480 | tf_op jit(solution)/shard_map/ppermute | solution.py:188
  554.7 17.3 %collective-permute-start.69 = (bf16[96,3072]{1,0:T(8,128)(2,1)S(1)}, bf16[96,3072]{1,0:T(8,128)(2,1)S(1)}, u32[]{:S(2)}, u32[]{:S(2)}) collective-permute-start(bf16[96,3072]{1,0:T(8,128)(2,1)S(1)} %get-tuple-element.385), channel_id=1, source_target_pairs={{112,128},{113,129},{114,130},{115,131},{116,132},{117,133},{118,1... | collective-permute-start | bytes 1769480 | tf_op jit(solution)/shard_map/ppermute | solution.py:188
  558.5 14.9 %collective-permute-start.85 = (bf16[96,3072]{1,0:T(8,128)(2,1)S(1)}, bf16[96,3072]{1,0:T(8,128)(2,1)S(1)}, u32[]{:S(2)}, u32[]{:S(2)}) collective-permute-start(bf16[96,3072]{1,0:T(8,128)(2,1)S(1)} %get-tuple-element.436), channel_id=1, source_target_pairs={{32,48},{33,49},{34,50},{35,51},{36,52},{37,53},{38,54},{39,55},{4... | collective-permute-start | bytes 1769480 | tf_op jit(solution)/shard_map/ppermute | solution.py:188
  592.0 13.5 %collective-permute-start.75 = (bf16[96,3072]{1,0:T(8,128)(2,1)S(1)}, bf16[96,3072]{1,0:T(8,128)(2,1)S(1)}, u32[]{:S(2)}, u32[]{:S(2)}) collective-permute-start(bf16[96,3072]{1,0:T(8,128)(2,1)S(1)} %get-tuple-element.403), channel_id=1, source_target_pairs={{16,32},{17,33},{18,34},{19,35},{20,36},{21,37},{22,38},{23,39},{2... | collective-permute-start | bytes 1769480 | tf_op jit(solution)/shard_map/ppermute | solution.py:188
  597.0 26.9 %collective-permute-start.91 = (bf16[96,3072]{1,0:T(8,128)(2,1)}, bf16[96,3072]{1,0:T(8,128)(2,1)}, u32[]{:S(2)}, u32[]{:S(2)}) collective-permute-start(bf16[96,3072]{1,0:T(8,128)(2,1)} %get-tuple-element.454), channel_id=1, source_target_pairs={{0,16},{1,17},{2,18},{3,19},{4,20},{5,21},{6,22},{7,23},{8,24},{9,... | collective-permute-start | bytes 1769480 | tf_op jit(solution)/shard_map/ppermute | solution.py:188
  606.9 28.2 %collective-permute-start.76 = (bf16[96,3072]{1,0:T(8,128)(2,1)}, bf16[96,3072]{1,0:T(8,128)(2,1)S(1)}, u32[]{:S(2)}, u32[]{:S(2)}) collective-permute-start(bf16[96,3072]{1,0:T(8,128)(2,1)} %get-tuple-element.406), channel_id=1, source_target_pairs={{0,16},{1,17},{2,18},{3,19},{4,20},{5,21},{6,22},{7,23},{8,24},{9,... | collective-permute-start | bytes 1769480 | tf_op jit(solution)/shard_map/ppermute | solution.py:188
  719.0 173.0 %collective-permute-start.114 = (bf16[384,1536]{1,0:T(8,128)(2,1)S(1)}, bf16[384,1536]{1,0:T(8,128)(2,1)S(1)}, u32[]{:S(2)}, u32[]{:S(2)}) collective-permute-start(bf16[384,1536]{1,0:T(8,128)(2,1)S(1)} %broadcast_select_fusion), channel_id=1, source_target_pairs={{0,128},{16,144},{32,160},{48,176},{64,192},{80,208},{96,224},{112... | collective-permute-start | bytes 3538952 | tf_op jit(solution)/shard_map/ppermute | solution.py:200
  776.1 73.1 %collective-permute-start.108 = (f32[1,3072]{1,0:T(1,128)S(1)}, f32[1,3072]{1,0:T(1,128)S(1)}, u32[]{:S(2)}, u32[]{:S(2)}) collective-permute-start(f32[1,3072]{1,0:T(1,128)S(1)} %add.187), channel_id=1, source_target_pairs={{0,1},{1,2},{2,3},{3,0},{4,5},{5,6},{6,7},{7,4},{8,9},{9,10},{10,1... | collective-permute-start | bytes 36872 | tf_op jit(solution)/shard_map/ppermute | solution.py:318
  781.3 13.8 %collective-permute-start.92 = (bf16[192,768]{1,0:T(8,128)(2,1)S(1)}, bf16[192,768]{1,0:T(8,128)(2,1)S(1)}, u32[]{:S(2)}, u32[]{:S(2)}) collective-permute-start(bf16[192,768]{1,0:T(8,128)(2,1)S(1)} %copy-done.63), channel_id=1, source_target_pairs={{128,129},{129,130},{130,131},{131,128},{132,133},{133,134},{134,1... | collective-permute-start | bytes 884744 | tf_op jit(solution)/shard_map/ppermute | solution.py:296
  783.3 12.9 %collective-permute-start.93 = (bf16[192,768]{1,0:T(8,128)(2,1)S(1)}, bf16[192,768]{1,0:T(8,128)(2,1)S(1)}, u32[]{:S(2)}, u32[]{:S(2)}) collective-permute-start(bf16[192,768]{1,0:T(8,128)(2,1)S(1)} %copy-done.62), channel_id=1, source_target_pairs={{128,130},{129,131},{130,128},{131,129},{132,134},{133,135},{134,1... | collective-permute-start | bytes 884744 | tf_op jit(solution)/shard_map/ppermute | solution.py:296
  787.1 10.5 %collective-permute-start.94 = (bf16[192,768]{1,0:T(8,128)(2,1)S(1)}, bf16[192,768]{1,0:T(8,128)(2,1)S(1)}, u32[]{:S(2)}, u32[]{:S(2)}) collective-permute-start(bf16[192,768]{1,0:T(8,128)(2,1)S(1)} %copy-done.61), channel_id=1, source_target_pairs={{128,131},{129,128},{130,129},{131,130},{132,135},{133,132},{134,1... | collective-permute-start | bytes 884744 | tf_op jit(solution)/shard_map/ppermute | solution.py:296
  795.1 55.6 %collective-permute-start.109 = (f32[1,3072]{1,0:T(1,128)S(1)}, f32[1,3072]{1,0:T(1,128)S(1)}, u32[]{:S(2)}, u32[]{:S(2)}) collective-permute-start(f32[1,3072]{1,0:T(1,128)S(1)} %add.187), channel_id=1, source_target_pairs={{0,2},{1,3},{2,0},{3,1},{4,6},{5,7},{6,4},{7,5},{8,10},{9,11},{10,... | collective-permute-start | bytes 36872 | tf_op jit(solution)/shard_map/ppermute | solution.py:318
  796.2 56.1 %collective-permute-start.110 = (f32[1,3072]{1,0:T(1,128)S(1)}, f32[1,3072]{1,0:T(1,128)S(1)}, u32[]{:S(2)}, u32[]{:S(2)}) collective-permute-start(f32[1,3072]{1,0:T(1,128)S(1)} %add.187), channel_id=1, source_target_pairs={{0,3},{1,0},{2,1},{3,2},{4,7},{5,4},{6,5},{7,6},{8,11},{9,8},{10,9... | collective-permute-start | bytes 36872 | tf_op jit(solution)/shard_map/ppermute | solution.py:318
  797.6 57.1 %collective-permute-start.100 = (bf16[192,768]{1,0:T(8,128)(2,1)S(1)}, bf16[192,768]{1,0:T(8,128)(2,1)S(1)}, u32[]{:S(2)}, u32[]{:S(2)}) collective-permute-start(bf16[192,768]{1,0:T(8,128)(2,1)S(1)} %get-tuple-element.473), channel_id=1, source_target_pairs={{0,4},{1,5},{2,6},{3,7},{4,12},{5,13},{6,14},{7,15},{8,0},{9,1},{1... | collective-permute-start | bytes 884744 | tf_op jit(solution)/shard_map/ppermute | solution.py:313
  850.7 15.9 %collective-permute-start.99 = (bf16[192,768]{1,0:T(8,128)(2,1)S(1)}, bf16[192,768]{1,0:T(8,128)(2,1)S(1)}, u32[]{:S(2)}, u32[]{:S(2)}) collective-permute-start(bf16[192,768]{1,0:T(8,128)(2,1)S(1)} %get-tuple-element.474), channel_id=1, source_target_pairs={{0,12},{1,13},{2,14},{3,15},{4,8},{5,9},{6,10},{7,11},{8,4},{9,5},... | collective-permute-start | bytes 884744 | tf_op jit(solution)/shard_map/ppermute | solution.py:313
  852.3 44.4 %collective-permute-start.95 = (bf16[4,192,768]{2,1,0:T(8,128)(2,1)}, bf16[4,192,768]{2,1,0:T(8,128)(2,1)S(1)}, u32[]{:S(2)}, u32[]{:S(2)}) collective-permute-start(bf16[4,192,768]{2,1,0:T(8,128)(2,1)} %shard_map.162), channel_id=1, source_target_pairs={{128,136},{129,137},{130,138},{131,139},{132,128},{133,129},{134,1... | collective-permute-start | bytes 3538952 | tf_op jit(solution)/shard_map/ppermute | solution.py:300
  854.7 39.1 %collective-permute-start.111 = (f32[1,3072]{1,0:T(1,128)S(1)}, f32[1,3072]{1,0:T(1,128)S(1)}, u32[]{:S(2)}, u32[]{:S(2)}) collective-permute-start(f32[1,3072]{1,0:T(1,128)S(1)} %add_add_fusion.1), channel_id=1, source_target_pairs={{0,8},{1,9},{2,10},{3,11},{4,0},{5,1},{6,2},{7,3},{8,12},{9,13},{1... | collective-permute-start | bytes 36872 | tf_op jit(solution)/shard_map/ppermute | solution.py:313
  859.4 37.2 %collective-permute-start.112 = (f32[1,3072]{1,0:T(1,128)S(1)}, f32[1,3072]{1,0:T(1,128)S(1)}, u32[]{:S(2)}, u32[]{:S(2)}) collective-permute-start(f32[1,3072]{1,0:T(1,128)S(1)} %add_add_fusion.1), channel_id=1, source_target_pairs={{0,12},{1,13},{2,14},{3,15},{4,8},{5,9},{6,10},{7,11},{8,4},{9,5},... | collective-permute-start | bytes 36872 | tf_op jit(solution)/shard_map/ppermute | solution.py:313
  866.6 32.8 %collective-permute-start.113 = (f32[1,3072]{1,0:T(1,128)S(1)}, f32[1,3072]{1,0:T(1,128)S(1)}, u32[]{:S(2)}, u32[]{:S(2)}) collective-permute-start(f32[1,3072]{1,0:T(1,128)S(1)} %add_add_fusion.1), channel_id=1, source_target_pairs={{0,4},{1,5},{2,6},{3,7},{4,12},{5,13},{6,14},{7,15},{8,0},{9,1},{1... | collective-permute-start | bytes 36872 | tf_op jit(solution)/shard_map/ppermute | solution.py:313
  892.0 28.8 %collective-permute-start.101 = (bf16[768,768]{1,0:T(8,128)(2,1)S(1)}, bf16[768,768]{1,0:T(8,128)(2,1)S(1)}, u32[]{:S(2)}, u32[]{:S(2)}) collective-permute-start(bf16[768,768]{1,0:T(8,128)(2,1)S(1)} %pad_maximum_fusion), channel_id=1, source_target_pairs={{0,1},{1,2},{2,3},{3,0},{4,5},{5,6},{6,7},{7,4},{8,9},{9,10},{10,1... | collective-permute-start | bytes 3538952 | tf_op jit(solution)/shard_map/ppermute | solution.py:318
  893.8 27.6 %collective-permute-start.103 = (bf16[768,768]{1,0:T(8,128)(2,1)S(1)}, bf16[768,768]{1,0:T(8,128)(2,1)S(1)}, u32[]{:S(2)}, u32[]{:S(2)}) collective-permute-start(bf16[768,768]{1,0:T(8,128)(2,1)S(1)} %pad_maximum_fusion), channel_id=1, source_target_pairs={{0,3},{1,0},{2,1},{3,2},{4,7},{5,4},{6,5},{7,6},{8,11},{9,8},{10,9... | collective-permute-start | bytes 3538952 | tf_op jit(solution)/shard_map/ppermute | solution.py:318
  896.6 28.6 %collective-permute-start.115 = (bf16[384,768]{1,0:T(8,128)(2,1)S(1)}, bf16[384,768]{1,0:T(8,128)(2,1)S(1)}, u32[]{:S(2)}, u32[]{:S(2)}) collective-permute-start(bf16[384,768]{1,0:T(8,128)(2,1)S(1)} %broadcast_select_fusion.1), channel_id=1, source_target_pairs={{0,64},{16,80},{32,96},{48,112},{64,0},{80,16},{96,32},{112,48},{1... | collective-permute-start | bytes 1769480 | tf_op jit(solution)/shard_map/ppermute | solution.py:200
  896.8 28.9 %collective-permute-start.96 = (bf16[4,192,768]{2,1,0:T(8,128)(2,1)S(1)}, bf16[4,192,768]{2,1,0:T(8,128)(2,1)S(1)}, u32[]{:S(2)}, u32[]{:S(2)}) collective-permute-start(bf16[4,192,768]{2,1,0:T(8,128)(2,1)S(1)} %collective-permute-done.95), channel_id=1, source_target_pairs={{128,136},{129,137},{130,138},{131,139},{132,128},{133,129},{134,1... | collective-permute-start | bytes 3538952 | tf_op jit(solution)/shard_map/ppermute | solution.py:300
  920.8 15.0 %collective-permute-start.102 = (bf16[384,768]{1,0:T(8,128)(2,1)S(1)}, bf16[384,768]{1,0:T(8,128)(2,1)S(1)}, u32[]{:S(2)}, u32[]{:S(2)}) collective-permute-start(bf16[384,768]{1,0:T(8,128)(2,1)S(1)} %slice.112), channel_id=1, source_target_pairs={{0,1},{1,2},{2,3},{3,0},{4,5},{5,6},{6,7},{7,4},{8,9},{9,10},{10,1... | collective-permute-start | bytes 1769480 | tf_op jit(solution)/shard_map/ppermute | solution.py:318
  921.5 15.0 %collective-permute-start.104 = (bf16[384,768]{1,0:T(8,128)(2,1)S(1)}, bf16[384,768]{1,0:T(8,128)(2,1)S(1)}, u32[]{:S(2)}, u32[]{:S(2)}) collective-permute-start(bf16[384,768]{1,0:T(8,128)(2,1)S(1)} %slice.113), channel_id=1, source_target_pairs={{0,3},{1,0},{2,1},{3,2},{4,7},{5,4},{6,5},{7,6},{8,11},{9,8},{10,9... | collective-permute-start | bytes 1769480 | tf_op jit(solution)/shard_map/ppermute | solution.py:318
  925.7 28.0 %collective-permute-start.97 = (bf16[4,192,768]{2,1,0:T(8,128)(2,1)S(1)}, bf16[4,192,768]{2,1,0:T(8,128)(2,1)S(1)}, u32[]{:S(2)}, u32[]{:S(2)}) collective-permute-start(bf16[4,192,768]{2,1,0:T(8,128)(2,1)S(1)} %collective-permute-done.96), channel_id=1, source_target_pairs={{128,136},{129,137},{130,138},{131,139},{132,128},{133,129},{134,1... | collective-permute-start | bytes 3538952 | tf_op jit(solution)/shard_map/ppermute | solution.py:300
  932.9 28.4 %collective-permute-start.117 = (bf16[384,192]{1,0:T(8,128)(2,1)S(1)}, bf16[384,192]{1,0:T(8,128)(2,1)S(1)}, u32[]{:S(2)}, u32[]{:S(2)}) collective-permute-start(bf16[384,192]{1,0:T(8,128)(2,1)S(1)} %broadcast_select_fusion.3), channel_id=1, source_target_pairs={{0,16},{16,0},{32,48},{48,32},{64,80},{80,64},{96,112},{112,96},{1... | collective-permute-start | bytes 442376 | tf_op jit(solution)/shard_map/ppermute | solution.py:200
  958.1 10.7 %collective-permute-start.105 = (bf16[192,768]{1,0:T(8,128)(2,1)S(1)}, bf16[192,768]{1,0:T(8,128)(2,1)S(1)}, u32[]{:S(2)}, u32[]{:S(2)}) collective-permute-start(bf16[192,768]{1,0:T(8,128)(2,1)S(1)} %get-tuple-element.470), channel_id=1, source_target_pairs={{0,8},{1,9},{2,10},{3,11},{4,0},{5,1},{6,2},{7,3},{8,12},{9,13},{1... | collective-permute-start | bytes 884744 | tf_op jit(solution)/shard_map/ppermute | solution.py:313
  961.5 15.4 %collective-permute-start.106 = (bf16[192,768]{1,0:T(8,128)(2,1)S(1)}, bf16[192,768]{1,0:T(8,128)(2,1)S(1)}, u32[]{:S(2)}, u32[]{:S(2)}) collective-permute-start(bf16[192,768]{1,0:T(8,128)(2,1)S(1)} %get-tuple-element.469), channel_id=1, source_target_pairs={{0,12},{1,13},{2,14},{3,15},{4,8},{5,9},{6,10},{7,11},{8,4},{9,5},... | collective-permute-start | bytes 884744 | tf_op jit(solution)/shard_map/ppermute | solution.py:313
  963.9 21.9 %collective-permute-start.107 = (bf16[192,768]{1,0:T(8,128)(2,1)S(1)}, bf16[192,768]{1,0:T(8,128)(2,1)S(1)}, u32[]{:S(2)}, u32[]{:S(2)}) collective-permute-start(bf16[192,768]{1,0:T(8,128)(2,1)S(1)} %get-tuple-element.468), channel_id=1, source_target_pairs={{0,4},{1,5},{2,6},{3,7},{4,12},{5,13},{6,14},{7,15},{8,0},{9,1},{1... | collective-permute-start | bytes 884744 | tf_op jit(solution)/shard_map/ppermute | solution.py:313
  (118 other events, 2007.2 us)

commit v6 on v5

--- a/solution.py
+++ b/solution.py
@@ -114,13 +114,13 @@
             copy.wait()
 
 
-def forward(t, m, section, x, gain_row, matrix, kept, after):
+def forward(t, m, section, x, gain_row, matrix, kept, after, held):
     shape = x.shape[-2:]
     wide, deep = pltpu.HBM(shape, BF), pltpu.HBM(shape, F32)
     return call(
         functools.partial(forward_kernel, t, m if x.ndim == 3 else None),
         (pltpu.VMEM(shape, BF), wide, wide, deep),
-        [SMEM] + [VMEM] * 3 + [HBM] * len(kept) + [VMEM] * len(after),
+        [SMEM] + [VMEM] * 3 + [HBM] * (len(kept) + len(after)) + [VMEM] * len(held),
         (VMEM, HBM, HBM, HBM),
         {4 + i: 1 + i for i in range(len(kept))},
         [
@@ -129,7 +129,7 @@
             pltpu.VMEM(shape, F32),
             pltpu.SemaphoreType.DMA((2 + shape[1] // TILE,)),
         ],
-        [section, x, gain_row, matrix, *kept, *after],
+        [section, x, gain_row, matrix, *kept, *after, *held],
     )
 
 
@@ -188,6 +188,10 @@
     return lax.ppermute(block, ("section", "dp"), sorted(pairs))
 
 
+def order(sections, micros):
+    return [(t + i, m) for t in range(0, sections, 2) for m in range(micros) for i in (0, 1)]
+
+
 def spread(block, sections, section):
     rows = block.shape[0] // 2
     owned = lax.broadcasted_iota(jnp.int32, (2 * rows, 1), 0) >= rows
@@ -251,14 +255,26 @@
     )
 
 
-def echo_kernel(here, _after, out):
-    out[0] = here[0]
-    out[1] = here[1]
-
-
-def echo(here, after):
-    shape = jax.ShapeDtypeStruct(here.shape, here.dtype)
-    return call(echo_kernel, shape, [SMEM, HBM], SMEM, {}, [], [here, in_hbm(after)])
+def pin_kernel(here, *refs):
+    for ref in refs:
+        if ref.shape == here.shape:
+            ref[0] = here[0]
+            ref[1] = here[1]
+
+
+def pin(here, arrays, after):
+    return call(
+        pin_kernel,
+        (
+            jax.ShapeDtypeStruct(here.shape, here.dtype),
+            *(pltpu.HBM(array.shape, array.dtype) for array in arrays),
+        ),
+        [SMEM] + [HBM] * (len(arrays) + len(after)),
+        (SMEM,) + (HBM,) * len(arrays),
+        {1 + i: 1 + i for i in range(len(arrays))},
+        [],
+        [here, *(in_hbm(array) for array in (*arrays, *after))],
+    )
 
 
 def pile_kernel(low, high, here, *refs):
@@ -387,37 +403,46 @@
 
     kept = [()] * micros
     current = [inputs] * micros
-    for t in range(sections):
-        after = ()
-        if t == half:
+    earlier, held = None, ()
+    for t, m in order(sections, micros):
+        if t == half and not held:
             turned = turn(matrix)
-            after = (turned,)
-        for m in range(micros):
-            result, *kept[m] = forward(t, m, here, current[m], gain_row, matrix, kept[m], after)
-            current[m] = hop(result, t, half, count) if t + 1 < sections else result
+            held = (turned,)
+        after = () if earlier in (None, m) else (in_hbm(kept[earlier][0]),)
+        result, *kept[m] = forward(
+            t, m, here, current[m], gain_row, matrix, kept[m], after, held if (t, m) == (half, 0) else ()
+        )
+        current[m] = hop(result, t, half, count) if t + 1 < sections else result
+        earlier = m
 
     normed = [kept[m][1] for m in range(micros)]
     early = exchange(normed, here, 0, EARLY, count)
     passed = [()] * micros
     arriving = [upstream] * micros
-    for t in reversed(range(sections)):
-        after = (in_hbm(early[-1]),) if t == sections - 1 else ()
-        for m in range(micros):
-            result, *passed[m] = backward(
-                t, m, here, arriving[m], kept[m][0], kept[m][2], gain_row, turned, passed[m], after
-            )
-            arriving[m] = hop(result, t - 1, half, count) if t else result
+    earlier = None
+    for step, m in order(sections, micros):
+        t = sections - 1 - step
+        if step == 0:
+            after = (in_hbm(early[-1]),)
+        else:
+            after = () if earlier == m else (in_hbm(passed[earlier][0]),)
+        result, *passed[m] = backward(
+            t, m, here, arriving[m], kept[m][0], kept[m][2], gain_row, turned, passed[m], after
+        )
+        arriving[m] = hop(result, t - 1, half, count) if t else result
+        earlier = m
     ended = [passed[m][0] for m in range(micros)]
     late = exchange(normed, here, EARLY, sections, count, ended)
     normed = [jnp.where(section < EARLY, a, b) for a, b in zip(early, late)]
 
-    slope = jnp.concatenate([passed[m][0] for m in range(micros)], axis=0)
+    slope = pile(ended, here, 0, sections).reshape(micros * rows, features)
     wide = features // 4
     slope = [
         lax.dynamic_slice_in_dim(slope, to_z[k] * wide, wide, axis=1) for k in range(4)
     ]
     slope = slope[:1] + [shift_z(slope[k], k, count) for k in (1, 2, 3)]
-    slope = from_all_y(jnp.concatenate(slope, axis=0), count)
+    behind_slope, *terms = pin(here, [passed[m][1] for m in range(micros)], slope[1:])
+    slope = from_all_y(pile(slope, here, 0, sections).reshape(-1, wide), count)
     slope = jnp.stack(slope).reshape(4, 4, micros * rows, features // 4)
     product = jnp.einsum(
         "jkra,kjrb->ab", jnp.stack(normed), slope, preferred_element_type=F32
@@ -430,11 +455,11 @@
         at = from_z[k] * (features // 4)
         weight_grad = lax.dynamic_update_slice_in_dim(weight_grad, piece, at, 1)
 
-    total = sum(passed[m][1] for m in range(micros))
+    total = sum(terms)
     total = total + (shift_y(total, 1, count) + shift_y(total, 2, count) + shift_y(total, 3, count))
     total = total + (shift_z(total, 1, count) + shift_z(total, 2, count) + shift_z(total, 3, count))
     ends = pile((*arriving, *current), here, 0, sections).reshape(-1, features)
-    first_share, final_share = spread(ends, sections, echo(here, ended[-1])[0])
+    first_share, final_share = spread(ends, sections, behind_slope[0])
     shape = (*batches, features // sections)
     return (
         weight_grad[None],

time: 998 us -> 1140 us (1.14)
  Pallas kernels: 221 us -> 285 us
  starting transfers between devices: 512 us -> 557 us
  waiting for transfers between devices: 193 us -> 226 us
    ppermute x60, starting transfers between devices: 317 us -> 399 us  [hop(): return lax.ppermute(block, ('section', 'dp'), sorted(pairs))]
    pallas_call x72 -> x74, Pallas kernels: 221 us -> 285 us  [call(): pl.pallas_call(kernel, out_shape=outs, in_specs=in_specs, out_specs=out_s...]
    ppermute x15, starting transfers between devices: 65.8 us -> 33.5 us  [shift_z(): return lax.ppermute(block, 'dp', pairs)]
    ppermute x27, waiting for transfers between devices: 55.4 us -> 31.1 us  [shift_y(): return lax.ppermute(block, 'dp', pairs)]
    ppermute x60, waiting for transfers between devices: 15.7 us -> 39 us  [hop(): return lax.ppermute(block, ('section', 'dp'), sorted(pairs))]
    ppermute x6, waiting for transfers between devices: 17.1 us -> 34.3 us  [exchange(): blocks.append(lax.ppermute(blocks[-1], ('section', 'dp'), pairs))]
    ppermute x15, waiting for transfers between devices: 98.4 us -> 113 us  [shift_z(): return lax.ppermute(block, 'dp', pairs)]
    unnamed x132 -> x121, local copies, waits for them, and re-layouts: 23.9 us -> 20.6 us
  transfers between devices with their start and end apart: 118 -> 118, of which waited for: 36 -> 38; matrix products, arithmetic and copies ran while one was open for 2% -> 2% of each run, Pallas kernels for 14% -> 17%
where the time goes in v6:
time: 1140 us; the launch traced here: 1130 us
  starting transfers between devices  557 us (49%)
  Pallas kernels  285 us (25%)
  waiting for transfers between devices  226 us (20%)
  local copies, waits for them, and re-layouts  32.3 us (3%)
  between operations  18.2 us (2%)
    ppermute x60, starting transfers between devices, hop(): return lax.ppermute(block, ('section', 'dp'), sorted(pairs))  399 us
    pallas_call x74, Pallas kernels, call(): pl.pallas_call(kernel, out_shape=outs, in_specs=in_specs, out_specs=out_s...  285 us
    ppermute x15, waiting for transfers between devices, shift_z(): return lax.ppermute(block, 'dp', pairs)  113 us
    ppermute x4, starting transfers between devices, spread(): arrived = lax.ppermute(jnp.where(upper, low, high), 'section', pairs)  51.3 us
    ppermute x27, starting transfers between devices, shift_y(): return lax.ppermute(block, 'dp', pairs)  43.7 us
    ppermute x60, waiting for transfers between devices, hop(): return lax.ppermute(block, ('section', 'dp'), sorted(pairs))  39 us
    ppermute x6, waiting for transfers between devices, exchange(): blocks.append(lax.ppermute(blocks[-1], ('section', 'dp'), pairs))  34.3 us
    ppermute x15, starting transfers between devices, shift_z(): return lax.ppermute(block, 'dp', pairs)  33.5 us
  transfers between devices with their start and end apart: 118, of which 38 were waited for; matrix products, arithmetic and copies ran while one was open for 2% of the time, Pallas kernels for 17%

profile of v6, /device:TPU:128, one launch (start us, length us, event | category | flops | bytes accessed | tf_op | source)
XLA Modules:
  0.0 1128.4 jit_solution(5730255973307155965)
XLA Ops:
  7.8 6.5 collective-permute-done.4
  18.1 4.3 collective-permute-done.5
  26.0 3.0 collective-permute-start.1
  29.0 17.0 %collective-permute-done.14.refs_12_ = bf16[192,2304]{1,0:T(8,128)(2,1)S(1)} collective-permute-done((bf16[192,2304]{1,0:T(8,128)(2,1)S(1)}, bf16[192,2304]{1,0:T(8,128)(2,1)S(1)}, u32[]{:S(2)}, u32[]{:S(2)}) %collective-permute-start.14) | collective-permute-done | bytes 884768 | tf_op jit(solution)/shard_map/ppermute | solution.py:329
  46.0 3.3 collective-permute-start.20
  49.3 3.0 collective-permute-start.10
  52.3 19.0 %collective-permute-done.13.refs_11_ = bf16[768,768]{1,0:T(8,128)(2,1)S(1)} collective-permute-done((bf16[768,768]{1,0:T(8,128)(2,1)S(1)}, bf16[768,768]{1,0:T(8,128)(2,1)S(1)}, u32[]{:S(2)}, u32[]{:S(2)}) %collective-permute-start.13) | collective-permute-done | bytes 1179680 | tf_op jit(solution)/shard_map/ppermute | solution.py:329
  71.3 3.3 collective-permute-start.19
  77.8 12.4 %collective-permute-done.20.refs_18_ = bf16[192,2304]{1,0:T(8,128)(2,1)S(1)} collective-permute-done((bf16[192,2304]{1,0:T(8,128)(2,1)S(1)}, bf16[192,2304]{1,0:T(8,128)(2,1)S(1)}, u32[]{:S(2)}, u32[]{:S(2)}) %collective-permute-start.20) | collective-permute-done | bytes 884768 | tf_op jit(solution)/shard_map/ppermute | solution.py:329
  93.7 20.0 %collective-permute-done.19.refs_17_ = bf16[768,768]{1,0:T(8,128)(2,1)} collective-permute-done((bf16[768,768]{1,0:T(8,128)(2,1)S(1)}, bf16[768,768]{1,0:T(8,128)(2,1)}, u32[]{:S(2)}, u32[]{:S(2)}) %collective-permute-start.19) | collective-permute-done | bytes 1179680 | tf_op jit(solution)/shard_map/ppermute | solution.py:329
  113.7 3.1 collective-permute-start.25
  134.4 2.9 collective-permute-start.18
  137.2 6.2 collective-permute-done.11.refs_9_
  146.8 6.0 collective-permute-done.17.refs_15_
  153.3 5.8 collective-permute-done.23.refs_21_
  160.0 7.2 shard_map.93.matrix.source
  184.3 3.1 shard_map.101
  188.0 17.2 %collective-permute-start.33 = (bf16[96,3072]{1,0:T(8,128)(2,1)S(1)}, bf16[96,3072]{1,0:T(8,128)(2,1)S(1)}, u32[]{:S(2)}, u32[]{:S(2)}) collective-permute-start(bf16[96,3072]{1,0:T(8,128)(2,1)S(1)} %get-tuple-element.268), channel_id=1, source_target_pairs={{0,16},{1,17},{2,18},{3,19},{4,20},{5,21},{6,22},{7,23},{8,24},{9,... | collective-permute-start | bytes 1769480 | tf_op jit(solution)/shard_map/ppermute | solution.py:188
  208.5 3.6 collective-permute-start.36
  219.5 77.4 %collective-permute-start.38 = (bf16[96,3072]{1,0:T(8,128)(2,1)}, bf16[96,3072]{1,0:T(8,128)(2,1)S(1)}, u32[]{:S(2)}, u32[]{:S(2)}) collective-permute-start(bf16[96,3072]{1,0:T(8,128)(2,1)} %get-tuple-element.288), channel_id=1, source_target_pairs={{112,128},{113,129},{114,130},{115,131},{116,132},{117,133},{118,1... | collective-permute-start | bytes 1769480 | tf_op jit(solution)/shard_map/ppermute | solution.py:188
  296.9 6.4 copy-done.5
  303.3 5.3 shard_map.110.refs_4_.turned
  309.5 6.0 shard_map.111
  320.0 14.7 %collective-permute-done.43.x_in = bf16[96,3072]{1,0:T(8,128)(2,1)S(1)} collective-permute-done((bf16[96,3072]{1,0:T(8,128)(2,1)S(1)}, bf16[96,3072]{1,0:T(8,128)(2,1)S(1)}, u32[]{:S(2)}, u32[]{:S(2)}) %collective-permute-start.43) | collective-permute-done | bytes 589856 | tf_op jit(solution)/shard_map/ppermute | solution.py:188
  334.7 5.5 shard_map.113
  350.4 4.7 shard_map.119
  355.0 20.8 %collective-permute-start.49 = (bf16[96,3072]{1,0:T(8,128)(2,1)S(1)}, bf16[96,3072]{1,0:T(8,128)(2,1)S(1)}, u32[]{:S(2)}, u32[]{:S(2)}) collective-permute-start(bf16[96,3072]{1,0:T(8,128)(2,1)S(1)} %get-tuple-element.332), channel_id=1, source_target_pairs={{0,16},{1,17},{2,18},{3,19},{4,20},{5,21},{6,22},{7,23},{8,24},{9,... | collective-permute-start | bytes 1769480 | tf_op jit(solution)/shard_map/ppermute | solution.py:188
  386.4 5.6 shard_map.125
  406.3 49.3 %collective-permute-start.65 = (bf16[96,3072]{1,0:T(8,128)(2,1)S(1)}, bf16[96,3072]{1,0:T(8,128)(2,1)S(1)}, u32[]{:S(2)}, u32[]{:S(2)}) collective-permute-start(bf16[96,3072]{1,0:T(8,128)(2,1)S(1)} %get-tuple-element.379), channel_id=1, source_target_pairs={{0,16},{1,17},{2,18},{3,19},{4,20},{5,21},{6,22},{7,23},{8,24},{9,... | collective-permute-start | bytes 1769480 | tf_op jit(solution)/shard_map/ppermute | solution.py:188
  458.7 11.0 collective-permute-start.68
  476.7 4.5 shard_map.140
  481.9 88.7 %collective-permute-start.73 = (bf16[96,3072]{1,0:T(8,128)(2,1)S(1)}, bf16[96,3072]{1,0:T(8,128)(2,1)S(1)}, u32[]{:S(2)}, u32[]{:S(2)}) collective-permute-start(bf16[96,3072]{1,0:T(8,128)(2,1)S(1)} %get-tuple-element.403), channel_id=1, source_target_pairs={{0,16},{1,17},{2,18},{3,19},{4,20},{5,21},{6,22},{7,23},{8,24},{9,... | collective-permute-start | bytes 1769480 | tf_op jit(solution)/shard_map/ppermute | solution.py:188
  572.1 4.6 shard_map.142
  577.4 10.9 collective-permute-start.76
  588.3 20.4 %collective-permute-start.74 = (bf16[96,3072]{1,0:T(8,128)(2,1)S(1)}, bf16[96,3072]{1,0:T(8,128)(2,1)S(1)}, u32[]{:S(2)}, u32[]{:S(2)}) collective-permute-start(bf16[96,3072]{1,0:T(8,128)(2,1)S(1)} %get-tuple-element.406), channel_id=1, source_target_pairs={{112,128},{113,129},{114,130},{115,131},{116,132},{117,133},{118,1... | collective-permute-start | bytes 1769480 | tf_op jit(solution)/shard_map/ppermute | solution.py:188
  608.7 4.6 shard_map.144
  613.3 3.0 collective-permute-done.74.u_in
  617.6 19.6 %collective-permute-start.79 = (bf16[96,3072]{1,0:T(8,128)(2,1)S(1)}, bf16[96,3072]{1,0:T(8,128)(2,1)S(1)}, u32[]{:S(2)}, u32[]{:S(2)}) collective-permute-start(bf16[96,3072]{1,0:T(8,128)(2,1)S(1)} %get-tuple-element.421), channel_id=1, source_target_pairs={{112,128},{113,129},{114,130},{115,131},{116,132},{117,133},{118,1... | collective-permute-start | bytes 1769480 | tf_op jit(solution)/shard_map/ppermute | solution.py:188
  637.8 7.1 collective-permute-done.79.u_in
  654.8 9.6 collective-permute-start.84
  675.0 18.3 %collective-permute-start.89 = (bf16[96,3072]{1,0:T(8,128)(2,1)S(1)}, bf16[96,3072]{1,0:T(8,128)(2,1)S(1)}, u32[]{:S(2)}, u32[]{:S(2)}) collective-permute-start(bf16[96,3072]{1,0:T(8,128)(2,1)S(1)} %get-tuple-element.451), channel_id=1, source_target_pairs={{0,16},{1,17},{2,18},{3,19},{4,20},{5,21},{6,22},{7,23},{8,24},{9,... | collective-permute-start | bytes 1769480 | tf_op jit(solution)/shard_map/ppermute | solution.py:188
  697.7 10.1 collective-permute-start.91
  710.2 6.4 copy-done.3
  718.7 37.4 %shard_map.163 = bf16[2,96,3072]{2,1,0:T(8,128)(2,1)} custom-call(s32[2]{0:T(128)S(1)} %pad_add_fusion.section.here, bf16[96,3072]{1,0:T(8,128)(2,1)} %get-tuple-element.454.refs_2_.refs_0_, bf16[96,3072]{1,0:T(8,128)(2,1)} %get-tuple-element.460.refs_3_.refs_1_), custom_call_target="tpu_custom_call" | custom-call | flops 1 | bytes 1 | tf_op jit(solution)/shard_map/pallas_call | solution.py:27
  758.1 7.8 collective-permute-start.100
  778.0 3.1 shard_map.161
  781.1 7.1 collective-permute-start.92
  788.2 3.8 collective-permute-start.93
  792.0 73.2 %shard_map.166 = bf16[4,96,3072]{2,1,0:T(8,128)(2,1)} custom-call(s32[2]{0:T(128)S(1)} %pad_add_fusion.section.here, bf16[96,3072]{1,0:T(8,128)(2,1)} %copy-done.15, bf16[96,3072]{1,0:T(8,128)(2,1)} %copy-done.16, bf16[96,3072]{1,0:T(8,128)(2,1)} %copy-done.13, bf16[96,3072]{1,0:T(8,128)(2,1)} %copy-done.14), custom_call_target="tpu_custom_call" | custom-call | flops 1 | bytes 1 | tf_op jit(solution)/shard_map/pallas_call | solution.py:27
  875.4 37.4 %shard_map.164 = bf16[4,192,768]{2,1,0:T(8,128)(2,1)} custom-call(s32[2]{0:T(128)S(1)} %pad_add_fusion.section.here, bf16[192,768]{1,0:T(8,128)(2,1)} %get-tuple-element.481.refs_0_, bf16[192,768]{1,0:T(8,128)(2,1)} %copy-done.31, bf16[192,768]{1,0:T(8,128)(2,1)} %copy-done.32, bf16[192,768]{1,0:T(8,128)(2,1)} %copy-done.30), custom_call_target="tpu_custom_call" | custom-call | flops 1 | bytes 1 | tf_op jit(solution)/shard_map/pallas_call | solution.py:27
  914.2 51.0 %collective-permute-start.114 = (bf16[384,1536]{1,0:T(8,128)(2,1)S(1)}, bf16[384,1536]{1,0:T(8,128)(2,1)S(1)}, u32[]{:S(2)}, u32[]{:S(2)}) collective-permute-start(bf16[384,1536]{1,0:T(8,128)(2,1)S(1)} %broadcast_select_fusion), channel_id=1, source_target_pairs={{0,128},{16,144},{32,160},{48,176},{64,192},{80,208},{96,224},{112... | collective-permute-start | bytes 3538952 | tf_op jit(solution)/shard_map/ppermute | solution.py:204
  966.3 37.4 %shard_map.162 = bf16[4,192,768]{2,1,0:T(8,128)(2,1)} custom-call(s32[2]{0:T(128)S(1)} %pad_add_fusion.section.here, bf16[192,768]{1,0:T(8,128)(2,1)} %get-tuple-element.461.refs_0_, bf16[192,768]{1,0:T(8,128)(2,1)} %copy-done.50, bf16[192,768]{1,0:T(8,128)(2,1)} %copy-done.51, bf16[192,768]{1,0:T(8,128)(2,1)} %copy-done.52), custom_call_target="tpu_custom_call" | custom-call | flops 1 | bytes 1 | tf_op jit(solution)/shard_map/pallas_call | solution.py:27
  1007.6 3.0 collective-permute-start.95
  1014.5 23.0 %collective-permute-done.111 = f32[1,3072]{1,0:T(1,128)S(1)} collective-permute-done((f32[1,3072]{1,0:T(1,128)S(1)}, f32[1,3072]{1,0:T(1,128)S(1)}, u32[]{:S(2)}, u32[]{:S(2)}) %collective-permute-start.111) | collective-permute-done | bytes 12320 | tf_op jit(solution)/shard_map/ppermute | solution.py:329
  1038.5 4.0 collective-permute-start.96
  1046.6 7.7 collective-permute-done.115
  1054.7 12.1 %collective-permute-done.96 = bf16[4,192,768]{2,1,0:T(8,128)(2,1)S(1)} collective-permute-done((bf16[4,192,768]{2,1,0:T(8,128)(2,1)S(1)}, bf16[4,192,768]{2,1,0:T(8,128)(2,1)S(1)}, u32[]{:S(2)}, u32[]{:S(2)}) %collective-permute-start.96) | collective-permute-done | bytes 1179680 | tf_op jit(solution)/shard_map/ppermute | solution.py:316
  1066.8 4.5 collective-permute-start.97
  1073.0 22.2 %collective-permute-done.97 = bf16[4,192,768]{2,1,0:T(8,128)(2,1)S(1)} collective-permute-done((bf16[4,192,768]{2,1,0:T(8,128)(2,1)S(1)}, bf16[4,192,768]{2,1,0:T(8,128)(2,1)S(1)}, u32[]{:S(2)}, u32[]{:S(2)}) %collective-permute-start.97) | collective-permute-done | bytes 1179680 | tf_op jit(solution)/shard_map/ppermute | solution.py:316
  1095.3 4.1 bitcast_convert_fusion
  1102.1 2.9 collective-permute-start.106
  1105.7 3.8 collective-permute-done.105
  1109.6 8.6 collective-permute-done.106
  1118.2 8.7 collective-permute-done.107
  (415 shorter events, 185.9 us)
Async XLA Ops:
  1.9 21.5 %collective-permute-start.8 = (bf16[192,2304]{1,0:T(8,128)(2,1)S(1)}, bf16[192,2304]{1,0:T(8,128)(2,1)S(1)}, u32[]{:S(2)}, u32[]{:S(2)}) collective-permute-start(bf16[192,2304]{1,0:T(8,128)(2,1)S(1)} %slice.100.refs_0_), channel_id=1, source_target_pairs={{0,8},{1,9},{2,10},{3,11},{4,0},{5,1},{6,2},{7,3},{8,12},{9,13},{1... | collective-permute-start | bytes 2654216 | tf_op jit(solution)/shard_map/ppermute | solution.py:329
  4.5 9.8 collective-permute-start.4
  6.1 10.1 collective-permute-start.6
  14.7 34.6 %collective-permute-start = (bf16[192,2304]{1,0:T(8,128)(2,1)S(1)}, bf16[192,2304]{1,0:T(8,128)(2,1)S(1)}, u32[]{:S(2)}, u32[]{:S(2)}) collective-permute-start(bf16[192,2304]{1,0:T(8,128)(2,1)S(1)} %slice.100.refs_0_), channel_id=1, source_target_pairs={{0,1},{1,2},{2,3},{3,0},{4,5},{5,6},{6,7},{7,4},{8,9},{9,10},{10,1... | collective-permute-start | bytes 2654216 | tf_op jit(solution)/shard_map/ppermute | solution.py:334
  23.4 22.6 %collective-permute-start.14 = (bf16[192,2304]{1,0:T(8,128)(2,1)S(1)}, bf16[192,2304]{1,0:T(8,128)(2,1)S(1)}, u32[]{:S(2)}, u32[]{:S(2)}) collective-permute-start(bf16[192,2304]{1,0:T(8,128)(2,1)S(1)} %collective-permute-done.8.refs_6_), channel_id=1, source_target_pairs={{0,8},{1,9},{2,10},{3,11},{4,0},{5,1},{6,2},{7,3},{8,12},{9,13},{1... | collective-permute-start | bytes 2654216 | tf_op jit(solution)/shard_map/ppermute | solution.py:329
  25.8 45.5 %collective-permute-start.13 = (bf16[768,768]{1,0:T(8,128)(2,1)S(1)}, bf16[768,768]{1,0:T(8,128)(2,1)S(1)}, u32[]{:S(2)}, u32[]{:S(2)}) collective-permute-start(bf16[768,768]{1,0:T(8,128)(2,1)S(1)} %constant_dynamic-update-slice_fusion.refs_5_), channel_id=1, source_target_pairs={{0,8},{1,9},{2,10},{3,11},{4,0},{5,1},{6,2},{7,3},{8,12},{9,13},{1... | collective-permute-start | bytes 3538952 | tf_op jit(solution)/shard_map/ppermute | solution.py:329
  26.0 48.5 %collective-permute-start.1 = (bf16[192,2304]{1,0:T(8,128)(2,1)S(1)}, bf16[192,2304]{1,0:T(8,128)(2,1)S(1)}, u32[]{:S(2)}, u32[]{:S(2)}) collective-permute-start(bf16[192,2304]{1,0:T(8,128)(2,1)S(1)} %slice.100.refs_0_), channel_id=1, source_target_pairs={{0,3},{1,0},{2,1},{3,2},{4,7},{5,4},{6,5},{7,6},{8,11},{9,8},{10,9... | collective-permute-start | bytes 2654216 | tf_op jit(solution)/shard_map/ppermute | solution.py:334
  29.0 47.1 %collective-permute-start.9 = (bf16[192,2304]{1,0:T(8,128)(2,1)S(1)}, bf16[192,2304]{1,0:T(8,128)(2,1)S(1)}, u32[]{:S(2)}, u32[]{:S(2)}) collective-permute-start(bf16[192,2304]{1,0:T(8,128)(2,1)S(1)} %collective-permute-done.8.refs_6_), channel_id=1, source_target_pairs={{0,1},{1,2},{2,3},{3,0},{4,5},{5,6},{6,7},{7,4},{8,9},{9,10},{10,1... | collective-permute-start | bytes 2654216 | tf_op jit(solution)/shard_map/ppermute | solution.py:334
  46.0 44.2 %collective-permute-start.20 = (bf16[192,2304]{1,0:T(8,128)(2,1)S(1)}, bf16[192,2304]{1,0:T(8,128)(2,1)S(1)}, u32[]{:S(2)}, u32[]{:S(2)}) collective-permute-start(bf16[192,2304]{1,0:T(8,128)(2,1)S(1)} %collective-permute-done.14.refs_12_), channel_id=1, source_target_pairs={{0,8},{1,9},{2,10},{3,11},{4,0},{5,1},{6,2},{7,3},{8,12},{9,13},{1... | collective-permute-start | bytes 2654216 | tf_op jit(solution)/shard_map/ppermute | solution.py:329
  49.3 42.7 %collective-permute-start.10 = (bf16[192,2304]{1,0:T(8,128)(2,1)S(1)}, bf16[192,2304]{1,0:T(8,128)(2,1)S(1)}, u32[]{:S(2)}, u32[]{:S(2)}) collective-permute-start(bf16[192,2304]{1,0:T(8,128)(2,1)S(1)} %collective-permute-done.8.refs_6_), channel_id=1, source_target_pairs={{0,3},{1,0},{2,1},{3,2},{4,7},{5,4},{6,5},{7,6},{8,11},{9,8},{10,9... | collective-permute-start | bytes 2654216 | tf_op jit(solution)/shard_map/ppermute | solution.py:334
  71.3 42.4 %collective-permute-start.19 = (bf16[768,768]{1,0:T(8,128)(2,1)S(1)}, bf16[768,768]{1,0:T(8,128)(2,1)}, u32[]{:S(2)}, u32[]{:S(2)}) collective-permute-start(bf16[768,768]{1,0:T(8,128)(2,1)S(1)} %collective-permute-done.13.refs_11_), channel_id=1, source_target_pairs={{0,8},{1,9},{2,10},{3,11},{4,0},{5,1},{6,2},{7,3},{8,12},{9,13},{1... | collective-permute-start | bytes 3538952 | tf_op jit(solution)/shard_map/ppermute | solution.py:329
  74.5 44.7 %collective-permute-start.15 = (bf16[192,2304]{1,0:T(8,128)(2,1)S(1)}, bf16[192,2304]{1,0:T(8,128)(2,1)S(1)}, u32[]{:S(2)}, u32[]{:S(2)}) collective-permute-start(bf16[192,2304]{1,0:T(8,128)(2,1)S(1)} %collective-permute-done.14.refs_12_), channel_id=1, source_target_pairs={{0,1},{1,2},{2,3},{3,0},{4,5},{5,6},{6,7},{7,4},{8,9},{9,10},{10,1... | collective-permute-start | bytes 2654216 | tf_op jit(solution)/shard_map/ppermute | solution.py:334
  76.1 44.8 %collective-permute-start.16 = (bf16[192,2304]{1,0:T(8,128)(2,1)S(1)}, bf16[192,2304]{1,0:T(8,128)(2,1)}, u32[]{:S(2)}, u32[]{:S(2)}) collective-permute-start(bf16[192,2304]{1,0:T(8,128)(2,1)S(1)} %collective-permute-done.14.refs_12_), channel_id=1, source_target_pairs={{0,3},{1,0},{2,1},{3,2},{4,7},{5,4},{6,5},{7,6},{8,11},{9,8},{10,9... | collective-permute-start | bytes 2654216 | tf_op jit(solution)/shard_map/ppermute | solution.py:334
  90.2 32.5 %collective-permute-start.21 = (bf16[192,2304]{1,0:T(8,128)(2,1)S(1)}, bf16[192,2304]{1,0:T(8,128)(2,1)}, u32[]{:S(2)}, u32[]{:S(2)}) collective-permute-start(bf16[192,2304]{1,0:T(8,128)(2,1)S(1)} %collective-permute-done.20.refs_18_), channel_id=1, source_target_pairs={{0,1},{1,2},{2,3},{3,0},{4,5},{5,6},{6,7},{7,4},{8,9},{9,10},{10,1... | collective-permute-start | bytes 2654216 | tf_op jit(solution)/shard_map/ppermute | solution.py:334
  92.0 31.1 %collective-permute-start.22 = (bf16[192,2304]{1,0:T(8,128)(2,1)S(1)}, bf16[192,2304]{1,0:T(8,128)(2,1)}, u32[]{:S(2)}, u32[]{:S(2)}) collective-permute-start(bf16[192,2304]{1,0:T(8,128)(2,1)S(1)} %collective-permute-done.20.refs_18_), channel_id=1, source_target_pairs={{0,3},{1,0},{2,1},{3,2},{4,7},{5,4},{6,5},{7,6},{8,11},{9,8},{10,9... | collective-permute-start | bytes 2654216 | tf_op jit(solution)/shard_map/ppermute | solution.py:334
  113.7 45.5 %collective-permute-start.25 = (bf16[768,768]{1,0:T(8,128)(2,1)}, bf16[768,768]{1,0:T(8,128)(2,1)}, u32[]{:S(2)}, u32[]{:S(2)}) collective-permute-start(bf16[768,768]{1,0:T(8,128)(2,1)} %collective-permute-done.19.refs_17_), channel_id=1, source_target_pairs={{0,8},{1,9},{2,10},{3,11},{4,0},{5,1},{6,2},{7,3},{8,12},{9,13},{1... | collective-permute-start | bytes 3538952 | tf_op jit(solution)/shard_map/ppermute | solution.py:329
  119.3 14.6 %collective-permute-start.2 = (bf16[96,2304]{1,0:T(8,128)(2,1)}, bf16[96,2304]{1,0:T(8,128)(2,1)S(1)}, u32[]{:S(2)}, u32[]{:S(2)}) collective-permute-start(bf16[96,2304]{1,0:T(8,128)(2,1)} %slice.101), channel_id=1, source_target_pairs={{0,1},{1,2},{2,3},{3,0},{4,5},{5,6},{6,7},{7,4},{8,9},{9,10},{10,1... | collective-permute-start | bytes 1327112 | tf_op jit(solution)/shard_map/ppermute | solution.py:334
  121.0 13.4 %collective-permute-start.3 = (bf16[96,2304]{1,0:T(8,128)(2,1)}, bf16[96,2304]{1,0:T(8,128)(2,1)S(1)}, u32[]{:S(2)}, u32[]{:S(2)}) collective-permute-start(bf16[96,2304]{1,0:T(8,128)(2,1)} %slice.102), channel_id=1, source_target_pairs={{0,3},{1,0},{2,1},{3,2},{4,7},{5,4},{6,5},{7,6},{8,11},{9,8},{10,9... | collective-permute-start | bytes 1327112 | tf_op jit(solution)/shard_map/ppermute | solution.py:334
  122.7 20.7 %collective-permute-start.11 = (bf16[96,2304]{1,0:T(8,128)(2,1)}, bf16[96,2304]{1,0:T(8,128)(2,1)S(1)}, u32[]{:S(2)}, u32[]{:S(2)}) collective-permute-start(bf16[96,2304]{1,0:T(8,128)(2,1)} %slice.106), channel_id=1, source_target_pairs={{0,1},{1,2},{2,3},{3,0},{4,5},{5,6},{6,7},{7,4},{8,9},{9,10},{10,1... | collective-permute-start | bytes 1327112 | tf_op jit(solution)/shard_map/ppermute | solution.py:334
  123.1 20.8 %collective-permute-start.12 = (bf16[96,2304]{1,0:T(8,128)(2,1)S(1)}, bf16[96,2304]{1,0:T(8,128)(2,1)S(1)}, u32[]{:S(2)}, u32[]{:S(2)}) collective-permute-start(bf16[96,2304]{1,0:T(8,128)(2,1)S(1)} %slice.107), channel_id=1, source_target_pairs={{0,3},{1,0},{2,1},{3,2},{4,7},{5,4},{6,5},{7,6},{8,11},{9,8},{10,9... | collective-permute-start | bytes 1327112 | tf_op jit(solution)/shard_map/ppermute | solution.py:334
  133.9 19.0 %collective-permute-start.17 = (bf16[96,2304]{1,0:T(8,128)(2,1)S(1)}, bf16[96,2304]{1,0:T(8,128)(2,1)S(1)}, u32[]{:S(2)}, u32[]{:S(2)}) collective-permute-start(bf16[96,2304]{1,0:T(8,128)(2,1)S(1)} %slice.108), channel_id=1, source_target_pairs={{0,1},{1,2},{2,3},{3,0},{4,5},{5,6},{6,7},{7,4},{8,9},{9,10},{10,1... | collective-permute-start | bytes 1327112 | tf_op jit(solution)/shard_map/ppermute | solution.py:334
  134.4 19.0 %collective-permute-start.18 = (bf16[96,2304]{1,0:T(8,128)(2,1)S(1)}, bf16[96,2304]{1,0:T(8,128)(2,1)S(1)}, u32[]{:S(2)}, u32[]{:S(2)}) collective-permute-start(bf16[96,2304]{1,0:T(8,128)(2,1)S(1)} %slice.109), channel_id=1, source_target_pairs={{0,3},{1,0},{2,1},{3,2},{4,7},{5,4},{6,5},{7,6},{8,11},{9,8},{10,9... | collective-permute-start | bytes 1327112 | tf_op jit(solution)/shard_map/ppermute | solution.py:334
  143.4 15.7 %collective-permute-start.23 = (bf16[96,2304]{1,0:T(8,128)(2,1)S(1)}, bf16[96,2304]{1,0:T(8,128)(2,1)S(1)}, u32[]{:S(2)}, u32[]{:S(2)}) collective-permute-start(bf16[96,2304]{1,0:T(8,128)(2,1)S(1)} %slice.110), channel_id=1, source_target_pairs={{0,1},{1,2},{2,3},{3,0},{4,5},{5,6},{6,7},{7,4},{8,9},{9,10},{10,1... | collective-permute-start | bytes 1327112 | tf_op jit(solution)/shard_map/ppermute | solution.py:334
  143.8 15.4 %collective-permute-start.24 = (bf16[96,2304]{1,0:T(8,128)(2,1)S(1)}, bf16[96,2304]{1,0:T(8,128)(2,1)S(1)}, u32[]{:S(2)}, u32[]{:S(2)}) collective-permute-start(bf16[96,2304]{1,0:T(8,128)(2,1)S(1)} %slice.111), channel_id=1, source_target_pairs={{0,3},{1,0},{2,1},{3,2},{4,7},{5,4},{6,5},{7,6},{8,11},{9,8},{10,9... | collective-permute-start | bytes 1327112 | tf_op jit(solution)/shard_map/ppermute | solution.py:334
  188.0 18.8 %collective-permute-start.33 = (bf16[96,3072]{1,0:T(8,128)(2,1)S(1)}, bf16[96,3072]{1,0:T(8,128)(2,1)S(1)}, u32[]{:S(2)}, u32[]{:S(2)}) collective-permute-start(bf16[96,3072]{1,0:T(8,128)(2,1)S(1)} %get-tuple-element.268), channel_id=1, source_target_pairs={{0,16},{1,17},{2,18},{3,19},{4,20},{5,21},{6,22},{7,23},{8,24},{9,... | collective-permute-start | bytes 1769480 | tf_op jit(solution)/shard_map/ppermute | solution.py:188
  218.8 89.9 %collective-permute-start.40 = (bf16[96,3072]{1,0:T(8,128)(2,1)S(1)}, bf16[96,3072]{1,0:T(8,128)(2,1)S(1)}, u32[]{:S(2)}, u32[]{:S(2)}) collective-permute-start(bf16[96,3072]{1,0:T(8,128)(2,1)S(1)} %get-tuple-element.295), channel_id=1, source_target_pairs={{32,48},{33,49},{34,50},{35,51},{36,52},{37,53},{38,54},{39,55},{4... | collective-permute-start | bytes 1769480 | tf_op jit(solution)/shard_map/ppermute | solution.py:188
  219.5 90.0 %collective-permute-start.38 = (bf16[96,3072]{1,0:T(8,128)(2,1)}, bf16[96,3072]{1,0:T(8,128)(2,1)S(1)}, u32[]{:S(2)}, u32[]{:S(2)}) collective-permute-start(bf16[96,3072]{1,0:T(8,128)(2,1)} %get-tuple-element.288), channel_id=1, source_target_pairs={{112,128},{113,129},{114,130},{115,131},{116,132},{117,133},{118,1... | collective-permute-start | bytes 1769480 | tf_op jit(solution)/shard_map/ppermute | solution.py:188
  317.4 17.3 %collective-permute-start.43 = (bf16[96,3072]{1,0:T(8,128)(2,1)S(1)}, bf16[96,3072]{1,0:T(8,128)(2,1)S(1)}, u32[]{:S(2)}, u32[]{:S(2)}) collective-permute-start(bf16[96,3072]{1,0:T(8,128)(2,1)S(1)} %get-tuple-element.308), channel_id=1, source_target_pairs={{112,128},{113,129},{114,130},{115,131},{116,132},{117,133},{118,1... | collective-permute-start | bytes 1769480 | tf_op jit(solution)/shard_map/ppermute | solution.py:188
  355.0 22.4 %collective-permute-start.49 = (bf16[96,3072]{1,0:T(8,128)(2,1)S(1)}, bf16[96,3072]{1,0:T(8,128)(2,1)S(1)}, u32[]{:S(2)}, u32[]{:S(2)}) collective-permute-start(bf16[96,3072]{1,0:T(8,128)(2,1)S(1)} %get-tuple-element.332), channel_id=1, source_target_pairs={{0,16},{1,17},{2,18},{3,19},{4,20},{5,21},{6,22},{7,23},{8,24},{9,... | collective-permute-start | bytes 1769480 | tf_op jit(solution)/shard_map/ppermute | solution.py:188
  406.3 51.2 %collective-permute-start.65 = (bf16[96,3072]{1,0:T(8,128)(2,1)S(1)}, bf16[96,3072]{1,0:T(8,128)(2,1)S(1)}, u32[]{:S(2)}, u32[]{:S(2)}) collective-permute-start(bf16[96,3072]{1,0:T(8,128)(2,1)S(1)} %get-tuple-element.379), channel_id=1, source_target_pairs={{0,16},{1,17},{2,18},{3,19},{4,20},{5,21},{6,22},{7,23},{8,24},{9,... | collective-permute-start | bytes 1769480 | tf_op jit(solution)/shard_map/ppermute | solution.py:188
  458.7 12.7 %collective-permute-start.68 = (bf16[96,3072]{1,0:T(8,128)(2,1)S(1)}, bf16[96,3072]{1,0:T(8,128)(2,1)S(1)}, u32[]{:S(2)}, u32[]{:S(2)}) collective-permute-start(bf16[96,3072]{1,0:T(8,128)(2,1)S(1)} %get-tuple-element.387), channel_id=1, source_target_pairs={{0,16},{1,17},{2,18},{3,19},{4,20},{5,21},{6,22},{7,23},{8,24},{9,... | collective-permute-start | bytes 1769480 | tf_op jit(solution)/shard_map/ppermute | solution.py:188
  481.9 90.3 %collective-permute-start.73 = (bf16[96,3072]{1,0:T(8,128)(2,1)S(1)}, bf16[96,3072]{1,0:T(8,128)(2,1)S(1)}, u32[]{:S(2)}, u32[]{:S(2)}) collective-permute-start(bf16[96,3072]{1,0:T(8,128)(2,1)S(1)} %get-tuple-element.403), channel_id=1, source_target_pairs={{0,16},{1,17},{2,18},{3,19},{4,20},{5,21},{6,22},{7,23},{8,24},{9,... | collective-permute-start | bytes 1769480 | tf_op jit(solution)/shard_map/ppermute | solution.py:188
  577.4 31.3 %collective-permute-start.76 = (bf16[96,3072]{1,0:T(8,128)(2,1)S(1)}, bf16[96,3072]{1,0:T(8,128)(2,1)S(1)}, u32[]{:S(2)}, u32[]{:S(2)}) collective-permute-start(bf16[96,3072]{1,0:T(8,128)(2,1)S(1)} %get-tuple-element.411), channel_id=1, source_target_pairs={{0,16},{1,17},{2,18},{3,19},{4,20},{5,21},{6,22},{7,23},{8,24},{9,... | collective-permute-start | bytes 1769480 | tf_op jit(solution)/shard_map/ppermute | solution.py:188
  588.3 28.0 %collective-permute-start.74 = (bf16[96,3072]{1,0:T(8,128)(2,1)S(1)}, bf16[96,3072]{1,0:T(8,128)(2,1)S(1)}, u32[]{:S(2)}, u32[]{:S(2)}) collective-permute-start(bf16[96,3072]{1,0:T(8,128)(2,1)S(1)} %get-tuple-element.406), channel_id=1, source_target_pairs={{112,128},{113,129},{114,130},{115,131},{116,132},{117,133},{118,1... | collective-permute-start | bytes 1769480 | tf_op jit(solution)/shard_map/ppermute | solution.py:188
  616.9 20.3 %collective-permute-start.77 = (bf16[96,3072]{1,0:T(8,128)(2,1)S(1)}, bf16[96,3072]{1,0:T(8,128)(2,1)S(1)}, u32[]{:S(2)}, u32[]{:S(2)}) collective-permute-start(bf16[96,3072]{1,0:T(8,128)(2,1)S(1)} %get-tuple-element.415), channel_id=1, source_target_pairs={{32,48},{33,49},{34,50},{35,51},{36,52},{37,53},{38,54},{39,55},{4... | collective-permute-start | bytes 1769480 | tf_op jit(solution)/shard_map/ppermute | solution.py:188
  617.6 27.3 %collective-permute-start.79 = (bf16[96,3072]{1,0:T(8,128)(2,1)S(1)}, bf16[96,3072]{1,0:T(8,128)(2,1)S(1)}, u32[]{:S(2)}, u32[]{:S(2)}) collective-permute-start(bf16[96,3072]{1,0:T(8,128)(2,1)S(1)} %get-tuple-element.421), channel_id=1, source_target_pairs={{112,128},{113,129},{114,130},{115,131},{116,132},{117,133},{118,1... | collective-permute-start | bytes 1769480 | tf_op jit(solution)/shard_map/ppermute | solution.py:188
  654.8 11.2 collective-permute-start.84
  675.0 19.9 %collective-permute-start.89 = (bf16[96,3072]{1,0:T(8,128)(2,1)S(1)}, bf16[96,3072]{1,0:T(8,128)(2,1)S(1)}, u32[]{:S(2)}, u32[]{:S(2)}) collective-permute-start(bf16[96,3072]{1,0:T(8,128)(2,1)S(1)} %get-tuple-element.451), channel_id=1, source_target_pairs={{0,16},{1,17},{2,18},{3,19},{4,20},{5,21},{6,22},{7,23},{8,24},{9,... | collective-permute-start | bytes 1769480 | tf_op jit(solution)/shard_map/ppermute | solution.py:188
  697.7 12.5 %collective-permute-start.91 = (bf16[96,3072]{1,0:T(8,128)(2,1)}, bf16[96,3072]{1,0:T(8,128)(2,1)S(1)}, u32[]{:S(2)}, u32[]{:S(2)}) collective-permute-start(bf16[96,3072]{1,0:T(8,128)(2,1)} %get-tuple-element.457), channel_id=1, source_target_pairs={{0,16},{1,17},{2,18},{3,19},{4,20},{5,21},{6,22},{7,23},{8,24},{9,... | collective-permute-start | bytes 1769480 | tf_op jit(solution)/shard_map/ppermute | solution.py:188
  758.1 107.0 %collective-permute-start.100 = (bf16[192,768]{1,0:T(8,128)(2,1)S(1)}, bf16[192,768]{1,0:T(8,128)(2,1)S(1)}, u32[]{:S(2)}, u32[]{:S(2)}) collective-permute-start(bf16[192,768]{1,0:T(8,128)(2,1)S(1)} %get-tuple-element.478), channel_id=1, source_target_pairs={{0,4},{1,5},{2,6},{3,7},{4,12},{5,13},{6,14},{7,15},{8,0},{9,1},{1... | collective-permute-start | bytes 884744 | tf_op jit(solution)/shard_map/ppermute | solution.py:329
  765.9 101.9 %collective-permute-start.98 = (bf16[192,768]{1,0:T(8,128)(2,1)S(1)}, bf16[192,768]{1,0:T(8,128)(2,1)S(1)}, u32[]{:S(2)}, u32[]{:S(2)}) collective-permute-start(bf16[192,768]{1,0:T(8,128)(2,1)S(1)} %get-tuple-element.480), channel_id=1, source_target_pairs={{0,8},{1,9},{2,10},{3,11},{4,0},{5,1},{6,2},{7,3},{8,12},{9,13},{1... | collective-permute-start | bytes 884744 | tf_op jit(solution)/shard_map/ppermute | solution.py:329
  766.7 101.2 %collective-permute-start.99 = (bf16[192,768]{1,0:T(8,128)(2,1)S(1)}, bf16[192,768]{1,0:T(8,128)(2,1)S(1)}, u32[]{:S(2)}, u32[]{:S(2)}) collective-permute-start(bf16[192,768]{1,0:T(8,128)(2,1)S(1)} %get-tuple-element.479), channel_id=1, source_target_pairs={{0,12},{1,13},{2,14},{3,15},{4,8},{5,9},{6,10},{7,11},{8,4},{9,5},... | collective-permute-start | bytes 884744 | tf_op jit(solution)/shard_map/ppermute | solution.py:329
  781.1 131.9 %collective-permute-start.92 = (bf16[192,768]{1,0:T(8,128)(2,1)}, bf16[192,768]{1,0:T(8,128)(2,1)S(1)}, u32[]{:S(2)}, u32[]{:S(2)}) collective-permute-start(bf16[192,768]{1,0:T(8,128)(2,1)} %get-tuple-element.462), channel_id=1, source_target_pairs={{128,129},{129,130},{130,131},{131,128},{132,133},{133,134},{134,1... | collective-permute-start | bytes 884744 | tf_op jit(solution)/shard_map/ppermute | solution.py:312
  788.2 126.0 %collective-permute-start.93 = (bf16[192,768]{1,0:T(8,128)(2,1)}, bf16[192,768]{1,0:T(8,128)(2,1)S(1)}, u32[]{:S(2)}, u32[]{:S(2)}) collective-permute-start(bf16[192,768]{1,0:T(8,128)(2,1)} %get-tuple-element.463), channel_id=1, source_target_pairs={{128,130},{129,131},{130,128},{131,129},{132,134},{133,135},{134,1... | collective-permute-start | bytes 884744 | tf_op jit(solution)/shard_map/ppermute | solution.py:312
  865.1 100.0 %collective-permute-start.94 = (bf16[192,768]{1,0:T(8,128)(2,1)S(1)}, bf16[192,768]{1,0:T(8,128)(2,1)S(1)}, u32[]{:S(2)}, u32[]{:S(2)}) collective-permute-start(bf16[192,768]{1,0:T(8,128)(2,1)S(1)} %copy-done.58), channel_id=1, source_target_pairs={{128,131},{129,128},{130,129},{131,130},{132,135},{133,132},{134,1... | collective-permute-start | bytes 884744 | tf_op jit(solution)/shard_map/ppermute | solution.py:312
  870.6 134.8 %collective-permute-start.108 = (f32[1,3072]{1,0:T(1,128)S(1)}, f32[1,3072]{1,0:T(1,128)S(1)}, u32[]{:S(2)}, u32[]{:S(2)}) collective-permute-start(f32[1,3072]{1,0:T(1,128)S(1)} %add.187), channel_id=1, source_target_pairs={{0,1},{1,2},{2,3},{3,0},{4,5},{5,6},{6,7},{7,4},{8,9},{9,10},{10,1... | collective-permute-start | bytes 36872 | tf_op jit(solution)/shard_map/ppermute | solution.py:334
  871.9 135.7 %collective-permute-start.109 = (f32[1,3072]{1,0:T(1,128)S(1)}, f32[1,3072]{1,0:T(1,128)S(1)}, u32[]{:S(2)}, u32[]{:S(2)}) collective-permute-start(f32[1,3072]{1,0:T(1,128)S(1)} %add.187), channel_id=1, source_target_pairs={{0,2},{1,3},{2,0},{3,1},{4,6},{5,7},{6,4},{7,5},{8,10},{9,11},{10,... | collective-permute-start | bytes 36872 | tf_op jit(solution)/shard_map/ppermute | solution.py:334
  913.0 97.7 %collective-permute-start.110 = (f32[1,3072]{1,0:T(1,128)S(1)}, f32[1,3072]{1,0:T(1,128)S(1)}, u32[]{:S(2)}, u32[]{:S(2)}) collective-permute-start(f32[1,3072]{1,0:T(1,128)S(1)} %add.187), channel_id=1, source_target_pairs={{0,3},{1,0},{2,1},{3,2},{4,7},{5,4},{6,5},{7,6},{8,11},{9,8},{10,9... | collective-permute-start | bytes 36872 | tf_op jit(solution)/shard_map/ppermute | solution.py:334
  914.2 98.5 %collective-permute-start.114 = (bf16[384,1536]{1,0:T(8,128)(2,1)S(1)}, bf16[384,1536]{1,0:T(8,128)(2,1)S(1)}, u32[]{:S(2)}, u32[]{:S(2)}) collective-permute-start(bf16[384,1536]{1,0:T(8,128)(2,1)S(1)} %broadcast_select_fusion), channel_id=1, source_target_pairs={{0,128},{16,144},{32,160},{48,176},{64,192},{80,208},{96,224},{112... | collective-permute-start | bytes 3538952 | tf_op jit(solution)/shard_map/ppermute | solution.py:204
  965.1 78.0 %collective-permute-start.101 = (bf16[768,768]{1,0:T(8,128)(2,1)}, bf16[768,768]{1,0:T(8,128)(2,1)S(1)}, u32[]{:S(2)}, u32[]{:S(2)}) collective-permute-start(bf16[768,768]{1,0:T(8,128)(2,1)} %bitcast.85), channel_id=1, source_target_pairs={{0,1},{1,2},{2,3},{3,0},{4,5},{5,6},{6,7},{7,4},{8,9},{9,10},{10,1... | collective-permute-start | bytes 3538952 | tf_op jit(solution)/shard_map/ppermute | solution.py:334
  1005.4 38.7 %collective-permute-start.103 = (bf16[768,768]{1,0:T(8,128)(2,1)S(1)}, bf16[768,768]{1,0:T(8,128)(2,1)S(1)}, u32[]{:S(2)}, u32[]{:S(2)}) collective-permute-start(bf16[768,768]{1,0:T(8,128)(2,1)S(1)} %bitcast.86), channel_id=1, source_target_pairs={{0,3},{1,0},{2,1},{3,2},{4,7},{5,4},{6,5},{7,6},{8,11},{9,8},{10,9... | collective-permute-start | bytes 3538952 | tf_op jit(solution)/shard_map/ppermute | solution.py:334
  1007.6 30.9 %collective-permute-start.95 = (bf16[4,192,768]{2,1,0:T(8,128)(2,1)S(1)}, bf16[4,192,768]{2,1,0:T(8,128)(2,1)S(1)}, u32[]{:S(2)}, u32[]{:S(2)}) collective-permute-start(bf16[4,192,768]{2,1,0:T(8,128)(2,1)S(1)} %copy-done.21), channel_id=1, source_target_pairs={{128,136},{129,137},{130,138},{131,139},{132,128},{133,129},{134,1... | collective-permute-start | bytes 3538952 | tf_op jit(solution)/shard_map/ppermute | solution.py:316
  1010.7 26.8 %collective-permute-start.111 = (f32[1,3072]{1,0:T(1,128)S(1)}, f32[1,3072]{1,0:T(1,128)S(1)}, u32[]{:S(2)}, u32[]{:S(2)}) collective-permute-start(f32[1,3072]{1,0:T(1,128)S(1)} %add_add_fusion.1), channel_id=1, source_target_pairs={{0,8},{1,9},{2,10},{3,11},{4,0},{5,1},{6,2},{7,3},{8,12},{9,13},{1... | collective-permute-start | bytes 36872 | tf_op jit(solution)/shard_map/ppermute | solution.py:329
  1012.6 25.7 %collective-permute-start.112 = (f32[1,3072]{1,0:T(1,128)S(1)}, f32[1,3072]{1,0:T(1,128)S(1)}, u32[]{:S(2)}, u32[]{:S(2)}) collective-permute-start(f32[1,3072]{1,0:T(1,128)S(1)} %add_add_fusion.1), channel_id=1, source_target_pairs={{0,12},{1,13},{2,14},{3,15},{4,8},{5,9},{6,10},{7,11},{8,4},{9,5},... | collective-permute-start | bytes 36872 | tf_op jit(solution)/shard_map/ppermute | solution.py:329
  1038.4 16.0 %collective-permute-start.115 = (bf16[384,768]{1,0:T(8,128)(2,1)S(1)}, bf16[384,768]{1,0:T(8,128)(2,1)S(1)}, u32[]{:S(2)}, u32[]{:S(2)}) collective-permute-start(bf16[384,768]{1,0:T(8,128)(2,1)S(1)} %broadcast_select_fusion.1), channel_id=1, source_target_pairs={{0,64},{16,80},{32,96},{48,112},{64,0},{80,16},{96,32},{112,48},{1... | collective-permute-start | bytes 1769480 | tf_op jit(solution)/shard_map/ppermute | solution.py:204
  1038.5 28.3 %collective-permute-start.96 = (bf16[4,192,768]{2,1,0:T(8,128)(2,1)S(1)}, bf16[4,192,768]{2,1,0:T(8,128)(2,1)S(1)}, u32[]{:S(2)}, u32[]{:S(2)}) collective-permute-start(bf16[4,192,768]{2,1,0:T(8,128)(2,1)S(1)} %collective-permute-done.95), channel_id=1, source_target_pairs={{128,136},{129,137},{130,138},{131,139},{132,128},{133,129},{134,1... | collective-permute-start | bytes 3538952 | tf_op jit(solution)/shard_map/ppermute | solution.py:316
  1043.2 28.3 %collective-permute-start.102 = (bf16[384,768]{1,0:T(8,128)(2,1)S(1)}, bf16[384,768]{1,0:T(8,128)(2,1)S(1)}, u32[]{:S(2)}, u32[]{:S(2)}) collective-permute-start(bf16[384,768]{1,0:T(8,128)(2,1)S(1)} %slice.112), channel_id=1, source_target_pairs={{0,1},{1,2},{2,3},{3,0},{4,5},{5,6},{6,7},{7,4},{8,9},{9,10},{10,1... | collective-permute-start | bytes 1769480 | tf_op jit(solution)/shard_map/ppermute | solution.py:334
  1044.2 27.3 %collective-permute-start.104 = (bf16[384,768]{1,0:T(8,128)(2,1)S(1)}, bf16[384,768]{1,0:T(8,128)(2,1)S(1)}, u32[]{:S(2)}, u32[]{:S(2)}) collective-permute-start(bf16[384,768]{1,0:T(8,128)(2,1)S(1)} %slice.113), channel_id=1, source_target_pairs={{0,3},{1,0},{2,1},{3,2},{4,7},{5,4},{6,5},{7,6},{8,11},{9,8},{10,9... | collective-permute-start | bytes 1769480 | tf_op jit(solution)/shard_map/ppermute | solution.py:334
  1054.6 17.0 %collective-permute-start.116 = (bf16[384,384]{1,0:T(8,128)(2,1)S(1)}, bf16[384,384]{1,0:T(8,128)(2,1)S(1)}, u32[]{:S(2)}, u32[]{:S(2)}) collective-permute-start(bf16[384,384]{1,0:T(8,128)(2,1)S(1)} %broadcast_select_fusion.2), channel_id=1, source_target_pairs={{0,32},{16,48},{32,0},{48,16},{64,96},{80,112},{96,64},{112,80},{1... | collective-permute-start | bytes 884744 | tf_op jit(solution)/shard_map/ppermute | solution.py:204
  1066.8 28.4 %collective-permute-start.97 = (bf16[4,192,768]{2,1,0:T(8,128)(2,1)S(1)}, bf16[4,192,768]{2,1,0:T(8,128)(2,1)S(1)}, u32[]{:S(2)}, u32[]{:S(2)}) collective-permute-start(bf16[4,192,768]{2,1,0:T(8,128)(2,1)S(1)} %collective-permute-done.96), channel_id=1, source_target_pairs={{128,136},{129,137},{130,138},{131,139},{132,128},{133,129},{134,1... | collective-permute-start | bytes 3538952 | tf_op jit(solution)/shard_map/ppermute | solution.py:316
  1071.9 30.0 %collective-permute-start.117 = (bf16[384,192]{1,0:T(8,128)(2,1)S(1)}, bf16[384,192]{1,0:T(8,128)(2,1)S(1)}, u32[]{:S(2)}, u32[]{:S(2)}) collective-permute-start(bf16[384,192]{1,0:T(8,128)(2,1)S(1)} %broadcast_select_fusion.3), channel_id=1, source_target_pairs={{0,16},{16,0},{32,48},{48,32},{64,80},{80,64},{96,112},{112,96},{1... | collective-permute-start | bytes 442376 | tf_op jit(solution)/shard_map/ppermute | solution.py:204
  1099.7 9.8 collective-permute-start.105
  1102.1 16.1 %collective-permute-start.106 = (bf16[192,768]{1,0:T(8,128)(2,1)S(1)}, bf16[192,768]{1,0:T(8,128)(2,1)S(1)}, u32[]{:S(2)}, u32[]{:S(2)}) collective-permute-start(bf16[192,768]{1,0:T(8,128)(2,1)S(1)} %get-tuple-element.475), channel_id=1, source_target_pairs={{0,12},{1,13},{2,14},{3,15},{4,8},{5,9},{6,10},{7,11},{8,4},{9,5},... | collective-permute-start | bytes 884744 | tf_op jit(solution)/shard_map/ppermute | solution.py:329
  1105.7 21.2 %collective-permute-start.107 = (bf16[192,768]{1,0:T(8,128)(2,1)S(1)}, bf16[192,768]{1,0:T(8,128)(2,1)S(1)}, u32[]{:S(2)}, u32[]{:S(2)}) collective-permute-start(bf16[192,768]{1,0:T(8,128)(2,1)S(1)} %get-tuple-element.474), channel_id=1, source_target_pairs={{0,4},{1,5},{2,6},{3,7},{4,12},{5,13},{6,14},{7,15},{8,0},{9,1},{1... | collective-permute-start | bytes 884744 | tf_op jit(solution)/shard_map/ppermute | solution.py:329
  (113 other events, 1832.2 us)

commit v7 on v6

--- a/solution.py
+++ b/solution.py
@@ -189,7 +189,7 @@
 
 
 def order(sections, micros):
-    return [(t + i, m) for t in range(0, sections, 2) for m in range(micros) for i in (0, 1)]
+    return [(t, m) for t in range(sections) for m in range(micros)]
 
 
 def spread(block, sections, section):
@@ -278,27 +278,31 @@
 
 
 def pile_kernel(low, high, here, *refs):
-    *parts, out, sems = refs
+    *parts, out, held, sems = refs
 
     @pl.when((here[0] >= low) & (here[0] < high))
     def _():
         copies = [
-            pltpu.make_async_copy(part, out.at[k], sems.at[k]) for k, part in enumerate(parts)
+            pltpu.make_async_copy(part, held.at[k], sems.at[k]) for k, part in enumerate(parts)
         ]
         for copy in copies:
             copy.start()
         for copy in copies:
             copy.wait()
+        store = pltpu.make_async_copy(held, out, sems.at[0])
+        store.start()
+        store.wait()
 
 
 def pile(parts, here, low, high):
+    shape = (len(parts), *parts[0].shape)
     return call(
         functools.partial(pile_kernel, low, high),
-        pltpu.HBM((len(parts), *parts[0].shape), BF),
+        pltpu.HBM(shape, BF),
         [SMEM] + [HBM] * len(parts),
         HBM,
         {},
-        [pltpu.SemaphoreType.DMA((len(parts),))],
+        [pltpu.VMEM(shape, BF), pltpu.SemaphoreType.DMA((len(parts),))],
         [here, *(in_hbm(part) for part in parts)],
     )
 
@@ -403,34 +407,27 @@
 
     kept = [()] * micros
     current = [inputs] * micros
-    earlier, held = None, ()
+    held = ()
     for t, m in order(sections, micros):
         if t == half and not held:
             turned = turn(matrix)
             held = (turned,)
-        after = () if earlier in (None, m) else (in_hbm(kept[earlier][0]),)
         result, *kept[m] = forward(
-            t, m, here, current[m], gain_row, matrix, kept[m], after, held if (t, m) == (half, 0) else ()
+            t, m, here, current[m], gain_row, matrix, kept[m], (), held if (t, m) == (half, 0) else ()
         )
         current[m] = hop(result, t, half, count) if t + 1 < sections else result
-        earlier = m
 
     normed = [kept[m][1] for m in range(micros)]
     early = exchange(normed, here, 0, EARLY, count)
     passed = [()] * micros
     arriving = [upstream] * micros
-    earlier = None
     for step, m in order(sections, micros):
         t = sections - 1 - step
-        if step == 0:
-            after = (in_hbm(early[-1]),)
-        else:
-            after = () if earlier == m else (in_hbm(passed[earlier][0]),)
+        after = () if step else (in_hbm(early[-1]),)
         result, *passed[m] = backward(
             t, m, here, arriving[m], kept[m][0], kept[m][2], gain_row, turned, passed[m], after
         )
         arriving[m] = hop(result, t - 1, half, count) if t else result
-        earlier = m
     ended = [passed[m][0] for m in range(micros)]
     late = exchange(normed, here, EARLY, sections, count, ended)
     normed = [jnp.where(section < EARLY, a, b) for a, b in zip(early, late)]

time: 1140 us -> 898 us (0.79)
  Pallas kernels: 285 us -> 123 us
  starting transfers between devices: 557 us -> 464 us
    pallas_call x74, Pallas kernels: 285 us -> 123 us  [call(): pl.pallas_call(kernel, out_shape=outs, in_specs=in_specs, out_specs=out_s...]
    ppermute x60, starting transfers between devices: 399 us -> 303 us  [hop(): return lax.ppermute(block, ('section', 'dp'), sorted(pairs))]
    ppermute x4, waiting for transfers between devices: 7.73 us -> 45.4 us  [spread(): arrived = lax.ppermute(jnp.where(upper, low, high), 'section', pairs)]
    ppermute x60, waiting for transfers between devices: 39 us -> 11.9 us  [hop(): return lax.ppermute(block, ('section', 'dp'), sorted(pairs))]
    unnamed x121 -> x127, local copies, waits for them, and re-layouts: 20.6 us -> 25.7 us
  transfers between devices with their start and end apart: 118 -> 118, of which waited for: 38 -> 30; matrix products, arithmetic and copies ran while one was open for 2% -> 2% of each run, Pallas kernels for 17% -> 12%
where the time goes in v7:
time: 898 us; the launch traced here: 887 us
  starting transfers between devices  464 us (52%)
  waiting for transfers between devices  234 us (26%)
  Pallas kernels  123 us (14%)
  local copies, waits for them, and re-layouts  37.5 us (4%)
  between operations  18.3 us (2%)
    ppermute x60, starting transfers between devices, hop(): return lax.ppermute(block, ('section', 'dp'), sorted(pairs))  303 us
    pallas_call x74, Pallas kernels, call(): pl.pallas_call(kernel, out_shape=outs, in_specs=in_specs, out_specs=out_s...  123 us
    ppermute x15, waiting for transfers between devices, shift_z(): return lax.ppermute(block, 'dp', pairs)  109 us
    ppermute x4, starting transfers between devices, spread(): arrived = lax.ppermute(jnp.where(upper, low, high), 'section', pairs)  50.3 us
    ppermute x4, waiting for transfers between devices, spread(): arrived = lax.ppermute(jnp.where(upper, low, high), 'section', pairs)  45.4 us
    ppermute x27, starting transfers between devices, shift_y(): return lax.ppermute(block, 'dp', pairs)  43.4 us
    ppermute x15, starting transfers between devices, shift_z(): return lax.ppermute(block, 'dp', pairs)  37.2 us
    ppermute x6, waiting for transfers between devices, exchange(): blocks.append(lax.ppermute(blocks[-1], ('section', 'dp'), pairs))  36.8 us
  transfers between devices with their start and end apart: 118, of which 30 were waited for; matrix products, arithmetic and copies ran while one was open for 2% of the time, Pallas kernels for 12%

profile of v7, /device:TPU:128, one launch (start us, length us, event | category | flops | bytes accessed | tf_op | source)
XLA Modules:
  0.0 886.9 jit_solution(1904836897004793405)
XLA Ops:
  7.8 6.5 collective-permute-done.4
  18.1 4.3 collective-permute-done.5
  26.0 3.0 collective-permute-start.1
  29.0 17.0 %collective-permute-done.14.refs_12_ = bf16[192,2304]{1,0:T(8,128)(2,1)S(1)} collective-permute-done((bf16[192,2304]{1,0:T(8,128)(2,1)S(1)}, bf16[192,2304]{1,0:T(8,128)(2,1)S(1)}, u32[]{:S(2)}, u32[]{:S(2)}) %collective-permute-start.14) | collective-permute-done | bytes 884768 | tf_op jit(solution)/shard_map/ppermute | solution.py:333
  46.0 3.3 collective-permute-start.20
  49.3 3.0 collective-permute-start.10
  52.3 19.0 %collective-permute-done.13.refs_11_ = bf16[768,768]{1,0:T(8,128)(2,1)S(1)} collective-permute-done((bf16[768,768]{1,0:T(8,128)(2,1)S(1)}, bf16[768,768]{1,0:T(8,128)(2,1)S(1)}, u32[]{:S(2)}, u32[]{:S(2)}) %collective-permute-start.13) | collective-permute-done | bytes 1179680 | tf_op jit(solution)/shard_map/ppermute | solution.py:333
  71.3 3.3 collective-permute-start.19
  77.8 12.4 %collective-permute-done.20.refs_18_ = bf16[192,2304]{1,0:T(8,128)(2,1)S(1)} collective-permute-done((bf16[192,2304]{1,0:T(8,128)(2,1)S(1)}, bf16[192,2304]{1,0:T(8,128)(2,1)S(1)}, u32[]{:S(2)}, u32[]{:S(2)}) %collective-permute-start.20) | collective-permute-done | bytes 884768 | tf_op jit(solution)/shard_map/ppermute | solution.py:333
  93.7 20.0 %collective-permute-done.19.refs_17_ = bf16[768,768]{1,0:T(8,128)(2,1)} collective-permute-done((bf16[768,768]{1,0:T(8,128)(2,1)S(1)}, bf16[768,768]{1,0:T(8,128)(2,1)}, u32[]{:S(2)}, u32[]{:S(2)}) %collective-permute-start.19) | collective-permute-done | bytes 1179680 | tf_op jit(solution)/shard_map/ppermute | solution.py:333
  113.7 3.1 collective-permute-start.25
  137.2 6.2 collective-permute-done.11.refs_9_
  146.8 6.0 collective-permute-done.17.refs_15_
  153.3 5.8 collective-permute-done.23.refs_21_
  160.0 7.2 shard_map.93.matrix.source
  181.6 3.9 shard_map.97
  186.8 11.5 %collective-permute-start.45 = (bf16[96,3072]{1,0:T(8,128)(2,1)S(1)}, bf16[96,3072]{1,0:T(8,128)(2,1)S(1)}, u32[]{:S(2)}, u32[]{:S(2)}) collective-permute-start(bf16[96,3072]{1,0:T(8,128)(2,1)S(1)} %get-tuple-element.316), channel_id=1, source_target_pairs={{0,16},{1,17},{2,18},{3,19},{4,20},{5,21},{6,22},{7,23},{8,24},{9,... | collective-permute-start | bytes 1769480 | tf_op jit(solution)/shard_map/ppermute | solution.py:188
  205.5 3.6 shard_map.100
  210.5 71.3 %collective-permute-start.48 = (bf16[96,3072]{1,0:T(8,128)(2,1)S(1)}, bf16[96,3072]{1,0:T(8,128)(2,1)S(1)}, u32[]{:S(2)}, u32[]{:S(2)}) collective-permute-start(bf16[96,3072]{1,0:T(8,128)(2,1)S(1)} %get-tuple-element.328), channel_id=1, source_target_pairs={{112,128},{113,129},{114,130},{115,131},{116,132},{117,133},{118,1... | collective-permute-start | bytes 1769480 | tf_op jit(solution)/shard_map/ppermute | solution.py:188
  283.3 6.6 collective-permute-start.33
  289.9 6.4 copy-done.6
  296.2 5.3 shard_map.102.refs_3_.turned
  301.6 6.0 shard_map.119
  309.6 5.1 shard_map.103
  321.2 3.6 shard_map.105
  328.3 3.9 shard_map.123
  332.2 18.7 %collective-permute-start.53 = (bf16[96,3072]{1,0:T(8,128)(2,1)S(1)}, bf16[96,3072]{1,0:T(8,128)(2,1)S(1)}, u32[]{:S(2)}, u32[]{:S(2)}) collective-permute-start(bf16[96,3072]{1,0:T(8,128)(2,1)S(1)} %get-tuple-element.348), channel_id=1, source_target_pairs={{0,16},{1,17},{2,18},{3,19},{4,20},{5,21},{6,22},{7,23},{8,24},{9,... | collective-permute-start | bytes 1769480 | tf_op jit(solution)/shard_map/ppermute | solution.py:188
  359.9 4.8 shard_map.126
  378.6 3.7 shard_map.147
  382.3 28.6 %collective-permute-start.79 = (bf16[96,3072]{1,0:T(8,128)(2,1)S(1)}, bf16[96,3072]{1,0:T(8,128)(2,1)S(1)}, u32[]{:S(2)}, u32[]{:S(2)}) collective-permute-start(bf16[96,3072]{1,0:T(8,128)(2,1)S(1)} %get-tuple-element.421), channel_id=1, source_target_pairs={{0,16},{1,17},{2,18},{3,19},{4,20},{5,21},{6,22},{7,23},{8,24},{9,... | collective-permute-start | bytes 1769480 | tf_op jit(solution)/shard_map/ppermute | solution.py:188
  411.4 5.3 collective-permute-start.64
  422.4 3.5 shard_map.150
  428.5 90.0 %collective-permute-start.83 = (bf16[96,3072]{1,0:T(8,128)(2,1)S(1)}, bf16[96,3072]{1,0:T(8,128)(2,1)S(1)}, u32[]{:S(2)}, u32[]{:S(2)}) collective-permute-start(bf16[96,3072]{1,0:T(8,128)(2,1)S(1)} %get-tuple-element.433), channel_id=1, source_target_pairs={{0,16},{1,17},{2,18},{3,19},{4,20},{5,21},{6,22},{7,23},{8,24},{9,... | collective-permute-start | bytes 1769480 | tf_op jit(solution)/shard_map/ppermute | solution.py:188
  519.5 6.0 collective-permute-start.68
  525.5 4.6 shard_map.152
  532.0 4.6 shard_map.136
  536.7 5.6 collective-permute-start.69
  542.3 5.1 collective-permute-done.84.u_in
  548.9 5.0 collective-permute-done.69.u_in
  567.8 3.4 shard_map.141
  574.6 4.2 shard_map.159
  578.8 8.5 collective-permute-start.91
  588.7 4.7 collective-permute-start.76
  595.9 6.4 copy-done.3
  605.6 4.7 copy-done.4
  616.6 12.8 %collective-permute-start.100 = (bf16[192,768]{1,0:T(8,128)(2,1)S(1)}, bf16[192,768]{1,0:T(8,128)(2,1)S(1)}, u32[]{:S(2)}, u32[]{:S(2)}) collective-permute-start(bf16[192,768]{1,0:T(8,128)(2,1)S(1)} %get-tuple-element.478), channel_id=1, source_target_pairs={{0,4},{1,5},{2,6},{3,7},{4,12},{5,13},{6,14},{7,15},{8,0},{9,1},{1... | collective-permute-start | bytes 884744 | tf_op jit(solution)/shard_map/ppermute | solution.py:333
  641.6 3.2 shard_map.161
  644.7 3.4 collective-permute-start.92
  648.2 4.7 collective-permute-start.93
  652.9 3.6 shard_map.166
  656.6 3.0 collective-permute-start.94
  670.9 50.0 %collective-permute-start.114 = (bf16[384,1536]{1,0:T(8,128)(2,1)S(1)}, bf16[384,1536]{1,0:T(8,128)(2,1)S(1)}, u32[]{:S(2)}, u32[]{:S(2)}) collective-permute-start(bf16[384,1536]{1,0:T(8,128)(2,1)S(1)} %broadcast_select_fusion), channel_id=1, source_target_pairs={{0,128},{16,144},{32,160},{48,176},{64,192},{80,208},{96,224},{112... | collective-permute-start | bytes 3538952 | tf_op jit(solution)/shard_map/ppermute | solution.py:204
  728.9 5.7 collective-permute-start.95
  734.9 37.7 %collective-permute-done.114 = bf16[384,1536]{1,0:T(8,128)(2,1)S(1)} collective-permute-done((bf16[384,1536]{1,0:T(8,128)(2,1)S(1)}, bf16[384,1536]{1,0:T(8,128)(2,1)S(1)}, u32[]{:S(2)}, u32[]{:S(2)}) %collective-permute-start.114) | collective-permute-done | bytes 1179680 | tf_op jit(solution)/shard_map/ppermute | solution.py:204
  775.0 17.6 %collective-permute-done.111 = f32[1,3072]{1,0:T(1,128)S(1)} collective-permute-done((f32[1,3072]{1,0:T(1,128)S(1)}, f32[1,3072]{1,0:T(1,128)S(1)}, u32[]{:S(2)}, u32[]{:S(2)}) %collective-permute-start.111) | collective-permute-done | bytes 12320 | tf_op jit(solution)/shard_map/ppermute | solution.py:333
  793.5 4.2 collective-permute-start.96
  801.8 7.7 collective-permute-done.115
  809.9 13.6 %collective-permute-done.96 = bf16[4,192,768]{2,1,0:T(8,128)(2,1)S(1)} collective-permute-done((bf16[4,192,768]{2,1,0:T(8,128)(2,1)S(1)}, bf16[4,192,768]{2,1,0:T(8,128)(2,1)S(1)}, u32[]{:S(2)}, u32[]{:S(2)}) %collective-permute-start.96) | collective-permute-done | bytes 1179680 | tf_op jit(solution)/shard_map/ppermute | solution.py:320
  823.4 4.6 collective-permute-start.97
  829.7 23.2 %collective-permute-done.97 = bf16[4,192,768]{2,1,0:T(8,128)(2,1)S(1)} collective-permute-done((bf16[4,192,768]{2,1,0:T(8,128)(2,1)S(1)}, bf16[4,192,768]{2,1,0:T(8,128)(2,1)S(1)}, u32[]{:S(2)}, u32[]{:S(2)}) %collective-permute-start.97) | collective-permute-done | bytes 1179680 | tf_op jit(solution)/shard_map/ppermute | solution.py:320
  853.0 4.1 bitcast_convert_fusion
  863.4 4.2 collective-permute-done.105
  867.7 9.0 %collective-permute-done.106 = bf16[192,768]{1,0:T(8,128)(2,1)S(1)} collective-permute-done((bf16[192,768]{1,0:T(8,128)(2,1)S(1)}, bf16[192,768]{1,0:T(8,128)(2,1)S(1)}, u32[]{:S(2)}, u32[]{:S(2)}) %collective-permute-start.106) | collective-permute-done | bytes 294944 | tf_op jit(solution)/shard_map/ppermute | solution.py:333
  876.8 8.9 %collective-permute-done.107 = bf16[192,768]{1,0:T(8,128)(2,1)S(1)} collective-permute-done((bf16[192,768]{1,0:T(8,128)(2,1)S(1)}, bf16[192,768]{1,0:T(8,128)(2,1)S(1)}, u32[]{:S(2)}, u32[]{:S(2)}) %collective-permute-start.107) | collective-permute-done | bytes 294944 | tf_op jit(solution)/shard_map/ppermute | solution.py:333
  (421 shorter events, 182.8 us)
Async XLA Ops:
  1.9 21.5 %collective-permute-start.8 = (bf16[192,2304]{1,0:T(8,128)(2,1)S(1)}, bf16[192,2304]{1,0:T(8,128)(2,1)S(1)}, u32[]{:S(2)}, u32[]{:S(2)}) collective-permute-start(bf16[192,2304]{1,0:T(8,128)(2,1)S(1)} %slice.100.refs_0_), channel_id=1, source_target_pairs={{0,8},{1,9},{2,10},{3,11},{4,0},{5,1},{6,2},{7,3},{8,12},{9,13},{1... | collective-permute-start | bytes 2654216 | tf_op jit(solution)/shard_map/ppermute | solution.py:333
  14.7 34.6 %collective-permute-start = (bf16[192,2304]{1,0:T(8,128)(2,1)S(1)}, bf16[192,2304]{1,0:T(8,128)(2,1)S(1)}, u32[]{:S(2)}, u32[]{:S(2)}) collective-permute-start(bf16[192,2304]{1,0:T(8,128)(2,1)S(1)} %slice.100.refs_0_), channel_id=1, source_target_pairs={{0,1},{1,2},{2,3},{3,0},{4,5},{5,6},{6,7},{7,4},{8,9},{9,10},{10,1... | collective-permute-start | bytes 2654216 | tf_op jit(solution)/shard_map/ppermute | solution.py:338
  23.4 22.6 %collective-permute-start.14 = (bf16[192,2304]{1,0:T(8,128)(2,1)S(1)}, bf16[192,2304]{1,0:T(8,128)(2,1)S(1)}, u32[]{:S(2)}, u32[]{:S(2)}) collective-permute-start(bf16[192,2304]{1,0:T(8,128)(2,1)S(1)} %collective-permute-done.8.refs_6_), channel_id=1, source_target_pairs={{0,8},{1,9},{2,10},{3,11},{4,0},{5,1},{6,2},{7,3},{8,12},{9,13},{1... | collective-permute-start | bytes 2654216 | tf_op jit(solution)/shard_map/ppermute | solution.py:333
  25.8 45.5 %collective-permute-start.13 = (bf16[768,768]{1,0:T(8,128)(2,1)S(1)}, bf16[768,768]{1,0:T(8,128)(2,1)S(1)}, u32[]{:S(2)}, u32[]{:S(2)}) collective-permute-start(bf16[768,768]{1,0:T(8,128)(2,1)S(1)} %constant_dynamic-update-slice_fusion.refs_5_), channel_id=1, source_target_pairs={{0,8},{1,9},{2,10},{3,11},{4,0},{5,1},{6,2},{7,3},{8,12},{9,13},{1... | collective-permute-start | bytes 3538952 | tf_op jit(solution)/shard_map/ppermute | solution.py:333
  26.0 48.5 %collective-permute-start.1 = (bf16[192,2304]{1,0:T(8,128)(2,1)S(1)}, bf16[192,2304]{1,0:T(8,128)(2,1)S(1)}, u32[]{:S(2)}, u32[]{:S(2)}) collective-permute-start(bf16[192,2304]{1,0:T(8,128)(2,1)S(1)} %slice.100.refs_0_), channel_id=1, source_target_pairs={{0,3},{1,0},{2,1},{3,2},{4,7},{5,4},{6,5},{7,6},{8,11},{9,8},{10,9... | collective-permute-start | bytes 2654216 | tf_op jit(solution)/shard_map/ppermute | solution.py:338
  29.0 47.1 %collective-permute-start.9 = (bf16[192,2304]{1,0:T(8,128)(2,1)S(1)}, bf16[192,2304]{1,0:T(8,128)(2,1)S(1)}, u32[]{:S(2)}, u32[]{:S(2)}) collective-permute-start(bf16[192,2304]{1,0:T(8,128)(2,1)S(1)} %collective-permute-done.8.refs_6_), channel_id=1, source_target_pairs={{0,1},{1,2},{2,3},{3,0},{4,5},{5,6},{6,7},{7,4},{8,9},{9,10},{10,1... | collective-permute-start | bytes 2654216 | tf_op jit(solution)/shard_map/ppermute | solution.py:338
  46.0 44.2 %collective-permute-start.20 = (bf16[192,2304]{1,0:T(8,128)(2,1)S(1)}, bf16[192,2304]{1,0:T(8,128)(2,1)S(1)}, u32[]{:S(2)}, u32[]{:S(2)}) collective-permute-start(bf16[192,2304]{1,0:T(8,128)(2,1)S(1)} %collective-permute-done.14.refs_12_), channel_id=1, source_target_pairs={{0,8},{1,9},{2,10},{3,11},{4,0},{5,1},{6,2},{7,3},{8,12},{9,13},{1... | collective-permute-start | bytes 2654216 | tf_op jit(solution)/shard_map/ppermute | solution.py:333
  49.3 42.7 %collective-permute-start.10 = (bf16[192,2304]{1,0:T(8,128)(2,1)S(1)}, bf16[192,2304]{1,0:T(8,128)(2,1)S(1)}, u32[]{:S(2)}, u32[]{:S(2)}) collective-permute-start(bf16[192,2304]{1,0:T(8,128)(2,1)S(1)} %collective-permute-done.8.refs_6_), channel_id=1, source_target_pairs={{0,3},{1,0},{2,1},{3,2},{4,7},{5,4},{6,5},{7,6},{8,11},{9,8},{10,9... | collective-permute-start | bytes 2654216 | tf_op jit(solution)/shard_map/ppermute | solution.py:338
  71.3 42.4 %collective-permute-start.19 = (bf16[768,768]{1,0:T(8,128)(2,1)S(1)}, bf16[768,768]{1,0:T(8,128)(2,1)}, u32[]{:S(2)}, u32[]{:S(2)}) collective-permute-start(bf16[768,768]{1,0:T(8,128)(2,1)S(1)} %collective-permute-done.13.refs_11_), channel_id=1, source_target_pairs={{0,8},{1,9},{2,10},{3,11},{4,0},{5,1},{6,2},{7,3},{8,12},{9,13},{1... | collective-permute-start | bytes 3538952 | tf_op jit(solution)/shard_map/ppermute | solution.py:333
  74.5 44.7 %collective-permute-start.15 = (bf16[192,2304]{1,0:T(8,128)(2,1)S(1)}, bf16[192,2304]{1,0:T(8,128)(2,1)S(1)}, u32[]{:S(2)}, u32[]{:S(2)}) collective-permute-start(bf16[192,2304]{1,0:T(8,128)(2,1)S(1)} %collective-permute-done.14.refs_12_), channel_id=1, source_target_pairs={{0,1},{1,2},{2,3},{3,0},{4,5},{5,6},{6,7},{7,4},{8,9},{9,10},{10,1... | collective-permute-start | bytes 2654216 | tf_op jit(solution)/shard_map/ppermute | solution.py:338
  76.1 44.8 %collective-permute-start.16 = (bf16[192,2304]{1,0:T(8,128)(2,1)S(1)}, bf16[192,2304]{1,0:T(8,128)(2,1)}, u32[]{:S(2)}, u32[]{:S(2)}) collective-permute-start(bf16[192,2304]{1,0:T(8,128)(2,1)S(1)} %collective-permute-done.14.refs_12_), channel_id=1, source_target_pairs={{0,3},{1,0},{2,1},{3,2},{4,7},{5,4},{6,5},{7,6},{8,11},{9,8},{10,9... | collective-permute-start | bytes 2654216 | tf_op jit(solution)/shard_map/ppermute | solution.py:338
  90.2 32.5 %collective-permute-start.21 = (bf16[192,2304]{1,0:T(8,128)(2,1)S(1)}, bf16[192,2304]{1,0:T(8,128)(2,1)}, u32[]{:S(2)}, u32[]{:S(2)}) collective-permute-start(bf16[192,2304]{1,0:T(8,128)(2,1)S(1)} %collective-permute-done.20.refs_18_), channel_id=1, source_target_pairs={{0,1},{1,2},{2,3},{3,0},{4,5},{5,6},{6,7},{7,4},{8,9},{9,10},{10,1... | collective-permute-start | bytes 2654216 | tf_op jit(solution)/shard_map/ppermute | solution.py:338
  92.0 31.1 %collective-permute-start.22 = (bf16[192,2304]{1,0:T(8,128)(2,1)S(1)}, bf16[192,2304]{1,0:T(8,128)(2,1)}, u32[]{:S(2)}, u32[]{:S(2)}) collective-permute-start(bf16[192,2304]{1,0:T(8,128)(2,1)S(1)} %collective-permute-done.20.refs_18_), channel_id=1, source_target_pairs={{0,3},{1,0},{2,1},{3,2},{4,7},{5,4},{6,5},{7,6},{8,11},{9,8},{10,9... | collective-permute-start | bytes 2654216 | tf_op jit(solution)/shard_map/ppermute | solution.py:338
  113.7 45.5 %collective-permute-start.25 = (bf16[768,768]{1,0:T(8,128)(2,1)}, bf16[768,768]{1,0:T(8,128)(2,1)}, u32[]{:S(2)}, u32[]{:S(2)}) collective-permute-start(bf16[768,768]{1,0:T(8,128)(2,1)} %collective-permute-done.19.refs_17_), channel_id=1, source_target_pairs={{0,8},{1,9},{2,10},{3,11},{4,0},{5,1},{6,2},{7,3},{8,12},{9,13},{1... | collective-permute-start | bytes 3538952 | tf_op jit(solution)/shard_map/ppermute | solution.py:333
  119.3 14.6 %collective-permute-start.2 = (bf16[96,2304]{1,0:T(8,128)(2,1)}, bf16[96,2304]{1,0:T(8,128)(2,1)S(1)}, u32[]{:S(2)}, u32[]{:S(2)}) collective-permute-start(bf16[96,2304]{1,0:T(8,128)(2,1)} %slice.101), channel_id=1, source_target_pairs={{0,1},{1,2},{2,3},{3,0},{4,5},{5,6},{6,7},{7,4},{8,9},{9,10},{10,1... | collective-permute-start | bytes 1327112 | tf_op jit(solution)/shard_map/ppermute | solution.py:338
  121.0 13.4 %collective-permute-start.3 = (bf16[96,2304]{1,0:T(8,128)(2,1)}, bf16[96,2304]{1,0:T(8,128)(2,1)S(1)}, u32[]{:S(2)}, u32[]{:S(2)}) collective-permute-start(bf16[96,2304]{1,0:T(8,128)(2,1)} %slice.102), channel_id=1, source_target_pairs={{0,3},{1,0},{2,1},{3,2},{4,7},{5,4},{6,5},{7,6},{8,11},{9,8},{10,9... | collective-permute-start | bytes 1327112 | tf_op jit(solution)/shard_map/ppermute | solution.py:338
  122.7 20.7 %collective-permute-start.11 = (bf16[96,2304]{1,0:T(8,128)(2,1)}, bf16[96,2304]{1,0:T(8,128)(2,1)S(1)}, u32[]{:S(2)}, u32[]{:S(2)}) collective-permute-start(bf16[96,2304]{1,0:T(8,128)(2,1)} %slice.106), channel_id=1, source_target_pairs={{0,1},{1,2},{2,3},{3,0},{4,5},{5,6},{6,7},{7,4},{8,9},{9,10},{10,1... | collective-permute-start | bytes 1327112 | tf_op jit(solution)/shard_map/ppermute | solution.py:338
  123.1 20.8 %collective-permute-start.12 = (bf16[96,2304]{1,0:T(8,128)(2,1)S(1)}, bf16[96,2304]{1,0:T(8,128)(2,1)S(1)}, u32[]{:S(2)}, u32[]{:S(2)}) collective-permute-start(bf16[96,2304]{1,0:T(8,128)(2,1)S(1)} %slice.107), channel_id=1, source_target_pairs={{0,3},{1,0},{2,1},{3,2},{4,7},{5,4},{6,5},{7,6},{8,11},{9,8},{10,9... | collective-permute-start | bytes 1327112 | tf_op jit(solution)/shard_map/ppermute | solution.py:338
  133.9 19.0 %collective-permute-start.17 = (bf16[96,2304]{1,0:T(8,128)(2,1)S(1)}, bf16[96,2304]{1,0:T(8,128)(2,1)S(1)}, u32[]{:S(2)}, u32[]{:S(2)}) collective-permute-start(bf16[96,2304]{1,0:T(8,128)(2,1)S(1)} %slice.108), channel_id=1, source_target_pairs={{0,1},{1,2},{2,3},{3,0},{4,5},{5,6},{6,7},{7,4},{8,9},{9,10},{10,1... | collective-permute-start | bytes 1327112 | tf_op jit(solution)/shard_map/ppermute | solution.py:338
  134.4 19.0 %collective-permute-start.18 = (bf16[96,2304]{1,0:T(8,128)(2,1)S(1)}, bf16[96,2304]{1,0:T(8,128)(2,1)S(1)}, u32[]{:S(2)}, u32[]{:S(2)}) collective-permute-start(bf16[96,2304]{1,0:T(8,128)(2,1)S(1)} %slice.109), channel_id=1, source_target_pairs={{0,3},{1,0},{2,1},{3,2},{4,7},{5,4},{6,5},{7,6},{8,11},{9,8},{10,9... | collective-permute-start | bytes 1327112 | tf_op jit(solution)/shard_map/ppermute | solution.py:338
  143.4 15.7 %collective-permute-start.23 = (bf16[96,2304]{1,0:T(8,128)(2,1)S(1)}, bf16[96,2304]{1,0:T(8,128)(2,1)S(1)}, u32[]{:S(2)}, u32[]{:S(2)}) collective-permute-start(bf16[96,2304]{1,0:T(8,128)(2,1)S(1)} %slice.110), channel_id=1, source_target_pairs={{0,1},{1,2},{2,3},{3,0},{4,5},{5,6},{6,7},{7,4},{8,9},{9,10},{10,1... | collective-permute-start | bytes 1327112 | tf_op jit(solution)/shard_map/ppermute | solution.py:338
  143.8 15.4 %collective-permute-start.24 = (bf16[96,2304]{1,0:T(8,128)(2,1)S(1)}, bf16[96,2304]{1,0:T(8,128)(2,1)S(1)}, u32[]{:S(2)}, u32[]{:S(2)}) collective-permute-start(bf16[96,2304]{1,0:T(8,128)(2,1)S(1)} %slice.111), channel_id=1, source_target_pairs={{0,3},{1,0},{2,1},{3,2},{4,7},{5,4},{6,5},{7,6},{8,11},{9,8},{10,9... | collective-permute-start | bytes 1327112 | tf_op jit(solution)/shard_map/ppermute | solution.py:338
  185.4 12.8 %collective-permute-start.29 = (bf16[96,3072]{1,0:T(8,128)(2,1)S(1)}, bf16[96,3072]{1,0:T(8,128)(2,1)S(1)}, u32[]{:S(2)}, u32[]{:S(2)}) collective-permute-start(bf16[96,3072]{1,0:T(8,128)(2,1)S(1)} %get-tuple-element.251), channel_id=1, source_target_pairs={{48,64},{49,65},{50,66},{51,67},{52,68},{53,69},{54,70},{55,71},{5... | collective-permute-start | bytes 1769480 | tf_op jit(solution)/shard_map/ppermute | solution.py:188
  186.8 14.1 %collective-permute-start.45 = (bf16[96,3072]{1,0:T(8,128)(2,1)S(1)}, bf16[96,3072]{1,0:T(8,128)(2,1)S(1)}, u32[]{:S(2)}, u32[]{:S(2)}) collective-permute-start(bf16[96,3072]{1,0:T(8,128)(2,1)S(1)} %get-tuple-element.316), channel_id=1, source_target_pairs={{0,16},{1,17},{2,18},{3,19},{4,20},{5,21},{6,22},{7,23},{8,24},{9,... | collective-permute-start | bytes 1769480 | tf_op jit(solution)/shard_map/ppermute | solution.py:188
  209.1 72.7 %collective-permute-start.32 = (bf16[96,3072]{1,0:T(8,128)(2,1)S(1)}, bf16[96,3072]{1,0:T(8,128)(2,1)S(1)}, u32[]{:S(2)}, u32[]{:S(2)}) collective-permute-start(bf16[96,3072]{1,0:T(8,128)(2,1)S(1)} %get-tuple-element.263), channel_id=1, source_target_pairs={{32,48},{33,49},{34,50},{35,51},{36,52},{37,53},{38,54},{39,55},{4... | collective-permute-start | bytes 1769480 | tf_op jit(solution)/shard_map/ppermute | solution.py:188
  210.5 91.1 %collective-permute-start.48 = (bf16[96,3072]{1,0:T(8,128)(2,1)S(1)}, bf16[96,3072]{1,0:T(8,128)(2,1)S(1)}, u32[]{:S(2)}, u32[]{:S(2)}) collective-permute-start(bf16[96,3072]{1,0:T(8,128)(2,1)S(1)} %get-tuple-element.328), channel_id=1, source_target_pairs={{112,128},{113,129},{114,130},{115,131},{116,132},{117,133},{118,1... | collective-permute-start | bytes 1769480 | tf_op jit(solution)/shard_map/ppermute | solution.py:188
  283.3 26.3 %collective-permute-start.33 = (bf16[96,3072]{1,0:T(8,128)(2,1)}, bf16[96,3072]{1,0:T(8,128)(2,1)S(1)}, u32[]{:S(2)}, u32[]{:S(2)}) collective-permute-start(bf16[96,3072]{1,0:T(8,128)(2,1)} %get-tuple-element.267), channel_id=1, source_target_pairs={{112,128},{113,129},{114,130},{115,131},{116,132},{117,133},{118,1... | collective-permute-start | bytes 1769480 | tf_op jit(solution)/shard_map/ppermute | solution.py:188
  327.6 23.3 %collective-permute-start.37 = (bf16[96,3072]{1,0:T(8,128)(2,1)S(1)}, bf16[96,3072]{1,0:T(8,128)(2,1)S(1)}, u32[]{:S(2)}, u32[]{:S(2)}) collective-permute-start(bf16[96,3072]{1,0:T(8,128)(2,1)S(1)} %get-tuple-element.283), channel_id=1, source_target_pairs={{48,64},{49,65},{50,66},{51,67},{52,68},{53,69},{54,70},{55,71},{5... | collective-permute-start | bytes 1769480 | tf_op jit(solution)/shard_map/ppermute | solution.py:188
  332.2 21.3 %collective-permute-start.53 = (bf16[96,3072]{1,0:T(8,128)(2,1)S(1)}, bf16[96,3072]{1,0:T(8,128)(2,1)S(1)}, u32[]{:S(2)}, u32[]{:S(2)}) collective-permute-start(bf16[96,3072]{1,0:T(8,128)(2,1)S(1)} %get-tuple-element.348), channel_id=1, source_target_pairs={{0,16},{1,17},{2,18},{3,19},{4,20},{5,21},{6,22},{7,23},{8,24},{9,... | collective-permute-start | bytes 1769480 | tf_op jit(solution)/shard_map/ppermute | solution.py:188
  377.9 33.0 %collective-permute-start.63 = (bf16[96,3072]{1,0:T(8,128)(2,1)S(1)}, bf16[96,3072]{1,0:T(8,128)(2,1)S(1)}, u32[]{:S(2)}, u32[]{:S(2)}) collective-permute-start(bf16[96,3072]{1,0:T(8,128)(2,1)S(1)} %get-tuple-element.370), channel_id=1, source_target_pairs={{16,32},{17,33},{18,34},{19,35},{20,36},{21,37},{22,38},{23,39},{2... | collective-permute-start | bytes 1769480 | tf_op jit(solution)/shard_map/ppermute | solution.py:188
  382.3 34.5 %collective-permute-start.79 = (bf16[96,3072]{1,0:T(8,128)(2,1)S(1)}, bf16[96,3072]{1,0:T(8,128)(2,1)S(1)}, u32[]{:S(2)}, u32[]{:S(2)}) collective-permute-start(bf16[96,3072]{1,0:T(8,128)(2,1)S(1)} %get-tuple-element.421), channel_id=1, source_target_pairs={{0,16},{1,17},{2,18},{3,19},{4,20},{5,21},{6,22},{7,23},{8,24},{9,... | collective-permute-start | bytes 1769480 | tf_op jit(solution)/shard_map/ppermute | solution.py:188
  427.2 91.3 %collective-permute-start.67 = (bf16[96,3072]{1,0:T(8,128)(2,1)S(1)}, bf16[96,3072]{1,0:T(8,128)(2,1)S(1)}, u32[]{:S(2)}, u32[]{:S(2)}) collective-permute-start(bf16[96,3072]{1,0:T(8,128)(2,1)S(1)} %get-tuple-element.382), channel_id=1, source_target_pairs={{16,32},{17,33},{18,34},{19,35},{20,36},{21,37},{22,38},{23,39},{2... | collective-permute-start | bytes 1769480 | tf_op jit(solution)/shard_map/ppermute | solution.py:188
  428.5 97.0 %collective-permute-start.83 = (bf16[96,3072]{1,0:T(8,128)(2,1)S(1)}, bf16[96,3072]{1,0:T(8,128)(2,1)S(1)}, u32[]{:S(2)}, u32[]{:S(2)}) collective-permute-start(bf16[96,3072]{1,0:T(8,128)(2,1)S(1)} %get-tuple-element.433), channel_id=1, source_target_pairs={{0,16},{1,17},{2,18},{3,19},{4,20},{5,21},{6,22},{7,23},{8,24},{9,... | collective-permute-start | bytes 1769480 | tf_op jit(solution)/shard_map/ppermute | solution.py:188
  519.5 12.6 %collective-permute-start.68 = (bf16[96,3072]{1,0:T(8,128)(2,1)S(1)}, bf16[96,3072]{1,0:T(8,128)(2,1)S(1)}, u32[]{:S(2)}, u32[]{:S(2)}) collective-permute-start(bf16[96,3072]{1,0:T(8,128)(2,1)S(1)} %get-tuple-element.385), channel_id=1, source_target_pairs={{0,16},{1,17},{2,18},{3,19},{4,20},{5,21},{6,22},{7,23},{8,24},{9,... | collective-permute-start | bytes 1769480 | tf_op jit(solution)/shard_map/ppermute | solution.py:188
  530.1 17.3 %collective-permute-start.84 = (bf16[96,3072]{1,0:T(8,128)(2,1)S(1)}, bf16[96,3072]{1,0:T(8,128)(2,1)S(1)}, u32[]{:S(2)}, u32[]{:S(2)}) collective-permute-start(bf16[96,3072]{1,0:T(8,128)(2,1)S(1)} %get-tuple-element.436), channel_id=1, source_target_pairs={{112,128},{113,129},{114,130},{115,131},{116,132},{117,133},{118,1... | collective-permute-start | bytes 1769480 | tf_op jit(solution)/shard_map/ppermute | solution.py:188
  536.7 17.2 %collective-permute-start.69 = (bf16[96,3072]{1,0:T(8,128)(2,1)S(1)}, bf16[96,3072]{1,0:T(8,128)(2,1)S(1)}, u32[]{:S(2)}, u32[]{:S(2)}) collective-permute-start(bf16[96,3072]{1,0:T(8,128)(2,1)S(1)} %get-tuple-element.388), channel_id=1, source_target_pairs={{112,128},{113,129},{114,130},{115,131},{116,132},{117,133},{118,1... | collective-permute-start | bytes 1769480 | tf_op jit(solution)/shard_map/ppermute | solution.py:188
  573.8 13.4 %collective-permute-start.75 = (bf16[96,3072]{1,0:T(8,128)(2,1)S(1)}, bf16[96,3072]{1,0:T(8,128)(2,1)S(1)}, u32[]{:S(2)}, u32[]{:S(2)}) collective-permute-start(bf16[96,3072]{1,0:T(8,128)(2,1)S(1)} %get-tuple-element.406), channel_id=1, source_target_pairs={{16,32},{17,33},{18,34},{19,35},{20,36},{21,37},{22,38},{23,39},{2... | collective-permute-start | bytes 1769480 | tf_op jit(solution)/shard_map/ppermute | solution.py:188
  578.8 17.1 %collective-permute-start.91 = (bf16[96,3072]{1,0:T(8,128)(2,1)}, bf16[96,3072]{1,0:T(8,128)(2,1)}, u32[]{:S(2)}, u32[]{:S(2)}) collective-permute-start(bf16[96,3072]{1,0:T(8,128)(2,1)} %get-tuple-element.457), channel_id=1, source_target_pairs={{0,16},{1,17},{2,18},{3,19},{4,20},{5,21},{6,22},{7,23},{8,24},{9,... | collective-permute-start | bytes 1769480 | tf_op jit(solution)/shard_map/ppermute | solution.py:188
  588.7 16.9 %collective-permute-start.76 = (bf16[96,3072]{1,0:T(8,128)(2,1)}, bf16[96,3072]{1,0:T(8,128)(2,1)S(1)}, u32[]{:S(2)}, u32[]{:S(2)}) collective-permute-start(bf16[96,3072]{1,0:T(8,128)(2,1)} %get-tuple-element.409), channel_id=1, source_target_pairs={{0,16},{1,17},{2,18},{3,19},{4,20},{5,21},{6,22},{7,23},{8,24},{9,... | collective-permute-start | bytes 1769480 | tf_op jit(solution)/shard_map/ppermute | solution.py:188
  616.6 40.0 %collective-permute-start.100 = (bf16[192,768]{1,0:T(8,128)(2,1)S(1)}, bf16[192,768]{1,0:T(8,128)(2,1)S(1)}, u32[]{:S(2)}, u32[]{:S(2)}) collective-permute-start(bf16[192,768]{1,0:T(8,128)(2,1)S(1)} %get-tuple-element.478), channel_id=1, source_target_pairs={{0,4},{1,5},{2,6},{3,7},{4,12},{5,13},{6,14},{7,15},{8,0},{9,1},{1... | collective-permute-start | bytes 884744 | tf_op jit(solution)/shard_map/ppermute | solution.py:333
  629.3 30.3 %collective-permute-start.98 = (bf16[192,768]{1,0:T(8,128)(2,1)S(1)}, bf16[192,768]{1,0:T(8,128)(2,1)S(1)}, u32[]{:S(2)}, u32[]{:S(2)}) collective-permute-start(bf16[192,768]{1,0:T(8,128)(2,1)S(1)} %get-tuple-element.480), channel_id=1, source_target_pairs={{0,8},{1,9},{2,10},{3,11},{4,0},{5,1},{6,2},{7,3},{8,12},{9,13},{1... | collective-permute-start | bytes 884744 | tf_op jit(solution)/shard_map/ppermute | solution.py:333
  629.4 30.2 %collective-permute-start.99 = (bf16[192,768]{1,0:T(8,128)(2,1)S(1)}, bf16[192,768]{1,0:T(8,128)(2,1)S(1)}, u32[]{:S(2)}, u32[]{:S(2)}) collective-permute-start(bf16[192,768]{1,0:T(8,128)(2,1)S(1)} %get-tuple-element.479), channel_id=1, source_target_pairs={{0,12},{1,13},{2,14},{3,15},{4,8},{5,9},{6,10},{7,11},{8,4},{9,5},... | collective-permute-start | bytes 884744 | tf_op jit(solution)/shard_map/ppermute | solution.py:333
  644.7 24.0 %collective-permute-start.92 = (bf16[192,768]{1,0:T(8,128)(2,1)}, bf16[192,768]{1,0:T(8,128)(2,1)S(1)}, u32[]{:S(2)}, u32[]{:S(2)}) collective-permute-start(bf16[192,768]{1,0:T(8,128)(2,1)} %get-tuple-element.462), channel_id=1, source_target_pairs={{128,129},{129,130},{130,131},{131,128},{132,133},{133,134},{134,1... | collective-permute-start | bytes 884744 | tf_op jit(solution)/shard_map/ppermute | solution.py:316
  648.2 22.8 %collective-permute-start.93 = (bf16[192,768]{1,0:T(8,128)(2,1)}, bf16[192,768]{1,0:T(8,128)(2,1)S(1)}, u32[]{:S(2)}, u32[]{:S(2)}) collective-permute-start(bf16[192,768]{1,0:T(8,128)(2,1)} %get-tuple-element.463), channel_id=1, source_target_pairs={{128,130},{129,131},{130,128},{131,129},{132,134},{133,135},{134,1... | collective-permute-start | bytes 884744 | tf_op jit(solution)/shard_map/ppermute | solution.py:316
  656.6 64.4 %collective-permute-start.94 = (bf16[192,768]{1,0:T(8,128)(2,1)S(1)}, bf16[192,768]{1,0:T(8,128)(2,1)S(1)}, u32[]{:S(2)}, u32[]{:S(2)}) collective-permute-start(bf16[192,768]{1,0:T(8,128)(2,1)S(1)} %copy-done.61), channel_id=1, source_target_pairs={{128,131},{129,128},{130,129},{131,130},{132,135},{133,132},{134,1... | collective-permute-start | bytes 884744 | tf_op jit(solution)/shard_map/ppermute | solution.py:316
  662.3 64.2 %collective-permute-start.108 = (f32[1,3072]{1,0:T(1,128)S(1)}, f32[1,3072]{1,0:T(1,128)S(1)}, u32[]{:S(2)}, u32[]{:S(2)}) collective-permute-start(f32[1,3072]{1,0:T(1,128)S(1)} %add.187), channel_id=1, source_target_pairs={{0,1},{1,2},{2,3},{3,0},{4,5},{5,6},{6,7},{7,4},{8,9},{9,10},{10,1... | collective-permute-start | bytes 36872 | tf_op jit(solution)/shard_map/ppermute | solution.py:338
  663.3 65.6 %collective-permute-start.109 = (f32[1,3072]{1,0:T(1,128)S(1)}, f32[1,3072]{1,0:T(1,128)S(1)}, u32[]{:S(2)}, u32[]{:S(2)}) collective-permute-start(f32[1,3072]{1,0:T(1,128)S(1)} %add.187), channel_id=1, source_target_pairs={{0,2},{1,3},{2,0},{3,1},{4,6},{5,7},{6,4},{7,5},{8,10},{9,11},{10,... | collective-permute-start | bytes 36872 | tf_op jit(solution)/shard_map/ppermute | solution.py:338
  668.8 65.8 %collective-permute-start.110 = (f32[1,3072]{1,0:T(1,128)S(1)}, f32[1,3072]{1,0:T(1,128)S(1)}, u32[]{:S(2)}, u32[]{:S(2)}) collective-permute-start(f32[1,3072]{1,0:T(1,128)S(1)} %add.187), channel_id=1, source_target_pairs={{0,3},{1,0},{2,1},{3,2},{4,7},{5,4},{6,5},{7,6},{8,11},{9,8},{10,9... | collective-permute-start | bytes 36872 | tf_op jit(solution)/shard_map/ppermute | solution.py:338
  670.9 101.6 %collective-permute-start.114 = (bf16[384,1536]{1,0:T(8,128)(2,1)S(1)}, bf16[384,1536]{1,0:T(8,128)(2,1)S(1)}, u32[]{:S(2)}, u32[]{:S(2)}) collective-permute-start(bf16[384,1536]{1,0:T(8,128)(2,1)S(1)} %broadcast_select_fusion), channel_id=1, source_target_pairs={{0,128},{16,144},{32,160},{48,176},{64,192},{80,208},{96,224},{112... | collective-permute-start | bytes 3538952 | tf_op jit(solution)/shard_map/ppermute | solution.py:204
  720.9 77.4 %collective-permute-start.101 = (bf16[768,768]{1,0:T(8,128)(2,1)}, bf16[768,768]{1,0:T(8,128)(2,1)S(1)}, u32[]{:S(2)}, u32[]{:S(2)}) collective-permute-start(bf16[768,768]{1,0:T(8,128)(2,1)} %bitcast.85), channel_id=1, source_target_pairs={{0,1},{1,2},{2,3},{3,0},{4,5},{5,6},{6,7},{7,4},{8,9},{9,10},{10,1... | collective-permute-start | bytes 3538952 | tf_op jit(solution)/shard_map/ppermute | solution.py:338
  726.5 72.8 %collective-permute-start.103 = (bf16[768,768]{1,0:T(8,128)(2,1)S(1)}, bf16[768,768]{1,0:T(8,128)(2,1)S(1)}, u32[]{:S(2)}, u32[]{:S(2)}) collective-permute-start(bf16[768,768]{1,0:T(8,128)(2,1)S(1)} %bitcast.86), channel_id=1, source_target_pairs={{0,3},{1,0},{2,1},{3,2},{4,7},{5,4},{6,5},{7,6},{8,11},{9,8},{10,9... | collective-permute-start | bytes 3538952 | tf_op jit(solution)/shard_map/ppermute | solution.py:338
  728.9 64.6 %collective-permute-start.95 = (bf16[4,192,768]{2,1,0:T(8,128)(2,1)S(1)}, bf16[4,192,768]{2,1,0:T(8,128)(2,1)S(1)}, u32[]{:S(2)}, u32[]{:S(2)}) collective-permute-start(bf16[4,192,768]{2,1,0:T(8,128)(2,1)S(1)} %copy-done.24), channel_id=1, source_target_pairs={{128,136},{129,137},{130,138},{131,139},{132,128},{133,129},{134,1... | collective-permute-start | bytes 3538952 | tf_op jit(solution)/shard_map/ppermute | solution.py:320
  734.6 58.0 %collective-permute-start.111 = (f32[1,3072]{1,0:T(1,128)S(1)}, f32[1,3072]{1,0:T(1,128)S(1)}, u32[]{:S(2)}, u32[]{:S(2)}) collective-permute-start(f32[1,3072]{1,0:T(1,128)S(1)} %add_add_fusion.1), channel_id=1, source_target_pairs={{0,8},{1,9},{2,10},{3,11},{4,0},{5,1},{6,2},{7,3},{8,12},{9,13},{1... | collective-permute-start | bytes 36872 | tf_op jit(solution)/shard_map/ppermute | solution.py:333
  772.6 20.8 %collective-permute-start.112 = (f32[1,3072]{1,0:T(1,128)S(1)}, f32[1,3072]{1,0:T(1,128)S(1)}, u32[]{:S(2)}, u32[]{:S(2)}) collective-permute-start(f32[1,3072]{1,0:T(1,128)S(1)} %add_add_fusion.1), channel_id=1, source_target_pairs={{0,12},{1,13},{2,14},{3,15},{4,8},{5,9},{6,10},{7,11},{8,4},{9,5},... | collective-permute-start | bytes 36872 | tf_op jit(solution)/shard_map/ppermute | solution.py:333
  793.4 16.2 %collective-permute-start.115 = (bf16[384,768]{1,0:T(8,128)(2,1)S(1)}, bf16[384,768]{1,0:T(8,128)(2,1)S(1)}, u32[]{:S(2)}, u32[]{:S(2)}) collective-permute-start(bf16[384,768]{1,0:T(8,128)(2,1)S(1)} %broadcast_select_fusion.1), channel_id=1, source_target_pairs={{0,64},{16,80},{32,96},{48,112},{64,0},{80,16},{96,32},{112,48},{1... | collective-permute-start | bytes 1769480 | tf_op jit(solution)/shard_map/ppermute | solution.py:204
  793.5 30.0 %collective-permute-start.96 = (bf16[4,192,768]{2,1,0:T(8,128)(2,1)S(1)}, bf16[4,192,768]{2,1,0:T(8,128)(2,1)S(1)}, u32[]{:S(2)}, u32[]{:S(2)}) collective-permute-start(bf16[4,192,768]{2,1,0:T(8,128)(2,1)S(1)} %collective-permute-done.95), channel_id=1, source_target_pairs={{128,136},{129,137},{130,138},{131,139},{132,128},{133,129},{134,1... | collective-permute-start | bytes 3538952 | tf_op jit(solution)/shard_map/ppermute | solution.py:320
  798.4 29.8 %collective-permute-start.102 = (bf16[384,768]{1,0:T(8,128)(2,1)S(1)}, bf16[384,768]{1,0:T(8,128)(2,1)S(1)}, u32[]{:S(2)}, u32[]{:S(2)}) collective-permute-start(bf16[384,768]{1,0:T(8,128)(2,1)S(1)} %slice.112), channel_id=1, source_target_pairs={{0,1},{1,2},{2,3},{3,0},{4,5},{5,6},{6,7},{7,4},{8,9},{9,10},{10,1... | collective-permute-start | bytes 1769480 | tf_op jit(solution)/shard_map/ppermute | solution.py:338
  799.4 28.8 %collective-permute-start.104 = (bf16[384,768]{1,0:T(8,128)(2,1)S(1)}, bf16[384,768]{1,0:T(8,128)(2,1)S(1)}, u32[]{:S(2)}, u32[]{:S(2)}) collective-permute-start(bf16[384,768]{1,0:T(8,128)(2,1)S(1)} %slice.113), channel_id=1, source_target_pairs={{0,3},{1,0},{2,1},{3,2},{4,7},{5,4},{6,5},{7,6},{8,11},{9,8},{10,9... | collective-permute-start | bytes 1769480 | tf_op jit(solution)/shard_map/ppermute | solution.py:338
  809.8 18.6 %collective-permute-start.116 = (bf16[384,384]{1,0:T(8,128)(2,1)S(1)}, bf16[384,384]{1,0:T(8,128)(2,1)S(1)}, u32[]{:S(2)}, u32[]{:S(2)}) collective-permute-start(bf16[384,384]{1,0:T(8,128)(2,1)S(1)} %broadcast_select_fusion.2), channel_id=1, source_target_pairs={{0,32},{16,48},{32,0},{48,16},{64,96},{80,112},{96,64},{112,80},{1... | collective-permute-start | bytes 884744 | tf_op jit(solution)/shard_map/ppermute | solution.py:204
  823.4 29.5 %collective-permute-start.97 = (bf16[4,192,768]{2,1,0:T(8,128)(2,1)S(1)}, bf16[4,192,768]{2,1,0:T(8,128)(2,1)S(1)}, u32[]{:S(2)}, u32[]{:S(2)}) collective-permute-start(bf16[4,192,768]{2,1,0:T(8,128)(2,1)S(1)} %collective-permute-done.96), channel_id=1, source_target_pairs={{128,136},{129,137},{130,138},{131,139},{132,128},{133,129},{134,1... | collective-permute-start | bytes 3538952 | tf_op jit(solution)/shard_map/ppermute | solution.py:320
  828.6 31.6 %collective-permute-start.117 = (bf16[384,192]{1,0:T(8,128)(2,1)S(1)}, bf16[384,192]{1,0:T(8,128)(2,1)S(1)}, u32[]{:S(2)}, u32[]{:S(2)}) collective-permute-start(bf16[384,192]{1,0:T(8,128)(2,1)S(1)} %broadcast_select_fusion.3), channel_id=1, source_target_pairs={{0,16},{16,0},{32,48},{48,32},{64,80},{80,64},{96,112},{112,96},{1... | collective-permute-start | bytes 442376 | tf_op jit(solution)/shard_map/ppermute | solution.py:204
  857.4 10.2 %collective-permute-start.105 = (bf16[192,768]{1,0:T(8,128)(2,1)S(1)}, bf16[192,768]{1,0:T(8,128)(2,1)S(1)}, u32[]{:S(2)}, u32[]{:S(2)}) collective-permute-start(bf16[192,768]{1,0:T(8,128)(2,1)S(1)} %get-tuple-element.476), channel_id=1, source_target_pairs={{0,8},{1,9},{2,10},{3,11},{4,0},{5,1},{6,2},{7,3},{8,12},{9,13},{1... | collective-permute-start | bytes 884744 | tf_op jit(solution)/shard_map/ppermute | solution.py:333
  860.4 16.3 %collective-permute-start.106 = (bf16[192,768]{1,0:T(8,128)(2,1)S(1)}, bf16[192,768]{1,0:T(8,128)(2,1)S(1)}, u32[]{:S(2)}, u32[]{:S(2)}) collective-permute-start(bf16[192,768]{1,0:T(8,128)(2,1)S(1)} %get-tuple-element.475), channel_id=1, source_target_pairs={{0,12},{1,13},{2,14},{3,15},{4,8},{5,9},{6,10},{7,11},{8,4},{9,5},... | collective-permute-start | bytes 884744 | tf_op jit(solution)/shard_map/ppermute | solution.py:333
  863.4 22.2 %collective-permute-start.107 = (bf16[192,768]{1,0:T(8,128)(2,1)S(1)}, bf16[192,768]{1,0:T(8,128)(2,1)S(1)}, u32[]{:S(2)}, u32[]{:S(2)}) collective-permute-start(bf16[192,768]{1,0:T(8,128)(2,1)S(1)} %get-tuple-element.474), channel_id=1, source_target_pairs={{0,4},{1,5},{2,6},{3,7},{4,12},{5,13},{6,14},{7,15},{8,0},{9,1},{1... | collective-permute-start | bytes 884744 | tf_op jit(solution)/shard_map/ppermute | solution.py:333
  (116 other events, 1734.3 us)

commit v8 on v7

--- a/solution.py
+++ b/solution.py
@@ -438,7 +438,7 @@
         lax.dynamic_slice_in_dim(slope, to_z[k] * wide, wide, axis=1) for k in range(4)
     ]
     slope = slope[:1] + [shift_z(slope[k], k, count) for k in (1, 2, 3)]
-    behind_slope, *terms = pin(here, [passed[m][1] for m in range(micros)], slope[1:])
+    behind_slope, *terms = pin(here, [passed[m][1] for m in range(micros)], (*slope[1:], late[-1]))
     slope = from_all_y(pile(slope, here, 0, sections).reshape(-1, wide), count)
     slope = jnp.stack(slope).reshape(4, 4, micros * rows, features // 4)
     product = jnp.einsum(

time: 898 us -> 883 us (0.983)
  the two profiles are of different devices: /device:TPU:128 before, /device:TPU:41 now
where the time goes in v8:
time: 883 us; the launch traced here: 872 us
  waiting for transfers between devices  369 us (42%)
  starting transfers between devices  347 us (39%)
  Pallas kernels  101 us (11%)
  local copies, waits for them, and re-layouts  28.2 us (3%)
  between operations  18.2 us (2%)
    ppermute x60, starting transfers between devices, hop(): return lax.ppermute(block, ('section', 'dp'), sorted(pairs))  248 us
    ppermute x15, waiting for transfers between devices, shift_z(): return lax.ppermute(block, 'dp', pairs)  127 us
    pallas_call x74, Pallas kernels, call(): pl.pallas_call(kernel, out_shape=outs, in_specs=in_specs, out_specs=out_s...  101 us
    ppermute x60, waiting for transfers between devices, hop(): return lax.ppermute(block, ('section', 'dp'), sorted(pairs))  66.8 us
    ppermute x6, waiting for transfers between devices, exchange(): blocks.append(lax.ppermute(blocks[-1], ('section', 'dp'), pairs))  63.5 us
    ppermute x4, waiting for transfers between devices, spread(): arrived = lax.ppermute(jnp.where(upper, low, high), 'section', pairs)  55.7 us
    ppermute x27, waiting for transfers between devices, shift_y(): return lax.ppermute(block, 'dp', pairs)  50.9 us
    ppermute x4, starting transfers between devices, spread(): arrived = lax.ppermute(jnp.where(upper, low, high), 'section', pairs)  40.2 us
  transfers between devices with their start and end apart: 118, of which 50 were waited for; matrix products, arithmetic and copies ran while one was open for 2% of the time, Pallas kernels for 9%

profile of v8, /device:TPU:41, one launch (start us, length us, event | category | flops | bytes accessed | tf_op | source)
XLA Modules:
  0.0 872.2 jit_solution(17306072163168867862)
XLA Ops:
  4.8 6.4 collective-permute-done.4
  18.0 6.4 collective-permute-done.8.refs_6_
  27.8 17.4 %collective-permute-done.14.refs_12_ = bf16[192,2304]{1,0:T(8,128)(2,1)S(1)} collective-permute-done((bf16[192,2304]{1,0:T(8,128)(2,1)S(1)}, bf16[192,2304]{1,0:T(8,128)(2,1)S(1)}, u32[]{:S(2)}, u32[]{:S(2)}) %collective-permute-start.14) | collective-permute-done | bytes 884768 | tf_op jit(solution)/shard_map/ppermute | solution.py:333
  45.5 25.0 %collective-permute-done.13.refs_11_ = bf16[768,768]{1,0:T(8,128)(2,1)S(1)} collective-permute-done((bf16[768,768]{1,0:T(8,128)(2,1)S(1)}, bf16[768,768]{1,0:T(8,128)(2,1)S(1)}, u32[]{:S(2)}, u32[]{:S(2)}) %collective-permute-start.13) | collective-permute-done | bytes 1179680 | tf_op jit(solution)/shard_map/ppermute | solution.py:333
  72.0 17.4 %collective-permute-done.20.refs_18_ = bf16[192,2304]{1,0:T(8,128)(2,1)S(1)} collective-permute-done((bf16[192,2304]{1,0:T(8,128)(2,1)S(1)}, bf16[192,2304]{1,0:T(8,128)(2,1)S(1)}, u32[]{:S(2)}, u32[]{:S(2)}) %collective-permute-start.20) | collective-permute-done | bytes 884768 | tf_op jit(solution)/shard_map/ppermute | solution.py:333
  91.1 23.7 %collective-permute-done.19.refs_17_ = bf16[768,768]{1,0:T(8,128)(2,1)} collective-permute-done((bf16[768,768]{1,0:T(8,128)(2,1)S(1)}, bf16[768,768]{1,0:T(8,128)(2,1)}, u32[]{:S(2)}, u32[]{:S(2)}) %collective-permute-start.19) | collective-permute-done | bytes 1179680 | tf_op jit(solution)/shard_map/ppermute | solution.py:333
  129.7 7.0 collective-permute-done.11.refs_9_
  138.3 7.8 collective-permute-done.17.refs_15_
  147.2 8.4 collective-permute-done.23.refs_21_
  157.4 7.2 shard_map.93.matrix.source
  165.3 10.6 %collective-permute-start.41 = (bf16[96,3072]{1,0:T(8,128)(2,1)S(1)}, bf16[96,3072]{1,0:T(8,128)(2,1)S(1)}, u32[]{:S(2)}, u32[]{:S(2)}) collective-permute-start(bf16[96,3072]{1,0:T(8,128)(2,1)S(1)} %get-tuple-element.300), channel_id=1, source_target_pairs={{0,16},{1,17},{2,18},{3,19},{4,20},{5,21},{6,22},{7,23},{8,24},{9,... | collective-permute-start | bytes 1769480 | tf_op jit(solution)/shard_map/ppermute | solution.py:188
  176.8 6.4 collective-permute-start.26
  183.2 5.1 shard_map.112
  190.2 5.1 shard_map.95
  201.2 5.3 collective-permute-done.27.x_in
  217.3 8.7 collective-permute-start.46
  228.6 5.0 collective-permute-done.46.x_in
  234.9 5.0 collective-permute-done.31.x_in
  244.4 4.1 collective-permute-start.33
  248.6 6.4 copy-done.3
  254.9 5.3 shard_map.102.refs_3_.turned
  266.7 4.3 collective-permute-start.50
  273.6 5.0 collective-permute-done.50.x_in
  279.9 5.0 collective-permute-done.35.x_in
  289.3 3.8 shard_map.123
  301.6 3.6 collective-permute-start.39
  305.3 4.8 collective-permute-done.54.x_in
  311.4 5.0 collective-permute-done.39.x_in
  320.2 3.1 shard_map.127
  329.2 3.9 collective-permute-start.58
  342.2 3.5 collective-permute-start.59
  345.7 21.2 %collective-permute-done.59 = bf16[4,192,768]{2,1,0:T(8,128)(2,1)S(1)} collective-permute-done((bf16[4,192,768]{2,1,0:T(8,128)(2,1)}, bf16[4,192,768]{2,1,0:T(8,128)(2,1)S(1)}, u32[]{:S(2)}, u32[]{:S(2)}) %collective-permute-start.59) | collective-permute-done | bytes 1179680 | tf_op jit(solution)/shard_map/ppermute | solution.py:320
  366.9 3.4 collective-permute-start.60
  370.3 21.0 %collective-permute-done.60 = bf16[4,192,768]{2,1,0:T(8,128)(2,1)S(1)} collective-permute-done((bf16[4,192,768]{2,1,0:T(8,128)(2,1)S(1)}, bf16[4,192,768]{2,1,0:T(8,128)(2,1)S(1)}, u32[]{:S(2)}, u32[]{:S(2)}) %collective-permute-start.60) | collective-permute-done | bytes 1179680 | tf_op jit(solution)/shard_map/ppermute | solution.py:320
  391.3 3.4 collective-permute-start.61
  394.7 21.4 %collective-permute-done.61.refs_0_ = bf16[4,192,768]{2,1,0:T(8,128)(2,1)S(1)} collective-permute-done((bf16[4,192,768]{2,1,0:T(8,128)(2,1)S(1)}, bf16[4,192,768]{2,1,0:T(8,128)(2,1)S(1)}, u32[]{:S(2)}, u32[]{:S(2)}) %collective-permute-start.61) | collective-permute-done | bytes 1179680 | tf_op jit(solution)/shard_map/ppermute | solution.py:320
  420.6 40.5 %collective-permute-start.78 = (bf16[96,3072]{1,0:T(8,128)(2,1)S(1)}, bf16[96,3072]{1,0:T(8,128)(2,1)S(1)}, u32[]{:S(2)}, u32[]{:S(2)}) collective-permute-start(bf16[96,3072]{1,0:T(8,128)(2,1)S(1)} %get-tuple-element.418), channel_id=1, source_target_pairs={{16,32},{17,33},{18,34},{19,35},{20,36},{21,37},{22,38},{23,39},{2... | collective-permute-start | bytes 1769480 | tf_op jit(solution)/shard_map/ppermute | solution.py:188
  463.7 5.0 collective-permute-done.78.u_in
  471.4 3.6 collective-permute-done.63.u_in
  483.8 3.4 shard_map.150
  487.2 37.7 %collective-permute-start.82 = (bf16[96,3072]{1,0:T(8,128)(2,1)S(1)}, bf16[96,3072]{1,0:T(8,128)(2,1)S(1)}, u32[]{:S(2)}, u32[]{:S(2)}) collective-permute-start(bf16[96,3072]{1,0:T(8,128)(2,1)S(1)} %get-tuple-element.430), channel_id=1, source_target_pairs={{16,32},{17,33},{18,34},{19,35},{20,36},{21,37},{22,38},{23,39},{2... | collective-permute-start | bytes 1769480 | tf_op jit(solution)/shard_map/ppermute | solution.py:188
  527.4 5.0 collective-permute-done.82.u_in
  535.0 3.8 collective-permute-done.67.u_in
  549.1 6.6 collective-permute-start.86
  558.4 4.9 collective-permute-done.86.u_in
  565.8 3.8 collective-permute-done.71.u_in
  576.7 3.2 shard_map.141
  581.2 56.5 %collective-permute-start.90 = (bf16[96,3072]{1,0:T(8,128)(2,1)S(1)}, bf16[96,3072]{1,0:T(8,128)(2,1)S(1)}, u32[]{:S(2)}, u32[]{:S(2)}) collective-permute-start(bf16[96,3072]{1,0:T(8,128)(2,1)S(1)} %get-tuple-element.454), channel_id=1, source_target_pairs={{16,32},{17,33},{18,34},{19,35},{20,36},{21,37},{22,38},{23,39},{2... | collective-permute-start | bytes 1769480 | tf_op jit(solution)/shard_map/ppermute | solution.py:188
  638.2 6.0 collective-permute-start.75
  645.2 4.8 shard_map.159
  651.9 4.6 shard_map.143
  679.2 3.3 collective-permute-done.98.refs_1_.refs_2_
  682.6 13.2 %collective-permute-done.99.refs_2_.refs_3_ = bf16[192,768]{1,0:T(8,128)(2,1)S(1)} collective-permute-done((bf16[192,768]{1,0:T(8,128)(2,1)S(1)}, bf16[192,768]{1,0:T(8,128)(2,1)S(1)}, u32[]{:S(2)}, u32[]{:S(2)}) %collective-permute-start.99) | collective-permute-done | bytes 294944 | tf_op jit(solution)/shard_map/ppermute | solution.py:333
  711.5 3.6 shard_map.166
  715.1 6.9 collective-permute-done.101
  726.8 6.9 collective-permute-done.102
  743.1 37.7 %collective-permute-start.114 = (bf16[384,1536]{1,0:T(8,128)(2,1)S(1)}, bf16[384,1536]{1,0:T(8,128)(2,1)S(1)}, u32[]{:S(2)}, u32[]{:S(2)}) collective-permute-start(bf16[384,1536]{1,0:T(8,128)(2,1)S(1)} %broadcast_select_fusion), channel_id=1, source_target_pairs={{0,128},{16,144},{32,160},{48,176},{64,192},{80,208},{96,224},{112... | collective-permute-start | bytes 3538952 | tf_op jit(solution)/shard_map/ppermute | solution.py:204
  780.9 5.7 bitcast_convert_fusion
  787.6 3.1 collective-permute-start.111
  791.2 32.6 %collective-permute-done.114 = bf16[384,1536]{1,0:T(8,128)(2,1)S(1)} collective-permute-done((bf16[384,1536]{1,0:T(8,128)(2,1)S(1)}, bf16[384,1536]{1,0:T(8,128)(2,1)S(1)}, u32[]{:S(2)}, u32[]{:S(2)}) %collective-permute-start.114) | collective-permute-done | bytes 1179680 | tf_op jit(solution)/shard_map/ppermute | solution.py:204
  824.1 9.6 %collective-permute-done.111 = f32[1,3072]{1,0:T(1,128)S(1)} collective-permute-done((f32[1,3072]{1,0:T(1,128)S(1)}, f32[1,3072]{1,0:T(1,128)S(1)}, u32[]{:S(2)}, u32[]{:S(2)}) %collective-permute-start.111) | collective-permute-done | bytes 12320 | tf_op jit(solution)/shard_map/ppermute | solution.py:333
  835.4 8.6 collective-permute-done.112
  844.6 15.2 %collective-permute-done.115 = bf16[384,768]{1,0:T(8,128)(2,1)S(1)} collective-permute-done((bf16[384,768]{1,0:T(8,128)(2,1)S(1)}, bf16[384,768]{1,0:T(8,128)(2,1)S(1)}, u32[]{:S(2)}, u32[]{:S(2)}) %collective-permute-start.115) | collective-permute-done | bytes 589856 | tf_op jit(solution)/shard_map/ppermute | solution.py:204
  860.2 6.9 collective-permute-done.116
  (411 shorter events, 205.2 us)
Async XLA Ops:
  1.9 22.4 %collective-permute-start.8 = (bf16[192,2304]{1,0:T(8,128)(2,1)S(1)}, bf16[192,2304]{1,0:T(8,128)(2,1)S(1)}, u32[]{:S(2)}, u32[]{:S(2)}) collective-permute-start(bf16[192,2304]{1,0:T(8,128)(2,1)S(1)} %slice.100.refs_0_), channel_id=1, source_target_pairs={{0,8},{1,9},{2,10},{3,11},{4,0},{5,1},{6,2},{7,3},{8,12},{9,13},{1... | collective-permute-start | bytes 2654216 | tf_op jit(solution)/shard_map/ppermute | solution.py:333
  12.6 32.6 %collective-permute-start = (bf16[192,2304]{1,0:T(8,128)(2,1)S(1)}, bf16[192,2304]{1,0:T(8,128)(2,1)S(1)}, u32[]{:S(2)}, u32[]{:S(2)}) collective-permute-start(bf16[192,2304]{1,0:T(8,128)(2,1)S(1)} %slice.100.refs_0_), channel_id=1, source_target_pairs={{0,1},{1,2},{2,3},{3,0},{4,5},{5,6},{6,7},{7,4},{8,9},{9,10},{10,1... | collective-permute-start | bytes 2654216 | tf_op jit(solution)/shard_map/ppermute | solution.py:338
  24.4 20.8 %collective-permute-start.14 = (bf16[192,2304]{1,0:T(8,128)(2,1)S(1)}, bf16[192,2304]{1,0:T(8,128)(2,1)S(1)}, u32[]{:S(2)}, u32[]{:S(2)}) collective-permute-start(bf16[192,2304]{1,0:T(8,128)(2,1)S(1)} %collective-permute-done.8.refs_6_), channel_id=1, source_target_pairs={{0,8},{1,9},{2,10},{3,11},{4,0},{5,1},{6,2},{7,3},{8,12},{9,13},{1... | collective-permute-start | bytes 2654216 | tf_op jit(solution)/shard_map/ppermute | solution.py:333
  24.4 46.1 %collective-permute-start.13 = (bf16[768,768]{1,0:T(8,128)(2,1)S(1)}, bf16[768,768]{1,0:T(8,128)(2,1)S(1)}, u32[]{:S(2)}, u32[]{:S(2)}) collective-permute-start(bf16[768,768]{1,0:T(8,128)(2,1)S(1)} %constant_dynamic-update-slice_fusion.refs_5_), channel_id=1, source_target_pairs={{0,8},{1,9},{2,10},{3,11},{4,0},{5,1},{6,2},{7,3},{8,12},{9,13},{1... | collective-permute-start | bytes 3538952 | tf_op jit(solution)/shard_map/ppermute | solution.py:333
  26.4 44.1 %collective-permute-start.1 = (bf16[192,2304]{1,0:T(8,128)(2,1)S(1)}, bf16[192,2304]{1,0:T(8,128)(2,1)S(1)}, u32[]{:S(2)}, u32[]{:S(2)}) collective-permute-start(bf16[192,2304]{1,0:T(8,128)(2,1)S(1)} %slice.100.refs_0_), channel_id=1, source_target_pairs={{0,3},{1,0},{2,1},{3,2},{4,7},{5,4},{6,5},{7,6},{8,11},{9,8},{10,9... | collective-permute-start | bytes 2654216 | tf_op jit(solution)/shard_map/ppermute | solution.py:338
  26.5 45.3 %collective-permute-start.9 = (bf16[192,2304]{1,0:T(8,128)(2,1)S(1)}, bf16[192,2304]{1,0:T(8,128)(2,1)S(1)}, u32[]{:S(2)}, u32[]{:S(2)}) collective-permute-start(bf16[192,2304]{1,0:T(8,128)(2,1)S(1)} %collective-permute-done.8.refs_6_), channel_id=1, source_target_pairs={{0,1},{1,2},{2,3},{3,0},{4,5},{5,6},{6,7},{7,4},{8,9},{9,10},{10,1... | collective-permute-start | bytes 2654216 | tf_op jit(solution)/shard_map/ppermute | solution.py:338
  45.2 44.2 %collective-permute-start.20 = (bf16[192,2304]{1,0:T(8,128)(2,1)S(1)}, bf16[192,2304]{1,0:T(8,128)(2,1)S(1)}, u32[]{:S(2)}, u32[]{:S(2)}) collective-permute-start(bf16[192,2304]{1,0:T(8,128)(2,1)S(1)} %collective-permute-done.14.refs_12_), channel_id=1, source_target_pairs={{0,8},{1,9},{2,10},{3,11},{4,0},{5,1},{6,2},{7,3},{8,12},{9,13},{1... | collective-permute-start | bytes 2654216 | tf_op jit(solution)/shard_map/ppermute | solution.py:333
  45.2 45.7 %collective-permute-start.10 = (bf16[192,2304]{1,0:T(8,128)(2,1)S(1)}, bf16[192,2304]{1,0:T(8,128)(2,1)S(1)}, u32[]{:S(2)}, u32[]{:S(2)}) collective-permute-start(bf16[192,2304]{1,0:T(8,128)(2,1)S(1)} %collective-permute-done.8.refs_6_), channel_id=1, source_target_pairs={{0,3},{1,0},{2,1},{3,2},{4,7},{5,4},{6,5},{7,6},{8,11},{9,8},{10,9... | collective-permute-start | bytes 2654216 | tf_op jit(solution)/shard_map/ppermute | solution.py:338
  70.5 44.3 %collective-permute-start.19 = (bf16[768,768]{1,0:T(8,128)(2,1)S(1)}, bf16[768,768]{1,0:T(8,128)(2,1)}, u32[]{:S(2)}, u32[]{:S(2)}) collective-permute-start(bf16[768,768]{1,0:T(8,128)(2,1)S(1)} %collective-permute-done.13.refs_11_), channel_id=1, source_target_pairs={{0,8},{1,9},{2,10},{3,11},{4,0},{5,1},{6,2},{7,3},{8,12},{9,13},{1... | collective-permute-start | bytes 3538952 | tf_op jit(solution)/shard_map/ppermute | solution.py:333
  70.5 46.8 %collective-permute-start.15 = (bf16[192,2304]{1,0:T(8,128)(2,1)S(1)}, bf16[192,2304]{1,0:T(8,128)(2,1)S(1)}, u32[]{:S(2)}, u32[]{:S(2)}) collective-permute-start(bf16[192,2304]{1,0:T(8,128)(2,1)S(1)} %collective-permute-done.14.refs_12_), channel_id=1, source_target_pairs={{0,1},{1,2},{2,3},{3,0},{4,5},{5,6},{6,7},{7,4},{8,9},{9,10},{10,1... | collective-permute-start | bytes 2654216 | tf_op jit(solution)/shard_map/ppermute | solution.py:338
  71.9 46.8 %collective-permute-start.16 = (bf16[192,2304]{1,0:T(8,128)(2,1)S(1)}, bf16[192,2304]{1,0:T(8,128)(2,1)}, u32[]{:S(2)}, u32[]{:S(2)}) collective-permute-start(bf16[192,2304]{1,0:T(8,128)(2,1)S(1)} %collective-permute-done.14.refs_12_), channel_id=1, source_target_pairs={{0,3},{1,0},{2,1},{3,2},{4,7},{5,4},{6,5},{7,6},{8,11},{9,8},{10,9... | collective-permute-start | bytes 2654216 | tf_op jit(solution)/shard_map/ppermute | solution.py:338
  89.4 29.5 %collective-permute-start.21 = (bf16[192,2304]{1,0:T(8,128)(2,1)S(1)}, bf16[192,2304]{1,0:T(8,128)(2,1)}, u32[]{:S(2)}, u32[]{:S(2)}) collective-permute-start(bf16[192,2304]{1,0:T(8,128)(2,1)S(1)} %collective-permute-done.20.refs_18_), channel_id=1, source_target_pairs={{0,1},{1,2},{2,3},{3,0},{4,5},{5,6},{6,7},{7,4},{8,9},{9,10},{10,1... | collective-permute-start | bytes 2654216 | tf_op jit(solution)/shard_map/ppermute | solution.py:338
  90.9 29.4 %collective-permute-start.22 = (bf16[192,2304]{1,0:T(8,128)(2,1)S(1)}, bf16[192,2304]{1,0:T(8,128)(2,1)}, u32[]{:S(2)}, u32[]{:S(2)}) collective-permute-start(bf16[192,2304]{1,0:T(8,128)(2,1)S(1)} %collective-permute-done.20.refs_18_), channel_id=1, source_target_pairs={{0,3},{1,0},{2,1},{3,2},{4,7},{5,4},{6,5},{7,6},{8,11},{9,8},{10,9... | collective-permute-start | bytes 2654216 | tf_op jit(solution)/shard_map/ppermute | solution.py:338
  114.8 41.8 %collective-permute-start.25 = (bf16[768,768]{1,0:T(8,128)(2,1)}, bf16[768,768]{1,0:T(8,128)(2,1)}, u32[]{:S(2)}, u32[]{:S(2)}) collective-permute-start(bf16[768,768]{1,0:T(8,128)(2,1)} %collective-permute-done.19.refs_17_), channel_id=1, source_target_pairs={{0,8},{1,9},{2,10},{3,11},{4,0},{5,1},{6,2},{7,3},{8,12},{9,13},{1... | collective-permute-start | bytes 3538952 | tf_op jit(solution)/shard_map/ppermute | solution.py:333
  118.9 17.7 %collective-permute-start.11 = (bf16[96,2304]{1,0:T(8,128)(2,1)}, bf16[96,2304]{1,0:T(8,128)(2,1)S(1)}, u32[]{:S(2)}, u32[]{:S(2)}) collective-permute-start(bf16[96,2304]{1,0:T(8,128)(2,1)} %slice.106), channel_id=1, source_target_pairs={{0,1},{1,2},{2,3},{3,0},{4,5},{5,6},{6,7},{7,4},{8,9},{9,10},{10,1... | collective-permute-start | bytes 1327112 | tf_op jit(solution)/shard_map/ppermute | solution.py:338
  120.2 17.7 %collective-permute-start.12 = (bf16[96,2304]{1,0:T(8,128)(2,1)S(1)}, bf16[96,2304]{1,0:T(8,128)(2,1)S(1)}, u32[]{:S(2)}, u32[]{:S(2)}) collective-permute-start(bf16[96,2304]{1,0:T(8,128)(2,1)S(1)} %slice.107), channel_id=1, source_target_pairs={{0,3},{1,0},{2,1},{3,2},{4,7},{5,4},{6,5},{7,6},{8,11},{9,8},{10,9... | collective-permute-start | bytes 1327112 | tf_op jit(solution)/shard_map/ppermute | solution.py:338
  127.2 18.9 %collective-permute-start.17 = (bf16[96,2304]{1,0:T(8,128)(2,1)S(1)}, bf16[96,2304]{1,0:T(8,128)(2,1)S(1)}, u32[]{:S(2)}, u32[]{:S(2)}) collective-permute-start(bf16[96,2304]{1,0:T(8,128)(2,1)S(1)} %slice.108), channel_id=1, source_target_pairs={{0,1},{1,2},{2,3},{3,0},{4,5},{5,6},{6,7},{7,4},{8,9},{9,10},{10,1... | collective-permute-start | bytes 1327112 | tf_op jit(solution)/shard_map/ppermute | solution.py:338
  128.5 18.7 %collective-permute-start.18 = (bf16[96,2304]{1,0:T(8,128)(2,1)S(1)}, bf16[96,2304]{1,0:T(8,128)(2,1)S(1)}, u32[]{:S(2)}, u32[]{:S(2)}) collective-permute-start(bf16[96,2304]{1,0:T(8,128)(2,1)S(1)} %slice.109), channel_id=1, source_target_pairs={{0,3},{1,0},{2,1},{3,2},{4,7},{5,4},{6,5},{7,6},{8,11},{9,8},{10,9... | collective-permute-start | bytes 1327112 | tf_op jit(solution)/shard_map/ppermute | solution.py:338
  136.7 18.9 %collective-permute-start.23 = (bf16[96,2304]{1,0:T(8,128)(2,1)S(1)}, bf16[96,2304]{1,0:T(8,128)(2,1)S(1)}, u32[]{:S(2)}, u32[]{:S(2)}) collective-permute-start(bf16[96,2304]{1,0:T(8,128)(2,1)S(1)} %slice.110), channel_id=1, source_target_pairs={{0,1},{1,2},{2,3},{3,0},{4,5},{5,6},{6,7},{7,4},{8,9},{9,10},{10,1... | collective-permute-start | bytes 1327112 | tf_op jit(solution)/shard_map/ppermute | solution.py:338
  138.0 18.7 %collective-permute-start.24 = (bf16[96,2304]{1,0:T(8,128)(2,1)S(1)}, bf16[96,2304]{1,0:T(8,128)(2,1)S(1)}, u32[]{:S(2)}, u32[]{:S(2)}) collective-permute-start(bf16[96,2304]{1,0:T(8,128)(2,1)S(1)} %slice.111), channel_id=1, source_target_pairs={{0,3},{1,0},{2,1},{3,2},{4,7},{5,4},{6,5},{7,6},{8,11},{9,8},{10,9... | collective-permute-start | bytes 1327112 | tf_op jit(solution)/shard_map/ppermute | solution.py:338
  165.3 17.9 %collective-permute-start.41 = (bf16[96,3072]{1,0:T(8,128)(2,1)S(1)}, bf16[96,3072]{1,0:T(8,128)(2,1)S(1)}, u32[]{:S(2)}, u32[]{:S(2)}) collective-permute-start(bf16[96,3072]{1,0:T(8,128)(2,1)S(1)} %get-tuple-element.300), channel_id=1, source_target_pairs={{0,16},{1,17},{2,18},{3,19},{4,20},{5,21},{6,22},{7,23},{8,24},{9,... | collective-permute-start | bytes 1769480 | tf_op jit(solution)/shard_map/ppermute | solution.py:188
  176.8 13.5 %collective-permute-start.26 = (bf16[96,3072]{1,0:T(8,128)(2,1)S(1)}, bf16[96,3072]{1,0:T(8,128)(2,1)S(1)}, u32[]{:S(2)}, u32[]{:S(2)}) collective-permute-start(bf16[96,3072]{1,0:T(8,128)(2,1)S(1)} %get-tuple-element.239), channel_id=1, source_target_pairs={{0,16},{1,17},{2,18},{3,19},{4,20},{5,21},{6,22},{7,23},{8,24},{9,... | collective-permute-start | bytes 1769480 | tf_op jit(solution)/shard_map/ppermute | solution.py:188
  188.3 11.2 %collective-permute-start.42 = (bf16[96,3072]{1,0:T(8,128)(2,1)S(1)}, bf16[96,3072]{1,0:T(8,128)(2,1)S(1)}, u32[]{:S(2)}, u32[]{:S(2)}) collective-permute-start(bf16[96,3072]{1,0:T(8,128)(2,1)S(1)} %get-tuple-element.304), channel_id=1, source_target_pairs={{16,32},{17,33},{18,34},{19,35},{20,36},{21,37},{22,38},{23,39},{2... | collective-permute-start | bytes 1769480 | tf_op jit(solution)/shard_map/ppermute | solution.py:188
  195.3 11.2 %collective-permute-start.27 = (bf16[96,3072]{1,0:T(8,128)(2,1)S(1)}, bf16[96,3072]{1,0:T(8,128)(2,1)S(1)}, u32[]{:S(2)}, u32[]{:S(2)}) collective-permute-start(bf16[96,3072]{1,0:T(8,128)(2,1)S(1)} %get-tuple-element.243), channel_id=1, source_target_pairs={{16,32},{17,33},{18,34},{19,35},{20,36},{21,37},{22,38},{23,39},{2... | collective-permute-start | bytes 1769480 | tf_op jit(solution)/shard_map/ppermute | solution.py:188
  213.9 12.0 %collective-permute-start.30 = (bf16[96,3072]{1,0:T(8,128)(2,1)S(1)}, bf16[96,3072]{1,0:T(8,128)(2,1)S(1)}, u32[]{:S(2)}, u32[]{:S(2)}) collective-permute-start(bf16[96,3072]{1,0:T(8,128)(2,1)S(1)} %get-tuple-element.255), channel_id=1, source_target_pairs={{0,16},{1,17},{2,18},{3,19},{4,20},{5,21},{6,22},{7,23},{8,24},{9,... | collective-permute-start | bytes 1769480 | tf_op jit(solution)/shard_map/ppermute | solution.py:188
  217.3 16.2 %collective-permute-start.46 = (bf16[96,3072]{1,0:T(8,128)(2,1)S(1)}, bf16[96,3072]{1,0:T(8,128)(2,1)S(1)}, u32[]{:S(2)}, u32[]{:S(2)}) collective-permute-start(bf16[96,3072]{1,0:T(8,128)(2,1)S(1)} %get-tuple-element.320), channel_id=1, source_target_pairs={{16,32},{17,33},{18,34},{19,35},{20,36},{21,37},{22,38},{23,39},{2... | collective-permute-start | bytes 1769480 | tf_op jit(solution)/shard_map/ppermute | solution.py:188
  226.6 13.2 %collective-permute-start.31 = (bf16[96,3072]{1,0:T(8,128)(2,1)S(1)}, bf16[96,3072]{1,0:T(8,128)(2,1)S(1)}, u32[]{:S(2)}, u32[]{:S(2)}) collective-permute-start(bf16[96,3072]{1,0:T(8,128)(2,1)S(1)} %get-tuple-element.259), channel_id=1, source_target_pairs={{16,32},{17,33},{18,34},{19,35},{20,36},{21,37},{22,38},{23,39},{2... | collective-permute-start | bytes 1769480 | tf_op jit(solution)/shard_map/ppermute | solution.py:188
  242.2 18.0 %collective-permute-start.48 = (bf16[96,3072]{1,0:T(8,128)(2,1)S(1)}, bf16[96,3072]{1,0:T(8,128)(2,1)S(1)}, u32[]{:S(2)}, u32[]{:S(2)}) collective-permute-start(bf16[96,3072]{1,0:T(8,128)(2,1)S(1)} %get-tuple-element.328), channel_id=1, source_target_pairs={{112,128},{113,129},{114,130},{115,131},{116,132},{117,133},{118,1... | collective-permute-start | bytes 1769480 | tf_op jit(solution)/shard_map/ppermute | solution.py:188
  244.4 18.4 %collective-permute-start.33 = (bf16[96,3072]{1,0:T(8,128)(2,1)}, bf16[96,3072]{1,0:T(8,128)(2,1)S(1)}, u32[]{:S(2)}, u32[]{:S(2)}) collective-permute-start(bf16[96,3072]{1,0:T(8,128)(2,1)} %get-tuple-element.267), channel_id=1, source_target_pairs={{112,128},{113,129},{114,130},{115,131},{116,132},{117,133},{118,1... | collective-permute-start | bytes 1769480 | tf_op jit(solution)/shard_map/ppermute | solution.py:188
  266.7 11.8 %collective-permute-start.50 = (bf16[96,3072]{1,0:T(8,128)(2,1)S(1)}, bf16[96,3072]{1,0:T(8,128)(2,1)S(1)}, u32[]{:S(2)}, u32[]{:S(2)}) collective-permute-start(bf16[96,3072]{1,0:T(8,128)(2,1)S(1)} %get-tuple-element.336), channel_id=1, source_target_pairs={{16,32},{17,33},{18,34},{19,35},{20,36},{21,37},{22,38},{23,39},{2... | collective-permute-start | bytes 1769480 | tf_op jit(solution)/shard_map/ppermute | solution.py:188
  271.7 13.2 %collective-permute-start.35 = (bf16[96,3072]{1,0:T(8,128)(2,1)S(1)}, bf16[96,3072]{1,0:T(8,128)(2,1)S(1)}, u32[]{:S(2)}, u32[]{:S(2)}) collective-permute-start(bf16[96,3072]{1,0:T(8,128)(2,1)S(1)} %get-tuple-element.275), channel_id=1, source_target_pairs={{16,32},{17,33},{18,34},{19,35},{20,36},{21,37},{22,38},{23,39},{2... | collective-permute-start | bytes 1769480 | tf_op jit(solution)/shard_map/ppermute | solution.py:188
  298.8 11.2 %collective-permute-start.54 = (bf16[96,3072]{1,0:T(8,128)(2,1)S(1)}, bf16[96,3072]{1,0:T(8,128)(2,1)S(1)}, u32[]{:S(2)}, u32[]{:S(2)}) collective-permute-start(bf16[96,3072]{1,0:T(8,128)(2,1)S(1)} %get-tuple-element.352), channel_id=1, source_target_pairs={{16,32},{17,33},{18,34},{19,35},{20,36},{21,37},{22,38},{23,39},{2... | collective-permute-start | bytes 1769480 | tf_op jit(solution)/shard_map/ppermute | solution.py:188
  301.6 14.7 %collective-permute-start.39 = (bf16[96,3072]{1,0:T(8,128)(2,1)S(1)}, bf16[96,3072]{1,0:T(8,128)(2,1)S(1)}, u32[]{:S(2)}, u32[]{:S(2)}) collective-permute-start(bf16[96,3072]{1,0:T(8,128)(2,1)S(1)} %get-tuple-element.291), channel_id=1, source_target_pairs={{16,32},{17,33},{18,34},{19,35},{20,36},{21,37},{22,38},{23,39},{2... | collective-permute-start | bytes 1769480 | tf_op jit(solution)/shard_map/ppermute | solution.py:188
  342.2 24.7 %collective-permute-start.59 = (bf16[4,192,768]{2,1,0:T(8,128)(2,1)}, bf16[4,192,768]{2,1,0:T(8,128)(2,1)S(1)}, u32[]{:S(2)}, u32[]{:S(2)}) collective-permute-start(bf16[4,192,768]{2,1,0:T(8,128)(2,1)} %shard_map.128), channel_id=1, source_target_pairs={{0,8},{1,9},{2,10},{3,11},{4,0},{5,1},{6,2},{7,3},{8,12},{9,13},{1... | collective-permute-start | bytes 3538952 | tf_op jit(solution)/shard_map/ppermute | solution.py:320
  366.9 24.4 %collective-permute-start.60 = (bf16[4,192,768]{2,1,0:T(8,128)(2,1)S(1)}, bf16[4,192,768]{2,1,0:T(8,128)(2,1)S(1)}, u32[]{:S(2)}, u32[]{:S(2)}) collective-permute-start(bf16[4,192,768]{2,1,0:T(8,128)(2,1)S(1)} %collective-permute-done.59), channel_id=1, source_target_pairs={{0,8},{1,9},{2,10},{3,11},{4,0},{5,1},{6,2},{7,3},{8,12},{9,13},{1... | collective-permute-start | bytes 3538952 | tf_op jit(solution)/shard_map/ppermute | solution.py:320
  391.3 24.8 %collective-permute-start.61 = (bf16[4,192,768]{2,1,0:T(8,128)(2,1)S(1)}, bf16[4,192,768]{2,1,0:T(8,128)(2,1)S(1)}, u32[]{:S(2)}, u32[]{:S(2)}) collective-permute-start(bf16[4,192,768]{2,1,0:T(8,128)(2,1)S(1)} %collective-permute-done.60), channel_id=1, source_target_pairs={{0,8},{1,9},{2,10},{3,11},{4,0},{5,1},{6,2},{7,3},{8,12},{9,13},{1... | collective-permute-start | bytes 3538952 | tf_op jit(solution)/shard_map/ppermute | solution.py:320
  419.3 41.8 %collective-permute-start.62 = (bf16[96,3072]{1,0:T(8,128)(2,1)S(1)}, bf16[96,3072]{1,0:T(8,128)(2,1)S(1)}, u32[]{:S(2)}, u32[]{:S(2)}) collective-permute-start(bf16[96,3072]{1,0:T(8,128)(2,1)S(1)} %get-tuple-element.367), channel_id=1, source_target_pairs={{32,48},{33,49},{34,50},{35,51},{36,52},{37,53},{38,54},{39,55},{4... | collective-permute-start | bytes 1769480 | tf_op jit(solution)/shard_map/ppermute | solution.py:188
  420.6 48.1 %collective-permute-start.78 = (bf16[96,3072]{1,0:T(8,128)(2,1)S(1)}, bf16[96,3072]{1,0:T(8,128)(2,1)S(1)}, u32[]{:S(2)}, u32[]{:S(2)}) collective-permute-start(bf16[96,3072]{1,0:T(8,128)(2,1)S(1)} %get-tuple-element.418), channel_id=1, source_target_pairs={{16,32},{17,33},{18,34},{19,35},{20,36},{21,37},{22,38},{23,39},{2... | collective-permute-start | bytes 1769480 | tf_op jit(solution)/shard_map/ppermute | solution.py:188
  461.7 13.3 %collective-permute-start.63 = (bf16[96,3072]{1,0:T(8,128)(2,1)S(1)}, bf16[96,3072]{1,0:T(8,128)(2,1)S(1)}, u32[]{:S(2)}, u32[]{:S(2)}) collective-permute-start(bf16[96,3072]{1,0:T(8,128)(2,1)S(1)} %get-tuple-element.370), channel_id=1, source_target_pairs={{16,32},{17,33},{18,34},{19,35},{20,36},{21,37},{22,38},{23,39},{2... | collective-permute-start | bytes 1769480 | tf_op jit(solution)/shard_map/ppermute | solution.py:188
  483.1 41.9 %collective-permute-start.66 = (bf16[96,3072]{1,0:T(8,128)(2,1)S(1)}, bf16[96,3072]{1,0:T(8,128)(2,1)S(1)}, u32[]{:S(2)}, u32[]{:S(2)}) collective-permute-start(bf16[96,3072]{1,0:T(8,128)(2,1)S(1)} %get-tuple-element.379), channel_id=1, source_target_pairs={{32,48},{33,49},{34,50},{35,51},{36,52},{37,53},{38,54},{39,55},{4... | collective-permute-start | bytes 1769480 | tf_op jit(solution)/shard_map/ppermute | solution.py:188
  487.2 45.3 %collective-permute-start.82 = (bf16[96,3072]{1,0:T(8,128)(2,1)S(1)}, bf16[96,3072]{1,0:T(8,128)(2,1)S(1)}, u32[]{:S(2)}, u32[]{:S(2)}) collective-permute-start(bf16[96,3072]{1,0:T(8,128)(2,1)S(1)} %get-tuple-element.430), channel_id=1, source_target_pairs={{16,32},{17,33},{18,34},{19,35},{20,36},{21,37},{22,38},{23,39},{2... | collective-permute-start | bytes 1769480 | tf_op jit(solution)/shard_map/ppermute | solution.py:188
  525.5 13.3 %collective-permute-start.67 = (bf16[96,3072]{1,0:T(8,128)(2,1)S(1)}, bf16[96,3072]{1,0:T(8,128)(2,1)S(1)}, u32[]{:S(2)}, u32[]{:S(2)}) collective-permute-start(bf16[96,3072]{1,0:T(8,128)(2,1)S(1)} %get-tuple-element.382), channel_id=1, source_target_pairs={{16,32},{17,33},{18,34},{19,35},{20,36},{21,37},{22,38},{23,39},{2... | collective-permute-start | bytes 1769480 | tf_op jit(solution)/shard_map/ppermute | solution.py:188
  549.1 14.1 %collective-permute-start.86 = (bf16[96,3072]{1,0:T(8,128)(2,1)S(1)}, bf16[96,3072]{1,0:T(8,128)(2,1)S(1)}, u32[]{:S(2)}, u32[]{:S(2)}) collective-permute-start(bf16[96,3072]{1,0:T(8,128)(2,1)S(1)} %get-tuple-element.442), channel_id=1, source_target_pairs={{16,32},{17,33},{18,34},{19,35},{20,36},{21,37},{22,38},{23,39},{2... | collective-permute-start | bytes 1769480 | tf_op jit(solution)/shard_map/ppermute | solution.py:188
  556.5 13.1 %collective-permute-start.71 = (bf16[96,3072]{1,0:T(8,128)(2,1)S(1)}, bf16[96,3072]{1,0:T(8,128)(2,1)S(1)}, u32[]{:S(2)}, u32[]{:S(2)}) collective-permute-start(bf16[96,3072]{1,0:T(8,128)(2,1)S(1)} %get-tuple-element.394), channel_id=1, source_target_pairs={{16,32},{17,33},{18,34},{19,35},{20,36},{21,37},{22,38},{23,39},{2... | collective-permute-start | bytes 1769480 | tf_op jit(solution)/shard_map/ppermute | solution.py:188
  579.9 57.8 %collective-permute-start.74 = (bf16[96,3072]{1,0:T(8,128)(2,1)S(1)}, bf16[96,3072]{1,0:T(8,128)(2,1)S(1)}, u32[]{:S(2)}, u32[]{:S(2)}) collective-permute-start(bf16[96,3072]{1,0:T(8,128)(2,1)S(1)} %get-tuple-element.403), channel_id=1, source_target_pairs={{32,48},{33,49},{34,50},{35,51},{36,52},{37,53},{38,54},{39,55},{4... | collective-permute-start | bytes 1769480 | tf_op jit(solution)/shard_map/ppermute | solution.py:188
  581.2 64.0 %collective-permute-start.90 = (bf16[96,3072]{1,0:T(8,128)(2,1)S(1)}, bf16[96,3072]{1,0:T(8,128)(2,1)S(1)}, u32[]{:S(2)}, u32[]{:S(2)}) collective-permute-start(bf16[96,3072]{1,0:T(8,128)(2,1)S(1)} %get-tuple-element.454), channel_id=1, source_target_pairs={{16,32},{17,33},{18,34},{19,35},{20,36},{21,37},{22,38},{23,39},{2... | collective-permute-start | bytes 1769480 | tf_op jit(solution)/shard_map/ppermute | solution.py:188
  638.2 13.7 %collective-permute-start.75 = (bf16[96,3072]{1,0:T(8,128)(2,1)S(1)}, bf16[96,3072]{1,0:T(8,128)(2,1)S(1)}, u32[]{:S(2)}, u32[]{:S(2)}) collective-permute-start(bf16[96,3072]{1,0:T(8,128)(2,1)S(1)} %get-tuple-element.406), channel_id=1, source_target_pairs={{16,32},{17,33},{18,34},{19,35},{20,36},{21,37},{22,38},{23,39},{2... | collective-permute-start | bytes 1769480 | tf_op jit(solution)/shard_map/ppermute | solution.py:188
  675.1 20.7 %collective-permute-start.99 = (bf16[192,768]{1,0:T(8,128)(2,1)S(1)}, bf16[192,768]{1,0:T(8,128)(2,1)S(1)}, u32[]{:S(2)}, u32[]{:S(2)}) collective-permute-start(bf16[192,768]{1,0:T(8,128)(2,1)S(1)} %get-tuple-element.479), channel_id=1, source_target_pairs={{0,12},{1,13},{2,14},{3,15},{4,8},{5,9},{6,10},{7,11},{8,4},{9,5},... | collective-permute-start | bytes 884744 | tf_op jit(solution)/shard_map/ppermute | solution.py:333
  675.5 25.4 %collective-permute-start.96 = (bf16[4,192,768]{2,1,0:T(8,128)(2,1)S(1)}, bf16[4,192,768]{2,1,0:T(8,128)(2,1)}, u32[]{:S(2)}, u32[]{:S(2)}) collective-permute-start(bf16[4,192,768]{2,1,0:T(8,128)(2,1)S(1)} %collective-permute-done.95), channel_id=1, source_target_pairs={{128,136},{129,137},{130,138},{131,139},{132,128},{133,129},{134,1... | collective-permute-start | bytes 3538952 | tf_op jit(solution)/shard_map/ppermute | solution.py:320
  699.4 22.7 %collective-permute-start.101 = (bf16[768,768]{1,0:T(8,128)(2,1)}, bf16[768,768]{1,0:T(8,128)(2,1)}, u32[]{:S(2)}, u32[]{:S(2)}) collective-permute-start(bf16[768,768]{1,0:T(8,128)(2,1)} %bitcast.85), channel_id=1, source_target_pairs={{0,1},{1,2},{2,3},{3,0},{4,5},{5,6},{6,7},{7,4},{8,9},{9,10},{10,1... | collective-permute-start | bytes 3538952 | tf_op jit(solution)/shard_map/ppermute | solution.py:338
  700.4 23.8 %collective-permute-start.103 = (bf16[768,768]{1,0:T(8,128)(2,1)}, bf16[768,768]{1,0:T(8,128)(2,1)}, u32[]{:S(2)}, u32[]{:S(2)}) collective-permute-start(bf16[768,768]{1,0:T(8,128)(2,1)} %bitcast.86), channel_id=1, source_target_pairs={{0,3},{1,0},{2,1},{3,2},{4,7},{5,4},{6,5},{7,6},{8,11},{9,8},{10,9... | collective-permute-start | bytes 3538952 | tf_op jit(solution)/shard_map/ppermute | solution.py:338
  700.9 34.3 %collective-permute-start.97 = (bf16[4,192,768]{2,1,0:T(8,128)(2,1)}, bf16[4,192,768]{2,1,0:T(8,128)(2,1)S(1)}, u32[]{:S(2)}, u32[]{:S(2)}) collective-permute-start(bf16[4,192,768]{2,1,0:T(8,128)(2,1)} %collective-permute-done.96), channel_id=1, source_target_pairs={{128,136},{129,137},{130,138},{131,139},{132,128},{133,129},{134,1... | collective-permute-start | bytes 3538952 | tf_op jit(solution)/shard_map/ppermute | solution.py:320
  723.1 10.5 %collective-permute-start.102 = (bf16[384,768]{1,0:T(8,128)(2,1)S(1)}, bf16[384,768]{1,0:T(8,128)(2,1)S(1)}, u32[]{:S(2)}, u32[]{:S(2)}) collective-permute-start(bf16[384,768]{1,0:T(8,128)(2,1)S(1)} %slice.112), channel_id=1, source_target_pairs={{0,1},{1,2},{2,3},{3,0},{4,5},{5,6},{6,7},{7,4},{8,9},{9,10},{10,1... | collective-permute-start | bytes 1769480 | tf_op jit(solution)/shard_map/ppermute | solution.py:338
  738.1 49.0 %collective-permute-start.108 = (f32[1,3072]{1,0:T(1,128)S(1)}, f32[1,3072]{1,0:T(1,128)S(1)}, u32[]{:S(2)}, u32[]{:S(2)}) collective-permute-start(f32[1,3072]{1,0:T(1,128)S(1)} %add.187), channel_id=1, source_target_pairs={{0,1},{1,2},{2,3},{3,0},{4,5},{5,6},{6,7},{7,4},{8,9},{9,10},{10,1... | collective-permute-start | bytes 36872 | tf_op jit(solution)/shard_map/ppermute | solution.py:338
  739.5 48.1 %collective-permute-start.109 = (f32[1,3072]{1,0:T(1,128)S(1)}, f32[1,3072]{1,0:T(1,128)S(1)}, u32[]{:S(2)}, u32[]{:S(2)}) collective-permute-start(f32[1,3072]{1,0:T(1,128)S(1)} %add.187), channel_id=1, source_target_pairs={{0,2},{1,3},{2,0},{3,1},{4,6},{5,7},{6,4},{7,5},{8,10},{9,11},{10,... | collective-permute-start | bytes 36872 | tf_op jit(solution)/shard_map/ppermute | solution.py:338
  740.9 46.7 %collective-permute-start.110 = (f32[1,3072]{1,0:T(1,128)S(1)}, f32[1,3072]{1,0:T(1,128)S(1)}, u32[]{:S(2)}, u32[]{:S(2)}) collective-permute-start(f32[1,3072]{1,0:T(1,128)S(1)} %add.187), channel_id=1, source_target_pairs={{0,3},{1,0},{2,1},{3,2},{4,7},{5,4},{6,5},{7,6},{8,11},{9,8},{10,9... | collective-permute-start | bytes 36872 | tf_op jit(solution)/shard_map/ppermute | solution.py:338
  743.1 80.6 %collective-permute-start.114 = (bf16[384,1536]{1,0:T(8,128)(2,1)S(1)}, bf16[384,1536]{1,0:T(8,128)(2,1)S(1)}, u32[]{:S(2)}, u32[]{:S(2)}) collective-permute-start(bf16[384,1536]{1,0:T(8,128)(2,1)S(1)} %broadcast_select_fusion), channel_id=1, source_target_pairs={{0,128},{16,144},{32,160},{48,176},{64,192},{80,208},{96,224},{112... | collective-permute-start | bytes 3538952 | tf_op jit(solution)/shard_map/ppermute | solution.py:204
  787.0 73.1 %collective-permute-start.105 = (bf16[192,768]{1,0:T(8,128)(2,1)S(1)}, bf16[192,768]{1,0:T(8,128)(2,1)S(1)}, u32[]{:S(2)}, u32[]{:S(2)}) collective-permute-start(bf16[192,768]{1,0:T(8,128)(2,1)S(1)} %get-tuple-element.476), channel_id=1, source_target_pairs={{0,8},{1,9},{2,10},{3,11},{4,0},{5,1},{6,2},{7,3},{8,12},{9,13},{1... | collective-permute-start | bytes 884744 | tf_op jit(solution)/shard_map/ppermute | solution.py:333
  787.1 73.0 %collective-permute-start.106 = (bf16[192,768]{1,0:T(8,128)(2,1)S(1)}, bf16[192,768]{1,0:T(8,128)(2,1)S(1)}, u32[]{:S(2)}, u32[]{:S(2)}) collective-permute-start(bf16[192,768]{1,0:T(8,128)(2,1)S(1)} %get-tuple-element.475), channel_id=1, source_target_pairs={{0,12},{1,13},{2,14},{3,15},{4,8},{5,9},{6,10},{7,11},{8,4},{9,5},... | collective-permute-start | bytes 884744 | tf_op jit(solution)/shard_map/ppermute | solution.py:333
  787.6 46.0 %collective-permute-start.111 = (f32[1,3072]{1,0:T(1,128)S(1)}, f32[1,3072]{1,0:T(1,128)S(1)}, u32[]{:S(2)}, u32[]{:S(2)}) collective-permute-start(f32[1,3072]{1,0:T(1,128)S(1)} %add_add_fusion.1), channel_id=1, source_target_pairs={{0,8},{1,9},{2,10},{3,11},{4,0},{5,1},{6,2},{7,3},{8,12},{9,13},{1... | collective-permute-start | bytes 36872 | tf_op jit(solution)/shard_map/ppermute | solution.py:333
  790.8 53.2 %collective-permute-start.112 = (f32[1,3072]{1,0:T(1,128)S(1)}, f32[1,3072]{1,0:T(1,128)S(1)}, u32[]{:S(2)}, u32[]{:S(2)}) collective-permute-start(f32[1,3072]{1,0:T(1,128)S(1)} %add_add_fusion.1), channel_id=1, source_target_pairs={{0,12},{1,13},{2,14},{3,15},{4,8},{5,9},{6,10},{7,11},{8,4},{9,5},... | collective-permute-start | bytes 36872 | tf_op jit(solution)/shard_map/ppermute | solution.py:333
  823.8 20.2 %collective-permute-start.113 = (f32[1,3072]{1,0:T(1,128)S(1)}, f32[1,3072]{1,0:T(1,128)S(1)}, u32[]{:S(2)}, u32[]{:S(2)}) collective-permute-start(f32[1,3072]{1,0:T(1,128)S(1)} %add_add_fusion.1), channel_id=1, source_target_pairs={{0,4},{1,5},{2,6},{3,7},{4,12},{5,13},{6,14},{7,15},{8,0},{9,1},{1... | collective-permute-start | bytes 36872 | tf_op jit(solution)/shard_map/ppermute | solution.py:333
  833.7 36.2 %collective-permute-start.107 = (bf16[192,768]{1,0:T(8,128)(2,1)S(1)}, bf16[192,768]{1,0:T(8,128)(2,1)S(1)}, u32[]{:S(2)}, u32[]{:S(2)}) collective-permute-start(bf16[192,768]{1,0:T(8,128)(2,1)S(1)} %get-tuple-element.474), channel_id=1, source_target_pairs={{0,4},{1,5},{2,6},{3,7},{4,12},{5,13},{6,14},{7,15},{8,0},{9,1},{1... | collective-permute-start | bytes 884744 | tf_op jit(solution)/shard_map/ppermute | solution.py:333
  844.0 15.8 %collective-permute-start.115 = (bf16[384,768]{1,0:T(8,128)(2,1)S(1)}, bf16[384,768]{1,0:T(8,128)(2,1)S(1)}, u32[]{:S(2)}, u32[]{:S(2)}) collective-permute-start(bf16[384,768]{1,0:T(8,128)(2,1)S(1)} %broadcast_select_fusion.1), channel_id=1, source_target_pairs={{0,64},{16,80},{32,96},{48,112},{64,0},{80,16},{96,32},{112,48},{1... | collective-permute-start | bytes 1769480 | tf_op jit(solution)/shard_map/ppermute | solution.py:204
  (111 other events, 1750.7 us)
